TPU v7x, 32 devices: a whole 2x2x4 slice. The times are simulated.
32 devices in a mesh: res: 8 (over z, x), grp: 4 (over y, core).
Axes of the slice: x: 2, y: 2, z: 4, core: 2. Of those that a mesh axis runs over, the one named last changes fastest.
Arguments:
- right_side: float32 [3, 16, 64, 512], P(None, 'res', 'grp'), may hold values from -30 to 30
- accumulation: float32 [3, 3, 16, 64, 512], P(None, None, 'res', 'grp'), may hold values from -1 to 2, as said below
- transmissibility: float32 [6, 3, 3, 16, 64, 512], P(None, None, None, 'res', 'grp'), may hold values from -1 to 2, as said below
- completion: int32 [256, 256], P(('res', 'grp')), may hold values from 0 to 16383, as said below
- live_count: int32 [256], P(('res', 'grp')), may hold values from 64 to 256
- owner: int32 [256, 1], P(('res', 'grp')), may hold values from 0 to 3; in each aligned block of 8 rows (0 to 7, 8 to 15, ...) at most 4 rows name the same one
- cell_to_well: float32 [256, 3, 256], P(('res', 'grp')), may hold values from -3 to 3
- well_to_cell: float32 [256, 3, 256], P(('res', 'grp')), may hold values from -3 to 3
- inverse: float32 [32, 4, 4, 256, 256], P(('res', 'grp')), may hold values from -1 to 2
Outputs:
- solution: float32 [3, 16, 64, 512], P(None, 'res', 'grp')
- residual: float32 [3, 16, 64, 512], P(None, 'res', 'grp')
Inputs may be any that keep to these rules, and one draw needn't show every extreme that they name: `completion`: cells may repeat. Among the 8 wells of one device at most 4 name the same owner. `accumulation`: diagonal entries positive. `transmissibility`: diagonal entries positive.
All inputs are finite; a program needn't handle non-finite values.
Results may differ from a plain program's by a relative error of at most 0.0003.
Values sent between devices are 32-bit elements; how exact they have to be, the bound alone decides.
No kernel may reach another device: no remote copies, remote signals or barrier semaphores. Data moves between devices by JAX's collectives and lax.ppermute only.
A program may use at most 128 MiB of HBM per device.

v0:
```python
import jax
import jax.numpy as jnp
from jax import lax
from jax.sharding import PartitionSpec as P

ITERS = 3


def with_halo(block, sides, width):
    for axis, dim in sides:
        count = lax.axis_size(axis)
        forward = [(i, i + 1) for i in range(count - 1)]
        backward = [(target, source) for source, target in forward]
        low = lax.ppermute(
            lax.slice_in_dim(block, block.shape[dim] - width, None, axis=dim), axis, forward
        )
        high = lax.ppermute(lax.slice_in_dim(block, 0, width, axis=dim), axis, backward)
        block = jnp.concatenate([low, block, high], axis=dim)
    return block


def neighbours(vector):
    padded = with_halo(vector, (("res", 1), ("grp", 2)), 1)
    zpadded = jnp.pad(vector, ((0, 0), (0, 0), (0, 0), (1, 1)))
    return [
        padded[:, 2:, 1:-1, :],
        padded[:, :-2, 1:-1, :],
        padded[:, 1:-1, 2:, :],
        padded[:, 1:-1, :-2, :],
        zpadded[..., 2:],
        zpadded[..., :-2],
    ]


def stencil(vector, diag_total, transmissibility):
    beside_list = neighbours(vector)
    result = jnp.sum(diag_total * vector[None], axis=1)
    for face in range(6):
        result = result - jnp.sum(transmissibility[face] * beside_list[face][None], axis=1)
    return result


def body(
    right_side,
    accumulation,
    transmissibility,
    completion,
    live_count,
    owner,
    cell_to_well,
    well_to_cell,
    inverse,
):
    highest = lax.Precision.HIGHEST
    components, cells_x, cells_y, cells_z = right_side.shape
    blocks, segb = completion.shape
    capacity = inverse.shape[2]
    groups = lax.axis_size("grp")
    flat_index = completion.reshape(-1)
    open_mask = (jnp.arange(segb, dtype=jnp.int32)[None, :] < live_count[:, None]).astype(
        jnp.float32
    )
    owner_eq = (owner == jnp.arange(groups, dtype=jnp.int32)[None, :]).astype(jnp.int32)
    prior = jnp.cumsum(owner_eq, axis=0) - owner_eq
    slot_number = jnp.sum(prior * owner_eq, axis=1)
    target = owner[:, 0] * capacity + slot_number
    packing = (target[:, None] == jnp.arange(groups * capacity, dtype=jnp.int32)[None, :]).astype(
        jnp.float32
    )
    diag_total = accumulation
    for face in range(6):
        diag_total = diag_total + transmissibility[face]
    moved = lax.all_to_all(inverse[0], "grp", split_axis=0, concat_axis=0, tiled=True)
    block_inverse = jnp.einsum(
        "bq,qst->bst", packing, moved.reshape(groups * capacity, segb, segb), precision=highest
    )

    def solve_wells(coupled):
        return jnp.einsum("bst,bt->bs", block_inverse, coupled, precision=highest)

    def operator(vector):
        result = stencil(vector, diag_total, transmissibility)
        flat = vector.reshape(components, -1)
        picked = jnp.moveaxis(flat[:, flat_index].reshape(components, blocks, segb), 0, 1)
        coupled = jnp.sum(cell_to_well * picked, axis=1) * open_mask
        well_value = solve_wells(coupled)
        correction = well_to_cell * (well_value * open_mask)[:, None, :]
        correction = jnp.moveaxis(correction, 0, 1).reshape(components, -1)
        out_flat = result.reshape(components, -1).at[:, flat_index].add(-correction)
        return out_flat.reshape(vector.shape)

    solution = jnp.zeros_like(right_side)
    residual = right_side
    search = right_side
    rho = lax.psum(jnp.sum(residual * residual), ("res", "grp"))
    for index in range(ITERS):
        image = operator(search)
        alpha = rho / lax.psum(jnp.sum(right_side * image), ("res", "grp"))
        middle = residual - alpha * image
        second = operator(middle)
        rho_next = rho
        inner, square = lax.psum(
            (jnp.sum(second * middle), jnp.sum(second * second)), ("res", "grp")
        )
        omega = inner / square
        solution = solution + alpha * search + omega * middle
        residual = middle - omega * second
        if index + 1 < ITERS:
            rho_next = lax.psum(jnp.sum(right_side * residual), ("res", "grp"))
        if index + 1 < ITERS:
            search = residual + rho_next / rho * (alpha / omega) * (search - omega * image)
            rho = rho_next
    return (solution, residual)


def solution(mesh):
    return jax.shard_map(
        body,
        mesh=mesh,
        in_specs=(
            P(None, "res", "grp", None),
            P(None, None, "res", "grp", None),
            P(None, None, None, "res", "grp", None),
            P(("res", "grp"), None),
            P(("res", "grp")),
            P(("res", "grp"), None),
            P(("res", "grp"), None, None),
            P(("res", "grp"), None, None),
            P(("res", "grp"), None, None, None, None),
        ),
        out_specs=(P(None, "res", "grp", None), P(None, "res", "grp", None)),
        check_vma=False,
    )
```

profile of v0, /device:TPU:0, one launch (start us, length us, event | category | flops | bytes accessed | tf_op | source)
XLA Modules:
  0.0 861.7 jit_solution(8939476665833787477)
XLA Ops:
  0.7 5.2 all-to-all-start
  7.5 5.5 collective-permute-start.1
  14.3 5.6 copy.85
  19.9 11.0 %gather_fusion = f32[2048,3]{1,0:T(8,128)} fusion(f32[3,16384]{0,1:T(8,128)} %bitcast.284, s32[2048]{0:T(1024)S(1)} %broadcast_clamp_fusion), kind=kCustom, calls=%fused_computation | custom fusion | bytes 57344 | tf_op jit(solution)/shard_map/gather | solution.py:84
  52.7 5.6 copy.83
  58.3 6.1 fusion
  71.7 17.4 %scatter_fusion = f32[3,16384]{0,1:T(8,128)} fusion(f32[3,16384]{0,1:T(8,128)} %bitcast.273, s32[2048]{0:T(1024)S(1)} %bitcast.299, f32[2048,3]{1,0:T(8,128)} %bitcast.291), kind=kCustom, calls=%fused_computation.6 | custom fusion | flops 6144 | bytes 81920 | tf_op jit(solution)/shard_map/scatter-add | solution.py:89
  89.1 5.9 copy.88
  96.7 44.2 %all-reduce.9 = (f32[]{:T(128)}, f32[]{:T(128)}) all-reduce(f32[]{:T(128)} %get-tuple-element.39, f32[]{:T(128)} %get-tuple-element.38), channel_id=1, replica_groups=mesh['res'=8,'grp'=4] {'res','grp'}, use_global_device_ids=true, to_apply=%region_1.2 | all-reduce | flops 2 | bytes 16 | tf_op jit(solution)/shard_map/psum | solution.py:95
  144.6 5.6 copy.91
  150.2 4.8 collective-permute-start.5
  156.3 10.9 %gather_fusion.1 = f32[2048,3]{1,0:T(8,128)} fusion(f32[3,16384]{0,1:T(8,128)} %bitcast.280, s32[2048]{0:T(1024)S(1)} %broadcast_clamp_fusion), kind=kCustom, calls=%fused_computation.1 | custom fusion | bytes 57344 | tf_op jit(solution)/shard_map/gather | solution.py:84
  189.8 5.6 copy.90
  195.4 17.3 %scatter_fusion.1 = f32[3,16384]{0,1:T(8,128)} fusion(f32[3,16384]{0,1:T(8,128)} %bitcast.269, s32[2048]{0:T(1024)S(1)} %bitcast.300, f32[2048,3]{1,0:T(8,128)} %bitcast.288), kind=kCustom, calls=%fused_computation.7 | custom fusion | flops 6144 | bytes 81920 | tf_op jit(solution)/shard_map/scatter-add | solution.py:89
  212.7 5.2 multiply_reduce_fusion.2
  217.9 5.9 copy.94
  225.4 43.1 %all-reduce.8 = (f32[]{:T(128)}, f32[]{:T(128)}) all-reduce(f32[]{:T(128)} %multiply_reduce_fusion.15, f32[]{:T(128)} %multiply_reduce_fusion.2), channel_id=1, replica_groups=mesh['res'=8,'grp'=4] {'res','grp'}, use_global_device_ids=true, to_apply=%region_25.26 | all-reduce | flops 2 | bytes 16 | tf_op jit(solution)/shard_map/psum | solution.py:102
  274.2 40.8 %psum.88 = f32[]{:T(128)} all-reduce(f32[]{:T(128)} %multiply_reduce_fusion.14), channel_id=1, replica_groups=mesh['res'=8,'grp'=4] {'res','grp'}, use_global_device_ids=true, to_apply=%region_29.30 | all-reduce | flops 1 | bytes 8 | tf_op jit(solution)/shard_map/psum | solution.py:109
  319.1 5.6 copy.98
  324.7 4.8 collective-permute-start.9
  331.0 10.9 %gather_fusion.2 = f32[2048,3]{1,0:T(8,128)} fusion(f32[3,16384]{0,1:T(8,128)} %bitcast.281, s32[2048]{0:T(1024)S(1)} %broadcast_clamp_fusion), kind=kCustom, calls=%fused_computation.2 | custom fusion | bytes 57344 | tf_op jit(solution)/shard_map/gather | solution.py:84
  364.6 5.6 copy.97
  370.2 17.3 %scatter_fusion.2 = f32[3,16384]{0,1:T(8,128)} fusion(f32[3,16384]{0,1:T(8,128)} %bitcast.275, s32[2048]{0:T(1024)S(1)} %bitcast.301, f32[2048,3]{1,0:T(8,128)} %bitcast.289), kind=kCustom, calls=%fused_computation.8 | custom fusion | flops 6144 | bytes 81920 | tf_op jit(solution)/shard_map/scatter-add | solution.py:89
  387.5 5.9 copy.101
  395.0 43.1 %psum.89 = f32[]{:T(128)} all-reduce(f32[]{:T(128)} %multiply_reduce_fusion.13), channel_id=1, replica_groups=mesh['res'=8,'grp'=4] {'res','grp'}, use_global_device_ids=true, to_apply=%region_40.41 | all-reduce | flops 1 | bytes 8 | tf_op jit(solution)/shard_map/psum | solution.py:98
  441.8 5.6 copy.104
  447.5 4.8 collective-permute-start.13
  453.6 10.9 %gather_fusion.3 = f32[2048,3]{1,0:T(8,128)} fusion(f32[3,16384]{0,1:T(8,128)} %bitcast.282, s32[2048]{0:T(1024)S(1)} %broadcast_clamp_fusion), kind=kCustom, calls=%fused_computation.3 | custom fusion | bytes 57344 | tf_op jit(solution)/shard_map/gather | solution.py:84
  487.5 5.6 copy.103
  493.1 17.3 %scatter_fusion.3 = f32[3,16384]{0,1:T(8,128)} fusion(f32[3,16384]{0,1:T(8,128)} %bitcast.271, s32[2048]{0:T(1024)S(1)} %bitcast.302, f32[2048,3]{1,0:T(8,128)} %bitcast.290), kind=kCustom, calls=%fused_computation.9 | custom fusion | flops 6144 | bytes 81920 | tf_op jit(solution)/shard_map/scatter-add | solution.py:89
  510.4 5.1 multiply_reduce_fusion.1
  515.5 5.9 copy.107
  523.0 42.9 %all-reduce.7 = (f32[]{:T(128)}, f32[]{:T(128)}) all-reduce(f32[]{:T(128)} %multiply_reduce_fusion.12, f32[]{:T(128)} %multiply_reduce_fusion.1), channel_id=1, replica_groups=mesh['res'=8,'grp'=4] {'res','grp'}, use_global_device_ids=true, to_apply=%region_51.52 | all-reduce | flops 2 | bytes 16 | tf_op jit(solution)/shard_map/psum | solution.py:102
  571.2 41.0 %psum.92 = f32[]{:T(128)} all-reduce(f32[]{:T(128)} %multiply_reduce_fusion.11), channel_id=1, replica_groups=mesh['res'=8,'grp'=4] {'res','grp'}, use_global_device_ids=true, to_apply=%region_55.56 | all-reduce | flops 1 | bytes 8 | tf_op jit(solution)/shard_map/psum | solution.py:109
  616.3 5.6 copy.111
  621.9 4.8 collective-permute-start.17
  628.0 10.9 %gather_fusion.4 = f32[2048,3]{1,0:T(8,128)} fusion(f32[3,16384]{0,1:T(8,128)} %bitcast.283, s32[2048]{0:T(1024)S(1)} %broadcast_clamp_fusion), kind=kCustom, calls=%fused_computation.4 | custom fusion | bytes 57344 | tf_op jit(solution)/shard_map/gather | solution.py:84
  661.5 5.6 copy.110
  667.1 17.3 %scatter_fusion.4 = f32[3,16384]{0,1:T(8,128)} fusion(f32[3,16384]{0,1:T(8,128)} %bitcast.277, s32[2048]{0:T(1024)S(1)} %bitcast.303, f32[2048,3]{1,0:T(8,128)} %bitcast.286), kind=kCustom, calls=%fused_computation.10 | custom fusion | flops 6144 | bytes 81920 | tf_op jit(solution)/shard_map/scatter-add | solution.py:89
  684.4 5.9 copy.114
  692.0 42.7 %psum.93 = f32[]{:T(128)} all-reduce(f32[]{:T(128)} %multiply_reduce_fusion.10), channel_id=1, replica_groups=mesh['res'=8,'grp'=4] {'res','grp'}, use_global_device_ids=true, to_apply=%region_66.67 | all-reduce | flops 1 | bytes 8 | tf_op jit(solution)/shard_map/psum | solution.py:98
  738.6 5.6 copy.117
  744.2 4.8 collective-permute-start.21
  750.3 10.9 %gather_fusion.5 = f32[2048,3]{1,0:T(8,128)} fusion(f32[3,16384]{0,1:T(8,128)} %bitcast.279, s32[2048]{0:T(1024)S(1)} %broadcast_clamp_fusion), kind=kCustom, calls=%fused_computation.5 | custom fusion | bytes 57344 | tf_op jit(solution)/shard_map/gather | solution.py:84
  789.5 17.3 %scatter_fusion.5 = f32[3,16384]{0,1:T(8,128)} fusion(f32[3,16384]{0,1:T(8,128)} %bitcast.267, s32[2048]{0:T(1024)S(1)} %bitcast.304, f32[2048,3]{1,0:T(8,128)} %bitcast.287), kind=kCustom, calls=%fused_computation.11 | custom fusion | flops 6144 | bytes 81920 | tf_op jit(solution)/shard_map/scatter-add | solution.py:89
  806.8 5.2 multiply_reduce_fusion
  812.0 5.2 copy.120
  817.9 41.4 %all-reduce.6 = (f32[]{:T(128)}, f32[]{:T(128)}) all-reduce(f32[]{:T(128)} %multiply_reduce_fusion.9, f32[]{:T(128)} %multiply_reduce_fusion), channel_id=1, replica_groups=mesh['res'=8,'grp'=4] {'res','grp'}, use_global_device_ids=true, to_apply=%region_77.78 | all-reduce | flops 2 | bytes 16 | tf_op jit(solution)/shard_map/psum | solution.py:102
  (180 shorter events, 183.8 us)
Async XLA Ops:
  0.6 19.3 %copy-start.16 = (s32[8,256]{1,0:T(8,128)S(1)}, s32[8,256]{1,0:T(8,128)}, u32[]{:S(2)}) copy-start(s32[8,256]{1,0:T(8,128)} %param.12) | copy-start | bytes 24580
  0.6 37.2 %copy-start = (f32[6,3,3,2,16,512]{5,4,3,2,1,0:T(8,128)S(1)}, f32[6,3,3,2,16,512]{5,4,3,2,1,0:T(8,128)}, u32[]{:S(2)}) copy-start(f32[6,3,3,2,16,512]{5,4,3,2,1,0:T(8,128)} %param.11) | copy-start | bytes 10616836
  0.7 57.7 %all-to-all-start = ((f32[4,4,256,256]{3,2,1,0:T(8,128)}), f32[4,4,256,256]{3,2,1,0:T(8,128)}, u32[]{:S(2)}, u32[]{:S(2)}) async-start(f32[4,4,256,256]{3,2,1,0:T(8,128)} %bitcast.285), calls=%async_computation | async-start | bytes 8388608 | tf_op jit(solution)/shard_map/all_to_all | solution.py:73
  7.5 33.6 %collective-permute-start.1 = (f32[3,1,16,512]{3,2,1,0:T(8,128)}, f32[3,1,16,512]{3,2,1,0:T(8,128)}, u32[]{:S(2)}, u32[]{:S(2)}) collective-permute-start(f32[3,1,16,512]{3,2,1,0:T(8,128)} %get-tuple-element.127), channel_id=1, source_target_pairs={{0,4},{4,8},{8,12},{12,16},{16,20},{20,24},{24,28},{1,5},{5,9},{9,... | collective-permute-start | bytes 294920 | tf_op jit(solution)/shard_map/ppermute | solution.py:14
  13.0 29.0 %collective-permute-start = (f32[3,1,16,512]{3,2,1,0:T(8,128)}, f32[3,1,16,512]{3,2,1,0:T(8,128)}, u32[]{:S(2)}, u32[]{:S(2)}) collective-permute-start(f32[3,1,16,512]{3,2,1,0:T(8,128)} %get-tuple-element.128), channel_id=1, source_target_pairs={{4,0},{8,4},{12,8},{16,12},{20,16},{24,20},{28,24},{5,1},{9,5},{13... | collective-permute-start | bytes 294920 | tf_op jit(solution)/shard_map/ppermute | solution.py:17
  44.6 4.6 collective-permute-start.3
  46.7 4.5 collective-permute-start.2
  58.3 10.6 %copy-start.15 = (s32[8]{0:T(128)S(1)}, s32[8]{0:T(128)}, u32[]{:S(2)}) copy-start(s32[8]{0:T(128)} %param.13) | copy-start | bytes 100
  58.3 10.6 %copy-start.14 = (f32[8,3,256]{2,0,1:T(8,128)S(1)}, f32[8,3,256]{2,0,1:T(8,128)}, u32[]{:S(2)}) copy-start(f32[8,3,256]{2,0,1:T(8,128)} %param.16) | copy-start | bytes 73732
  64.4 1.4 copy-start.1
  143.2 0.7 copy-start.3
  150.2 26.7 %collective-permute-start.5 = (f32[3,1,16,512]{3,2,1,0:T(8,128)}, f32[3,1,16,512]{3,2,1,0:T(8,128)}, u32[]{:S(2)}, u32[]{:S(2)}) collective-permute-start(f32[3,1,16,512]{3,2,1,0:T(8,128)} %get-tuple-element.120), channel_id=1, source_target_pairs={{0,4},{4,8},{8,12},{12,16},{16,20},{20,24},{24,28},{1,5},{5,9},{9,... | collective-permute-start | bytes 294920 | tf_op jit(solution)/shard_map/ppermute | solution.py:14
  155.0 21.9 %collective-permute-start.4 = (f32[3,1,16,512]{3,2,1,0:T(8,128)}, f32[3,1,16,512]{3,2,1,0:T(8,128)}, u32[]{:S(2)}, u32[]{:S(2)}) collective-permute-start(f32[3,1,16,512]{3,2,1,0:T(8,128)} %get-tuple-element.121), channel_id=1, source_target_pairs={{4,0},{8,4},{12,8},{16,12},{20,16},{24,20},{28,24},{5,1},{9,5},{13... | collective-permute-start | bytes 294920 | tf_op jit(solution)/shard_map/ppermute | solution.py:17
  178.6 7.1 collective-permute-start.7
  180.4 5.2 collective-permute-start.6
  317.7 0.7 copy-start.7
  324.7 26.9 %collective-permute-start.9 = (f32[3,1,16,512]{3,2,1,0:T(8,128)}, f32[3,1,16,512]{3,2,1,0:T(8,128)}, u32[]{:S(2)}, u32[]{:S(2)}) collective-permute-start(f32[3,1,16,512]{3,2,1,0:T(8,128)} %get-tuple-element.112), channel_id=1, source_target_pairs={{0,4},{4,8},{8,12},{12,16},{16,20},{20,24},{24,28},{1,5},{5,9},{9,... | collective-permute-start | bytes 294920 | tf_op jit(solution)/shard_map/ppermute | solution.py:14
  329.5 22.1 %collective-permute-start.8 = (f32[3,1,16,512]{3,2,1,0:T(8,128)}, f32[3,1,16,512]{3,2,1,0:T(8,128)}, u32[]{:S(2)}, u32[]{:S(2)}) collective-permute-start(f32[3,1,16,512]{3,2,1,0:T(8,128)} %get-tuple-element.113), channel_id=1, source_target_pairs={{4,0},{8,4},{12,8},{16,12},{20,16},{24,20},{28,24},{5,1},{9,5},{13... | collective-permute-start | bytes 294920 | tf_op jit(solution)/shard_map/ppermute | solution.py:17
  353.3 7.1 collective-permute-start.11
  355.1 5.2 collective-permute-start.10
  440.5 0.7 copy-start.5
  447.5 26.7 %collective-permute-start.13 = (f32[3,1,16,512]{3,2,1,0:T(8,128)}, f32[3,1,16,512]{3,2,1,0:T(8,128)}, u32[]{:S(2)}, u32[]{:S(2)}) collective-permute-start(f32[3,1,16,512]{3,2,1,0:T(8,128)} %get-tuple-element.104), channel_id=1, source_target_pairs={{0,4},{4,8},{8,12},{12,16},{16,20},{20,24},{24,28},{1,5},{5,9},{9,... | collective-permute-start | bytes 294920 | tf_op jit(solution)/shard_map/ppermute | solution.py:14
  452.3 21.9 %collective-permute-start.12 = (f32[3,1,16,512]{3,2,1,0:T(8,128)}, f32[3,1,16,512]{3,2,1,0:T(8,128)}, u32[]{:S(2)}, u32[]{:S(2)}) collective-permute-start(f32[3,1,16,512]{3,2,1,0:T(8,128)} %get-tuple-element.105), channel_id=1, source_target_pairs={{4,0},{8,4},{12,8},{16,12},{20,16},{24,20},{28,24},{5,1},{9,5},{13... | collective-permute-start | bytes 294920 | tf_op jit(solution)/shard_map/ppermute | solution.py:17
  475.8 7.6 collective-permute-start.15
  477.8 5.6 collective-permute-start.14
  614.9 0.7 copy-start.12
  621.9 26.7 %collective-permute-start.17 = (f32[3,1,16,512]{3,2,1,0:T(8,128)}, f32[3,1,16,512]{3,2,1,0:T(8,128)}, u32[]{:S(2)}, u32[]{:S(2)}) collective-permute-start(f32[3,1,16,512]{3,2,1,0:T(8,128)} %get-tuple-element.96), channel_id=1, source_target_pairs={{0,4},{4,8},{8,12},{12,16},{16,20},{20,24},{24,28},{1,5},{5,9},{9,... | collective-permute-start | bytes 294920 | tf_op jit(solution)/shard_map/ppermute | solution.py:14
  626.7 21.9 %collective-permute-start.16 = (f32[3,1,16,512]{3,2,1,0:T(8,128)}, f32[3,1,16,512]{3,2,1,0:T(8,128)}, u32[]{:S(2)}, u32[]{:S(2)}) collective-permute-start(f32[3,1,16,512]{3,2,1,0:T(8,128)} %get-tuple-element.97), channel_id=1, source_target_pairs={{4,0},{8,4},{12,8},{16,12},{20,16},{24,20},{28,24},{5,1},{9,5},{13... | collective-permute-start | bytes 294920 | tf_op jit(solution)/shard_map/ppermute | solution.py:17
  650.2 7.3 collective-permute-start.19
  652.1 5.4 collective-permute-start.18
  737.3 0.7 copy-start.9
  744.2 26.7 %collective-permute-start.21 = (f32[3,1,16,512]{3,2,1,0:T(8,128)}, f32[3,1,16,512]{3,2,1,0:T(8,128)}, u32[]{:S(2)}, u32[]{:S(2)}) collective-permute-start(f32[3,1,16,512]{3,2,1,0:T(8,128)} %get-tuple-element.88), channel_id=1, source_target_pairs={{0,4},{4,8},{8,12},{12,16},{16,20},{20,24},{24,28},{1,5},{5,9},{9,... | collective-permute-start | bytes 294920 | tf_op jit(solution)/shard_map/ppermute | solution.py:14
  749.1 21.9 %collective-permute-start.20 = (f32[3,1,16,512]{3,2,1,0:T(8,128)}, f32[3,1,16,512]{3,2,1,0:T(8,128)}, u32[]{:S(2)}, u32[]{:S(2)}) collective-permute-start(f32[3,1,16,512]{3,2,1,0:T(8,128)} %get-tuple-element.89), channel_id=1, source_target_pairs={{4,0},{8,4},{12,8},{16,12},{20,16},{24,20},{28,24},{5,1},{9,5},{13... | collective-permute-start | bytes 294920 | tf_op jit(solution)/shard_map/ppermute | solution.py:17
  772.6 9.0 %collective-permute-start.22 = (f32[3,4,1,512]{3,2,1,0:T(1,128)}, f32[3,4,1,512]{3,2,1,0:T(1,128)}, u32[]{:S(2)}, u32[]{:S(2)}) collective-permute-start(f32[3,4,1,512]{3,2,1,0:T(1,128)} %get-tuple-element.52), channel_id=1, source_target_pairs={{1,0},{2,1},{3,2},{5,4},{6,5},{7,6},{9,8},{10,9},{11,10},{13,12},{... | collective-permute-start | bytes 73736 | tf_op jit(solution)/shard_map/ppermute | solution.py:17
  773.9 7.7 collective-permute-start.23
  806.8 10.5 %copy-start.10 = (f32[3,2,16,512]{3,2,1,0:T(8,128)S(1)}, f32[3,2,16,512]{3,2,1,0:T(8,128)}, u32[]{:S(2)}) copy-start(f32[3,2,16,512]{3,2,1,0:T(8,128)} %copy-done.9) | copy-start | bytes 589828
  806.8 53.8 %copy-start.2 = (f32[3,2,16,512]{3,2,1,0:T(8,128)S(1)}, f32[3,2,16,512]{3,2,1,0:T(8,128)}, u32[]{:S(2)}) copy-start(f32[3,2,16,512]{3,2,1,0:T(8,128)} %param.9) | copy-start | bytes 589828
  806.8 53.8 %copy-start.4 = (f32[3,2,16,512]{3,2,1,0:T(8,128)S(1)}, f32[3,2,16,512]{3,2,1,0:T(8,128)}, u32[]{:S(2)}) copy-start(f32[3,2,16,512]{3,2,1,0:T(8,128)} %copy-done.3) | copy-start | bytes 589828
  806.8 53.8 %copy-start.6 = (f32[3,2,16,512]{3,2,1,0:T(8,128)S(1)}, f32[3,2,16,512]{3,2,1,0:T(8,128)}, u32[]{:S(2)}) copy-start(f32[3,2,16,512]{3,2,1,0:T(8,128)} %copy-done.5) | copy-start | bytes 589828
  806.8 53.8 %copy-start.8 = (f32[3,2,16,512]{3,2,1,0:T(8,128)S(1)}, f32[3,2,16,512]{3,2,1,0:T(8,128)}, u32[]{:S(2)}) copy-start(f32[3,2,16,512]{3,2,1,0:T(8,128)} %copy-done.7) | copy-start | bytes 589828
  806.8 53.8 %copy-start.11 = (f32[3,2,16,512]{3,2,1,0:T(8,128)S(1)}, f32[3,2,16,512]{3,2,1,0:T(8,128)}, u32[]{:S(2)}) copy-start(f32[3,2,16,512]{3,2,1,0:T(8,128)} %copy.107) | copy-start | bytes 589828
  806.8 53.8 %copy-start.13 = (f32[3,2,16,512]{3,2,1,0:T(8,128)S(1)}, f32[3,2,16,512]{3,2,1,0:T(8,128)}, u32[]{:S(2)}) copy-start(f32[3,2,16,512]{3,2,1,0:T(8,128)} %copy.101) | copy-start | bytes 589828
where the time goes:
time: 876 us; the launch traced here: 862 us
  blocking collectives  339 us (39%)
  other arithmetic  207 us (24%)
  local copies, waits for them, and re-layouts  204 us (23%)
  starting transfers between devices  64.2 us (7%)
  matrix products  28.8 us (3%)
  between operations  16.6 us (2%)
    psum x3, blocking collectives, body(): lax.psum((jnp.sum(second * middle), jnp.sum(second * second)), ('res', 'g...  127 us
    scatter-add x6, other arithmetic, operator(): out_flat = result.reshape(components, -1).at[:, flat_index].add(-correction)  104 us
    psum x2, blocking collectives, body(): alpha = rho / lax.psum(jnp.sum(right_side * image), ('res', 'grp'))  85.7 us
    psum x2, blocking collectives, body(): rho_next = lax.psum(jnp.sum(right_side * residual), ('res', 'grp'))  81.8 us
    gather x6, local copies, waits for them, and re-layouts, operator(): flat[:, flat_index].reshape(components, blocks, segb)  65.7 us
    psum x1, blocking collectives, body(): rho = lax.psum(jnp.sum(residual * residual), ('res', 'grp'))  44.2 us
    ppermute x12, starting transfers between devices, with_halo(): lax.ppermute(lax.slice_in_dim(block, block.shape[dim] - width, None, axis...  42.8 us
    reshape x6, local copies, waits for them, and re-layouts, operator(): return out_flat.reshape(vector.shape)  34.6 us
  transfers between devices with their start and end apart: 25, of which 1 were waited for; matrix products, arithmetic and copies ran while one was open for 19% of the time, Pallas kernels for 0%

commit v1 on v0

v1 whole, which is shorter than its diff:
```python
import functools

import jax
import jax.numpy as jnp
from jax import lax
from jax.experimental import pallas as pl
from jax.experimental.pallas import tpu as pltpu
from jax.sharding import PartitionSpec as P

ITERS = 3
F32 = jnp.float32
BF16 = jnp.bfloat16
VMEM = pl.BlockSpec(memory_space=pltpu.VMEM)
SMEM = pl.BlockSpec(memory_space=pltpu.SMEM)
LIMIT = 20 * 1024 * 1024
NAMES = ("br", "bs", "bw", "bz", "rw", "rz", "sw", "sz", "ww", "wz", "zz")


def call(kernel, outs, args, specs=None, scratch=(), flops=1_000_000, moved=1_000_000):
    return pl.pallas_call(
        kernel,
        out_shape=[jax.ShapeDtypeStruct(shape, dtype) for shape, dtype in outs],
        in_specs=specs or [VMEM] * len(args),
        out_specs=[VMEM] * len(outs),
        scratch_shapes=list(scratch),
        compiler_params=pltpu.CompilerParams(vmem_limit_bytes=LIMIT),
        cost_estimate=pl.CostEstimate(flops=flops, bytes_accessed=moved, transcendentals=0),
    )(*args)


def pairings(count):
    first = [(i, i ^ 1) for i in range(count)]
    second = [(i, (i + 1 if i % 2 else i - 1) % count) for i in range(count)]
    return first, second


def exchange(faces):
    out = []
    for pair, axis in zip((faces[:2], faces[2:]), ("res", "grp")):
        for face, pairs in zip(pair, pairings(lax.axis_size(axis))):
            out.append(lax.ppermute(face, axis, pairs))
    return out


def is_even(axis):
    return lax.rem(lax.axis_index(axis), 2) == 0


def write_faces(field, refs):
    xfirst, xsecond, yfirst, ysecond = refs
    components = xfirst.shape[0]
    cells_x = yfirst.shape[0] // components
    cells_y = xfirst.shape[1]
    xeven, yeven = is_even("res"), is_even("grp")
    for j in range(components):
        low, high = field(j, 0), field(j, cells_x - 1)
        xfirst[j] = jnp.where(xeven, high, low)
        xsecond[j] = jnp.where(xeven, low, high)
        for x in range(cells_x):
            plane = field(j, x)
            row = j * cells_x + x
            low, high = plane[0:1], plane[cells_y - 1 : cells_y]
            yfirst[row : row + 1] = jnp.where(yeven, high, low)
            ysecond[row : row + 1] = jnp.where(yeven, low, high)


def halo_terms(halo, trans):
    xfirst, xsecond, yfirst, ysecond = halo
    components, cells_y, cells_z = xfirst.shape
    cells_x = yfirst.shape[0] // components
    xeven, yeven = is_even("res"), is_even("grp")
    r, g = lax.axis_index("res"), lax.axis_index("grp")
    xlow_on = (r > 0).astype(F32)
    xhigh_on = (r < lax.axis_size("res") - 1).astype(F32)
    ylow_on = (g > 0).astype(F32)
    yhigh_on = (g < lax.axis_size("grp") - 1).astype(F32)
    xhigh = [jnp.where(xeven, xfirst[j], xsecond[j]) * xhigh_on for j in range(components)]
    xlow = [jnp.where(xeven, xsecond[j], xfirst[j]) * xlow_on for j in range(components)]
    yhigh = jnp.where(yeven, yfirst[...], ysecond[...]) * yhigh_on
    ylow = jnp.where(yeven, ysecond[...], yfirst[...]) * ylow_on
    rows = lax.broadcasted_iota(jnp.int32, (cells_y, cells_z), 0)

    def terms(i, x):
        low = jnp.zeros((1, cells_z), F32)
        high = jnp.zeros((1, cells_z), F32)
        for j in range(components):
            k = j * cells_x + x
            high = high + trans[2, i, j, x, cells_y - 1 : cells_y] * yhigh[k : k + 1]
            low = low + trans[3, i, j, x, 0:1] * ylow[k : k + 1]
        total = jnp.where(rows == cells_y - 1, high, 0.0) + jnp.where(rows == 0, low, 0.0)
        for j in range(components):
            if x == cells_x - 1:
                total = total + trans[0, i, j, x] * xhigh[j]
            if x == 0:
                total = total + trans[1, i, j, x] * xlow[j]
        return total

    return terms


def inner_stencil(vec, trans, diag, shifted, out):
    components, cells_x, cells_y, cells_z = vec.shape
    rows = lax.broadcasted_iota(jnp.int32, (cells_y, cells_z), 0)
    lanes = lax.broadcasted_iota(jnp.int32, (cells_y, cells_z), 1)
    for j in range(components):
        for x in range(cells_x):
            plane = vec[j, x]
            up = pltpu.roll(plane, cells_y - 1, 0)
            shifted[0, j, x] = jnp.where(rows == cells_y - 1, 0.0, up)
            shifted[1, j, x] = jnp.where(rows == 0, 0.0, pltpu.roll(plane, 1, 0))
            up = pltpu.roll(plane, cells_z - 1, 1)
            shifted[2, j, x] = jnp.where(lanes == cells_z - 1, 0.0, up)
            shifted[3, j, x] = jnp.where(lanes == 0, 0.0, pltpu.roll(plane, 1, 1))
    for i in range(components):
        for x in range(cells_x):
            total = diag[i, 0, x] * vec[0, x]
            for j in range(1, components):
                total = total + diag[i, j, x] * vec[j, x]
            for j in range(components):
                if x + 1 < cells_x:
                    total = total - trans[0, i, j, x] * vec[j, x + 1]
                if x > 0:
                    total = total - trans[1, i, j, x] * vec[j, x - 1]
                for side in range(4):
                    total = total - trans[2 + side, i, j, x] * shifted[side, j, x]
            out[i, x] = total


def halves(value):
    high = value.astype(BF16)
    low = (value - high.astype(F32)).astype(BF16)
    return high, low


def dot(a, b, transposed=False):
    dims = (((1,), (1 if transposed else 0,)), ((), ()))
    return lax.dot_general(a, b, dims, preferred_element_type=F32)


def gather_well(both, place, column, weight, b):
    segb = weight.shape[2]
    components = weight.shape[1]
    part = slice(b * segb, (b + 1) * segb)
    found = dot(both, place[:, part])
    rows = found.shape[0] // 2
    found = found[:rows] + found[rows:]
    per = rows // components
    here = lax.broadcasted_iota(jnp.int32, (per, segb), 0) == column[b : b + 1, :]
    coupled = jnp.zeros((1, segb), F32)
    for i in range(components):
        part = jnp.where(here, found[i * per : (i + 1) * per], 0.0)
        coupled = coupled + jnp.sum(part, axis=0, keepdims=True) * weight[b, i : i + 1]
    return coupled


def solve_well(coupled, first, second):
    high = coupled.astype(BF16).astype(F32)
    low = coupled - high
    rows = lax.broadcasted_iota(jnp.int32, (16, coupled.shape[1]), 0)
    left = jnp.where(rows == 0, high, jnp.where(rows == 1, low, 0.0)).astype(BF16)
    return jnp.sum(dot(left, first, True) + dot(left, second, True), axis=0, keepdims=True)


def scatter_well(value, place, column, weight, rows, b):
    segb = weight.shape[2]
    components = weight.shape[1]
    per = rows // components
    part = slice(b * segb, (b + 1) * segb)
    here = lax.broadcasted_iota(jnp.int32, (per, segb), 0) == column[b : b + 1, :]
    blocks = [
        jnp.where(here, weight[b, i : i + 1] * value, 0.0) for i in range(components)
    ]
    high, low = halves(jnp.concatenate(blocks, axis=0))
    return dot(jnp.concatenate([high, low], axis=0), place[:, part], True)


def inner_kernel(vec, trans, diag, place, column, take, give, first, second, out, shifted):
    inner_stencil(vec, trans, diag, shifted, out)
    components, cells_x, cells_y, cells_z = vec.shape
    rows = components * cells_x * cells_y
    high, low = halves(vec[...].reshape(rows, cells_z))
    both = jnp.concatenate([high, low], axis=0)
    total = None
    for b in range(column.shape[0]):
        coupled = gather_well(both, place, column, take, b)
        value = solve_well(coupled, first[b], second[b])
        term = scatter_well(value, place, column, give, rows, b)
        total = term if total is None else total + term
    total = total[:rows] + total[rows:]
    out[...] = out[...] - total.reshape(out.shape)


def prepare_kernel(acc, trans, completion, live, take, give, diag, place, column, take_out, give_out):
    components = acc.shape[0]
    cells_z = acc.shape[-1]
    for i in range(components):
        for j in range(components):
            total = acc[i, j]
            for face in range(trans.shape[0]):
                total = total + trans[face, i, j]
            diag[i, j] = total
    wells, segb = completion.shape
    depth = lax.broadcasted_iota(jnp.int32, (cells_z, segb), 0)
    lanes = lax.broadcasted_iota(jnp.int32, (1, segb), 1)
    for b in range(wells):
        cell = completion[b : b + 1, :]
        row = cell // cells_z
        column[b : b + 1, :] = row
        hit = depth == cell - row * cells_z
        place[:, b * segb : (b + 1) * segb] = jnp.where(hit, 1.0, 0.0).astype(BF16)
        is_open = (lanes < live[b]).astype(F32)
        for i in range(components):
            take_out[b, i : i + 1] = take[b, i : i + 1] * is_open
            give_out[b, i : i + 1] = give[b, i : i + 1] * is_open


def pick_kernel(owner, moved, first, second):
    capacity = moved.shape[1]
    for b in range(first.shape[0]):
        mine = owner[b, 0]
        slot = jnp.int32(0)
        for c in range(b):
            slot = slot + (owner[c, 0] == mine).astype(jnp.int32)
        high, low = halves(moved[mine, jnp.minimum(slot, capacity - 1)])
        first[b] = high
        second[b] = low


def face_kernel(vec, *faces):
    write_faces(lambda j, x: vec[j, x], faces)


def apply_kernel(part, trans, h0, h1, h2, h3, out, *faces):
    terms = halo_terms((h0, h1, h2, h3), trans)
    for i in range(out.shape[0]):
        for x in range(out.shape[1]):
            out[i, x] = part[i, x] - terms(i, x)
    write_faces(lambda j, x: out[j, x], faces)


def put_sums(sums, vecs):
    b, r, s, w, z = vecs
    table = {"b": b, "r": r, "s": s, "w": w, "z": z}
    lanes = lax.broadcasted_iota(jnp.int32, (1, sums.shape[2]), 1)
    row = jnp.zeros((1, sums.shape[2]), F32)
    for k, name in enumerate(NAMES):
        left, right = table[name[0]], table[name[1]]
        total = None
        for i in range(b.shape[0]):
            for x in range(b.shape[1]):
                term = left[i, x] * right[i, x]
                total = term if total is None else total + term
        total = jnp.sum(jnp.sum(total, axis=0, keepdims=True), axis=1, keepdims=True)
        row = jnp.where(lanes == k, total, row)
    for d in range(sums.shape[0]):
        sums[d] = row


def second_kernel(first_time, part, trans, h0, h1, h2, h3, b, r, w, *rest):
    if first_time:
        t, sums, *faces = rest
        s, z = w, t
    else:
        s_rest, z_rest, t, s, z, sums, *faces = rest
    terms = halo_terms((h0, h1, h2, h3), trans)
    for i in range(t.shape[0]):
        for x in range(t.shape[1]):
            t[i, x] = part[i, x] - terms(i, x)
            if not first_time:
                s[i, x] = w[i, x] + s_rest[i, x]
                z[i, x] = t[i, x] + z_rest[i, x]
    if faces:
        write_faces(lambda j, x: z[j, x], faces)
    put_sums(sums, (b, r, s, w, z))


def coefficients(sums):
    row = sums[0]
    for d in range(1, sums.shape[0]):
        row = row + sums[d]
    lanes = lax.broadcasted_iota(jnp.int32, row.shape, 1)
    v = {
        name: jnp.sum(jnp.where(lanes == k, row, 0.0), axis=1, keepdims=True)
        for k, name in enumerate(NAMES)
    }
    alpha = v["br"] / v["bs"]
    inner = v["rw"] - alpha * (v["rz"] + v["sw"]) + alpha * alpha * v["sz"]
    square = v["ww"] - 2.0 * alpha * v["wz"] + alpha * alpha * v["zz"]
    omega = inner / square
    beta = -(v["bw"] - alpha * v["bz"]) / v["bs"]
    return alpha, omega, beta


def third_kernel(first_time, part, trans, h0, h1, h2, h3, sums, r, w, t, *rest):
    if first_time:
        r_out, w_out, x_out, p_out, s_rest, z_rest, *faces = rest
        s, z, p, x_in = w, t, r, None
    else:
        s, z, p, x_in, r_out, w_out, x_out, p_out, s_rest, z_rest, *faces = rest
    terms = halo_terms((h0, h1, h2, h3), trans)
    alpha, omega, beta = coefficients(sums)
    for i in range(r.shape[0]):
        for x in range(r.shape[1]):
            v = part[i, x] - terms(i, x)
            q = r[i, x] - alpha * s[i, x]
            y = w[i, x] - alpha * z[i, x]
            new_r = q - omega * y
            r_out[i, x] = new_r
            w_out[i, x] = y - omega * (t[i, x] - alpha * v)
            step = alpha * p[i, x] + omega * q
            x_out[i, x] = step if x_in is None else x_in[i, x] + step
            p_out[i, x] = new_r + beta * (p[i, x] - omega * s[i, x])
            s_rest[i, x] = beta * (s[i, x] - omega * z[i, x])
            z_rest[i, x] = beta * (z[i, x] - omega * v)
    write_faces(lambda j, x: w_out[j, x], faces)


def last_kernel(sums, r, w, s, z, p, x_in, x_out, r_out):
    alpha, omega, _ = coefficients(sums)
    for i in range(r.shape[0]):
        for x in range(r.shape[1]):
            q = r[i, x] - alpha * s[i, x]
            y = w[i, x] - alpha * z[i, x]
            x_out[i, x] = x_in[i, x] + alpha * p[i, x] + omega * q
            r_out[i, x] = q - omega * y


def body(
    right_side,
    accumulation,
    transmissibility,
    completion,
    live_count,
    owner,
    cell_to_well,
    well_to_cell,
    inverse,
):
    components, cells_x, cells_y, cells_z = right_side.shape
    wells, segb = completion.shape
    devices = lax.axis_size("res") * lax.axis_size("grp")
    field = (right_side.shape, F32)
    face_outs = [((components, cells_y, cells_z), F32)] * 2 + [((components * cells_x, cells_z), F32)] * 2
    sums_out = ((devices, 1, 128), F32)
    trans = transmissibility

    faces = call(face_kernel, face_outs, [right_side])
    halo = exchange(faces)
    moved = lax.all_to_all(inverse[0], "grp", split_axis=0, concat_axis=0, tiled=True)
    diag, place, column, take, give = call(
        prepare_kernel,
        [
            (accumulation.shape, F32),
            ((cells_z, wells * segb), BF16),
            (completion.shape, jnp.int32),
            (cell_to_well.shape, F32),
            (well_to_cell.shape, F32),
        ],
        [accumulation, trans, completion, live_count, cell_to_well, well_to_cell],
        [VMEM, VMEM, VMEM, SMEM, VMEM, VMEM],
    )
    first, second = call(
        pick_kernel, [((wells, segb, segb), BF16)] * 2, [owner, moved], [SMEM, VMEM]
    )

    def inner(vec):
        return call(
            inner_kernel,
            [field],
            [vec, trans, diag, place, column, take, give, first, second],
            scratch=[pltpu.VMEM((4,) + vec.shape, F32)],
            flops=2_000_000_000,
            moved=8_000_000,
        )[0]

    def reduced(sums):
        return lax.all_to_all(sums, ("res", "grp"), split_axis=0, concat_axis=0, tiled=True)

    b = right_side
    w, *faces = call(apply_kernel, [field] + face_outs, [inner(b), trans, *halo])
    r, s, p, x = b, w, b, None
    for index in range(ITERS):
        start, end = index == 0, index + 1 == ITERS
        halo = exchange(faces)
        part = inner(w)
        tail = [] if end else face_outs
        if start:
            t, sums, *faces = call(
                functools.partial(second_kernel, True),
                [field, sums_out] + tail,
                [part, trans, *halo, b, r, w],
            )
            z = t
        else:
            t, s, z, sums, *faces = call(
                functools.partial(second_kernel, False),
                [field] * 3 + [sums_out] + tail,
                [part, trans, *halo, b, r, w, s_rest, z_rest],
            )
        if end:
            break
        halo = exchange(faces)
        sums = reduced(sums)
        part = inner(z)
        more = [] if start else [s, z, p, x]
        r, w, x, p, s_rest, z_rest, *faces = call(
            functools.partial(third_kernel, start),
            [field] * 6 + face_outs,
            [part, trans, *halo, sums, r, w, t, *more],
        )
    x, r = call(last_kernel, [field, field], [reduced(sums), r, w, s, z, p, x])
    return (x, r)


def solution(mesh):
    return jax.shard_map(
        body,
        mesh=mesh,
        in_specs=(
            P(None, "res", "grp", None),
            P(None, None, "res", "grp", None),
            P(None, None, None, "res", "grp", None),
            P(("res", "grp"), None),
            P(("res", "grp")),
            P(("res", "grp"), None),
            P(("res", "grp"), None, None),
            P(("res", "grp"), None, None),
            P(("res", "grp"), None, None, None, None),
        ),
        out_specs=(P(None, "res", "grp", None), P(None, "res", "grp", None)),
        check_vma=False,
    )
```

time: 876 us -> 176 us (0.20); the launches traced: 862 us -> 174 us
  blocking collectives: 339 us -> 10.1 us
  other arithmetic: 207 us -> 0 us
  local copies, waits for them, and re-layouts: 204 us -> 51.7 us
  waiting for transfers between devices: 2.1 us -> 35.6 us
  matrix products: 28.8 us -> 0 us
  Pallas kernels: 0 us -> 28.4 us
  starting transfers between devices: 64.2 us -> 47.3 us
  between operations: 16.6 us -> 1.24 us
    psum x8 -> x0, blocking collectives: 339 us -> none  [the longest x3 127 us: body(): lax.psum((jnp.sum(second * middle), jnp.sum(second * second)), ('res', 'g...]
    scatter-add x6 -> x0, other arithmetic: 104 us -> none  [operator(): out_flat = result.reshape(components, -1).at[:, flat_index].add(-correction)]
    gather x6 -> x0, local copies, waits for them, and re-layouts: 65.7 us -> none  [operator(): flat[:, flat_index].reshape(components, blocks, segb)]
    sub x9 -> x0, local copies, waits for them, and re-layouts: 49.6 us -> none  [the longest x6 32.8 us: stencil(): result - jnp.sum(transmissibility[face] * beside_list[face][None], axis=1)]
    reduce_sum x30 -> x0, other arithmetic: 49.4 us -> none  [the longest x3 15.6 us: body(): jnp.sum(second * second)]
    reshape x12 -> x0, local copies, waits for them, and re-layouts: 47.5 us -> none  [the longest x6 34.6 us: operator(): return out_flat.reshape(vector.shape)]
    unnamed x37 -> x173, local copies, waits for them, and re-layouts: 11.3 us -> 51.7 us
    all_to_all x1, waiting for transfers between devices: 0.01 us -> 30.8 us  [body(): lax.all_to_all(inverse[0], 'grp', split_axis=0, concat_axis=0, tiled=True)]
  transfers between devices with their start and end apart: 25 -> 27, of which waited for: 1 -> 4; matrix products, arithmetic and copies ran while one was open for 19% -> 1% of each run, Pallas kernels for 0% -> 13%
where the time goes in v1:
time: 176 us; the launch traced here: 174 us
  local copies, waits for them, and re-layouts  51.7 us (29%)
  starting transfers between devices  47.3 us (27%)
  waiting for transfers between devices  35.6 us (20%)
  Pallas kernels  28.4 us (16%)
  blocking collectives  10.1 us (6%)
    unnamed x173, local copies, waits for them, and re-layouts  51.7 us
    ppermute x24, starting transfers between devices, exchange(): out.append(lax.ppermute(face, axis, pairs))  33.6 us
    all_to_all x1, waiting for transfers between devices, body(): lax.all_to_all(inverse[0], 'grp', split_axis=0, concat_axis=0, tiled=True)  30.8 us
    pallas_call x16, Pallas kernels, call(): pl.pallas_call(kernel, out_shape=[jax.ShapeDtypeStruct(shape, dtype) for...  28.4 us
    all_to_all x1, blocking collectives, reduced(): lax.all_to_all(sums, ('res', 'grp'), split_axis=0, concat_axis=0, tiled=T...  10.1 us
    all_to_all x2, starting transfers between devices, reduced(): lax.all_to_all(sums, ('res', 'grp'), split_axis=0, concat_axis=0, tiled=T...  8.58 us
    all_to_all x1, starting transfers between devices, body(): lax.all_to_all(inverse[0], 'grp', split_axis=0, concat_axis=0, tiled=True)  5.13 us
    ppermute x24, waiting for transfers between devices, exchange(): out.append(lax.ppermute(face, axis, pairs))  4.8 us
  transfers between devices with their start and end apart: 27, of which 4 were waited for; matrix products, arithmetic and copies ran while one was open for 1% of the time, Pallas kernels for 13%

profile of v1, /device:TPU:0, one launch (start us, length us, event | category | flops | bytes accessed | tf_op | source)
XLA Modules:
  0.0 174.3 jit_solution(7669165905611425487)
XLA Ops:
  0.7 5.1 %all-to-all-start = ((f32[4,4,256,256]{3,2,1,0:T(8,128)}), f32[4,4,256,256]{3,2,1,0:T(8,128)}, u32[]{:S(2)}, u32[]{:S(2)}) async-start(f32[4,4,256,256]{3,2,1,0:T(8,128)} %bitcast.1), calls=%async_computation | async-start | bytes 8388608 | tf_op jit(solution)/shard_map/all_to_all | solution.py:349
  7.9 2.6 %collective-permute-start.3 = (f32[6,512]{1,0:T(8,128)}, f32[6,512]{1,0:T(8,128)}, u32[]{:S(2)}, u32[]{:S(2)}) collective-permute-start(f32[6,512]{1,0:T(8,128)} %get-tuple-element.65), channel_id=1, source_target_pairs={{0,3},{1,2},{2,1},{3,0},{4,7},{5,6},{6,5},{7,4},{8,11},{9,10},{10,... | collective-permute-start | bytes 36872 | tf_op jit(solution)/shard_map/ppermute | solution.py:41
  10.5 2.0 %collective-permute-start = (f32[3,16,512]{2,1,0:T(8,128)}, f32[3,16,512]{2,1,0:T(8,128)}, u32[]{:S(2)}, u32[]{:S(2)}) collective-permute-start(f32[3,16,512]{2,1,0:T(8,128)} %get-tuple-element.62), channel_id=1, source_target_pairs={{0,4},{4,0},{8,12},{12,8},{16,20},{20,16},{24,28},{28,24},{1,5},{5... | collective-permute-start | bytes 294920 | tf_op jit(solution)/shard_map/ppermute | solution.py:41
  12.4 3.6 %collective-permute-start.1 = (f32[3,16,512]{2,1,0:T(8,128)}, f32[3,16,512]{2,1,0:T(8,128)}, u32[]{:S(2)}, u32[]{:S(2)}) collective-permute-start(f32[3,16,512]{2,1,0:T(8,128)} %get-tuple-element.63), channel_id=1, source_target_pairs={{0,28},{4,8},{8,4},{12,16},{16,12},{20,24},{24,20},{28,0},{1,29},{... | collective-permute-start | bytes 294920 | tf_op jit(solution)/shard_map/ppermute | solution.py:41
  17.6 1.1 copy-done.55
  19.4 1.2 shard_map.104
  20.6 1.3 copy-done.1
  24.0 30.8 %all-to-all-done.moved = f32[4,4,256,256]{3,2,1,0:T(8,128)} async-done(((f32[4,4,256,256]{3,2,1,0:T(8,128)}), f32[4,4,256,256]{3,2,1,0:T(8,128)}, u32[]{:S(2)}, u32[]{:S(2)}) %all-to-all-start) | async-done | bytes 4194336 | tf_op jit(solution)/shard_map/all_to_all | solution.py:349
  54.9 2.7 %shard_map.105 = (bf16[8,256,256]{2,1,0:T(8,128)(2,1)S(1)}, bf16[8,256,256]{2,1,0:T(8,128)(2,1)S(1)}) custom-call(s32[8,1]{1,0:T(8,128)S(1)} %copy.13.owner, f32[4,4,256,256]{3,2,1,0:T(8,128)} %all-to-all-done.moved), custom_call_target="tpu_custom_call" | custom-call | flops 1000000 | bytes 1000000 | tf_op jit(solution)/shard_map/pallas_call | solution.py:20
  57.9 2.9 %shard_map.106.part = f32[3,2,16,512]{3,2,1,0:T(8,128)S(1)} custom-call(f32[3,2,16,512]{3,2,1,0:T(8,128)S(1)} %copy-done.24, f32[6,3,3,2,16,512]{5,4,3,2,1,0:T(8,128)S(1)} %copy-done, f32[3,3,2,16,512]{4,3,2,1,0:T(8,128)S(1)} %copy-done.18, bf16[512,2048]{1,0:T(8,128)(2,1)S(1)} %copy-done.2, s32[8,256]{1,0:T(8,128)S(1)} %get-tuple-element.57.column, ...), custom_call_target="tpu_custom_call" | custom-call | flops 2000000000 | bytes 8000000 | tf_op jit(solution)/shard_map/pallas_call | solution.py:20
  60.8 1.1 shard_map.108
  62.1 2.7 %collective-permute-start.4 = (f32[3,16,512]{2,1,0:T(8,128)S(1)}, f32[3,16,512]{2,1,0:T(8,128)S(1)}, u32[]{:S(2)}, u32[]{:S(2)}) collective-permute-start(f32[3,16,512]{2,1,0:T(8,128)S(1)} %get-tuple-element.67), channel_id=1, source_target_pairs={{0,4},{4,0},{8,12},{12,8},{16,20},{20,16},{24,28},{28,24},{1,5},{5... | collective-permute-start | bytes 294920 | tf_op jit(solution)/shard_map/ppermute | solution.py:41
  64.8 3.6 %collective-permute-start.5 = (f32[3,16,512]{2,1,0:T(8,128)S(1)}, f32[3,16,512]{2,1,0:T(8,128)S(1)}, u32[]{:S(2)}, u32[]{:S(2)}) collective-permute-start(f32[3,16,512]{2,1,0:T(8,128)S(1)} %get-tuple-element.68), channel_id=1, source_target_pairs={{0,28},{4,8},{8,4},{12,16},{16,12},{20,24},{24,20},{28,0},{1,29},{... | collective-permute-start | bytes 294920 | tf_op jit(solution)/shard_map/ppermute | solution.py:41
  68.3 2.9 %shard_map.109.part = f32[3,2,16,512]{3,2,1,0:T(8,128)S(1)} custom-call(f32[3,2,16,512]{3,2,1,0:T(8,128)S(1)} %get-tuple-element.66.vec.w, f32[6,3,3,2,16,512]{5,4,3,2,1,0:T(8,128)S(1)} %copy-done, f32[3,3,2,16,512]{4,3,2,1,0:T(8,128)S(1)} %copy-done.18, bf16[512,2048]{1,0:T(8,128)(2,1)S(1)} %copy-done.2, s32[8,256]{1,0:T(8,128)S(1)} %get-tuple-element.57.column, ...), custom_call_target="tpu_custom_call" | custom-call | flops 2000000000 | bytes 8000000 | tf_op jit(solution)/shard_map/pallas_call | solution.py:20
  76.2 5.3 %all-to-all-start.1 = ((f32[32,1,128]{2,1,0:T(1,128)}), f32[32,1,128]{2,1,0:T(1,128)}, u32[]{:S(2)}, u32[]{:S(2)}) async-start(f32[32,1,128]{2,1,0:T(1,128)} %copy-done.73), calls=%async_computation.1 | async-start | bytes 32768 | tf_op jit(solution)/shard_map/all_to_all | solution.py:377
  81.6 1.6 collective-permute-start.11
  83.2 1.5 collective-permute-start.8
  84.7 3.3 %collective-permute-start.9 = (f32[3,16,512]{2,1,0:T(8,128)}, f32[3,16,512]{2,1,0:T(8,128)}, u32[]{:S(2)}, u32[]{:S(2)}) collective-permute-start(f32[3,16,512]{2,1,0:T(8,128)} %copy-done.78), channel_id=1, source_target_pairs={{0,28},{4,8},{8,4},{12,16},{16,12},{20,24},{24,20},{28,0},{1,29},{... | collective-permute-start | bytes 294920 | tf_op jit(solution)/shard_map/ppermute | solution.py:41
  88.0 1.6 copy-done.3
  89.6 1.2 copy-done.8
  90.9 1.2 copy-done.13
  92.1 1.1 copy-done.19
  95.6 2.9 %shard_map.111.part = f32[3,2,16,512]{3,2,1,0:T(8,128)S(1)} custom-call(f32[3,2,16,512]{3,2,1,0:T(8,128)S(1)} %copy-done.46, f32[6,3,3,2,16,512]{5,4,3,2,1,0:T(8,128)S(1)} %copy-done, f32[3,3,2,16,512]{4,3,2,1,0:T(8,128)S(1)} %copy-done.19, bf16[512,2048]{1,0:T(8,128)(2,1)S(1)} %copy-done.3, s32[8,256]{1,0:T(8,128)S(1)} %get-tuple-element.57.column, ...), custom_call_target="tpu_custom_call" | custom-call | flops 2000000000 | bytes 8000000 | tf_op jit(solution)/shard_map/pallas_call | solution.py:20
  100.4 1.1 copy-done.25
  101.5 1.2 copy-done.28
  106.0 1.3 shard_map.112
  108.0 2.0 %collective-permute-start.13 = (f32[3,16,512]{2,1,0:T(8,128)S(1)}, f32[3,16,512]{2,1,0:T(8,128)S(1)}, u32[]{:S(2)}, u32[]{:S(2)}) collective-permute-start(f32[3,16,512]{2,1,0:T(8,128)S(1)} %get-tuple-element.79), channel_id=1, source_target_pairs={{0,28},{4,8},{8,4},{12,16},{16,12},{20,24},{24,20},{28,0},{1,29},{... | collective-permute-start | bytes 294920 | tf_op jit(solution)/shard_map/ppermute | solution.py:41
  110.0 1.1 copy-done.20
  111.1 2.9 %shard_map.113.part = f32[3,2,16,512]{3,2,1,0:T(8,128)S(1)} custom-call(f32[3,2,16,512]{3,2,1,0:T(8,128)S(1)} %get-tuple-element.77.vec.w, f32[6,3,3,2,16,512]{5,4,3,2,1,0:T(8,128)S(1)} %copy-done, f32[3,3,2,16,512]{4,3,2,1,0:T(8,128)S(1)} %copy-done.20, bf16[512,2048]{1,0:T(8,128)(2,1)S(1)} %copy-done.4, s32[8,256]{1,0:T(8,128)S(1)} %get-tuple-element.57.column, ...), custom_call_target="tpu_custom_call" | custom-call | flops 2000000000 | bytes 8000000 | tf_op jit(solution)/shard_map/pallas_call | solution.py:20
  114.0 1.4 collective-permute-done.13.h1
  121.0 3.2 %all-to-all-start.2 = ((f32[32,1,128]{2,1,0:T(1,128)}), f32[32,1,128]{2,1,0:T(1,128)}, u32[]{:S(2)}, u32[]{:S(2)}) async-start(f32[32,1,128]{2,1,0:T(1,128)} %copy-done.72), calls=%async_computation.2 | async-start | bytes 32768 | tf_op jit(solution)/shard_map/all_to_all | solution.py:377
  124.5 1.6 collective-permute-start.19
  126.2 1.5 collective-permute-start.16
  127.6 3.3 %collective-permute-start.17 = (f32[3,16,512]{2,1,0:T(8,128)}, f32[3,16,512]{2,1,0:T(8,128)}, u32[]{:S(2)}, u32[]{:S(2)}) collective-permute-start(f32[3,16,512]{2,1,0:T(8,128)} %copy-done.76), channel_id=1, source_target_pairs={{0,28},{4,8},{8,4},{12,16},{16,12},{20,24},{24,20},{28,0},{1,29},{... | collective-permute-start | bytes 294920 | tf_op jit(solution)/shard_map/ppermute | solution.py:41
  131.0 1.6 copy-done.5
  132.6 1.2 copy-done.10
  133.8 1.2 copy-done.15
  135.0 1.1 copy-done.21
  138.5 2.9 %shard_map.115.part = f32[3,2,16,512]{3,2,1,0:T(8,128)S(1)} custom-call(f32[3,2,16,512]{3,2,1,0:T(8,128)S(1)} %copy-done.51, f32[6,3,3,2,16,512]{5,4,3,2,1,0:T(8,128)S(1)} %copy-done, f32[3,3,2,16,512]{4,3,2,1,0:T(8,128)S(1)} %copy-done.21, bf16[512,2048]{1,0:T(8,128)(2,1)S(1)} %copy-done.5, s32[8,256]{1,0:T(8,128)S(1)} %get-tuple-element.57.column, ...), custom_call_target="tpu_custom_call" | custom-call | flops 2000000000 | bytes 8000000 | tf_op jit(solution)/shard_map/pallas_call | solution.py:20
  143.4 1.1 copy-done.30
  144.4 1.3 copy-done.44
  152.8 1.3 shard_map.116
  154.8 2.0 %collective-permute-start.21 = (f32[3,16,512]{2,1,0:T(8,128)S(1)}, f32[3,16,512]{2,1,0:T(8,128)S(1)}, u32[]{:S(2)}, u32[]{:S(2)}) collective-permute-start(f32[3,16,512]{2,1,0:T(8,128)S(1)} %get-tuple-element.97), channel_id=1, source_target_pairs={{0,28},{4,8},{8,4},{12,16},{16,12},{20,24},{24,20},{28,0},{1,29},{... | collective-permute-start | bytes 294920 | tf_op jit(solution)/shard_map/ppermute | solution.py:41
  156.8 2.9 %shard_map.117.part = f32[3,2,16,512]{3,2,1,0:T(8,128)S(1)} custom-call(f32[3,2,16,512]{3,2,1,0:T(8,128)S(1)} %get-tuple-element.95.vec.w, f32[6,3,3,2,16,512]{5,4,3,2,1,0:T(8,128)S(1)} %copy-done, f32[3,3,2,16,512]{4,3,2,1,0:T(8,128)S(1)} %copy-done.22, bf16[512,2048]{1,0:T(8,128)(2,1)S(1)} %copy-done.6, s32[8,256]{1,0:T(8,128)S(1)} %get-tuple-element.57.column, ...), custom_call_target="tpu_custom_call" | custom-call | flops 2000000000 | bytes 8000000 | tf_op jit(solution)/shard_map/pallas_call | solution.py:20
  159.8 2.5 %collective-permute-done.21.h1 = f32[3,16,512]{2,1,0:T(8,128)S(1)} collective-permute-done((f32[3,16,512]{2,1,0:T(8,128)S(1)}, f32[3,16,512]{2,1,0:T(8,128)S(1)}, u32[]{:S(2)}, u32[]{:S(2)}) %collective-permute-start.21) | collective-permute-done | bytes 98336 | tf_op jit(solution)/shard_map/ppermute | solution.py:41
  162.3 1.0 shard_map.118
  163.3 10.1 %all_to_all.20.sums = f32[32,1,128]{2,1,0:T(1,128)S(1)} all-to-all(f32[32,1,128]{2,1,0:T(1,128)S(1)} %get-tuple-element.103), channel_id=1, replica_groups=mesh['res'=8,'grp'=4] {'res','grp'}, dimensions={0} | all-to-all | bytes 32768 | tf_op jit(solution)/shard_map/all_to_all | solution.py:377
  173.3 0.9 shard_map.119
  (196 shorter events, 38.1 us)
Async XLA Ops:
  0.6 15.4 %copy-start.84 = (s32[8,1]{0,1:T(1,128)S(1)}, s32[8,1]{0,1:T(1,128)}, u32[]{:S(2)}) copy-start(s32[8,1]{0,1:T(1,128)} %param.14) | copy-start | bytes 100
  0.6 17.0 %copy-start = (f32[6,3,3,2,16,512]{5,4,3,2,1,0:T(8,128)S(1)}, f32[6,3,3,2,16,512]{5,4,3,2,1,0:T(8,128)}, u32[]{:S(2)}) copy-start(f32[6,3,3,2,16,512]{5,4,3,2,1,0:T(8,128)} %trans.25) | copy-start | bytes 10616836
  0.7 17.0 %copy-start.75 = (s32[8]{0:T(128)S(1)}, s32[8]{0:T(128)}, u32[]{:S(2)}) copy-start(s32[8]{0:T(128)} %live.1) | copy-start | bytes 100
  0.7 54.2 %all-to-all-start = ((f32[4,4,256,256]{3,2,1,0:T(8,128)}), f32[4,4,256,256]{3,2,1,0:T(8,128)}, u32[]{:S(2)}, u32[]{:S(2)}) async-start(f32[4,4,256,256]{3,2,1,0:T(8,128)} %bitcast.1), calls=%async_computation | async-start | bytes 8388608 | tf_op jit(solution)/shard_map/all_to_all | solution.py:349
  7.4 53.3 %collective-permute-start.2 = (f32[6,512]{1,0:T(8,128)}, f32[6,512]{1,0:T(8,128)}, u32[]{:S(2)}, u32[]{:S(2)}) collective-permute-start(f32[6,512]{1,0:T(8,128)} %get-tuple-element.64), channel_id=1, source_target_pairs={{0,1},{1,0},{2,3},{3,2},{4,5},{5,4},{6,7},{7,6},{8,9},{9,8},{10,11... | collective-permute-start | bytes 36872 | tf_op jit(solution)/shard_map/ppermute | solution.py:41
  7.9 52.9 %collective-permute-start.3 = (f32[6,512]{1,0:T(8,128)}, f32[6,512]{1,0:T(8,128)}, u32[]{:S(2)}, u32[]{:S(2)}) collective-permute-start(f32[6,512]{1,0:T(8,128)} %get-tuple-element.65), channel_id=1, source_target_pairs={{0,3},{1,2},{2,1},{3,0},{4,7},{5,6},{6,5},{7,4},{8,11},{9,10},{10,... | collective-permute-start | bytes 36872 | tf_op jit(solution)/shard_map/ppermute | solution.py:41
  10.5 50.3 %collective-permute-start = (f32[3,16,512]{2,1,0:T(8,128)}, f32[3,16,512]{2,1,0:T(8,128)}, u32[]{:S(2)}, u32[]{:S(2)}) collective-permute-start(f32[3,16,512]{2,1,0:T(8,128)} %get-tuple-element.62), channel_id=1, source_target_pairs={{0,4},{4,0},{8,12},{12,8},{16,20},{20,16},{24,28},{28,24},{1,5},{5... | collective-permute-start | bytes 294920 | tf_op jit(solution)/shard_map/ppermute | solution.py:41
  12.4 48.3 %collective-permute-start.1 = (f32[3,16,512]{2,1,0:T(8,128)}, f32[3,16,512]{2,1,0:T(8,128)}, u32[]{:S(2)}, u32[]{:S(2)}) collective-permute-start(f32[3,16,512]{2,1,0:T(8,128)} %get-tuple-element.63), channel_id=1, source_target_pairs={{0,28},{4,8},{8,4},{12,16},{16,12},{20,24},{24,20},{28,0},{1,29},{... | collective-permute-start | bytes 294920 | tf_op jit(solution)/shard_map/ppermute | solution.py:41
  57.6 10.8 %copy-start.7 = (bf16[8,256,256]{2,1,0:T(8,128)(2,1)}, bf16[8,256,256]{2,1,0:T(8,128)(2,1)S(1)}, u32[]{:S(2)}) copy-start(bf16[8,256,256]{2,1,0:T(8,128)(2,1)S(1)} %get-tuple-element.60.first) | copy-start | bytes 3145732
  57.6 10.8 %copy-start.12 = (bf16[8,256,256]{2,1,0:T(8,128)(2,1)}, bf16[8,256,256]{2,1,0:T(8,128)(2,1)S(1)}, u32[]{:S(2)}) copy-start(bf16[8,256,256]{2,1,0:T(8,128)(2,1)S(1)} %get-tuple-element.61.second) | copy-start | bytes 3145732
  61.9 10.2 %copy-start.27 = (f32[3,2,16,512]{3,2,1,0:T(8,128)}, f32[3,2,16,512]{3,2,1,0:T(8,128)S(1)}, u32[]{:S(2)}) copy-start(f32[3,2,16,512]{3,2,1,0:T(8,128)S(1)} %get-tuple-element.66.vec.w) | copy-start | bytes 589828
  61.9 9.3 %collective-permute-start.6 = (f32[6,512]{1,0:T(8,128)S(1)}, f32[6,512]{1,0:T(8,128)S(1)}, u32[]{:S(2)}, u32[]{:S(2)}) collective-permute-start(f32[6,512]{1,0:T(8,128)S(1)} %get-tuple-element.69), channel_id=1, source_target_pairs={{0,1},{1,0},{2,3},{3,2},{4,5},{5,4},{6,7},{7,6},{8,9},{9,8},{10,11... | collective-permute-start | bytes 36872 | tf_op jit(solution)/shard_map/ppermute | solution.py:41
  62.0 9.3 %collective-permute-start.7 = (f32[6,512]{1,0:T(8,128)S(1)}, f32[6,512]{1,0:T(8,128)S(1)}, u32[]{:S(2)}, u32[]{:S(2)}) collective-permute-start(f32[6,512]{1,0:T(8,128)S(1)} %get-tuple-element.70), channel_id=1, source_target_pairs={{0,3},{1,2},{2,1},{3,0},{4,7},{5,6},{6,5},{7,4},{8,11},{9,10},{10,... | collective-permute-start | bytes 36872 | tf_op jit(solution)/shard_map/ppermute | solution.py:41
  62.1 9.2 %collective-permute-start.4 = (f32[3,16,512]{2,1,0:T(8,128)S(1)}, f32[3,16,512]{2,1,0:T(8,128)S(1)}, u32[]{:S(2)}, u32[]{:S(2)}) collective-permute-start(f32[3,16,512]{2,1,0:T(8,128)S(1)} %get-tuple-element.67), channel_id=1, source_target_pairs={{0,4},{4,0},{8,12},{12,8},{16,20},{20,16},{24,28},{28,24},{1,5},{5... | collective-permute-start | bytes 294920 | tf_op jit(solution)/shard_map/ppermute | solution.py:41
  64.8 7.3 %collective-permute-start.5 = (f32[3,16,512]{2,1,0:T(8,128)S(1)}, f32[3,16,512]{2,1,0:T(8,128)S(1)}, u32[]{:S(2)}, u32[]{:S(2)}) collective-permute-start(f32[3,16,512]{2,1,0:T(8,128)S(1)} %get-tuple-element.68), channel_id=1, source_target_pairs={{0,28},{4,8},{8,4},{12,16},{16,12},{20,24},{24,20},{28,0},{1,29},{... | collective-permute-start | bytes 294920 | tf_op jit(solution)/shard_map/ppermute | solution.py:41
  76.2 24.2 %all-to-all-start.1 = ((f32[32,1,128]{2,1,0:T(1,128)}), f32[32,1,128]{2,1,0:T(1,128)}, u32[]{:S(2)}, u32[]{:S(2)}) async-start(f32[32,1,128]{2,1,0:T(1,128)} %copy-done.73), calls=%async_computation.1 | async-start | bytes 32768 | tf_op jit(solution)/shard_map/all_to_all | solution.py:377
  81.5 17.7 %collective-permute-start.10 = (f32[6,512]{1,0:T(8,128)}, f32[6,512]{1,0:T(8,128)S(1)}, u32[]{:S(2)}, u32[]{:S(2)}) collective-permute-start(f32[6,512]{1,0:T(8,128)} %copy-done.83), channel_id=1, source_target_pairs={{0,1},{1,0},{2,3},{3,2},{4,5},{5,4},{6,7},{7,6},{8,9},{9,8},{10,11... | collective-permute-start | bytes 36872 | tf_op jit(solution)/shard_map/ppermute | solution.py:41
  81.6 18.2 %collective-permute-start.11 = (f32[6,512]{1,0:T(8,128)}, f32[6,512]{1,0:T(8,128)S(1)}, u32[]{:S(2)}, u32[]{:S(2)}) collective-permute-start(f32[6,512]{1,0:T(8,128)} %copy-done.82), channel_id=1, source_target_pairs={{0,3},{1,2},{2,1},{3,0},{4,7},{5,6},{6,5},{7,4},{8,11},{9,10},{10,... | collective-permute-start | bytes 36872 | tf_op jit(solution)/shard_map/ppermute | solution.py:41
  83.2 17.2 %collective-permute-start.8 = (f32[3,16,512]{2,1,0:T(8,128)}, f32[3,16,512]{2,1,0:T(8,128)}, u32[]{:S(2)}, u32[]{:S(2)}) collective-permute-start(f32[3,16,512]{2,1,0:T(8,128)} %copy-done.79), channel_id=1, source_target_pairs={{0,4},{4,0},{8,12},{12,8},{16,20},{20,16},{24,28},{28,24},{1,5},{5... | collective-permute-start | bytes 294920 | tf_op jit(solution)/shard_map/ppermute | solution.py:41
  84.7 15.7 %collective-permute-start.9 = (f32[3,16,512]{2,1,0:T(8,128)}, f32[3,16,512]{2,1,0:T(8,128)}, u32[]{:S(2)}, u32[]{:S(2)}) collective-permute-start(f32[3,16,512]{2,1,0:T(8,128)} %copy-done.78), channel_id=1, source_target_pairs={{0,28},{4,8},{8,4},{12,16},{16,12},{20,24},{24,20},{28,0},{1,29},{... | collective-permute-start | bytes 294920 | tf_op jit(solution)/shard_map/ppermute | solution.py:41
  100.4 9.6 %copy-start.4 = (bf16[512,2048]{1,0:T(8,128)(2,1)S(1)}, bf16[512,2048]{1,0:T(8,128)(2,1)}, u32[]{:S(2)}) copy-start(bf16[512,2048]{1,0:T(8,128)(2,1)} %copy-done.1) | copy-start | bytes 6291460
  100.4 9.6 %copy-start.9 = (bf16[8,256,256]{2,1,0:T(8,128)(2,1)S(1)}, bf16[8,256,256]{2,1,0:T(8,128)(2,1)}, u32[]{:S(2)}) copy-start(bf16[8,256,256]{2,1,0:T(8,128)(2,1)} %copy-done.7) | copy-start | bytes 3145732
  100.4 9.6 %copy-start.14 = (bf16[8,256,256]{2,1,0:T(8,128)(2,1)S(1)}, bf16[8,256,256]{2,1,0:T(8,128)(2,1)}, u32[]{:S(2)}) copy-start(bf16[8,256,256]{2,1,0:T(8,128)(2,1)} %copy-done.12) | copy-start | bytes 3145732
  106.0 4.1 %copy-start.34 = (f32[8,3,256]{2,1,0:T(4,128)S(1)}, f32[8,3,256]{2,1,0:T(4,128)}, u32[]{:S(2)}) copy-start(f32[8,3,256]{2,1,0:T(4,128)} %copy-done.31) | copy-start | bytes 73732
  106.0 4.1 %copy-start.40 = (f32[8,3,256]{2,1,0:T(4,128)S(1)}, f32[8,3,256]{2,1,0:T(4,128)}, u32[]{:S(2)}) copy-start(f32[8,3,256]{2,1,0:T(4,128)} %copy-done.37) | copy-start | bytes 73732
  107.3 6.7 %copy-start.56 = (f32[3,2,16,512]{3,2,1,0:T(8,128)}, f32[3,2,16,512]{3,2,1,0:T(8,128)S(1)}, u32[]{:S(2)}) copy-start(f32[3,2,16,512]{3,2,1,0:T(8,128)S(1)} %get-tuple-element.94.rest_3_) | copy-start | bytes 589828
  107.3 6.7 %copy-start.58 = (f32[3,2,16,512]{3,2,1,0:T(8,128)}, f32[3,2,16,512]{3,2,1,0:T(8,128)S(1)}, u32[]{:S(2)}) copy-start(f32[3,2,16,512]{3,2,1,0:T(8,128)S(1)} %get-tuple-element.93.rest_2_) | copy-start | bytes 589828
  107.3 8.2 %copy-start.29 = (f32[3,2,16,512]{3,2,1,0:T(8,128)}, f32[3,2,16,512]{3,2,1,0:T(8,128)S(1)}, u32[]{:S(2)}) copy-start(f32[3,2,16,512]{3,2,1,0:T(8,128)S(1)} %get-tuple-element.77.vec.w) | copy-start | bytes 589828
  107.3 8.2 %copy-start.43 = (f32[3,2,16,512]{3,2,1,0:T(8,128)}, f32[3,2,16,512]{3,2,1,0:T(8,128)S(1)}, u32[]{:S(2)}) copy-start(f32[3,2,16,512]{3,2,1,0:T(8,128)S(1)} %get-tuple-element.82.r) | copy-start | bytes 589828
  107.3 6.7 %collective-permute-start.14 = (f32[6,512]{1,0:T(8,128)S(1)}, f32[6,512]{1,0:T(8,128)S(1)}, u32[]{:S(2)}, u32[]{:S(2)}) collective-permute-start(f32[6,512]{1,0:T(8,128)S(1)} %get-tuple-element.80), channel_id=1, source_target_pairs={{0,1},{1,0},{2,3},{3,2},{4,5},{5,4},{6,7},{7,6},{8,9},{9,8},{10,11... | collective-permute-start | bytes 36872 | tf_op jit(solution)/shard_map/ppermute | solution.py:41
  107.4 6.7 %collective-permute-start.15 = (f32[6,512]{1,0:T(8,128)S(1)}, f32[6,512]{1,0:T(8,128)S(1)}, u32[]{:S(2)}, u32[]{:S(2)}) collective-permute-start(f32[6,512]{1,0:T(8,128)S(1)} %get-tuple-element.81), channel_id=1, source_target_pairs={{0,3},{1,2},{2,1},{3,0},{4,7},{5,6},{6,5},{7,4},{8,11},{9,10},{10,... | collective-permute-start | bytes 36872 | tf_op jit(solution)/shard_map/ppermute | solution.py:41
  108.0 6.0 %collective-permute-start.12 = (f32[3,16,512]{2,1,0:T(8,128)S(1)}, f32[3,16,512]{2,1,0:T(8,128)S(1)}, u32[]{:S(2)}, u32[]{:S(2)}) collective-permute-start(f32[3,16,512]{2,1,0:T(8,128)S(1)} %get-tuple-element.78), channel_id=1, source_target_pairs={{0,4},{4,0},{8,12},{12,8},{16,20},{20,16},{24,28},{28,24},{1,5},{5... | collective-permute-start | bytes 294920 | tf_op jit(solution)/shard_map/ppermute | solution.py:41
  108.0 7.5 %collective-permute-start.13 = (f32[3,16,512]{2,1,0:T(8,128)S(1)}, f32[3,16,512]{2,1,0:T(8,128)S(1)}, u32[]{:S(2)}, u32[]{:S(2)}) collective-permute-start(f32[3,16,512]{2,1,0:T(8,128)S(1)} %get-tuple-element.79), channel_id=1, source_target_pairs={{0,28},{4,8},{8,4},{12,16},{16,12},{20,24},{24,20},{28,0},{1,29},{... | collective-permute-start | bytes 294920 | tf_op jit(solution)/shard_map/ppermute | solution.py:41
  121.0 22.3 %all-to-all-start.2 = ((f32[32,1,128]{2,1,0:T(1,128)}), f32[32,1,128]{2,1,0:T(1,128)}, u32[]{:S(2)}, u32[]{:S(2)}) async-start(f32[32,1,128]{2,1,0:T(1,128)} %copy-done.72), calls=%async_computation.2 | async-start | bytes 32768 | tf_op jit(solution)/shard_map/all_to_all | solution.py:377
  124.3 17.8 %collective-permute-start.18 = (f32[6,512]{1,0:T(8,128)}, f32[6,512]{1,0:T(8,128)S(1)}, u32[]{:S(2)}, u32[]{:S(2)}) collective-permute-start(f32[6,512]{1,0:T(8,128)} %copy-done.81), channel_id=1, source_target_pairs={{0,1},{1,0},{2,3},{3,2},{4,5},{5,4},{6,7},{7,6},{8,9},{9,8},{10,11... | collective-permute-start | bytes 36872 | tf_op jit(solution)/shard_map/ppermute | solution.py:41
  124.5 18.2 %collective-permute-start.19 = (f32[6,512]{1,0:T(8,128)}, f32[6,512]{1,0:T(8,128)S(1)}, u32[]{:S(2)}, u32[]{:S(2)}) collective-permute-start(f32[6,512]{1,0:T(8,128)} %copy-done.80), channel_id=1, source_target_pairs={{0,3},{1,2},{2,1},{3,0},{4,7},{5,6},{6,5},{7,4},{8,11},{9,10},{10,... | collective-permute-start | bytes 36872 | tf_op jit(solution)/shard_map/ppermute | solution.py:41
  126.2 17.2 %collective-permute-start.16 = (f32[3,16,512]{2,1,0:T(8,128)}, f32[3,16,512]{2,1,0:T(8,128)}, u32[]{:S(2)}, u32[]{:S(2)}) collective-permute-start(f32[3,16,512]{2,1,0:T(8,128)} %copy-done.77), channel_id=1, source_target_pairs={{0,4},{4,0},{8,12},{12,8},{16,20},{20,16},{24,28},{28,24},{1,5},{5... | collective-permute-start | bytes 294920 | tf_op jit(solution)/shard_map/ppermute | solution.py:41
  127.6 15.7 %collective-permute-start.17 = (f32[3,16,512]{2,1,0:T(8,128)}, f32[3,16,512]{2,1,0:T(8,128)}, u32[]{:S(2)}, u32[]{:S(2)}) collective-permute-start(f32[3,16,512]{2,1,0:T(8,128)} %copy-done.76), channel_id=1, source_target_pairs={{0,28},{4,8},{8,4},{12,16},{16,12},{20,24},{24,20},{28,0},{1,29},{... | collective-permute-start | bytes 294920 | tf_op jit(solution)/shard_map/ppermute | solution.py:41
  143.3 13.5 %copy-start.6 = (bf16[512,2048]{1,0:T(8,128)(2,1)S(1)}, bf16[512,2048]{1,0:T(8,128)(2,1)}, u32[]{:S(2)}) copy-start(bf16[512,2048]{1,0:T(8,128)(2,1)} %copy-done.1) | copy-start | bytes 6291460
  143.3 13.5 %copy-start.11 = (bf16[8,256,256]{2,1,0:T(8,128)(2,1)S(1)}, bf16[8,256,256]{2,1,0:T(8,128)(2,1)}, u32[]{:S(2)}) copy-start(bf16[8,256,256]{2,1,0:T(8,128)(2,1)} %copy-done.7) | copy-start | bytes 3145732
  143.3 13.5 %copy-start.16 = (bf16[8,256,256]{2,1,0:T(8,128)(2,1)S(1)}, bf16[8,256,256]{2,1,0:T(8,128)(2,1)}, u32[]{:S(2)}) copy-start(bf16[8,256,256]{2,1,0:T(8,128)(2,1)} %copy-done.12) | copy-start | bytes 3145732
  143.3 13.5 %copy-start.22 = (f32[3,3,2,16,512]{4,3,2,1,0:T(8,128)S(1)}, f32[3,3,2,16,512]{4,3,2,1,0:T(8,128)}, u32[]{:S(2)}) copy-start(f32[3,3,2,16,512]{4,3,2,1,0:T(8,128)} %copy-done.17) | copy-start | bytes 1769476
  152.8 4.0 %copy-start.42 = (f32[8,3,256]{2,1,0:T(4,128)S(1)}, f32[8,3,256]{2,1,0:T(4,128)}, u32[]{:S(2)}) copy-start(f32[8,3,256]{2,1,0:T(4,128)} %copy-done.37) | copy-start | bytes 73732
  154.1 5.7 %collective-permute-start.22 = (f32[6,512]{1,0:T(8,128)S(1)}, f32[6,512]{1,0:T(8,128)S(1)}, u32[]{:S(2)}, u32[]{:S(2)}) collective-permute-start(f32[6,512]{1,0:T(8,128)S(1)} %get-tuple-element.98), channel_id=1, source_target_pairs={{0,1},{1,0},{2,3},{3,2},{4,5},{5,4},{6,7},{7,6},{8,9},{9,8},{10,11... | collective-permute-start | bytes 36872 | tf_op jit(solution)/shard_map/ppermute | solution.py:41
  154.2 5.6 %collective-permute-start.23 = (f32[6,512]{1,0:T(8,128)S(1)}, f32[6,512]{1,0:T(8,128)S(1)}, u32[]{:S(2)}, u32[]{:S(2)}) collective-permute-start(f32[6,512]{1,0:T(8,128)S(1)} %get-tuple-element.99), channel_id=1, source_target_pairs={{0,3},{1,2},{2,1},{3,0},{4,7},{5,6},{6,5},{7,4},{8,11},{9,10},{10,... | collective-permute-start | bytes 36872 | tf_op jit(solution)/shard_map/ppermute | solution.py:41
  154.8 5.0 %collective-permute-start.20 = (f32[3,16,512]{2,1,0:T(8,128)S(1)}, f32[3,16,512]{2,1,0:T(8,128)S(1)}, u32[]{:S(2)}, u32[]{:S(2)}) collective-permute-start(f32[3,16,512]{2,1,0:T(8,128)S(1)} %get-tuple-element.96), channel_id=1, source_target_pairs={{0,4},{4,0},{8,12},{12,8},{16,20},{20,16},{24,28},{28,24},{1,5},{5... | collective-permute-start | bytes 294920 | tf_op jit(solution)/shard_map/ppermute | solution.py:41
  154.8 7.5 %collective-permute-start.21 = (f32[3,16,512]{2,1,0:T(8,128)S(1)}, f32[3,16,512]{2,1,0:T(8,128)S(1)}, u32[]{:S(2)}, u32[]{:S(2)}) collective-permute-start(f32[3,16,512]{2,1,0:T(8,128)S(1)} %get-tuple-element.97), channel_id=1, source_target_pairs={{0,28},{4,8},{8,4},{12,16},{16,12},{20,24},{24,20},{28,0},{1,29},{... | collective-permute-start | bytes 294920 | tf_op jit(solution)/shard_map/ppermute | solution.py:41
  156.8 5.5 %copy-start.26 = (f32[3,2,16,512]{3,2,1,0:T(8,128)S(1)}, f32[3,2,16,512]{3,2,1,0:T(8,128)}, u32[]{:S(2)}) copy-start(f32[3,2,16,512]{3,2,1,0:T(8,128)} %b.5) | copy-start | bytes 589828
  (64 other events, 68.6 us)

commit v2 on v1

--- a/solution.py
+++ b/solution.py
@@ -138,8 +138,7 @@
 
 
 def gather_well(both, place, column, weight, b):
-    segb = weight.shape[2]
-    components = weight.shape[1]
+    components, _, segb = weight.shape
     part = slice(b * segb, (b + 1) * segb)
     found = dot(both, place[:, part])
     rows = found.shape[0] // 2
@@ -149,7 +148,7 @@
     coupled = jnp.zeros((1, segb), F32)
     for i in range(components):
         part = jnp.where(here, found[i * per : (i + 1) * per], 0.0)
-        coupled = coupled + jnp.sum(part, axis=0, keepdims=True) * weight[b, i : i + 1]
+        coupled = coupled + jnp.sum(part, axis=0, keepdims=True) * weight[i, b : b + 1]
     return coupled
 
 
@@ -162,32 +161,85 @@
 
 
 def scatter_well(value, place, column, weight, rows, b):
-    segb = weight.shape[2]
-    components = weight.shape[1]
+    components, _, segb = weight.shape
     per = rows // components
     part = slice(b * segb, (b + 1) * segb)
     here = lax.broadcasted_iota(jnp.int32, (per, segb), 0) == column[b : b + 1, :]
     blocks = [
-        jnp.where(here, weight[b, i : i + 1] * value, 0.0) for i in range(components)
+        jnp.where(here, weight[i, b : b + 1] * value, 0.0) for i in range(components)
     ]
     high, low = halves(jnp.concatenate(blocks, axis=0))
     return dot(jnp.concatenate([high, low], axis=0), place[:, part], True)
 
 
-def inner_kernel(vec, trans, diag, place, column, take, give, first, second, out, shifted):
+def stencil_kernel(vec, trans, diag, out, shifted):
     inner_stencil(vec, trans, diag, shifted, out)
+
+
+def places(owner, capacity, wells):
+    g = lax.axis_index("grp")
+    out = []
+    for b in range(wells):
+        mine = owner[b, 0]
+        slot = jnp.int32(0)
+        for c in range(b):
+            slot = slot + (owner[c, 0] == mine).astype(jnp.int32)
+        out.append(jnp.bitwise_xor(g, mine) * capacity + slot)
+    return out
+
+
+def write_messages(vec, place, column, take, owner, messages, sums=None):
     components, cells_x, cells_y, cells_z = vec.shape
+    wells, segb = column.shape
+    capacity = messages[0].shape[0] - (sums is not None)
+    high, low = halves(vec[...].reshape(components * cells_x * cells_y, cells_z))
+    both = jnp.concatenate([high, low], axis=0)
+    coupled = [gather_well(both, place, column, take, b) for b in range(wells)]
+    where = places(owner, capacity, wells)
+    slots = lax.broadcasted_iota(jnp.int32, messages[0].shape, 0)
+    for k, message in enumerate(messages):
+        block = jnp.zeros(message.shape, F32)
+        for b in range(wells):
+            slot = where[b] - k * capacity
+            slot = jnp.where(slot < capacity, slot, -1)
+            block = jnp.where(slots == slot, coupled[b], block)
+        if sums is not None:
+            block = jnp.where(slots == capacity, sums, block)
+        message[...] = block
+
+
+def solve_kernel(with_sums, groups, first, second, *refs):
+    sent, back = refs[:groups], refs[groups : 2 * groups]
+    g = lax.axis_index("grp")
+    capacity = back[0].shape[0]
+    for k in range(groups):
+        home = jnp.bitwise_xor(g, k)
+        for slot in range(capacity):
+            value = solve_well(sent[k][slot : slot + 1], first[home, slot], second[home, slot])
+            back[k][slot : slot + 1] = value
+    if with_sums:
+        total = sent[0][capacity : capacity + 1]
+        for k in range(1, groups):
+            total = total + sent[k][capacity : capacity + 1]
+        refs[2 * groups][...] = total
+
+
+def well_terms(values, place, column, give, owner, shape):
+    components, cells_x, cells_y, cells_z = shape
     rows = components * cells_x * cells_y
-    high, low = halves(vec[...].reshape(rows, cells_z))
-    both = jnp.concatenate([high, low], axis=0)
+    wells, segb = column.shape
+    capacity = values[0].shape[0]
+    slots = lax.broadcasted_iota(jnp.int32, (capacity, segb), 0)
+    where = places(owner, capacity, wells)
     total = None
-    for b in range(column.shape[0]):
-        coupled = gather_well(both, place, column, take, b)
-        value = solve_well(coupled, first[b], second[b])
+    for b in range(wells):
+        value = jnp.zeros((capacity, segb), F32)
+        for k, ref in enumerate(values):
+            value = value + jnp.where(slots == where[b] - k * capacity, ref[...], 0.0)
+        value = jnp.sum(value, axis=0, keepdims=True)
         term = scatter_well(value, place, column, give, rows, b)
         total = term if total is None else total + term
-    total = total[:rows] + total[rows:]
-    out[...] = out[...] - total.reshape(out.shape)
+    return (total[:rows] + total[rows:]).reshape(shape)
 
 
 def prepare_kernel(acc, trans, completion, live, take, give, diag, place, column, take_out, give_out):
@@ -210,39 +262,57 @@
         place[:, b * segb : (b + 1) * segb] = jnp.where(hit, 1.0, 0.0).astype(BF16)
         is_open = (lanes < live[b]).astype(F32)
         for i in range(components):
-            take_out[b, i : i + 1] = take[b, i : i + 1] * is_open
-            give_out[b, i : i + 1] = give[b, i : i + 1] * is_open
-
-
-def pick_kernel(owner, moved, first, second):
-    capacity = moved.shape[1]
-    for b in range(first.shape[0]):
-        mine = owner[b, 0]
-        slot = jnp.int32(0)
-        for c in range(b):
-            slot = slot + (owner[c, 0] == mine).astype(jnp.int32)
-        high, low = halves(moved[mine, jnp.minimum(slot, capacity - 1)])
-        first[b] = high
-        second[b] = low
+            take_out[i, b : b + 1] = take[i, b : b + 1] * is_open
+            give_out[i, b : b + 1] = give[i, b : b + 1] * is_open
+
+
+def split_kernel(inverse, first, second):
+    for h in range(inverse.shape[0]):
+        for slot in range(inverse.shape[1]):
+            first[h, slot], second[h, slot] = halves(inverse[h, slot])
 
 
 def face_kernel(vec, *faces):
     write_faces(lambda j, x: vec[j, x], faces)
 
 
-def apply_kernel(part, trans, h0, h1, h2, h3, out, *faces):
-    terms = halo_terms((h0, h1, h2, h3), trans)
+def gather_kernel(vec, place, column, take, owner, *messages):
+    write_messages(vec, place, column, take, owner, messages)
+
+
+class Arrived:
+    def __init__(self, groups, refs):
+        self.part, self.trans, self.place, self.column, self.take, self.give, self.owner = refs[:7]
+        self.halo = refs[7:11]
+        self.values = refs[11 : 11 + groups]
+        self.rest = refs[11 + groups :]
+
+    def result(self):
+        shape = self.part.shape
+        wells = well_terms(self.values, self.place, self.column, self.give, self.owner, shape)
+        terms = halo_terms(self.halo, self.trans)
+        return lambda i, x: self.part[i, x] - wells[i, x] - terms(i, x)
+
+    def send(self, vec, messages, faces, sums=None):
+        write_messages(vec, self.place, self.column, self.take, self.owner, messages, sums)
+        write_faces(lambda j, x: vec[j, x], faces)
+
+
+def apply_kernel(groups, *refs):
+    got = Arrived(groups, refs)
+    out, *sends = got.rest
+    value = got.result()
     for i in range(out.shape[0]):
         for x in range(out.shape[1]):
-            out[i, x] = part[i, x] - terms(i, x)
-    write_faces(lambda j, x: out[j, x], faces)
-
-
-def put_sums(sums, vecs):
+            out[i, x] = value(i, x)
+    got.send(out, sends[:groups], sends[groups:])
+
+
+def local_sums(vecs, width):
     b, r, s, w, z = vecs
     table = {"b": b, "r": r, "s": s, "w": w, "z": z}
-    lanes = lax.broadcasted_iota(jnp.int32, (1, sums.shape[2]), 1)
-    row = jnp.zeros((1, sums.shape[2]), F32)
+    lanes = lax.broadcasted_iota(jnp.int32, (1, width), 1)
+    row = jnp.zeros((1, width), F32)
     for k, name in enumerate(NAMES):
         left, right = table[name[0]], table[name[1]]
         total = None
@@ -252,32 +322,34 @@
                 total = term if total is None else total + term
         total = jnp.sum(jnp.sum(total, axis=0, keepdims=True), axis=1, keepdims=True)
         row = jnp.where(lanes == k, total, row)
-    for d in range(sums.shape[0]):
-        sums[d] = row
-
-
-def second_kernel(first_time, part, trans, h0, h1, h2, h3, b, r, w, *rest):
+    return row
+
+
+def second_kernel(groups, first_time, end, *refs):
+    got = Arrived(groups, refs)
     if first_time:
-        t, sums, *faces = rest
+        b, r, w, t, *rest = got.rest
         s, z = w, t
     else:
-        s_rest, z_rest, t, s, z, sums, *faces = rest
-    terms = halo_terms((h0, h1, h2, h3), trans)
+        b, r, w, s_rest, z_rest, t, s, z, *rest = got.rest
+    value = got.result()
     for i in range(t.shape[0]):
         for x in range(t.shape[1]):
-            t[i, x] = part[i, x] - terms(i, x)
+            t[i, x] = value(i, x)
             if not first_time:
                 s[i, x] = w[i, x] + s_rest[i, x]
                 z[i, x] = t[i, x] + z_rest[i, x]
-    if faces:
-        write_faces(lambda j, x: z[j, x], faces)
-    put_sums(sums, (b, r, s, w, z))
-
-
-def coefficients(sums):
-    row = sums[0]
-    for d in range(1, sums.shape[0]):
-        row = row + sums[d]
+    if end:
+        sums = rest[0]
+        row = local_sums((b, r, s, w, z), sums.shape[-1])
+        for d in range(sums.shape[0]):
+            sums[d] = row
+    else:
+        row = local_sums((b, r, s, w, z), got.column.shape[1])
+        got.send(z, rest[:groups], rest[groups:], row)
+
+
+def coefficients(row):
     lanes = lax.broadcasted_iota(jnp.int32, row.shape, 1)
     v = {
         name: jnp.sum(jnp.where(lanes == k, row, 0.0), axis=1, keepdims=True)
@@ -291,17 +363,23 @@
     return alpha, omega, beta
 
 
-def third_kernel(first_time, part, trans, h0, h1, h2, h3, sums, r, w, t, *rest):
+def third_kernel(groups, count, first_time, *refs):
+    got = Arrived(groups, refs)
+    sums, rest = got.rest[:count], got.rest[count:]
+    r, w, t, *rest = rest
     if first_time:
-        r_out, w_out, x_out, p_out, s_rest, z_rest, *faces = rest
+        r_out, w_out, x_out, p_out, s_rest, z_rest, *sends = rest
         s, z, p, x_in = w, t, r, None
     else:
-        s, z, p, x_in, r_out, w_out, x_out, p_out, s_rest, z_rest, *faces = rest
-    terms = halo_terms((h0, h1, h2, h3), trans)
-    alpha, omega, beta = coefficients(sums)
+        s, z, p, x_in, r_out, w_out, x_out, p_out, s_rest, z_rest, *sends = rest
+    value = got.result()
+    row = sums[0][...]
+    for ref in sums[1:]:
+        row = row + ref[...]
+    alpha, omega, beta = coefficients(row)
     for i in range(r.shape[0]):
         for x in range(r.shape[1]):
-            v = part[i, x] - terms(i, x)
+            v = value(i, x)
             q = r[i, x] - alpha * s[i, x]
             y = w[i, x] - alpha * z[i, x]
             new_r = q - omega * y
@@ -312,17 +390,43 @@
             p_out[i, x] = new_r + beta * (p[i, x] - omega * s[i, x])
             s_rest[i, x] = beta * (s[i, x] - omega * z[i, x])
             z_rest[i, x] = beta * (z[i, x] - omega * v)
-    write_faces(lambda j, x: w_out[j, x], faces)
+    got.send(w_out, sends[:groups], sends[groups:])
 
 
 def last_kernel(sums, r, w, s, z, p, x_in, x_out, r_out):
-    alpha, omega, _ = coefficients(sums)
+    row = sums[0]
+    for d in range(1, sums.shape[0]):
+        row = row + sums[d]
+    alpha, omega, _ = coefficients(row)
     for i in range(r.shape[0]):
         for x in range(r.shape[1]):
             q = r[i, x] - alpha * s[i, x]
             y = w[i, x] - alpha * z[i, x]
             x_out[i, x] = x_in[i, x] + alpha * p[i, x] + omega * q
             r_out[i, x] = q - omega * y
+
+
+def swapped(messages):
+    groups = lax.axis_size("grp")
+    return [messages[0]] + [
+        lax.ppermute(messages[k], "grp", [(i, i ^ k) for i in range(groups)])
+        for k in range(1, groups)
+    ]
+
+
+def res_sums(row):
+    count, step = lax.axis_size("res"), 1
+    parts = [row]
+    while step < count:
+        many = min(8, count // step)
+        if len(parts) > 1:
+            row = functools.reduce(jnp.add, parts)
+        parts = [row] + [
+            lax.ppermute(row, "res", [(i, i ^ (k * step)) for i in range(count)])
+            for k in range(1, many)
+        ]
+        step *= many
+    return parts
 
 
 def body(
@@ -338,77 +442,95 @@
 ):
     components, cells_x, cells_y, cells_z = right_side.shape
     wells, segb = completion.shape
-    devices = lax.axis_size("res") * lax.axis_size("grp")
+    groups = lax.axis_size("grp")
+    capacity = inverse.shape[2]
+    devices = lax.axis_size("res") * groups
     field = (right_side.shape, F32)
     face_outs = [((components, cells_y, cells_z), F32)] * 2 + [((components * cells_x, cells_z), F32)] * 2
-    sums_out = ((devices, 1, 128), F32)
+    plain = [((capacity, segb), F32)] * groups
+    summed = [((capacity + 1, segb), F32)] * groups
     trans = transmissibility
-
-    faces = call(face_kernel, face_outs, [right_side])
-    halo = exchange(faces)
-    moved = lax.all_to_all(inverse[0], "grp", split_axis=0, concat_axis=0, tiled=True)
+    take = jnp.moveaxis(cell_to_well, 1, 0)
+    give = jnp.moveaxis(well_to_cell, 1, 0)
+    b = right_side
+
+    faces = call(face_kernel, face_outs, [b])
     diag, place, column, take, give = call(
         prepare_kernel,
         [
             (accumulation.shape, F32),
             ((cells_z, wells * segb), BF16),
             (completion.shape, jnp.int32),
-            (cell_to_well.shape, F32),
-            (well_to_cell.shape, F32),
+            (take.shape, F32),
+            (give.shape, F32),
         ],
-        [accumulation, trans, completion, live_count, cell_to_well, well_to_cell],
+        [accumulation, trans, completion, live_count, take, give],
         [VMEM, VMEM, VMEM, SMEM, VMEM, VMEM],
     )
-    first, second = call(
-        pick_kernel, [((wells, segb, segb), BF16)] * 2, [owner, moved], [SMEM, VMEM]
+    messages = call(
+        gather_kernel, plain, [b, place, column, take, owner], [VMEM] * 4 + [SMEM]
     )
-
-    def inner(vec):
-        return call(
-            inner_kernel,
+    first, second = call(split_kernel, [(inverse.shape[1:], BF16)] * 2, [inverse[0]])
+
+    def solve(messages, with_sums):
+        outs = plain + [((1, segb), F32)] * with_sums
+        back = call(
+            functools.partial(solve_kernel, with_sums, groups),
+            outs,
+            [first, second, *swapped(messages)],
+            flops=500_000_000,
+            moved=4_000_000,
+        )
+        return swapped(back[:groups]), back[groups:]
+
+    def finish(kernel, outs, vec, faces, messages, extra, with_sums=False):
+        values, sums = solve(messages, with_sums)
+        halo = exchange(faces)
+        part = call(
+            stencil_kernel,
             [field],
-            [vec, trans, diag, place, column, take, give, first, second],
+            [vec, trans, diag],
             scratch=[pltpu.VMEM((4,) + vec.shape, F32)],
-            flops=2_000_000_000,
-            moved=8_000_000,
+            flops=200_000_000,
+            moved=4_000_000,
         )[0]
-
-    def reduced(sums):
-        return lax.all_to_all(sums, ("res", "grp"), split_axis=0, concat_axis=0, tiled=True)
-
-    b = right_side
-    w, *faces = call(apply_kernel, [field] + face_outs, [inner(b), trans, *halo])
+        if with_sums:
+            sums = res_sums(sums[0])
+            kernel = functools.partial(kernel, len(sums))
+        args = [part, trans, place, column, take, give, owner, *halo, *values, *sums, *extra]
+        specs = [VMEM] * len(args)
+        specs[6] = SMEM
+        return call(kernel, outs, args, specs, flops=1_000_000_000, moved=8_000_000)
+
+    def split(outs):
+        return outs[:groups], outs[groups:]
+
+    w, *sends = finish(
+        functools.partial(apply_kernel, groups), [field] + plain + face_outs, b, faces, messages, []
+    )
     r, s, p, x = b, w, b, None
     for index in range(ITERS):
         start, end = index == 0, index + 1 == ITERS
-        halo = exchange(faces)
-        part = inner(w)
-        tail = [] if end else face_outs
+        messages, faces = split(sends)
+        tail = [((devices, 1, 128), F32)] if end else summed + face_outs
+        kernel = functools.partial(second_kernel, groups, start, end)
         if start:
-            t, sums, *faces = call(
-                functools.partial(second_kernel, True),
-                [field, sums_out] + tail,
-                [part, trans, *halo, b, r, w],
-            )
+            t, *sends = finish(kernel, [field] + tail, w, faces, messages, [b, r, w])
             z = t
         else:
-            t, s, z, sums, *faces = call(
-                functools.partial(second_kernel, False),
-                [field] * 3 + [sums_out] + tail,
-                [part, trans, *halo, b, r, w, s_rest, z_rest],
+            t, s, z, *sends = finish(
+                kernel, [field] * 3 + tail, w, faces, messages, [b, r, w, s_rest, z_rest]
             )
         if end:
             break
-        halo = exchange(faces)
-        sums = reduced(sums)
-        part = inner(z)
+        messages, faces = split(sends)
         more = [] if start else [s, z, p, x]
-        r, w, x, p, s_rest, z_rest, *faces = call(
-            functools.partial(third_kernel, start),
-            [field] * 6 + face_outs,
-            [part, trans, *halo, sums, r, w, t, *more],
+        kernel = lambda count, *refs, start=start: third_kernel(groups, count, start, *refs)
+        r, w, x, p, s_rest, z_rest, *sends = finish(
+            kernel, [field] * 6 + plain + face_outs, z, faces, messages, [r, w, t, *more], True
         )
-    x, r = call(last_kernel, [field, field], [reduced(sums), r, w, s, z, p, x])
+    sums = lax.all_to_all(sends[0], ("res", "grp"), split_axis=0, concat_axis=0, tiled=True)
+    x, r = call(last_kernel, [field, field], [sums, r, w, s, z, p, x])
     return (x, r)
 
 

time: 176 us -> 171 us (0.972)
  local copies, waits for them, and re-layouts: 51.7 us -> 7.55 us
  waiting for transfers between devices: 35.6 us -> 58.9 us
  starting transfers between devices: 47.3 us -> 65.1 us
    ppermute x0 -> x50, waiting for transfers between devices: none -> 58.9 us  [the longest x36 31.8 us: swapped(): lax.ppermute(messages[k], 'grp', [(i, i ^ k) for i in range(groups)])]
    unnamed x173 -> x21, local copies, waits for them, and re-layouts: 51.7 us -> 7.55 us
    ppermute x0 -> x50, starting transfers between devices: none -> 37.3 us  [the longest x36 21.2 us: swapped(): lax.ppermute(messages[k], 'grp', [(i, i ^ k) for i in range(groups)])]
    all_to_all x3 -> x0, waiting for transfers between devices: 30.8 us -> none  [the longest x1 30.8 us: body(): lax.all_to_all(inverse[0], 'grp', split_axis=0, concat_axis=0, tiled=True)]
    all_to_all x3 -> x0, starting transfers between devices: 13.7 us -> none  [the longest x2 8.58 us: reduced(): lax.all_to_all(sums, ('res', 'grp'), split_axis=0, concat_axis=0, tiled=T...]
    ppermute x24, starting transfers between devices: 33.6 us -> 27.8 us  [exchange(): out.append(lax.ppermute(face, axis, pairs))]
    ppermute x24, waiting for transfers between devices: 4.8 us -> 0.06 us  [exchange(): out.append(lax.ppermute(face, axis, pairs))]
    pallas_call x16 -> x23, Pallas kernels: 28.4 us -> 27.7 us  [call(): pl.pallas_call(kernel, out_shape=[jax.ShapeDtypeStruct(shape, dtype) for...]
  transfers between devices with their start and end apart: 27 -> 74, of which waited for: 4 -> 35; matrix products, arithmetic and copies ran while one was open for 1% -> 0% of each run, Pallas kernels for 13% -> 8%
where the time goes in v2:
time: 171 us; the launch traced here: 170 us
  starting transfers between devices  65.1 us (38%)
  waiting for transfers between devices  58.9 us (34%)
  Pallas kernels  27.7 us (16%)
  blocking collectives  10.1 us (6%)
  local copies, waits for them, and re-layouts  7.55 us (4%)
    ppermute x36, waiting for transfers between devices, swapped(): lax.ppermute(messages[k], 'grp', [(i, i ^ k) for i in range(groups)])  31.8 us
    ppermute x24, starting transfers between devices, exchange(): out.append(lax.ppermute(face, axis, pairs))  27.8 us
    pallas_call x23, Pallas kernels, call(): pl.pallas_call(kernel, out_shape=[jax.ShapeDtypeStruct(shape, dtype) for...  27.7 us
    ppermute x14, waiting for transfers between devices, res_sums(): lax.ppermute(row, 'res', [(i, i ^ k * step) for i in range(count)])  27.1 us
    ppermute x36, starting transfers between devices, swapped(): lax.ppermute(messages[k], 'grp', [(i, i ^ k) for i in range(groups)])  21.2 us
    ppermute x14, starting transfers between devices, res_sums(): lax.ppermute(row, 'res', [(i, i ^ k * step) for i in range(count)])  16.1 us
    all_to_all x1, blocking collectives, body(): lax.all_to_all(sends[0], ('res', 'grp'), split_axis=0, concat_axis=0, til...  10.1 us
    unnamed x21, local copies, waits for them, and re-layouts  7.55 us
  transfers between devices with their start and end apart: 74, of which 35 were waited for; matrix products, arithmetic and copies ran while one was open for 0% of the time, Pallas kernels for 8%

profile of v2, /device:TPU:0, one launch (start us, length us, event | category | flops | bytes accessed | tf_op | source)
XLA Modules:
  0.0 170.3 jit_solution(12724574322323738679)
XLA Ops:
  1.6 3.0 %collective-permute-start = (f32[3,16,512]{2,1,0:T(8,128)S(1)}, f32[3,16,512]{2,1,0:T(8,128)S(1)}, u32[]{:S(2)}, u32[]{:S(2)}) collective-permute-start(f32[3,16,512]{2,1,0:T(8,128)S(1)} %get-tuple-element.108), channel_id=1, source_target_pairs={{0,4},{4,0},{8,12},{12,8},{16,20},{20,16},{24,28},{28,24},{1,5},{5... | collective-permute-start | bytes 294920 | tf_op jit(solution)/shard_map/ppermute | solution.py:41
  4.6 3.6 %collective-permute-start.1 = (f32[3,16,512]{2,1,0:T(8,128)S(1)}, f32[3,16,512]{2,1,0:T(8,128)S(1)}, u32[]{:S(2)}, u32[]{:S(2)}) collective-permute-start(f32[3,16,512]{2,1,0:T(8,128)S(1)} %get-tuple-element.109), channel_id=1, source_target_pairs={{0,28},{4,8},{8,4},{12,16},{16,12},{20,24},{24,20},{28,0},{1,29},{... | collective-permute-start | bytes 294920 | tf_op jit(solution)/shard_map/ppermute | solution.py:41
  8.9 2.0 %copy-done = f32[6,3,3,2,16,512]{5,4,3,2,1,0:T(8,128)S(1)} copy-done((f32[6,3,3,2,16,512]{5,4,3,2,1,0:T(8,128)S(1)}, f32[6,3,3,2,16,512]{5,4,3,2,1,0:T(8,128)}, u32[]{:S(2)}) %copy-start) | copy-done | bytes 3538968
  17.3 1.6 collective-permute-start.5
  25.5 1.5 collective-permute-done.8.refs_13_
  27.4 2.6 %collective-permute-done.9.refs_14_ = f32[4,256]{1,0:T(4,128)S(1)} collective-permute-done((f32[4,256]{1,0:T(4,128)S(1)}, f32[4,256]{1,0:T(4,128)S(1)}, u32[]{:S(2)}, u32[]{:S(2)}) %collective-permute-start.9) | collective-permute-done | bytes 4128 | tf_op jit(solution)/shard_map/ppermute | solution.py:412
  30.1 2.1 %shard_map.110 = (f32[3,2,16,512]{3,2,1,0:T(8,128)S(1)}, f32[4,256]{1,0:T(4,128)S(1)}, f32[4,256]{1,0:T(4,128)S(1)}, f32[4,256]{1,0:T(4,128)S(1)}, f32[4,256]{1,...) custom-call(f32[3,2,16,512]{3,2,1,0:T(8,128)S(1)} %shard_map.105.ref, ...), custom_call_target="tpu_custom_call" | custom-call | flops 1000000000 | bytes 8000000 | tf_op jit(solution)/shard_map/pallas_call | solution.py:20
  32.2 1.9 %collective-permute-start.11 = (f32[3,16,512]{2,1,0:T(8,128)S(1)}, f32[3,16,512]{2,1,0:T(8,128)S(1)}, u32[]{:S(2)}, u32[]{:S(2)}) collective-permute-start(f32[3,16,512]{2,1,0:T(8,128)S(1)} %get-tuple-element.124), channel_id=1, source_target_pairs={{0,28},{4,8},{8,4},{12,16},{16,12},{20,24},{24,20},{28,0},{1,29},{... | collective-permute-start | bytes 294920 | tf_op jit(solution)/shard_map/ppermute | solution.py:41
  34.6 1.3 collective-permute-start.16
  36.0 1.7 %collective-permute-done.15.refs_2_ = f32[4,256]{1,0:T(4,128)S(1)} collective-permute-done((f32[4,256]{1,0:T(4,128)S(1)}, f32[4,256]{1,0:T(4,128)S(1)}, u32[]{:S(2)}, u32[]{:S(2)}) %collective-permute-start.15) | collective-permute-done | bytes 4128 | tf_op jit(solution)/shard_map/ppermute | solution.py:412
  39.2 1.8 %collective-permute-start.18 = (f32[4,256]{1,0:T(4,128)S(1)}, f32[4,256]{1,0:T(4,128)S(1)}, u32[]{:S(2)}, u32[]{:S(2)}) collective-permute-start(f32[4,256]{1,0:T(4,128)S(1)} %get-tuple-element.133), channel_id=1, source_target_pairs={{0,2},{1,3},{2,0},{3,1},{4,6},{5,7},{6,4},{7,5},{8,10},{9,11},{10,... | collective-permute-start | bytes 12296 | tf_op jit(solution)/shard_map/ppermute | solution.py:412
  43.6 2.3 %collective-permute-done.19.refs_14_ = f32[4,256]{1,0:T(4,128)S(1)} collective-permute-done((f32[4,256]{1,0:T(4,128)S(1)}, f32[4,256]{1,0:T(4,128)S(1)}, u32[]{:S(2)}, u32[]{:S(2)}) %collective-permute-start.19) | collective-permute-done | bytes 4128 | tf_op jit(solution)/shard_map/ppermute | solution.py:412
  45.9 2.2 %shard_map.113 = (f32[3,2,16,512]{3,2,1,0:T(8,128)S(1)}, f32[5,256]{1,0:T(8,128)S(1)}, f32[5,256]{1,0:T(8,128)S(1)}, f32[5,256]{1,0:T(8,128)S(1)}, f32[5,256]{1,...) custom-call(f32[3,2,16,512]{3,2,1,0:T(8,128)S(1)} %shard_map.111.ref, ...), custom_call_target="tpu_custom_call" | custom-call | flops 1000000000 | bytes 8000000 | tf_op jit(solution)/shard_map/pallas_call | solution.py:20
  48.7 2.7 %collective-permute-start.21 = (f32[3,16,512]{2,1,0:T(8,128)S(1)}, f32[3,16,512]{2,1,0:T(8,128)S(1)}, u32[]{:S(2)}, u32[]{:S(2)}) collective-permute-start(f32[3,16,512]{2,1,0:T(8,128)S(1)} %get-tuple-element.137), channel_id=1, source_target_pairs={{0,28},{4,8},{8,4},{12,16},{16,12},{20,24},{24,20},{28,0},{1,29},{... | collective-permute-start | bytes 294920 | tf_op jit(solution)/shard_map/ppermute | solution.py:41
  53.3 1.8 %collective-permute-done.25.refs_2_ = f32[5,256]{1,0:T(8,128)S(1)} collective-permute-done((f32[5,256]{1,0:T(8,128)S(1)}, f32[5,256]{1,0:T(8,128)S(1)}, u32[]{:S(2)}, u32[]{:S(2)}) %collective-permute-start.25) | collective-permute-done | bytes 5152 | tf_op jit(solution)/shard_map/ppermute | solution.py:412
  56.9 2.7 %collective-permute-start.36 = (f32[1,256]{1,0:T(1,128)S(1)}, f32[1,256]{1,0:T(1,128)S(1)}, u32[]{:S(2)}, u32[]{:S(2)}) collective-permute-start(f32[1,256]{1,0:T(1,128)S(1)} %get-tuple-element.148.refs_15_), channel_id=1, source_target_pairs={{0,28},{4,24},{8,20},{12,16},{16,12},{20,8},{24,4},{28,0},{1,29},{... | collective-permute-start | bytes 3080 | tf_op jit(solution)/shard_map/ppermute | solution.py:425
  61.4 1.8 %collective-permute-done.36.refs_22_ = f32[1,256]{1,0:T(1,128)S(1)} collective-permute-done((f32[1,256]{1,0:T(1,128)S(1)}, f32[1,256]{1,0:T(1,128)S(1)}, u32[]{:S(2)}, u32[]{:S(2)}) %collective-permute-start.36) | collective-permute-done | bytes 1056 | tf_op jit(solution)/shard_map/ppermute | solution.py:425
  63.3 1.4 collective-permute-start.33
  67.7 1.7 collective-permute-start.32
  69.4 2.8 %collective-permute-done.32.refs_18_ = f32[1,256]{1,0:T(1,128)S(1)} collective-permute-done((f32[1,256]{1,0:T(1,128)S(1)}, f32[1,256]{1,0:T(1,128)S(1)}, u32[]{:S(2)}, u32[]{:S(2)}) %collective-permute-start.32) | collective-permute-done | bytes 1056 | tf_op jit(solution)/shard_map/ppermute | solution.py:425
  72.2 3.6 %collective-permute-done.31.refs_17_ = f32[1,256]{1,0:T(1,128)S(1)} collective-permute-done((f32[1,256]{1,0:T(1,128)S(1)}, f32[1,256]{1,0:T(1,128)S(1)}, u32[]{:S(2)}, u32[]{:S(2)}) %collective-permute-start.31) | collective-permute-done | bytes 1056 | tf_op jit(solution)/shard_map/ppermute | solution.py:425
  76.5 2.8 %collective-permute-done.30.refs_16_ = f32[1,256]{1,0:T(1,128)S(1)} collective-permute-done((f32[1,256]{1,0:T(1,128)S(1)}, f32[1,256]{1,0:T(1,128)S(1)}, u32[]{:S(2)}, u32[]{:S(2)}) %collective-permute-start.30) | collective-permute-done | bytes 1056 | tf_op jit(solution)/shard_map/ppermute | solution.py:425
  81.5 1.8 %collective-permute-done.29.refs_14_ = f32[4,256]{1,0:T(4,128)S(1)} collective-permute-done((f32[4,256]{1,0:T(4,128)S(1)}, f32[4,256]{1,0:T(4,128)S(1)}, u32[]{:S(2)}, u32[]{:S(2)}) %collective-permute-start.29) | collective-permute-done | bytes 4128 | tf_op jit(solution)/shard_map/ppermute | solution.py:412
  83.3 2.3 %shard_map.116 = (f32[3,2,16,512]{3,2,1,0:T(8,128)S(1)}, f32[3,2,16,512]{3,2,1,0:T(8,128)S(1)}, f32[3,2,16,512]{3,2,1,0:T(8,128)S(1)}, f32[3,2,16,512]{3,2,1,0:T...) custom-call(f32[3,2,16,512]{3,2,1,0:T(8,128)S(1)} %shard_map.114.ref, ...), custom_call_target="tpu_custom_call" | custom-call | flops 1000000000 | bytes 8000000 | tf_op jit(solution)/shard_map/pallas_call | solution.py:20
  86.8 2.7 %collective-permute-start.38 = (f32[3,16,512]{2,1,0:T(8,128)S(1)}, f32[3,16,512]{2,1,0:T(8,128)S(1)}, u32[]{:S(2)}, u32[]{:S(2)}) collective-permute-start(f32[3,16,512]{2,1,0:T(8,128)S(1)} %get-tuple-element.151), channel_id=1, source_target_pairs={{0,28},{4,8},{8,4},{12,16},{16,12},{20,24},{24,20},{28,0},{1,29},{... | collective-permute-start | bytes 294920 | tf_op jit(solution)/shard_map/ppermute | solution.py:41
  91.3 1.7 %collective-permute-done.42.refs_2_ = f32[4,256]{1,0:T(4,128)S(1)} collective-permute-done((f32[4,256]{1,0:T(4,128)S(1)}, f32[4,256]{1,0:T(4,128)S(1)}, u32[]{:S(2)}, u32[]{:S(2)}) %collective-permute-start.42) | collective-permute-done | bytes 4128 | tf_op jit(solution)/shard_map/ppermute | solution.py:412
  93.1 1.4 shard_map.118
  95.1 1.4 collective-permute-start.45
  97.3 1.4 collective-permute-done.45.refs_13_
  99.1 2.6 %collective-permute-done.46.refs_14_ = f32[4,256]{1,0:T(4,128)S(1)} collective-permute-done((f32[4,256]{1,0:T(4,128)S(1)}, f32[4,256]{1,0:T(4,128)S(1)}, u32[]{:S(2)}, u32[]{:S(2)}) %collective-permute-start.46) | collective-permute-done | bytes 4128 | tf_op jit(solution)/shard_map/ppermute | solution.py:412
  101.8 2.4 %shard_map.119 = (f32[3,2,16,512]{3,2,1,0:T(8,128)S(1)}, f32[3,2,16,512]{3,2,1,0:T(8,128)S(1)}, f32[3,2,16,512]{3,2,1,0:T(8,128)S(1)}, f32[5,256]{1,0:T(8,128)S(...) custom-call(f32[3,2,16,512]{3,2,1,0:T(8,128)S(1)} %shard_map.117.ref, ...), custom_call_target="tpu_custom_call" | custom-call | flops 1000000000 | bytes 8000000 | tf_op jit(solution)/shard_map/pallas_call | solution.py:20
  104.4 2.4 %collective-permute-start.48 = (f32[3,16,512]{2,1,0:T(8,128)S(1)}, f32[3,16,512]{2,1,0:T(8,128)S(1)}, u32[]{:S(2)}, u32[]{:S(2)}) collective-permute-start(f32[3,16,512]{2,1,0:T(8,128)S(1)} %get-tuple-element.167), channel_id=1, source_target_pairs={{0,28},{4,8},{8,4},{12,16},{16,12},{20,24},{24,20},{28,0},{1,29},{... | collective-permute-start | bytes 294920 | tf_op jit(solution)/shard_map/ppermute | solution.py:41
  108.6 1.8 %collective-permute-done.52.refs_2_ = f32[5,256]{1,0:T(8,128)S(1)} collective-permute-done((f32[5,256]{1,0:T(8,128)S(1)}, f32[5,256]{1,0:T(8,128)S(1)}, u32[]{:S(2)}, u32[]{:S(2)}) %collective-permute-start.52) | collective-permute-done | bytes 5152 | tf_op jit(solution)/shard_map/ppermute | solution.py:412
  112.1 2.7 %collective-permute-start.63 = (f32[1,256]{1,0:T(1,128)S(1)}, f32[1,256]{1,0:T(1,128)S(1)}, u32[]{:S(2)}, u32[]{:S(2)}) collective-permute-start(f32[1,256]{1,0:T(1,128)S(1)} %get-tuple-element.178.refs_15_), channel_id=1, source_target_pairs={{0,28},{4,24},{8,20},{12,16},{16,12},{20,8},{24,4},{28,0},{1,29},{... | collective-permute-start | bytes 3080 | tf_op jit(solution)/shard_map/ppermute | solution.py:425
  115.8 2.6 %collective-permute-done.63.refs_22_ = f32[1,256]{1,0:T(1,128)S(1)} collective-permute-done((f32[1,256]{1,0:T(1,128)S(1)}, f32[1,256]{1,0:T(1,128)S(1)}, u32[]{:S(2)}, u32[]{:S(2)}) %collective-permute-start.63) | collective-permute-done | bytes 1056 | tf_op jit(solution)/shard_map/ppermute | solution.py:425
  118.4 1.4 collective-permute-start.60
  122.9 1.7 collective-permute-start.59
  124.5 2.8 %collective-permute-done.59.refs_18_ = f32[1,256]{1,0:T(1,128)S(1)} collective-permute-done((f32[1,256]{1,0:T(1,128)S(1)}, f32[1,256]{1,0:T(1,128)S(1)}, u32[]{:S(2)}, u32[]{:S(2)}) %collective-permute-start.59) | collective-permute-done | bytes 1056 | tf_op jit(solution)/shard_map/ppermute | solution.py:425
  127.3 3.6 %collective-permute-done.58.refs_17_ = f32[1,256]{1,0:T(1,128)S(1)} collective-permute-done((f32[1,256]{1,0:T(1,128)S(1)}, f32[1,256]{1,0:T(1,128)S(1)}, u32[]{:S(2)}, u32[]{:S(2)}) %collective-permute-start.58) | collective-permute-done | bytes 1056 | tf_op jit(solution)/shard_map/ppermute | solution.py:425
  131.9 2.6 %collective-permute-done.57.refs_16_ = f32[1,256]{1,0:T(1,128)S(1)} collective-permute-done((f32[1,256]{1,0:T(1,128)S(1)}, f32[1,256]{1,0:T(1,128)S(1)}, u32[]{:S(2)}, u32[]{:S(2)}) %collective-permute-start.57) | collective-permute-done | bytes 1056 | tf_op jit(solution)/shard_map/ppermute | solution.py:425
  136.7 2.0 %collective-permute-done.56.refs_14_ = f32[4,256]{1,0:T(4,128)S(1)} collective-permute-done((f32[4,256]{1,0:T(4,128)S(1)}, f32[4,256]{1,0:T(4,128)S(1)}, u32[]{:S(2)}, u32[]{:S(2)}) %collective-permute-start.56) | collective-permute-done | bytes 4128 | tf_op jit(solution)/shard_map/ppermute | solution.py:412
  138.7 2.3 %shard_map.122 = (f32[3,2,16,512]{3,2,1,0:T(8,128)S(1)}, f32[3,2,16,512]{3,2,1,0:T(8,128)S(1)}, f32[3,2,16,512]{3,2,1,0:T(8,128)S(1)}, f32[3,2,16,512]{3,2,1,0:T...) custom-call(f32[3,2,16,512]{3,2,1,0:T(8,128)S(1)} %shard_map.120.ref, ...), custom_call_target="tpu_custom_call" | custom-call | flops 1000000000 | bytes 8000000 | tf_op jit(solution)/shard_map/pallas_call | solution.py:20
  142.0 2.7 %collective-permute-start.65 = (f32[3,16,512]{2,1,0:T(8,128)S(1)}, f32[3,16,512]{2,1,0:T(8,128)S(1)}, u32[]{:S(2)}, u32[]{:S(2)}) collective-permute-start(f32[3,16,512]{2,1,0:T(8,128)S(1)} %get-tuple-element.185), channel_id=1, source_target_pairs={{0,28},{4,8},{8,4},{12,16},{16,12},{20,24},{24,20},{28,0},{1,29},{... | collective-permute-start | bytes 294920 | tf_op jit(solution)/shard_map/ppermute | solution.py:41
  146.5 1.7 %collective-permute-done.69.refs_2_ = f32[4,256]{1,0:T(4,128)S(1)} collective-permute-done((f32[4,256]{1,0:T(4,128)S(1)}, f32[4,256]{1,0:T(4,128)S(1)}, u32[]{:S(2)}, u32[]{:S(2)}) %collective-permute-start.69) | collective-permute-done | bytes 4128 | tf_op jit(solution)/shard_map/ppermute | solution.py:412
  152.4 1.5 collective-permute-done.72.refs_13_
  154.3 2.6 %collective-permute-done.73.refs_14_ = f32[4,256]{1,0:T(4,128)S(1)} collective-permute-done((f32[4,256]{1,0:T(4,128)S(1)}, f32[4,256]{1,0:T(4,128)S(1)}, u32[]{:S(2)}, u32[]{:S(2)}) %collective-permute-start.73) | collective-permute-done | bytes 4128 | tf_op jit(solution)/shard_map/ppermute | solution.py:412
  156.9 2.4 %shard_map.125 = (f32[3,2,16,512]{3,2,1,0:T(8,128)}, f32[3,2,16,512]{3,2,1,0:T(8,128)S(1)}, f32[3,2,16,512]{3,2,1,0:T(8,128)S(1)}, f32[32,1,128]{2,1,0:T(1,128)S(1)}) custom-call(f32[3,2,16,512]{3,2,1,0:T(8,128)S(1)} %shard_map.123.refs_0_, f32[6,3,3,2,16,512]{5,4,3,2,1,0:T(8,128)S(1)} %copy-done.1, bf16[512,2048]{1,0:T(8,128)(2,1)S(1)} %get-tuple-element.104.place.refs_2_, ...), custom_call_target="tpu_custom_call" | custom-call | flops 1000000000 | bytes 8000000 | tf_op jit(solution)/shard_map/pallas_call | solution.py:20
  159.3 10.1 %all_to_all.5.sums = f32[32,1,128]{2,1,0:T(1,128)S(1)} all-to-all(f32[32,1,128]{2,1,0:T(1,128)S(1)} %get-tuple-element.199), channel_id=1, replica_groups=mesh['res'=8,'grp'=4] {'res','grp'}, dimensions={0} | all-to-all | bytes 32768 | tf_op jit(solution)/shard_map/all_to_all | solution.py:532
  (145 shorter events, 56.2 us)
Async XLA Ops:
  1.6 28.4 %collective-permute-start = (f32[3,16,512]{2,1,0:T(8,128)S(1)}, f32[3,16,512]{2,1,0:T(8,128)S(1)}, u32[]{:S(2)}, u32[]{:S(2)}) collective-permute-start(f32[3,16,512]{2,1,0:T(8,128)S(1)} %get-tuple-element.108), channel_id=1, source_target_pairs={{0,4},{4,0},{8,12},{12,8},{16,20},{20,16},{24,28},{28,24},{1,5},{5... | collective-permute-start | bytes 294920 | tf_op jit(solution)/shard_map/ppermute | solution.py:41
  4.6 25.4 %collective-permute-start.1 = (f32[3,16,512]{2,1,0:T(8,128)S(1)}, f32[3,16,512]{2,1,0:T(8,128)S(1)}, u32[]{:S(2)}, u32[]{:S(2)}) collective-permute-start(f32[3,16,512]{2,1,0:T(8,128)S(1)} %get-tuple-element.109), channel_id=1, source_target_pairs={{0,28},{4,8},{8,4},{12,16},{16,12},{20,24},{24,20},{28,0},{1,29},{... | collective-permute-start | bytes 294920 | tf_op jit(solution)/shard_map/ppermute | solution.py:41
  17.3 3.7 %collective-permute-start.5 = (f32[4,256]{1,0:T(4,128)S(1)}, f32[4,256]{1,0:T(4,128)S(1)}, u32[]{:S(2)}, u32[]{:S(2)}) collective-permute-start(f32[4,256]{1,0:T(4,128)S(1)} %get-tuple-element.116), channel_id=1, source_target_pairs={{0,2},{1,3},{2,0},{3,1},{4,6},{5,7},{6,4},{7,5},{8,10},{9,11},{10,... | collective-permute-start | bytes 12296 | tf_op jit(solution)/shard_map/ppermute | solution.py:412
  23.4 3.6 %collective-permute-start.8 = (f32[4,256]{1,0:T(4,128)S(1)}, f32[4,256]{1,0:T(4,128)S(1)}, u32[]{:S(2)}, u32[]{:S(2)}) collective-permute-start(f32[4,256]{1,0:T(4,128)S(1)} %get-tuple-element.120), channel_id=1, source_target_pairs={{0,2},{1,3},{2,0},{3,1},{4,6},{5,7},{6,4},{7,5},{8,10},{9,11},{10,... | collective-permute-start | bytes 12296 | tf_op jit(solution)/shard_map/ppermute | solution.py:412
  23.9 6.1 %collective-permute-start.2 = (f32[6,512]{1,0:T(8,128)S(1)}, f32[6,512]{1,0:T(8,128)S(1)}, u32[]{:S(2)}, u32[]{:S(2)}) collective-permute-start(f32[6,512]{1,0:T(8,128)S(1)} %get-tuple-element.110), channel_id=1, source_target_pairs={{0,1},{1,0},{2,3},{3,2},{4,5},{5,4},{6,7},{7,6},{8,9},{9,8},{10,11... | collective-permute-start | bytes 36872 | tf_op jit(solution)/shard_map/ppermute | solution.py:41
  24.4 5.6 %collective-permute-start.3 = (f32[6,512]{1,0:T(8,128)S(1)}, f32[6,512]{1,0:T(8,128)S(1)}, u32[]{:S(2)}, u32[]{:S(2)}) collective-permute-start(f32[6,512]{1,0:T(8,128)S(1)} %get-tuple-element.111), channel_id=1, source_target_pairs={{0,3},{1,2},{2,1},{3,0},{4,7},{5,6},{6,5},{7,4},{8,11},{9,10},{10,... | collective-permute-start | bytes 36872 | tf_op jit(solution)/shard_map/ppermute | solution.py:41
  32.1 13.7 %collective-permute-start.10 = (f32[3,16,512]{2,1,0:T(8,128)S(1)}, f32[3,16,512]{2,1,0:T(8,128)S(1)}, u32[]{:S(2)}, u32[]{:S(2)}) collective-permute-start(f32[3,16,512]{2,1,0:T(8,128)S(1)} %get-tuple-element.123), channel_id=1, source_target_pairs={{0,4},{4,0},{8,12},{12,8},{16,20},{20,16},{24,28},{28,24},{1,5},{5... | collective-permute-start | bytes 294920 | tf_op jit(solution)/shard_map/ppermute | solution.py:41
  32.2 13.6 %collective-permute-start.11 = (f32[3,16,512]{2,1,0:T(8,128)S(1)}, f32[3,16,512]{2,1,0:T(8,128)S(1)}, u32[]{:S(2)}, u32[]{:S(2)}) collective-permute-start(f32[3,16,512]{2,1,0:T(8,128)S(1)} %get-tuple-element.124), channel_id=1, source_target_pairs={{0,28},{4,8},{8,4},{12,16},{16,12},{20,24},{24,20},{28,0},{1,29},{... | collective-permute-start | bytes 294920 | tf_op jit(solution)/shard_map/ppermute | solution.py:41
  34.1 3.6 %collective-permute-start.15 = (f32[4,256]{1,0:T(4,128)S(1)}, f32[4,256]{1,0:T(4,128)S(1)}, u32[]{:S(2)}, u32[]{:S(2)}) collective-permute-start(f32[4,256]{1,0:T(4,128)S(1)} %get-tuple-element.129), channel_id=1, source_target_pairs={{0,2},{1,3},{2,0},{3,1},{4,6},{5,7},{6,4},{7,5},{8,10},{9,11},{10,... | collective-permute-start | bytes 12296 | tf_op jit(solution)/shard_map/ppermute | solution.py:412
  39.2 3.6 %collective-permute-start.18 = (f32[4,256]{1,0:T(4,128)S(1)}, f32[4,256]{1,0:T(4,128)S(1)}, u32[]{:S(2)}, u32[]{:S(2)}) collective-permute-start(f32[4,256]{1,0:T(4,128)S(1)} %get-tuple-element.133), channel_id=1, source_target_pairs={{0,2},{1,3},{2,0},{3,1},{4,6},{5,7},{6,4},{7,5},{8,10},{9,11},{10,... | collective-permute-start | bytes 12296 | tf_op jit(solution)/shard_map/ppermute | solution.py:412
  41.0 4.8 %collective-permute-start.12 = (f32[6,512]{1,0:T(8,128)S(1)}, f32[6,512]{1,0:T(8,128)S(1)}, u32[]{:S(2)}, u32[]{:S(2)}) collective-permute-start(f32[6,512]{1,0:T(8,128)S(1)} %get-tuple-element.125), channel_id=1, source_target_pairs={{0,1},{1,0},{2,3},{3,2},{4,5},{5,4},{6,7},{7,6},{8,9},{9,8},{10,11... | collective-permute-start | bytes 36872 | tf_op jit(solution)/shard_map/ppermute | solution.py:41
  41.0 4.8 %collective-permute-start.13 = (f32[6,512]{1,0:T(8,128)S(1)}, f32[6,512]{1,0:T(8,128)S(1)}, u32[]{:S(2)}, u32[]{:S(2)}) collective-permute-start(f32[6,512]{1,0:T(8,128)S(1)} %get-tuple-element.126), channel_id=1, source_target_pairs={{0,3},{1,2},{2,1},{3,0},{4,7},{5,6},{6,5},{7,4},{8,11},{9,10},{10,... | collective-permute-start | bytes 36872 | tf_op jit(solution)/shard_map/ppermute | solution.py:41
  48.1 35.2 %collective-permute-start.20 = (f32[3,16,512]{2,1,0:T(8,128)S(1)}, f32[3,16,512]{2,1,0:T(8,128)S(1)}, u32[]{:S(2)}, u32[]{:S(2)}) collective-permute-start(f32[3,16,512]{2,1,0:T(8,128)S(1)} %get-tuple-element.136), channel_id=1, source_target_pairs={{0,4},{4,0},{8,12},{12,8},{16,20},{20,16},{24,28},{28,24},{1,5},{5... | collective-permute-start | bytes 294920 | tf_op jit(solution)/shard_map/ppermute | solution.py:41
  48.7 34.6 %collective-permute-start.21 = (f32[3,16,512]{2,1,0:T(8,128)S(1)}, f32[3,16,512]{2,1,0:T(8,128)S(1)}, u32[]{:S(2)}, u32[]{:S(2)}) collective-permute-start(f32[3,16,512]{2,1,0:T(8,128)S(1)} %get-tuple-element.137), channel_id=1, source_target_pairs={{0,28},{4,8},{8,4},{12,16},{16,12},{20,24},{24,20},{28,0},{1,29},{... | collective-permute-start | bytes 294920 | tf_op jit(solution)/shard_map/ppermute | solution.py:41
  51.4 3.7 %collective-permute-start.25 = (f32[5,256]{1,0:T(8,128)S(1)}, f32[5,256]{1,0:T(8,128)S(1)}, u32[]{:S(2)}, u32[]{:S(2)}) collective-permute-start(f32[5,256]{1,0:T(8,128)S(1)} %get-tuple-element.142), channel_id=1, source_target_pairs={{0,2},{1,3},{2,0},{3,1},{4,6},{5,7},{6,4},{7,5},{8,10},{9,11},{10,... | collective-permute-start | bytes 15368 | tf_op jit(solution)/shard_map/ppermute | solution.py:412
  56.9 6.3 %collective-permute-start.36 = (f32[1,256]{1,0:T(1,128)S(1)}, f32[1,256]{1,0:T(1,128)S(1)}, u32[]{:S(2)}, u32[]{:S(2)}) collective-permute-start(f32[1,256]{1,0:T(1,128)S(1)} %get-tuple-element.148.refs_15_), channel_id=1, source_target_pairs={{0,28},{4,24},{8,20},{12,16},{16,12},{20,8},{24,4},{28,0},{1,29},{... | collective-permute-start | bytes 3080 | tf_op jit(solution)/shard_map/ppermute | solution.py:425
  59.6 5.4 %collective-permute-start.35 = (f32[1,256]{1,0:T(1,128)S(1)}, f32[1,256]{1,0:T(1,128)S(1)}, u32[]{:S(2)}, u32[]{:S(2)}) collective-permute-start(f32[1,256]{1,0:T(1,128)S(1)} %get-tuple-element.148.refs_15_), channel_id=1, source_target_pairs={{0,24},{4,28},{8,16},{12,20},{16,8},{20,12},{24,0},{28,4},{1,25},{... | collective-permute-start | bytes 3080 | tf_op jit(solution)/shard_map/ppermute | solution.py:425
  60.9 5.4 %collective-permute-start.34 = (f32[1,256]{1,0:T(1,128)S(1)}, f32[1,256]{1,0:T(1,128)S(1)}, u32[]{:S(2)}, u32[]{:S(2)}) collective-permute-start(f32[1,256]{1,0:T(1,128)S(1)} %get-tuple-element.148.refs_15_), channel_id=1, source_target_pairs={{0,20},{4,16},{8,28},{12,24},{16,4},{20,0},{24,12},{28,8},{1,21},{... | collective-permute-start | bytes 3080 | tf_op jit(solution)/shard_map/ppermute | solution.py:425
  63.3 4.5 %collective-permute-start.33 = (f32[1,256]{1,0:T(1,128)S(1)}, f32[1,256]{1,0:T(1,128)S(1)}, u32[]{:S(2)}, u32[]{:S(2)}) collective-permute-start(f32[1,256]{1,0:T(1,128)S(1)} %get-tuple-element.148.refs_15_), channel_id=1, source_target_pairs={{0,16},{4,20},{8,24},{12,28},{16,0},{20,4},{24,8},{28,12},{1,17},{... | collective-permute-start | bytes 3080 | tf_op jit(solution)/shard_map/ppermute | solution.py:425
  65.0 14.3 %collective-permute-start.27 = (f32[4,256]{1,0:T(4,128)S(1)}, f32[4,256]{1,0:T(4,128)S(1)}, u32[]{:S(2)}, u32[]{:S(2)}) collective-permute-start(f32[4,256]{1,0:T(4,128)S(1)} %get-tuple-element.145), channel_id=1, source_target_pairs={{0,1},{1,0},{2,3},{3,2},{4,5},{5,4},{6,7},{7,6},{8,9},{9,8},{10,11... | collective-permute-start | bytes 12296 | tf_op jit(solution)/shard_map/ppermute | solution.py:412
  66.3 14.0 %collective-permute-start.28 = (f32[4,256]{1,0:T(4,128)S(1)}, f32[4,256]{1,0:T(4,128)S(1)}, u32[]{:S(2)}, u32[]{:S(2)}) collective-permute-start(f32[4,256]{1,0:T(4,128)S(1)} %get-tuple-element.146), channel_id=1, source_target_pairs={{0,2},{1,3},{2,0},{3,1},{4,6},{5,7},{6,4},{7,5},{8,10},{9,11},{10,... | collective-permute-start | bytes 12296 | tf_op jit(solution)/shard_map/ppermute | solution.py:412
  67.7 4.5 %collective-permute-start.32 = (f32[1,256]{1,0:T(1,128)S(1)}, f32[1,256]{1,0:T(1,128)S(1)}, u32[]{:S(2)}, u32[]{:S(2)}) collective-permute-start(f32[1,256]{1,0:T(1,128)S(1)} %get-tuple-element.148.refs_15_), channel_id=1, source_target_pairs={{0,12},{4,8},{8,4},{12,0},{16,28},{20,24},{24,20},{28,16},{1,13},{... | collective-permute-start | bytes 3080 | tf_op jit(solution)/shard_map/ppermute | solution.py:425
  79.3 4.0 %collective-permute-start.22 = (f32[6,512]{1,0:T(8,128)S(1)}, f32[6,512]{1,0:T(8,128)S(1)}, u32[]{:S(2)}, u32[]{:S(2)}) collective-permute-start(f32[6,512]{1,0:T(8,128)S(1)} %get-tuple-element.138), channel_id=1, source_target_pairs={{0,1},{1,0},{2,3},{3,2},{4,5},{5,4},{6,7},{7,6},{8,9},{9,8},{10,11... | collective-permute-start | bytes 36872 | tf_op jit(solution)/shard_map/ppermute | solution.py:41
  79.3 4.0 %collective-permute-start.23 = (f32[6,512]{1,0:T(8,128)S(1)}, f32[6,512]{1,0:T(8,128)S(1)}, u32[]{:S(2)}, u32[]{:S(2)}) collective-permute-start(f32[6,512]{1,0:T(8,128)S(1)} %get-tuple-element.139), channel_id=1, source_target_pairs={{0,3},{1,2},{2,1},{3,0},{4,7},{5,6},{6,5},{7,4},{8,11},{9,10},{10,... | collective-permute-start | bytes 36872 | tf_op jit(solution)/shard_map/ppermute | solution.py:41
  85.6 16.1 %collective-permute-start.37 = (f32[3,16,512]{2,1,0:T(8,128)S(1)}, f32[3,16,512]{2,1,0:T(8,128)S(1)}, u32[]{:S(2)}, u32[]{:S(2)}) collective-permute-start(f32[3,16,512]{2,1,0:T(8,128)S(1)} %get-tuple-element.150), channel_id=1, source_target_pairs={{0,4},{4,0},{8,12},{12,8},{16,20},{20,16},{24,28},{28,24},{1,5},{5... | collective-permute-start | bytes 294920 | tf_op jit(solution)/shard_map/ppermute | solution.py:41
  86.8 14.9 %collective-permute-start.38 = (f32[3,16,512]{2,1,0:T(8,128)S(1)}, f32[3,16,512]{2,1,0:T(8,128)S(1)}, u32[]{:S(2)}, u32[]{:S(2)}) collective-permute-start(f32[3,16,512]{2,1,0:T(8,128)S(1)} %get-tuple-element.151), channel_id=1, source_target_pairs={{0,28},{4,8},{8,4},{12,16},{16,12},{20,24},{24,20},{28,0},{1,29},{... | collective-permute-start | bytes 294920 | tf_op jit(solution)/shard_map/ppermute | solution.py:41
  89.5 3.6 %collective-permute-start.42 = (f32[4,256]{1,0:T(4,128)S(1)}, f32[4,256]{1,0:T(4,128)S(1)}, u32[]{:S(2)}, u32[]{:S(2)}) collective-permute-start(f32[4,256]{1,0:T(4,128)S(1)} %get-tuple-element.156), channel_id=1, source_target_pairs={{0,2},{1,3},{2,0},{3,1},{4,6},{5,7},{6,4},{7,5},{8,10},{9,11},{10,... | collective-permute-start | bytes 12296 | tf_op jit(solution)/shard_map/ppermute | solution.py:412
  95.1 3.6 %collective-permute-start.45 = (f32[4,256]{1,0:T(4,128)S(1)}, f32[4,256]{1,0:T(4,128)S(1)}, u32[]{:S(2)}, u32[]{:S(2)}) collective-permute-start(f32[4,256]{1,0:T(4,128)S(1)} %get-tuple-element.160), channel_id=1, source_target_pairs={{0,2},{1,3},{2,0},{3,1},{4,6},{5,7},{6,4},{7,5},{8,10},{9,11},{10,... | collective-permute-start | bytes 12296 | tf_op jit(solution)/shard_map/ppermute | solution.py:412
  96.5 5.2 %collective-permute-start.39 = (f32[6,512]{1,0:T(8,128)S(1)}, f32[6,512]{1,0:T(8,128)S(1)}, u32[]{:S(2)}, u32[]{:S(2)}) collective-permute-start(f32[6,512]{1,0:T(8,128)S(1)} %get-tuple-element.152), channel_id=1, source_target_pairs={{0,1},{1,0},{2,3},{3,2},{4,5},{5,4},{6,7},{7,6},{8,9},{9,8},{10,11... | collective-permute-start | bytes 36872 | tf_op jit(solution)/shard_map/ppermute | solution.py:41
  96.5 5.2 %collective-permute-start.40 = (f32[6,512]{1,0:T(8,128)S(1)}, f32[6,512]{1,0:T(8,128)S(1)}, u32[]{:S(2)}, u32[]{:S(2)}) collective-permute-start(f32[6,512]{1,0:T(8,128)S(1)} %get-tuple-element.153), channel_id=1, source_target_pairs={{0,3},{1,2},{2,1},{3,0},{4,7},{5,6},{6,5},{7,4},{8,11},{9,10},{10,... | collective-permute-start | bytes 36872 | tf_op jit(solution)/shard_map/ppermute | solution.py:41
  104.1 34.5 %collective-permute-start.47 = (f32[3,16,512]{2,1,0:T(8,128)S(1)}, f32[3,16,512]{2,1,0:T(8,128)S(1)}, u32[]{:S(2)}, u32[]{:S(2)}) collective-permute-start(f32[3,16,512]{2,1,0:T(8,128)S(1)} %get-tuple-element.166), channel_id=1, source_target_pairs={{0,4},{4,0},{8,12},{12,8},{16,20},{20,16},{24,28},{28,24},{1,5},{5... | collective-permute-start | bytes 294920 | tf_op jit(solution)/shard_map/ppermute | solution.py:41
  104.4 34.3 %collective-permute-start.48 = (f32[3,16,512]{2,1,0:T(8,128)S(1)}, f32[3,16,512]{2,1,0:T(8,128)S(1)}, u32[]{:S(2)}, u32[]{:S(2)}) collective-permute-start(f32[3,16,512]{2,1,0:T(8,128)S(1)} %get-tuple-element.167), channel_id=1, source_target_pairs={{0,28},{4,8},{8,4},{12,16},{16,12},{20,24},{24,20},{28,0},{1,29},{... | collective-permute-start | bytes 294920 | tf_op jit(solution)/shard_map/ppermute | solution.py:41
  106.8 3.7 %collective-permute-start.52 = (f32[5,256]{1,0:T(8,128)S(1)}, f32[5,256]{1,0:T(8,128)S(1)}, u32[]{:S(2)}, u32[]{:S(2)}) collective-permute-start(f32[5,256]{1,0:T(8,128)S(1)} %get-tuple-element.172), channel_id=1, source_target_pairs={{0,2},{1,3},{2,0},{3,1},{4,6},{5,7},{6,4},{7,5},{8,10},{9,11},{10,... | collective-permute-start | bytes 15368 | tf_op jit(solution)/shard_map/ppermute | solution.py:412
  112.1 6.3 %collective-permute-start.63 = (f32[1,256]{1,0:T(1,128)S(1)}, f32[1,256]{1,0:T(1,128)S(1)}, u32[]{:S(2)}, u32[]{:S(2)}) collective-permute-start(f32[1,256]{1,0:T(1,128)S(1)} %get-tuple-element.178.refs_15_), channel_id=1, source_target_pairs={{0,28},{4,24},{8,20},{12,16},{16,12},{20,8},{24,4},{28,0},{1,29},{... | collective-permute-start | bytes 3080 | tf_op jit(solution)/shard_map/ppermute | solution.py:425
  114.8 5.4 %collective-permute-start.62 = (f32[1,256]{1,0:T(1,128)S(1)}, f32[1,256]{1,0:T(1,128)S(1)}, u32[]{:S(2)}, u32[]{:S(2)}) collective-permute-start(f32[1,256]{1,0:T(1,128)S(1)} %get-tuple-element.178.refs_15_), channel_id=1, source_target_pairs={{0,24},{4,28},{8,16},{12,20},{16,8},{20,12},{24,0},{28,4},{1,25},{... | collective-permute-start | bytes 3080 | tf_op jit(solution)/shard_map/ppermute | solution.py:425
  115.3 5.4 %collective-permute-start.61 = (f32[1,256]{1,0:T(1,128)S(1)}, f32[1,256]{1,0:T(1,128)S(1)}, u32[]{:S(2)}, u32[]{:S(2)}) collective-permute-start(f32[1,256]{1,0:T(1,128)S(1)} %get-tuple-element.178.refs_15_), channel_id=1, source_target_pairs={{0,20},{4,16},{8,28},{12,24},{16,4},{20,0},{24,12},{28,8},{1,21},{... | collective-permute-start | bytes 3080 | tf_op jit(solution)/shard_map/ppermute | solution.py:425
  118.4 4.5 %collective-permute-start.60 = (f32[1,256]{1,0:T(1,128)S(1)}, f32[1,256]{1,0:T(1,128)S(1)}, u32[]{:S(2)}, u32[]{:S(2)}) collective-permute-start(f32[1,256]{1,0:T(1,128)S(1)} %get-tuple-element.178.refs_15_), channel_id=1, source_target_pairs={{0,16},{4,20},{8,24},{12,28},{16,0},{20,4},{24,8},{28,12},{1,17},{... | collective-permute-start | bytes 3080 | tf_op jit(solution)/shard_map/ppermute | solution.py:425
  120.1 14.3 %collective-permute-start.54 = (f32[4,256]{1,0:T(4,128)S(1)}, f32[4,256]{1,0:T(4,128)S(1)}, u32[]{:S(2)}, u32[]{:S(2)}) collective-permute-start(f32[4,256]{1,0:T(4,128)S(1)} %get-tuple-element.175), channel_id=1, source_target_pairs={{0,1},{1,0},{2,3},{3,2},{4,5},{5,4},{6,7},{7,6},{8,9},{9,8},{10,11... | collective-permute-start | bytes 12296 | tf_op jit(solution)/shard_map/ppermute | solution.py:412
  120.6 15.0 %collective-permute-start.55 = (f32[4,256]{1,0:T(4,128)S(1)}, f32[4,256]{1,0:T(4,128)S(1)}, u32[]{:S(2)}, u32[]{:S(2)}) collective-permute-start(f32[4,256]{1,0:T(4,128)S(1)} %get-tuple-element.176), channel_id=1, source_target_pairs={{0,2},{1,3},{2,0},{3,1},{4,6},{5,7},{6,4},{7,5},{8,10},{9,11},{10,... | collective-permute-start | bytes 12296 | tf_op jit(solution)/shard_map/ppermute | solution.py:412
  122.9 4.5 %collective-permute-start.59 = (f32[1,256]{1,0:T(1,128)S(1)}, f32[1,256]{1,0:T(1,128)S(1)}, u32[]{:S(2)}, u32[]{:S(2)}) collective-permute-start(f32[1,256]{1,0:T(1,128)S(1)} %get-tuple-element.178.refs_15_), channel_id=1, source_target_pairs={{0,12},{4,8},{8,4},{12,0},{16,28},{20,24},{24,20},{28,16},{1,13},{... | collective-permute-start | bytes 3080 | tf_op jit(solution)/shard_map/ppermute | solution.py:425
  134.5 4.2 %collective-permute-start.49 = (f32[6,512]{1,0:T(8,128)S(1)}, f32[6,512]{1,0:T(8,128)S(1)}, u32[]{:S(2)}, u32[]{:S(2)}) collective-permute-start(f32[6,512]{1,0:T(8,128)S(1)} %get-tuple-element.168), channel_id=1, source_target_pairs={{0,1},{1,0},{2,3},{3,2},{4,5},{5,4},{6,7},{7,6},{8,9},{9,8},{10,11... | collective-permute-start | bytes 36872 | tf_op jit(solution)/shard_map/ppermute | solution.py:41
  134.5 4.2 %collective-permute-start.50 = (f32[6,512]{1,0:T(8,128)S(1)}, f32[6,512]{1,0:T(8,128)S(1)}, u32[]{:S(2)}, u32[]{:S(2)}) collective-permute-start(f32[6,512]{1,0:T(8,128)S(1)} %get-tuple-element.169), channel_id=1, source_target_pairs={{0,3},{1,2},{2,1},{3,0},{4,7},{5,6},{6,5},{7,4},{8,11},{9,10},{10,... | collective-permute-start | bytes 36872 | tf_op jit(solution)/shard_map/ppermute | solution.py:41
  141.0 15.9 %collective-permute-start.64 = (f32[3,16,512]{2,1,0:T(8,128)S(1)}, f32[3,16,512]{2,1,0:T(8,128)S(1)}, u32[]{:S(2)}, u32[]{:S(2)}) collective-permute-start(f32[3,16,512]{2,1,0:T(8,128)S(1)} %get-tuple-element.184), channel_id=1, source_target_pairs={{0,4},{4,0},{8,12},{12,8},{16,20},{20,16},{24,28},{28,24},{1,5},{5... | collective-permute-start | bytes 294920 | tf_op jit(solution)/shard_map/ppermute | solution.py:41
  142.0 14.9 %collective-permute-start.65 = (f32[3,16,512]{2,1,0:T(8,128)S(1)}, f32[3,16,512]{2,1,0:T(8,128)S(1)}, u32[]{:S(2)}, u32[]{:S(2)}) collective-permute-start(f32[3,16,512]{2,1,0:T(8,128)S(1)} %get-tuple-element.185), channel_id=1, source_target_pairs={{0,28},{4,8},{8,4},{12,16},{16,12},{20,24},{24,20},{28,0},{1,29},{... | collective-permute-start | bytes 294920 | tf_op jit(solution)/shard_map/ppermute | solution.py:41
  144.7 3.6 %collective-permute-start.69 = (f32[4,256]{1,0:T(4,128)S(1)}, f32[4,256]{1,0:T(4,128)S(1)}, u32[]{:S(2)}, u32[]{:S(2)}) collective-permute-start(f32[4,256]{1,0:T(4,128)S(1)} %get-tuple-element.190), channel_id=1, source_target_pairs={{0,2},{1,3},{2,0},{3,1},{4,6},{5,7},{6,4},{7,5},{8,10},{9,11},{10,... | collective-permute-start | bytes 12296 | tf_op jit(solution)/shard_map/ppermute | solution.py:412
  150.3 3.6 %collective-permute-start.72 = (f32[4,256]{1,0:T(4,128)S(1)}, f32[4,256]{1,0:T(4,128)S(1)}, u32[]{:S(2)}, u32[]{:S(2)}) collective-permute-start(f32[4,256]{1,0:T(4,128)S(1)} %get-tuple-element.194), channel_id=1, source_target_pairs={{0,2},{1,3},{2,0},{3,1},{4,6},{5,7},{6,4},{7,5},{8,10},{9,11},{10,... | collective-permute-start | bytes 12296 | tf_op jit(solution)/shard_map/ppermute | solution.py:412
  151.5 5.4 %collective-permute-start.66 = (f32[6,512]{1,0:T(8,128)S(1)}, f32[6,512]{1,0:T(8,128)S(1)}, u32[]{:S(2)}, u32[]{:S(2)}) collective-permute-start(f32[6,512]{1,0:T(8,128)S(1)} %get-tuple-element.186), channel_id=1, source_target_pairs={{0,1},{1,0},{2,3},{3,2},{4,5},{5,4},{6,7},{7,6},{8,9},{9,8},{10,11... | collective-permute-start | bytes 36872 | tf_op jit(solution)/shard_map/ppermute | solution.py:41
  151.5 5.4 %collective-permute-start.67 = (f32[6,512]{1,0:T(8,128)S(1)}, f32[6,512]{1,0:T(8,128)S(1)}, u32[]{:S(2)}, u32[]{:S(2)}) collective-permute-start(f32[6,512]{1,0:T(8,128)S(1)} %get-tuple-element.187), channel_id=1, source_target_pairs={{0,3},{1,2},{2,1},{3,0},{4,7},{5,6},{6,5},{7,4},{8,11},{9,10},{10,... | collective-permute-start | bytes 36872 | tf_op jit(solution)/shard_map/ppermute | solution.py:41
  (36 other events, 87.3 us)

commit v3 on v2

v3 whole, which is shorter than its diff:
```python
import functools

import jax
import jax.numpy as jnp
from jax import lax
from jax.experimental import pallas as pl
from jax.experimental.pallas import tpu as pltpu
from jax.sharding import PartitionSpec as P

ITERS = 3
F32 = jnp.float32
BF16 = jnp.bfloat16
VMEM = pl.BlockSpec(memory_space=pltpu.VMEM)
SMEM = pl.BlockSpec(memory_space=pltpu.SMEM)
LIMIT = 20 * 1024 * 1024
SOLVE_FLOPS = 5_000_000_000
NAMES = ("br", "bs", "bw", "bz", "rw", "rz", "sw", "sz", "ww", "wz", "zz")


def call(kernel, outs, args, specs=None, scratch=(), flops=1_000_000, moved=1_000_000):
    return pl.pallas_call(
        kernel,
        out_shape=[jax.ShapeDtypeStruct(shape, dtype) for shape, dtype in outs],
        in_specs=specs or [VMEM] * len(args),
        out_specs=[VMEM] * len(outs),
        scratch_shapes=list(scratch),
        compiler_params=pltpu.CompilerParams(vmem_limit_bytes=LIMIT),
        cost_estimate=pl.CostEstimate(flops=flops, bytes_accessed=moved, transcendentals=0),
    )(*args)


def exchange(faces):
    count = lax.axis_size("res")
    first = [(i, i ^ 1) for i in range(count)]
    second = [(i, (i + 1 if i % 2 else i - 1) % count) for i in range(count)]
    return [lax.ppermute(face, "res", pairs) for face, pairs in zip(faces, (first, second))]


def is_even(axis):
    return lax.rem(lax.axis_index(axis), 2) == 0


def write_faces(field, refs):
    first, second = refs
    even = is_even("res")
    for j in range(first.shape[0]):
        low, high = field(j, 0), field(j, field.cells_x - 1)
        first[j] = jnp.where(even, high, low)
        second[j] = jnp.where(even, low, high)


def halo_terms(halo, messages, trans):
    first, second = halo
    components, cells_y, cells_z = first.shape
    cells_x = trans.shape[3]
    even = is_even("res")
    r, g = lax.axis_index("res"), lax.axis_index("grp")
    low_on = (r > 0).astype(F32)
    high_on = (r < lax.axis_size("res") - 1).astype(F32)
    xhigh = [jnp.where(even, first[j], second[j]) * high_on for j in range(components)]
    xlow = [jnp.where(even, second[j], first[j]) * low_on for j in range(components)]
    lines = components * cells_x
    yhigh = jnp.zeros((lines, cells_z), F32)
    ylow = jnp.zeros((lines, cells_z), F32)
    for k, message in enumerate(messages):
        if carries_face(k):
            line = message[message.shape[0] - lines :]
            above = (jnp.bitwise_xor(g, k) == g + 1).astype(F32)
            below = (jnp.bitwise_xor(g, k) == g - 1).astype(F32)
            yhigh = yhigh + line * above
            ylow = ylow + line * below
    rows = lax.broadcasted_iota(jnp.int32, (cells_y, cells_z), 0)

    def terms(i, x):
        low = jnp.zeros((1, cells_z), F32)
        high = jnp.zeros((1, cells_z), F32)
        for j in range(components):
            k = j * cells_x + x
            high = high + trans[2, i, j, x, cells_y - 1 : cells_y] * yhigh[k : k + 1]
            low = low + trans[3, i, j, x, 0:1] * ylow[k : k + 1]
        total = jnp.where(rows == cells_y - 1, high, 0.0) + jnp.where(rows == 0, low, 0.0)
        for j in range(components):
            if x == cells_x - 1:
                total = total + trans[0, i, j, x] * xhigh[j]
            if x == 0:
                total = total + trans[1, i, j, x] * xlow[j]
        return total

    return terms


class Planes:
    def __init__(self, ref):
        self.ref, self.cells_x = ref, ref.shape[1]

    def __call__(self, j, x):
        return self.ref[j, x]


def inner_stencil(vec, trans, diag, shifted, out):
    components, cells_x, cells_y, cells_z = vec.shape
    rows = lax.broadcasted_iota(jnp.int32, (cells_y, cells_z), 0)
    lanes = lax.broadcasted_iota(jnp.int32, (cells_y, cells_z), 1)
    for j in range(components):
        for x in range(cells_x):
            plane = vec[j, x]
            up = pltpu.roll(plane, cells_y - 1, 0)
            shifted[0, j, x] = jnp.where(rows == cells_y - 1, 0.0, up)
            shifted[1, j, x] = jnp.where(rows == 0, 0.0, pltpu.roll(plane, 1, 0))
            up = pltpu.roll(plane, cells_z - 1, 1)
            shifted[2, j, x] = jnp.where(lanes == cells_z - 1, 0.0, up)
            shifted[3, j, x] = jnp.where(lanes == 0, 0.0, pltpu.roll(plane, 1, 1))
    for i in range(components):
        for x in range(cells_x):
            total = diag[i, 0, x] * vec[0, x]
            for j in range(1, components):
                total = total + diag[i, j, x] * vec[j, x]
            for j in range(components):
                if x + 1 < cells_x:
                    total = total - trans[0, i, j, x] * vec[j, x + 1]
                if x > 0:
                    total = total - trans[1, i, j, x] * vec[j, x - 1]
                for side in range(4):
                    total = total - trans[2 + side, i, j, x] * shifted[side, j, x]
            out[i, x] = total


def halves(value):
    high = value.astype(BF16)
    low = (value - high.astype(F32)).astype(BF16)
    return high, low


def dot(a, b, transposed=False):
    dims = (((1,), (1 if transposed else 0,)), ((), ()))
    return lax.dot_general(a, b, dims, preferred_element_type=F32)


def gather_well(both, place, column, weight, b):
    components, _, segb = weight.shape
    part = slice(b * segb, (b + 1) * segb)
    found = dot(both, place[:, part])
    rows = found.shape[0] // 2
    found = found[:rows] + found[rows:]
    per = rows // components
    here = lax.broadcasted_iota(jnp.int32, (per, segb), 0) == column[b : b + 1, :]
    coupled = jnp.zeros((1, segb), F32)
    for i in range(components):
        part = jnp.where(here, found[i * per : (i + 1) * per], 0.0)
        coupled = coupled + jnp.sum(part, axis=0, keepdims=True) * weight[i, b : b + 1]
    return coupled


def solve_well(coupled, first, second):
    high = coupled.astype(BF16).astype(F32)
    low = coupled - high
    rows = lax.broadcasted_iota(jnp.int32, (16, coupled.shape[1]), 0)
    left = jnp.where(rows == 0, high, jnp.where(rows == 1, low, 0.0)).astype(BF16)
    return jnp.sum(dot(left, first, True) + dot(left, second, True), axis=0, keepdims=True)


def scatter_well(value, place, column, weight, rows, b):
    components, _, segb = weight.shape
    per = rows // components
    part = slice(b * segb, (b + 1) * segb)
    here = lax.broadcasted_iota(jnp.int32, (per, segb), 0) == column[b : b + 1, :]
    blocks = [
        jnp.where(here, weight[i, b : b + 1] * value, 0.0) for i in range(components)
    ]
    high, low = halves(jnp.concatenate(blocks, axis=0))
    return dot(jnp.concatenate([high, low], axis=0), place[:, part], True)


def stencil_kernel(after, with_sums, vec, trans, diag, *refs):
    refs = refs[after:]
    if with_sums:
        row, other, *refs = refs
        refs, total = (*refs[:2], *refs[3:]), refs[2]
        total[...] = row[...] + other[...]
    *faces, out, shifted = refs
    write_faces(Planes(vec), faces)
    inner_stencil(vec, trans, diag, shifted, out)


def first_stencil_kernel(vec, trans, acc, face0, face1, out, diag, shifted):
    write_faces(Planes(vec), (face0, face1))
    for i in range(acc.shape[0]):
        for j in range(acc.shape[1]):
            total = acc[i, j]
            for face in range(trans.shape[0]):
                total = total + trans[face, i, j]
            diag[i, j] = total
    inner_stencil(vec, trans, diag, shifted, out)


def carries_face(k):
    return k > 0 and k & (k + 1) == 0


def message_shapes(groups, capacity, segb, lines, cells_z):
    rows = -(-capacity // (cells_z // segb))
    return [
        (rows + lines, cells_z) if carries_face(k) else (capacity, segb) for k in range(groups)
    ]


def spot(message, slot, segb):
    each = message.shape[1] // segb
    row, part = slot // each, slot % each
    return slice(row, row + 1), slice(part * segb, (part + 1) * segb)


def places(owner, capacity, wells):
    g = lax.axis_index("grp")
    out = []
    for b in range(wells):
        mine = owner[b, 0]
        slot = jnp.int32(0)
        for c in range(b):
            slot = slot + (owner[c, 0] == mine).astype(jnp.int32)
        out.append(jnp.bitwise_xor(g, mine) * capacity + slot)
    return out


def write_messages(vec, place, column, take, owner, capacity, messages):
    components, cells_x, cells_y, cells_z = vec.shape
    wells, segb = column.shape
    high, low = halves(vec[...].reshape(components * cells_x * cells_y, cells_z))
    both = jnp.concatenate([high, low], axis=0)
    coupled = [gather_well(both, place, column, take, b) for b in range(wells)]
    where = places(owner, capacity, wells)
    slots = lax.broadcasted_iota(jnp.int32, (capacity, segb), 0)
    g = lax.axis_index("grp")
    for k, message in enumerate(messages):
        block = jnp.zeros((capacity, segb), F32)
        for b in range(wells):
            block = jnp.where(slots == where[b] - k * capacity, coupled[b], block)
        for slot in range(capacity):
            message[spot(message, slot, segb)] = block[slot : slot + 1]
        if carries_face(k):
            above = jnp.bitwise_xor(g, k) > g
            start = message.shape[0] - components * cells_x
            for j in range(components):
                for x in range(cells_x):
                    row = start + j * cells_x + x
                    plane = vec[j, x]
                    message[row : row + 1] = jnp.where(
                        above, plane[cells_y - 1 : cells_y], plane[0:1]
                    )


def solve_kernel(parts, groups, first, second, *refs):
    sums, sent, back = refs[:parts], refs[parts : parts + groups], refs[parts + groups :]
    g = lax.axis_index("grp")
    capacity, segb = first.shape[1], first.shape[2]
    for k in range(groups):
        home = jnp.bitwise_xor(g, k)
        for slot in range(capacity):
            coupled = sent[k][spot(sent[k], slot, segb)]
            back[k][slot : slot + 1] = solve_well(coupled, first[home, slot], second[home, slot])
    if parts:
        total = sums[0][...]
        for ref in sums[1:]:
            total = total + ref[...]
        for k in range(groups):
            back[k][capacity : capacity + 1] = total


def well_terms(values, place, column, give, owner, capacity, shape):
    components, cells_x, cells_y, cells_z = shape
    rows = components * cells_x * cells_y
    wells, segb = column.shape
    slots = lax.broadcasted_iota(jnp.int32, (capacity, segb), 0)
    where = places(owner, capacity, wells)
    values = [ref[0:capacity] for ref in values]
    total = None
    for b in range(wells):
        value = jnp.zeros((capacity, segb), F32)
        for k, rows_of in enumerate(values):
            value = value + jnp.where(slots == where[b] - k * capacity, rows_of, 0.0)
        value = jnp.sum(value, axis=0, keepdims=True)
        term = scatter_well(value, place, column, give, rows, b)
        total = term if total is None else total + term
    return (total[:rows] + total[rows:]).reshape(shape)


def start_kernel(groups, capacity, vec, completion, live, owner, take, give, place, column, take_out, give_out, *sends):
    components, cells_x, cells_y, cells_z = vec.shape
    wells, segb = completion.shape
    depth = lax.broadcasted_iota(jnp.int32, (cells_z, segb), 0)
    lanes = lax.broadcasted_iota(jnp.int32, (1, segb), 1)
    for b in range(wells):
        cell = completion[b : b + 1, :]
        row = cell // cells_z
        column[b : b + 1, :] = row
        hit = depth == cell - row * cells_z
        place[:, b * segb : (b + 1) * segb] = jnp.where(hit, 1.0, 0.0).astype(BF16)
        is_open = (lanes < live[b]).astype(F32)
        for i in range(components):
            take_out[i, b : b + 1] = take[i, b : b + 1] * is_open
            give_out[i, b : b + 1] = give[i, b : b + 1] * is_open
    write_messages(vec, place, column, take_out, owner, capacity, sends)


def split_kernel(inverse, first, second):
    for h in range(inverse.shape[0]):
        for slot in range(inverse.shape[1]):
            first[h, slot], second[h, slot] = halves(inverse[h, slot])


class Arrived:
    def __init__(self, groups, capacity, refs):
        self.capacity, self.groups = capacity, groups
        self.part, self.trans, self.place, self.column, self.take, self.give, self.owner = refs[:7]
        self.halo = refs[7:9]
        self.messages = refs[9 : 9 + groups]
        self.values = refs[9 + groups : 9 + 2 * groups]
        self.rest = refs[9 + 2 * groups :]

    def result(self):
        wells = well_terms(
            self.values, self.place, self.column, self.give, self.owner, self.capacity, self.part.shape
        )
        terms = halo_terms(self.halo, self.messages, self.trans)
        return lambda i, x: self.part[i, x] - wells[i, x] - terms(i, x)

    def send(self, vec, sends):
        write_messages(vec, self.place, self.column, self.take, self.owner, self.capacity, sends)


def apply_kernel(sizes, *refs):
    got = Arrived(*sizes, refs)
    out, *sends = got.rest
    value = got.result()
    for i in range(out.shape[0]):
        for x in range(out.shape[1]):
            out[i, x] = value(i, x)
    got.send(out, sends)


def local_sums(vecs, width):
    b, r, s, w, z = vecs
    table = {"b": b, "r": r, "s": s, "w": w, "z": z}
    lanes = lax.broadcasted_iota(jnp.int32, (1, width), 1)
    row = jnp.zeros((1, width), F32)
    for k, name in enumerate(NAMES):
        left, right = table[name[0]], table[name[1]]
        total = None
        for i in range(b.shape[0]):
            for x in range(b.shape[1]):
                term = left[i, x] * right[i, x]
                total = term if total is None else total + term
        total = jnp.sum(jnp.sum(total, axis=0, keepdims=True), axis=1, keepdims=True)
        row = jnp.where(lanes == k, total, row)
    return row


def second_kernel(sizes, first_time, end, *refs):
    got = Arrived(*sizes, refs)
    if first_time:
        b, r, w, t, *rest = got.rest
        s, z = w, t
    else:
        b, r, w, s_rest, z_rest, t, s, z, *rest = got.rest
    value = got.result()
    for i in range(t.shape[0]):
        for x in range(t.shape[1]):
            t[i, x] = value(i, x)
            if not first_time:
                s[i, x] = w[i, x] + s_rest[i, x]
                z[i, x] = t[i, x] + z_rest[i, x]
    sums, *sends = rest
    row = local_sums((b, r, s, w, z), sums.shape[-1])
    if end:
        for d in range(sums.shape[0]):
            sums[d] = row
    else:
        sums[...] = row
        got.send(z, sends)


def coefficients(row):
    lanes = lax.broadcasted_iota(jnp.int32, row.shape, 1)
    v = {
        name: jnp.sum(jnp.where(lanes == k, row, 0.0), axis=1, keepdims=True)
        for k, name in enumerate(NAMES)
    }
    alpha = v["br"] / v["bs"]
    inner = v["rw"] - alpha * (v["rz"] + v["sw"]) + alpha * alpha * v["sz"]
    square = v["ww"] - 2.0 * alpha * v["wz"] + alpha * alpha * v["zz"]
    omega = inner / square
    beta = -(v["bw"] - alpha * v["bz"]) / v["bs"]
    return alpha, omega, beta


def third_kernel(sizes, first_time, *refs):
    got = Arrived(*sizes, refs)
    r, w, t, *rest = got.rest
    if first_time:
        r_out, w_out, x_out, p_out, s_rest, z_rest, *sends = rest
        s, z, p, x_in = w, t, r, None
    else:
        s, z, p, x_in, r_out, w_out, x_out, p_out, s_rest, z_rest, *sends = rest
    value = got.result()
    last = slice(got.capacity, got.capacity + 1)
    row = got.values[0][last]
    for ref in got.values[1:]:
        row = row + ref[last]
    alpha, omega, beta = coefficients(row)
    for i in range(r.shape[0]):
        for x in range(r.shape[1]):
            v = value(i, x)
            q = r[i, x] - alpha * s[i, x]
            y = w[i, x] - alpha * z[i, x]
            new_r = q - omega * y
            r_out[i, x] = new_r
            w_out[i, x] = y - omega * (t[i, x] - alpha * v)
            step = alpha * p[i, x] + omega * q
            x_out[i, x] = step if x_in is None else x_in[i, x] + step
            p_out[i, x] = new_r + beta * (p[i, x] - omega * s[i, x])
            s_rest[i, x] = beta * (s[i, x] - omega * z[i, x])
            z_rest[i, x] = beta * (z[i, x] - omega * v)
    got.send(w_out, sends)


def last_kernel(sums, r, w, s, z, p, x_in, x_out, r_out):
    row = sums[0]
    for d in range(1, sums.shape[0]):
        row = row + sums[d]
    alpha, omega, _ = coefficients(row)
    for i in range(r.shape[0]):
        for x in range(r.shape[1]):
            q = r[i, x] - alpha * s[i, x]
            y = w[i, x] - alpha * z[i, x]
            x_out[i, x] = x_in[i, x] + alpha * p[i, x] + omega * q
            r_out[i, x] = q - omega * y


def swapped(messages):
    groups = lax.axis_size("grp")
    return [messages[0]] + [
        lax.ppermute(messages[k], "grp", [(i, i ^ k) for i in range(groups)])
        for k in range(1, groups)
    ]


def over_res(row, mask):
    return lax.ppermute(row, "res", [(i, i ^ mask) for i in range(lax.axis_size("res"))])


def res_sums(row):
    count, step = lax.axis_size("res"), 2
    parts = [row]
    while step < count:
        many = min(4, count // step)
        if len(parts) > 1:
            row = functools.reduce(jnp.add, parts)
        parts = [row] + [over_res(row, k * step) for k in range(1, many)]
        step *= many
    return parts


def body(
    right_side,
    accumulation,
    transmissibility,
    completion,
    live_count,
    owner,
    cell_to_well,
    well_to_cell,
    inverse,
):
    components, cells_x, cells_y, cells_z = right_side.shape
    wells, segb = completion.shape
    groups = lax.axis_size("grp")
    capacity = inverse.shape[2]
    devices = lax.axis_size("res") * groups
    field = (right_side.shape, F32)
    shapes = message_shapes(groups, capacity, segb, components * cells_x, cells_z)
    send_outs = [(shape, F32) for shape in shapes]
    face_outs = [((components, cells_y, cells_z), F32)] * 2
    trans = transmissibility
    take = jnp.moveaxis(cell_to_well, 1, 0)
    give = jnp.moveaxis(well_to_cell, 1, 0)
    b = right_side
    sizes = (groups, capacity)

    place, column, take, give, *sends = call(
        functools.partial(start_kernel, groups, capacity),
        [
            ((cells_z, wells * segb), BF16),
            (completion.shape, jnp.int32),
            (take.shape, F32),
            (give.shape, F32),
        ]
        + send_outs,
        [b, completion, live_count, owner, take, give],
        [VMEM, VMEM, SMEM, SMEM, VMEM, VMEM],
    )
    first, second = call(split_kernel, [(inverse.shape[1:], BF16)] * 2, [inverse[0]])
    shifted = [pltpu.VMEM((4,) + b.shape, F32)]

    cost = dict(scratch=shifted, flops=200_000_000, moved=4_000_000)

    def finish(kernel, outs, vec, sends, extra, row=None):
        messages = swapped(sends)
        if vec is b:
            *faces, part, diag_total = call(
                first_stencil_kernel,
                face_outs + [field, (accumulation.shape, F32)],
                [b, trans, accumulation],
                **cost,
            )
            diag.append(diag_total)
        elif row is None:
            *faces, part = call(
                functools.partial(stencil_kernel, 0, False),
                face_outs + [field],
                [vec, trans, *diag],
                **cost,
            )
        else:
            *faces, row, part = call(
                functools.partial(stencil_kernel, groups, True),
                face_outs + [((1, segb), F32), field],
                [vec, trans, *diag, *messages, row, over_res(row, 1)],
                **cost,
            )
        sums = [] if row is None else res_sums(row)
        halo = exchange(faces)
        values = call(
            functools.partial(solve_kernel, len(sums), groups),
            [((capacity + (len(sums) > 0), segb), F32)] * groups,
            [first, second, *sums, *messages],
            flops=SOLVE_FLOPS,
            moved=4_000_000,
        )
        values = swapped(values)
        args = [part, trans, place, column, take, give, owner, *halo, *messages, *values, *extra]
        specs = [VMEM] * len(args)
        specs[6] = SMEM
        return call(kernel, outs, args, specs, flops=1_000_000_000, moved=8_000_000)

    diag = []
    w, *sends = finish(
        functools.partial(apply_kernel, sizes), [field] + send_outs, b, sends, []
    )
    r, s, p, x = b, w, b, None
    for index in range(ITERS):
        start, end = index == 0, index + 1 == ITERS
        tail = [((devices, 1, 128), F32)] if end else [((1, segb), F32)] + send_outs
        kernel = functools.partial(second_kernel, sizes, start, end)
        if start:
            t, sums, *sends = finish(kernel, [field] + tail, w, sends, [b, r, w])
            z = t
        else:
            t, s, z, sums, *sends = finish(
                kernel, [field] * 3 + tail, w, sends, [b, r, w, s_rest, z_rest]
            )
        if end:
            break
        more = [] if start else [s, z, p, x]
        r, w, x, p, s_rest, z_rest, *sends = finish(
            functools.partial(third_kernel, sizes, start),
            [field] * 6 + send_outs,
            z,
            sends,
            [r, w, t, *more],
            sums,
        )
    sums = lax.all_to_all(sums, ("res", "grp"), split_axis=0, concat_axis=0, tiled=True)
    x, r = call(last_kernel, [field, field], [sums, r, w, s, z, p, x])
    return (x, r)


def solution(mesh):
    return jax.shard_map(
        body,
        mesh=mesh,
        in_specs=(
            P(None, "res", "grp", None),
            P(None, None, "res", "grp", None),
            P(None, None, None, "res", "grp", None),
            P(("res", "grp"), None),
            P(("res", "grp")),
            P(("res", "grp"), None),
            P(("res", "grp"), None, None),
            P(("res", "grp"), None, None),
            P(("res", "grp"), None, None, None, None),
        ),
        out_specs=(P(None, "res", "grp", None), P(None, "res", "grp", None)),
        check_vma=False,
    )
```

time: 171 us -> 121 us (0.71)
  waiting for transfers between devices: 58.9 us -> 22.1 us
  starting transfers between devices: 65.1 us -> 52.5 us
    ppermute x38 -> x20, waiting for transfers between devices: 27.1 us -> 7.09 us  [the longest x8 6.99 us: over_res(): lax.ppermute(row, 'res', [(i, i ^ mask) for i in range(lax.axis_size('res...]
    ppermute x38 -> x20, starting transfers between devices: 43.9 us -> 26.6 us  [the longest x12 17.5 us: exchange(): lax.ppermute(face, 'res', pairs)]
    ppermute x36, waiting for transfers between devices: 31.8 us -> 15 us  [swapped(): lax.ppermute(messages[k], 'grp', [(i, i ^ k) for i in range(groups)])]
    ppermute x36, starting transfers between devices: 21.2 us -> 25.9 us  [swapped(): lax.ppermute(messages[k], 'grp', [(i, i ^ k) for i in range(groups)])]
    pallas_call x23 -> x21, Pallas kernels: 27.7 us -> 26.9 us  [call(): pl.pallas_call(kernel, out_shape=[jax.ShapeDtypeStruct(shape, dtype) for...]
  transfers between devices with their start and end apart: 74 -> 56, of which waited for: 35 -> 15; matrix products, arithmetic and copies ran while one was open for 0% -> 0% of each run, Pallas kernels for 8% -> 8%
where the time goes in v3:
time: 121 us; the launch traced here: 120 us
  starting transfers between devices  52.5 us (43%)
  Pallas kernels  26.9 us (22%)
  waiting for transfers between devices  22.1 us (18%)
  blocking collectives  10.5 us (9%)
  local copies, waits for them, and re-layouts  7.56 us (6%)
    pallas_call x21, Pallas kernels, call(): pl.pallas_call(kernel, out_shape=[jax.ShapeDtypeStruct(shape, dtype) for...  26.9 us
    ppermute x36, starting transfers between devices, swapped(): lax.ppermute(messages[k], 'grp', [(i, i ^ k) for i in range(groups)])  25.9 us
    ppermute x12, starting transfers between devices, exchange(): lax.ppermute(face, 'res', pairs)  17.5 us
    ppermute x36, waiting for transfers between devices, swapped(): lax.ppermute(messages[k], 'grp', [(i, i ^ k) for i in range(groups)])  15 us
    all_to_all x1, blocking collectives, body(): lax.all_to_all(sums, ('res', 'grp'), split_axis=0, concat_axis=0, tiled=T...  10.5 us
    ppermute x8, starting transfers between devices, over_res(): lax.ppermute(row, 'res', [(i, i ^ mask) for i in range(lax.axis_size('res...  9.06 us
    unnamed x21, local copies, waits for them, and re-layouts  7.56 us
    ppermute x8, waiting for transfers between devices, over_res(): lax.ppermute(row, 'res', [(i, i ^ mask) for i in range(lax.axis_size('res...  6.99 us
  transfers between devices with their start and end apart: 56, of which 15 were waited for; matrix products, arithmetic and copies ran while one was open for 0% of the time, Pallas kernels for 8%

profile of v3, /device:TPU:0, one launch (start us, length us, event | category | flops | bytes accessed | tf_op | source)
XLA Modules:
  0.0 120.4 jit_solution(5301347636631114735)
XLA Ops:
  5.1 1.5 %shard_map.105 = (bf16[512,2048]{1,0:T(8,128)(2,1)S(1)}, s32[8,256]{1,0:T(8,128)S(1)}, f32[3,8,256]{2,1,0:T(8,128)S(1)}, f32[3,8,256]{2,1,0:T(8,128)S(1)}, f32[4...) custom-call(f32[3,2,16,512]{3,2,1,0:T(8,128)S(1)} %copy-done.2, ...), custom_call_target="tpu_custom_call" | custom-call | flops 1000000 | bytes 1000000 | tf_op jit(solution)/shard_map/pallas_call | solution.py:21
  6.6 3.0 %collective-permute-start.3 = (f32[4,256]{1,0:T(4,128)S(1)}, f32[4,256]{1,0:T(4,128)S(1)}, u32[]{:S(2)}, u32[]{:S(2)}) collective-permute-start(f32[4,256]{1,0:T(4,128)S(1)} %get-tuple-element.108), channel_id=1, source_target_pairs={{0,2},{1,3},{2,0},{3,1},{4,6},{5,7},{6,4},{7,5},{8,10},{9,11},{10,... | collective-permute-start | bytes 12296 | tf_op jit(solution)/shard_map/ppermute | solution.py:442
  9.8 2.0 %copy-done = f32[6,3,3,2,16,512]{5,4,3,2,1,0:T(8,128)S(1)} copy-done((f32[6,3,3,2,16,512]{5,4,3,2,1,0:T(8,128)S(1)}, f32[6,3,3,2,16,512]{5,4,3,2,1,0:T(8,128)}, u32[]{:S(2)}) %copy-start) | copy-done | bytes 3538968
  11.8 1.1 copy-done.5
  13.6 2.0 %collective-permute-start = (f32[3,16,512]{2,1,0:T(8,128)S(1)}, f32[3,16,512]{2,1,0:T(8,128)S(1)}, u32[]{:S(2)}, u32[]{:S(2)}) collective-permute-start(f32[3,16,512]{2,1,0:T(8,128)S(1)} %get-tuple-element.104), channel_id=1, source_target_pairs={{0,4},{4,0},{8,12},{12,8},{16,20},{20,16},{24,28},{28,24},{1,5},{5... | collective-permute-start | bytes 294920 | tf_op jit(solution)/shard_map/ppermute | solution.py:36
  15.5 3.6 %collective-permute-start.1 = (f32[3,16,512]{2,1,0:T(8,128)S(1)}, f32[3,16,512]{2,1,0:T(8,128)S(1)}, u32[]{:S(2)}, u32[]{:S(2)}) collective-permute-start(f32[3,16,512]{2,1,0:T(8,128)S(1)} %get-tuple-element.105), channel_id=1, source_target_pairs={{0,28},{4,8},{8,4},{12,16},{16,12},{20,24},{24,20},{28,0},{1,29},{... | collective-permute-start | bytes 294920 | tf_op jit(solution)/shard_map/ppermute | solution.py:36
  19.9 1.2 %shard_map.107 = (f32[4,256]{1,0:T(4,128)S(1)}, f32[4,256]{1,0:T(4,128)S(1)}, f32[4,256]{1,0:T(4,128)S(1)}, f32[4,256]{1,0:T(4,128)S(1)}) custom-call(bf16[4,4,256,256]{3,2,1,0:T(8,128)(2,1)S(1)} %get-tuple-element.110.first, bf16[4,4,256,256]{3,2,1,0:T(8,128)(2,1)S(1)} %get-tuple-element.111.second, f32[4,256]{1,0:T(4,128)S(1)} %get-tuple-element.106.refs_0_.refs_9_, ...), custom_call_target="tpu_custom_call" | custom-call | flops 5000000000 | bytes 4000000 | tf_op jit(solution)/shard_map/pallas_call | solution.py:21
  21.2 1.6 %collective-permute-start.6 = (f32[4,256]{1,0:T(4,128)S(1)}, f32[4,256]{1,0:T(4,128)S(1)}, u32[]{:S(2)}, u32[]{:S(2)}) collective-permute-start(f32[4,256]{1,0:T(4,128)S(1)} %get-tuple-element.114), channel_id=1, source_target_pairs={{0,2},{1,3},{2,0},{3,1},{4,6},{5,7},{6,4},{7,5},{8,10},{9,11},{10,... | collective-permute-start | bytes 12296 | tf_op jit(solution)/shard_map/ppermute | solution.py:442
  23.0 1.8 %collective-permute-done.6.refs_15_ = f32[4,256]{1,0:T(4,128)S(1)} collective-permute-done((f32[4,256]{1,0:T(4,128)S(1)}, f32[4,256]{1,0:T(4,128)S(1)}, u32[]{:S(2)}, u32[]{:S(2)}) %collective-permute-start.6) | collective-permute-done | bytes 4128 | tf_op jit(solution)/shard_map/ppermute | solution.py:442
  25.8 2.1 %shard_map.108 = (f32[3,2,16,512]{3,2,1,0:T(8,128)S(1)}, f32[4,256]{1,0:T(4,128)S(1)}, f32[8,512]{1,0:T(8,128)S(1)}, f32[4,256]{1,0:T(4,128)S(1)}, f32[8,512]{1,0:T(8,128)S(1)}) custom-call(f32[3,2,16,512]{3,2,1,0:T(8,128)S(1)} %get-tuple-element.99.refs_0_, f32[6,3,3,2,16,512]{5,4,3,2,1,0:T(8,128)S(1)} %copy-done.1, ...), custom_call_target="tpu_custom_call" | custom-call | flops 1000000000 | bytes 8000000 | tf_op jit(solution)/shard_map/pallas_call | solution.py:21
  28.5 1.6 %collective-permute-start.12 = (f32[8,512]{1,0:T(8,128)S(1)}, f32[8,512]{1,0:T(8,128)S(1)}, u32[]{:S(2)}, u32[]{:S(2)}) collective-permute-start(f32[8,512]{1,0:T(8,128)S(1)} %get-tuple-element.124), channel_id=1, source_target_pairs={{0,3},{1,2},{2,1},{3,0},{4,7},{5,6},{6,5},{7,4},{8,11},{9,10},{10,... | collective-permute-start | bytes 49160 | tf_op jit(solution)/shard_map/ppermute | solution.py:442
  30.6 1.9 %collective-permute-start.9 = (f32[3,16,512]{2,1,0:T(8,128)S(1)}, f32[3,16,512]{2,1,0:T(8,128)S(1)}, u32[]{:S(2)}, u32[]{:S(2)}) collective-permute-start(f32[3,16,512]{2,1,0:T(8,128)S(1)} %get-tuple-element.120), channel_id=1, source_target_pairs={{0,28},{4,8},{8,4},{12,16},{16,12},{20,24},{24,20},{28,0},{1,29},{... | collective-permute-start | bytes 294920 | tf_op jit(solution)/shard_map/ppermute | solution.py:36
  32.5 1.2 %shard_map.110 = (f32[4,256]{1,0:T(4,128)S(1)}, f32[4,256]{1,0:T(4,128)S(1)}, f32[4,256]{1,0:T(4,128)S(1)}, f32[4,256]{1,0:T(4,128)S(1)}) custom-call(bf16[4,4,256,256]{3,2,1,0:T(8,128)(2,1)S(1)} %get-tuple-element.110.first, bf16[4,4,256,256]{3,2,1,0:T(8,128)(2,1)S(1)} %get-tuple-element.111.second, f32[4,256]{1,0:T(4,128)S(1)} %get-tuple-element.121.refs_0_.refs_9_, ...), custom_call_target="tpu_custom_call" | custom-call | flops 5000000000 | bytes 4000000 | tf_op jit(solution)/shard_map/pallas_call | solution.py:21
  33.8 1.1 collective-permute-start.14
  35.7 1.8 %collective-permute-done.14.refs_15_ = f32[4,256]{1,0:T(4,128)S(1)} collective-permute-done((f32[4,256]{1,0:T(4,128)S(1)}, f32[4,256]{1,0:T(4,128)S(1)}, u32[]{:S(2)}, u32[]{:S(2)}) %collective-permute-start.14) | collective-permute-done | bytes 4128 | tf_op jit(solution)/shard_map/ppermute | solution.py:442
  38.1 2.2 %shard_map.111 = (f32[3,2,16,512]{3,2,1,0:T(8,128)S(1)}, f32[1,256]{1,0:T(1,128)S(1)}, f32[4,256]{1,0:T(4,128)S(1)}, f32[8,512]{1,0:T(8,128)S(1)}, f32[4,256]{1,0:T(4,128)S(1)}, /*index=5*/f32[8,512]{1,0:T(8,128)S(1)}) custom-call(f32[3,2,16,512]{3,2,1,0:T(8,128)S(1)} %get-tuple-element.118.refs_0_, f32[6,3,3,2,16,512]{5,4,3,2,1,0:T(8,128)S(1)} %copy-done.1, ...), custom_call_target="tpu_custom_call" | custom-call | flops 1000000000 | bytes 8000000 | tf_op jit(solution)/shard_map/pallas_call | solution.py:21
  41.4 1.1 collective-permute-start.17
  42.6 3.4 %collective-permute-done.19.refs_5_ = f32[1,256]{1,0:T(1,128)S(1)} collective-permute-done((f32[1,256]{1,0:T(1,128)S(1)}, f32[1,256]{1,0:T(1,128)S(1)}, u32[]{:S(2)}, u32[]{:S(2)}) %collective-permute-start.19) | collective-permute-done | bytes 1056 | tf_op jit(solution)/shard_map/ppermute | solution.py:448
  47.5 1.6 %collective-permute-start.23 = (f32[1,256]{1,0:T(1,128)S(1)}, f32[1,256]{1,0:T(1,128)S(1)}, u32[]{:S(2)}, u32[]{:S(2)}) collective-permute-start(f32[1,256]{1,0:T(1,128)S(1)} %get-tuple-element.138.refs_0_), channel_id=1, source_target_pairs={{0,16},{4,20},{8,24},{12,28},{16,0},{20,4},{24,8},{28,12},{1,17},{... | collective-permute-start | bytes 3080 | tf_op jit(solution)/shard_map/ppermute | solution.py:448
  49.1 1.9 %collective-permute-start.22 = (f32[1,256]{1,0:T(1,128)S(1)}, f32[1,256]{1,0:T(1,128)S(1)}, u32[]{:S(2)}, u32[]{:S(2)}) collective-permute-start(f32[1,256]{1,0:T(1,128)S(1)} %get-tuple-element.138.refs_0_), channel_id=1, source_target_pairs={{0,8},{4,12},{8,0},{12,4},{16,24},{20,28},{24,16},{28,20},{1,9},{5... | collective-permute-start | bytes 3080 | tf_op jit(solution)/shard_map/ppermute | solution.py:448
  51.1 2.3 %collective-permute-start.21 = (f32[3,16,512]{2,1,0:T(8,128)S(1)}, f32[3,16,512]{2,1,0:T(8,128)S(1)}, u32[]{:S(2)}, u32[]{:S(2)}) collective-permute-start(f32[3,16,512]{2,1,0:T(8,128)S(1)} %get-tuple-element.137), channel_id=1, source_target_pairs={{0,28},{4,8},{8,4},{12,16},{16,12},{20,24},{24,20},{28,0},{1,29},{... | collective-permute-start | bytes 294920 | tf_op jit(solution)/shard_map/ppermute | solution.py:36
  53.4 1.2 %shard_map.113 = (f32[5,256]{1,0:T(8,128)S(1)}, f32[5,256]{1,0:T(8,128)S(1)}, f32[5,256]{1,0:T(8,128)S(1)}, f32[5,256]{1,0:T(8,128)S(1)}) custom-call(bf16[4,4,256,256]{3,2,1,0:T(8,128)(2,1)S(1)} %get-tuple-element.110.first, bf16[4,4,256,256]{3,2,1,0:T(8,128)(2,1)S(1)} %get-tuple-element.111.second, f32[1,256]{1,0:T(1,128)S(1)} %get-tuple-element.138.refs_0_, ...), custom_call_target="tpu_custom_call" | custom-call | flops 5000000000 | bytes 4000000 | tf_op jit(solution)/shard_map/pallas_call | solution.py:21
  54.7 1.5 %collective-permute-start.26 = (f32[5,256]{1,0:T(8,128)S(1)}, f32[5,256]{1,0:T(8,128)S(1)}, u32[]{:S(2)}, u32[]{:S(2)}) collective-permute-start(f32[5,256]{1,0:T(8,128)S(1)} %get-tuple-element.141), channel_id=1, source_target_pairs={{0,2},{1,3},{2,0},{3,1},{4,6},{5,7},{6,4},{7,5},{8,10},{9,11},{10,... | collective-permute-start | bytes 15368 | tf_op jit(solution)/shard_map/ppermute | solution.py:442
  56.6 1.9 %collective-permute-done.26.refs_15_ = f32[5,256]{1,0:T(8,128)S(1)} collective-permute-done((f32[5,256]{1,0:T(8,128)S(1)}, f32[5,256]{1,0:T(8,128)S(1)}, u32[]{:S(2)}, u32[]{:S(2)}) %collective-permute-start.26) | collective-permute-done | bytes 5152 | tf_op jit(solution)/shard_map/ppermute | solution.py:442
  59.2 2.3 %shard_map.114 = (f32[3,2,16,512]{3,2,1,0:T(8,128)S(1)}, f32[3,2,16,512]{3,2,1,0:T(8,128)S(1)}, f32[3,2,16,512]{3,2,1,0:T(8,128)S(1)}, f32[3,2,16,512]{3,2,1,0:T...) custom-call(f32[3,2,16,512]{3,2,1,0:T(8,128)S(1)} %get-tuple-element, ...), custom_call_target="tpu_custom_call" | custom-call | flops 1000000000 | bytes 8000000 | tf_op jit(solution)/shard_map/pallas_call | solution.py:21
  62.3 1.5 %collective-permute-start.32 = (f32[8,512]{1,0:T(8,128)S(1)}, f32[8,512]{1,0:T(8,128)S(1)}, u32[]{:S(2)}, u32[]{:S(2)}) collective-permute-start(f32[8,512]{1,0:T(8,128)S(1)} %get-tuple-element.150), channel_id=1, source_target_pairs={{0,3},{1,2},{2,1},{3,0},{4,7},{5,6},{6,5},{7,4},{8,11},{9,10},{10,... | collective-permute-start | bytes 49160 | tf_op jit(solution)/shard_map/ppermute | solution.py:442
  64.8 1.9 %collective-permute-start.29 = (f32[3,16,512]{2,1,0:T(8,128)S(1)}, f32[3,16,512]{2,1,0:T(8,128)S(1)}, u32[]{:S(2)}, u32[]{:S(2)}) collective-permute-start(f32[3,16,512]{2,1,0:T(8,128)S(1)} %get-tuple-element.146), channel_id=1, source_target_pairs={{0,28},{4,8},{8,4},{12,16},{16,12},{20,24},{24,20},{28,0},{1,29},{... | collective-permute-start | bytes 294920 | tf_op jit(solution)/shard_map/ppermute | solution.py:36
  66.8 1.3 %shard_map.116 = (f32[4,256]{1,0:T(4,128)S(1)}, f32[4,256]{1,0:T(4,128)S(1)}, f32[4,256]{1,0:T(4,128)S(1)}, f32[4,256]{1,0:T(4,128)S(1)}) custom-call(bf16[4,4,256,256]{3,2,1,0:T(8,128)(2,1)S(1)} %get-tuple-element.110.first, bf16[4,4,256,256]{3,2,1,0:T(8,128)(2,1)S(1)} %get-tuple-element.111.second, f32[4,256]{1,0:T(4,128)S(1)} %get-tuple-element.147.refs_0_.refs_9_, ...), custom_call_target="tpu_custom_call" | custom-call | flops 5000000000 | bytes 4000000 | tf_op jit(solution)/shard_map/pallas_call | solution.py:21
  68.1 1.1 collective-permute-start.34
  70.0 1.8 %collective-permute-done.34.refs_15_ = f32[4,256]{1,0:T(4,128)S(1)} collective-permute-done((f32[4,256]{1,0:T(4,128)S(1)}, f32[4,256]{1,0:T(4,128)S(1)}, u32[]{:S(2)}, u32[]{:S(2)}) %collective-permute-start.34) | collective-permute-done | bytes 4128 | tf_op jit(solution)/shard_map/ppermute | solution.py:442
  72.3 2.3 %shard_map.117 = (f32[3,2,16,512]{3,2,1,0:T(8,128)S(1)}, f32[3,2,16,512]{3,2,1,0:T(8,128)S(1)}, f32[3,2,16,512]{3,2,1,0:T(8,128)S(1)}, f32[1,256]{1,0:T(1,128)S(...) custom-call(f32[3,2,16,512]{3,2,1,0:T(8,128)S(1)} %get-tuple-element.144.refs_0_,, ...), custom_call_target="tpu_custom_call" | custom-call | flops 1000000000 | bytes 8000000 | tf_op jit(solution)/shard_map/pallas_call | solution.py:21
  75.8 1.1 collective-permute-start.37
  76.9 3.5 %collective-permute-done.39.refs_5_ = f32[1,256]{1,0:T(1,128)S(1)} collective-permute-done((f32[1,256]{1,0:T(1,128)S(1)}, f32[1,256]{1,0:T(1,128)S(1)}, u32[]{:S(2)}, u32[]{:S(2)}) %collective-permute-start.39) | collective-permute-done | bytes 1056 | tf_op jit(solution)/shard_map/ppermute | solution.py:448
  80.9 1.1 collective-permute-start.44
  81.9 1.1 collective-permute-start.43
  83.0 2.3 %collective-permute-start.42 = (f32[1,256]{1,0:T(1,128)S(1)}, f32[1,256]{1,0:T(1,128)S(1)}, u32[]{:S(2)}, u32[]{:S(2)}) collective-permute-start(f32[1,256]{1,0:T(1,128)S(1)} %get-tuple-element.167.refs_0_), channel_id=1, source_target_pairs={{0,8},{4,12},{8,0},{12,4},{16,24},{20,28},{24,16},{28,20},{1,9},{5... | collective-permute-start | bytes 3080 | tf_op jit(solution)/shard_map/ppermute | solution.py:448
  85.3 2.4 %collective-permute-start.41 = (f32[3,16,512]{2,1,0:T(8,128)S(1)}, f32[3,16,512]{2,1,0:T(8,128)S(1)}, u32[]{:S(2)}, u32[]{:S(2)}) collective-permute-start(f32[3,16,512]{2,1,0:T(8,128)S(1)} %get-tuple-element.166), channel_id=1, source_target_pairs={{0,28},{4,8},{8,4},{12,16},{16,12},{20,24},{24,20},{28,0},{1,29},{... | collective-permute-start | bytes 294920 | tf_op jit(solution)/shard_map/ppermute | solution.py:36
  87.8 1.2 %shard_map.119 = (f32[5,256]{1,0:T(8,128)S(1)}, f32[5,256]{1,0:T(8,128)S(1)}, f32[5,256]{1,0:T(8,128)S(1)}, f32[5,256]{1,0:T(8,128)S(1)}) custom-call(bf16[4,4,256,256]{3,2,1,0:T(8,128)(2,1)S(1)} %get-tuple-element.110.first, bf16[4,4,256,256]{3,2,1,0:T(8,128)(2,1)S(1)} %get-tuple-element.111.second, f32[1,256]{1,0:T(1,128)S(1)} %get-tuple-element.167.refs_0_, ...), custom_call_target="tpu_custom_call" | custom-call | flops 5000000000 | bytes 4000000 | tf_op jit(solution)/shard_map/pallas_call | solution.py:21
  89.1 1.4 %collective-permute-start.46 = (f32[5,256]{1,0:T(8,128)S(1)}, f32[5,256]{1,0:T(8,128)S(1)}, u32[]{:S(2)}, u32[]{:S(2)}) collective-permute-start(f32[5,256]{1,0:T(8,128)S(1)} %get-tuple-element.170), channel_id=1, source_target_pairs={{0,2},{1,3},{2,0},{3,1},{4,6},{5,7},{6,4},{7,5},{8,10},{9,11},{10,... | collective-permute-start | bytes 15368 | tf_op jit(solution)/shard_map/ppermute | solution.py:442
  91.0 1.9 %collective-permute-done.46.refs_15_ = f32[5,256]{1,0:T(8,128)S(1)} collective-permute-done((f32[5,256]{1,0:T(8,128)S(1)}, f32[5,256]{1,0:T(8,128)S(1)}, u32[]{:S(2)}, u32[]{:S(2)}) %collective-permute-start.46) | collective-permute-done | bytes 5152 | tf_op jit(solution)/shard_map/ppermute | solution.py:442
  93.6 2.3 %shard_map.120 = (f32[3,2,16,512]{3,2,1,0:T(8,128)S(1)}, f32[3,2,16,512]{3,2,1,0:T(8,128)S(1)}, f32[3,2,16,512]{3,2,1,0:T(8,128)S(1)}, f32[3,2,16,512]{3,2,1,0:T...) custom-call(f32[3,2,16,512]{3,2,1,0:T(8,128)S(1)} %get-tuple-element, ...), custom_call_target="tpu_custom_call" | custom-call | flops 1000000000 | bytes 8000000 | tf_op jit(solution)/shard_map/pallas_call | solution.py:21
  96.6 1.4 %collective-permute-start.52 = (f32[8,512]{1,0:T(8,128)S(1)}, f32[8,512]{1,0:T(8,128)S(1)}, u32[]{:S(2)}, u32[]{:S(2)}) collective-permute-start(f32[8,512]{1,0:T(8,128)S(1)} %get-tuple-element.183), channel_id=1, source_target_pairs={{0,3},{1,2},{2,1},{3,0},{4,7},{5,6},{6,5},{7,4},{8,11},{9,10},{10,... | collective-permute-start | bytes 49160 | tf_op jit(solution)/shard_map/ppermute | solution.py:442
  99.2 1.9 %collective-permute-start.49 = (f32[3,16,512]{2,1,0:T(8,128)S(1)}, f32[3,16,512]{2,1,0:T(8,128)S(1)}, u32[]{:S(2)}, u32[]{:S(2)}) collective-permute-start(f32[3,16,512]{2,1,0:T(8,128)S(1)} %get-tuple-element.179), channel_id=1, source_target_pairs={{0,28},{4,8},{8,4},{12,16},{16,12},{20,24},{24,20},{28,0},{1,29},{... | collective-permute-start | bytes 294920 | tf_op jit(solution)/shard_map/ppermute | solution.py:36
  101.1 1.2 %shard_map.122 = (f32[4,256]{1,0:T(4,128)S(1)}, f32[4,256]{1,0:T(4,128)S(1)}, f32[4,256]{1,0:T(4,128)S(1)}, f32[4,256]{1,0:T(4,128)S(1)}) custom-call(bf16[4,4,256,256]{3,2,1,0:T(8,128)(2,1)S(1)} %get-tuple-element.110.first, bf16[4,4,256,256]{3,2,1,0:T(8,128)(2,1)S(1)} %get-tuple-element.111.second, f32[4,256]{1,0:T(4,128)S(1)} %get-tuple-element.180.refs_0_.refs_9_, ...), custom_call_target="tpu_custom_call" | custom-call | flops 5000000000 | bytes 4000000 | tf_op jit(solution)/shard_map/pallas_call | solution.py:21
  102.4 1.1 collective-permute-start.54
  104.3 1.8 %collective-permute-done.54.refs_15_ = f32[4,256]{1,0:T(4,128)S(1)} collective-permute-done((f32[4,256]{1,0:T(4,128)S(1)}, f32[4,256]{1,0:T(4,128)S(1)}, u32[]{:S(2)}, u32[]{:S(2)}) %collective-permute-start.54) | collective-permute-done | bytes 4128 | tf_op jit(solution)/shard_map/ppermute | solution.py:442
  106.6 2.4 %shard_map.123 = (f32[3,2,16,512]{3,2,1,0:T(8,128)}, f32[3,2,16,512]{3,2,1,0:T(8,128)S(1)}, f32[3,2,16,512]{3,2,1,0:T(8,128)S(1)}, f32[32,1,128]{2,1,0:T(1,128)S(1)}) custom-call(f32[3,2,16,512]{3,2,1,0:T(8,128)S(1)} %get-tuple-element.177.refs_0_, f32[6,3,3,2,16,512]{5,4,3,2,1,0:T(8,128)S(1)} %copy-done.1, ...), custom_call_target="tpu_custom_call" | custom-call | flops 1000000000 | bytes 8000000 | tf_op jit(solution)/shard_map/pallas_call | solution.py:21
  109.0 10.5 %all_to_all.5.sums = f32[32,1,128]{2,1,0:T(1,128)S(1)} all-to-all(f32[32,1,128]{2,1,0:T(1,128)S(1)} %get-tuple-element.191), channel_id=1, replica_groups=mesh['res'=8,'grp'=4] {'res','grp'}, dimensions={0} | all-to-all | bytes 32768 | tf_op jit(solution)/shard_map/all_to_all | solution.py:572
  (107 shorter events, 24.3 us)
Async XLA Ops:
  6.6 13.2 %collective-permute-start.3 = (f32[4,256]{1,0:T(4,128)S(1)}, f32[4,256]{1,0:T(4,128)S(1)}, u32[]{:S(2)}, u32[]{:S(2)}) collective-permute-start(f32[4,256]{1,0:T(4,128)S(1)} %get-tuple-element.108), channel_id=1, source_target_pairs={{0,2},{1,3},{2,0},{3,1},{4,6},{5,7},{6,4},{7,5},{8,10},{9,11},{10,... | collective-permute-start | bytes 12296 | tf_op jit(solution)/shard_map/ppermute | solution.py:442
  9.6 10.2 %collective-permute-start.2 = (f32[8,512]{1,0:T(8,128)S(1)}, f32[8,512]{1,0:T(8,128)S(1)}, u32[]{:S(2)}, u32[]{:S(2)}) collective-permute-start(f32[8,512]{1,0:T(8,128)S(1)} %get-tuple-element.107), channel_id=1, source_target_pairs={{0,1},{1,0},{2,3},{3,2},{4,5},{5,4},{6,7},{7,6},{8,9},{9,8},{10,11... | collective-permute-start | bytes 49160 | tf_op jit(solution)/shard_map/ppermute | solution.py:442
  9.6 10.2 %collective-permute-start.4 = (f32[8,512]{1,0:T(8,128)S(1)}, f32[8,512]{1,0:T(8,128)S(1)}, u32[]{:S(2)}, u32[]{:S(2)}) collective-permute-start(f32[8,512]{1,0:T(8,128)S(1)} %get-tuple-element.109), channel_id=1, source_target_pairs={{0,3},{1,2},{2,1},{3,0},{4,7},{5,6},{6,5},{7,4},{8,11},{9,10},{10,... | collective-permute-start | bytes 49160 | tf_op jit(solution)/shard_map/ppermute | solution.py:442
  13.6 12.2 %collective-permute-start = (f32[3,16,512]{2,1,0:T(8,128)S(1)}, f32[3,16,512]{2,1,0:T(8,128)S(1)}, u32[]{:S(2)}, u32[]{:S(2)}) collective-permute-start(f32[3,16,512]{2,1,0:T(8,128)S(1)} %get-tuple-element.104), channel_id=1, source_target_pairs={{0,4},{4,0},{8,12},{12,8},{16,20},{20,16},{24,28},{28,24},{1,5},{5... | collective-permute-start | bytes 294920 | tf_op jit(solution)/shard_map/ppermute | solution.py:36
  15.5 10.2 %collective-permute-start.1 = (f32[3,16,512]{2,1,0:T(8,128)S(1)}, f32[3,16,512]{2,1,0:T(8,128)S(1)}, u32[]{:S(2)}, u32[]{:S(2)}) collective-permute-start(f32[3,16,512]{2,1,0:T(8,128)S(1)} %get-tuple-element.105), channel_id=1, source_target_pairs={{0,28},{4,8},{8,4},{12,16},{16,12},{20,24},{24,20},{28,0},{1,29},{... | collective-permute-start | bytes 294920 | tf_op jit(solution)/shard_map/ppermute | solution.py:36
  21.2 3.7 %collective-permute-start.6 = (f32[4,256]{1,0:T(4,128)S(1)}, f32[4,256]{1,0:T(4,128)S(1)}, u32[]{:S(2)}, u32[]{:S(2)}) collective-permute-start(f32[4,256]{1,0:T(4,128)S(1)} %get-tuple-element.114), channel_id=1, source_target_pairs={{0,2},{1,3},{2,0},{3,1},{4,6},{5,7},{6,4},{7,5},{8,10},{9,11},{10,... | collective-permute-start | bytes 12296 | tf_op jit(solution)/shard_map/ppermute | solution.py:442
  22.8 3.0 %collective-permute-start.7 = (f32[4,256]{1,0:T(4,128)S(1)}, f32[4,256]{1,0:T(4,128)S(1)}, u32[]{:S(2)}, u32[]{:S(2)}) collective-permute-start(f32[4,256]{1,0:T(4,128)S(1)} %get-tuple-element.115), channel_id=1, source_target_pairs={{0,3},{1,2},{2,1},{3,0},{4,7},{5,6},{6,5},{7,4},{8,11},{9,10},{10,... | collective-permute-start | bytes 12296 | tf_op jit(solution)/shard_map/ppermute | solution.py:442
  27.9 4.6 %collective-permute-start.11 = (f32[4,256]{1,0:T(4,128)S(1)}, f32[4,256]{1,0:T(4,128)S(1)}, u32[]{:S(2)}, u32[]{:S(2)}) collective-permute-start(f32[4,256]{1,0:T(4,128)S(1)} %get-tuple-element.123), channel_id=1, source_target_pairs={{0,2},{1,3},{2,0},{3,1},{4,6},{5,7},{6,4},{7,5},{8,10},{9,11},{10,... | collective-permute-start | bytes 12296 | tf_op jit(solution)/shard_map/ppermute | solution.py:442
  28.5 4.0 %collective-permute-start.10 = (f32[8,512]{1,0:T(8,128)S(1)}, f32[8,512]{1,0:T(8,128)S(1)}, u32[]{:S(2)}, u32[]{:S(2)}) collective-permute-start(f32[8,512]{1,0:T(8,128)S(1)} %get-tuple-element.122), channel_id=1, source_target_pairs={{0,1},{1,0},{2,3},{3,2},{4,5},{5,4},{6,7},{7,6},{8,9},{9,8},{10,11... | collective-permute-start | bytes 49160 | tf_op jit(solution)/shard_map/ppermute | solution.py:442
  28.5 4.0 %collective-permute-start.12 = (f32[8,512]{1,0:T(8,128)S(1)}, f32[8,512]{1,0:T(8,128)S(1)}, u32[]{:S(2)}, u32[]{:S(2)}) collective-permute-start(f32[8,512]{1,0:T(8,128)S(1)} %get-tuple-element.124), channel_id=1, source_target_pairs={{0,3},{1,2},{2,1},{3,0},{4,7},{5,6},{6,5},{7,4},{8,11},{9,10},{10,... | collective-permute-start | bytes 49160 | tf_op jit(solution)/shard_map/ppermute | solution.py:442
  30.5 7.5 %collective-permute-start.8 = (f32[3,16,512]{2,1,0:T(8,128)S(1)}, f32[3,16,512]{2,1,0:T(8,128)S(1)}, u32[]{:S(2)}, u32[]{:S(2)}) collective-permute-start(f32[3,16,512]{2,1,0:T(8,128)S(1)} %get-tuple-element.119), channel_id=1, source_target_pairs={{0,4},{4,0},{8,12},{12,8},{16,20},{20,16},{24,28},{28,24},{1,5},{5... | collective-permute-start | bytes 294920 | tf_op jit(solution)/shard_map/ppermute | solution.py:36
  30.6 7.5 %collective-permute-start.9 = (f32[3,16,512]{2,1,0:T(8,128)S(1)}, f32[3,16,512]{2,1,0:T(8,128)S(1)}, u32[]{:S(2)}, u32[]{:S(2)}) collective-permute-start(f32[3,16,512]{2,1,0:T(8,128)S(1)} %get-tuple-element.120), channel_id=1, source_target_pairs={{0,28},{4,8},{8,4},{12,16},{16,12},{20,24},{24,20},{28,0},{1,29},{... | collective-permute-start | bytes 294920 | tf_op jit(solution)/shard_map/ppermute | solution.py:36
  33.8 3.7 %collective-permute-start.14 = (f32[4,256]{1,0:T(4,128)S(1)}, f32[4,256]{1,0:T(4,128)S(1)}, u32[]{:S(2)}, u32[]{:S(2)}) collective-permute-start(f32[4,256]{1,0:T(4,128)S(1)} %get-tuple-element.127), channel_id=1, source_target_pairs={{0,2},{1,3},{2,0},{3,1},{4,6},{5,7},{6,4},{7,5},{8,10},{9,11},{10,... | collective-permute-start | bytes 12296 | tf_op jit(solution)/shard_map/ppermute | solution.py:442
  34.9 3.1 %collective-permute-start.15 = (f32[4,256]{1,0:T(4,128)S(1)}, f32[4,256]{1,0:T(4,128)S(1)}, u32[]{:S(2)}, u32[]{:S(2)}) collective-permute-start(f32[4,256]{1,0:T(4,128)S(1)} %get-tuple-element.128), channel_id=1, source_target_pairs={{0,3},{1,2},{2,1},{3,0},{4,7},{5,6},{6,5},{7,4},{8,11},{9,10},{10,... | collective-permute-start | bytes 12296 | tf_op jit(solution)/shard_map/ppermute | solution.py:442
  40.3 5.8 %collective-permute-start.16 = (f32[8,512]{1,0:T(8,128)S(1)}, f32[8,512]{1,0:T(8,128)S(1)}, u32[]{:S(2)}, u32[]{:S(2)}) collective-permute-start(f32[8,512]{1,0:T(8,128)S(1)} %get-tuple-element.131), channel_id=1, source_target_pairs={{0,1},{1,0},{2,3},{3,2},{4,5},{5,4},{6,7},{7,6},{8,9},{9,8},{10,11... | collective-permute-start | bytes 49160 | tf_op jit(solution)/shard_map/ppermute | solution.py:442
  40.4 5.7 %collective-permute-start.18 = (f32[8,512]{1,0:T(8,128)S(1)}, f32[8,512]{1,0:T(8,128)S(1)}, u32[]{:S(2)}, u32[]{:S(2)}) collective-permute-start(f32[8,512]{1,0:T(8,128)S(1)} %get-tuple-element.133), channel_id=1, source_target_pairs={{0,3},{1,2},{2,1},{3,0},{4,7},{5,6},{6,5},{7,4},{8,11},{9,10},{10,... | collective-permute-start | bytes 49160 | tf_op jit(solution)/shard_map/ppermute | solution.py:442
  41.4 4.7 %collective-permute-start.17 = (f32[4,256]{1,0:T(4,128)S(1)}, f32[4,256]{1,0:T(4,128)S(1)}, u32[]{:S(2)}, u32[]{:S(2)}) collective-permute-start(f32[4,256]{1,0:T(4,128)S(1)} %get-tuple-element.132), channel_id=1, source_target_pairs={{0,2},{1,3},{2,0},{3,1},{4,6},{5,7},{6,4},{7,5},{8,10},{9,11},{10,... | collective-permute-start | bytes 12296 | tf_op jit(solution)/shard_map/ppermute | solution.py:442
  42.5 3.6 %collective-permute-start.19 = (f32[1,256]{1,0:T(1,128)S(1)}, f32[1,256]{1,0:T(1,128)S(1)}, u32[]{:S(2)}, u32[]{:S(2)}) collective-permute-start(f32[1,256]{1,0:T(1,128)S(1)} %get-tuple-element.134.refs_4_), channel_id=1, source_target_pairs={{0,4},{4,0},{8,12},{12,8},{16,20},{20,16},{24,28},{28,24},{1,5},{5... | collective-permute-start | bytes 3080 | tf_op jit(solution)/shard_map/ppermute | solution.py:448
  46.5 6.8 %collective-permute-start.24 = (f32[1,256]{1,0:T(1,128)S(1)}, f32[1,256]{1,0:T(1,128)S(1)}, u32[]{:S(2)}, u32[]{:S(2)}) collective-permute-start(f32[1,256]{1,0:T(1,128)S(1)} %get-tuple-element.138.refs_0_), channel_id=1, source_target_pairs={{0,24},{4,28},{8,16},{12,20},{16,8},{20,12},{24,0},{28,4},{1,25},{... | collective-permute-start | bytes 3080 | tf_op jit(solution)/shard_map/ppermute | solution.py:448
  47.5 5.9 %collective-permute-start.23 = (f32[1,256]{1,0:T(1,128)S(1)}, f32[1,256]{1,0:T(1,128)S(1)}, u32[]{:S(2)}, u32[]{:S(2)}) collective-permute-start(f32[1,256]{1,0:T(1,128)S(1)} %get-tuple-element.138.refs_0_), channel_id=1, source_target_pairs={{0,16},{4,20},{8,24},{12,28},{16,0},{20,4},{24,8},{28,12},{1,17},{... | collective-permute-start | bytes 3080 | tf_op jit(solution)/shard_map/ppermute | solution.py:448
  49.1 4.2 %collective-permute-start.22 = (f32[1,256]{1,0:T(1,128)S(1)}, f32[1,256]{1,0:T(1,128)S(1)}, u32[]{:S(2)}, u32[]{:S(2)}) collective-permute-start(f32[1,256]{1,0:T(1,128)S(1)} %get-tuple-element.138.refs_0_), channel_id=1, source_target_pairs={{0,8},{4,12},{8,0},{12,4},{16,24},{20,28},{24,16},{28,20},{1,9},{5... | collective-permute-start | bytes 3080 | tf_op jit(solution)/shard_map/ppermute | solution.py:448
  51.0 8.3 %collective-permute-start.20 = (f32[3,16,512]{2,1,0:T(8,128)S(1)}, f32[3,16,512]{2,1,0:T(8,128)S(1)}, u32[]{:S(2)}, u32[]{:S(2)}) collective-permute-start(f32[3,16,512]{2,1,0:T(8,128)S(1)} %get-tuple-element.136), channel_id=1, source_target_pairs={{0,4},{4,0},{8,12},{12,8},{16,20},{20,16},{24,28},{28,24},{1,5},{5... | collective-permute-start | bytes 294920 | tf_op jit(solution)/shard_map/ppermute | solution.py:36
  51.1 8.1 %collective-permute-start.21 = (f32[3,16,512]{2,1,0:T(8,128)S(1)}, f32[3,16,512]{2,1,0:T(8,128)S(1)}, u32[]{:S(2)}, u32[]{:S(2)}) collective-permute-start(f32[3,16,512]{2,1,0:T(8,128)S(1)} %get-tuple-element.137), channel_id=1, source_target_pairs={{0,28},{4,8},{8,4},{12,16},{16,12},{20,24},{24,20},{28,0},{1,29},{... | collective-permute-start | bytes 294920 | tf_op jit(solution)/shard_map/ppermute | solution.py:36
  54.7 3.7 %collective-permute-start.26 = (f32[5,256]{1,0:T(8,128)S(1)}, f32[5,256]{1,0:T(8,128)S(1)}, u32[]{:S(2)}, u32[]{:S(2)}) collective-permute-start(f32[5,256]{1,0:T(8,128)S(1)} %get-tuple-element.141), channel_id=1, source_target_pairs={{0,2},{1,3},{2,0},{3,1},{4,6},{5,7},{6,4},{7,5},{8,10},{9,11},{10,... | collective-permute-start | bytes 15368 | tf_op jit(solution)/shard_map/ppermute | solution.py:442
  56.2 3.1 %collective-permute-start.27 = (f32[5,256]{1,0:T(8,128)S(1)}, f32[5,256]{1,0:T(8,128)S(1)}, u32[]{:S(2)}, u32[]{:S(2)}) collective-permute-start(f32[5,256]{1,0:T(8,128)S(1)} %get-tuple-element.142), channel_id=1, source_target_pairs={{0,3},{1,2},{2,1},{3,0},{4,7},{5,6},{6,5},{7,4},{8,11},{9,10},{10,... | collective-permute-start | bytes 15368 | tf_op jit(solution)/shard_map/ppermute | solution.py:442
  61.5 5.2 %collective-permute-start.31 = (f32[4,256]{1,0:T(4,128)S(1)}, f32[4,256]{1,0:T(4,128)S(1)}, u32[]{:S(2)}, u32[]{:S(2)}) collective-permute-start(f32[4,256]{1,0:T(4,128)S(1)} %get-tuple-element.149), channel_id=1, source_target_pairs={{0,2},{1,3},{2,0},{3,1},{4,6},{5,7},{6,4},{7,5},{8,10},{9,11},{10,... | collective-permute-start | bytes 12296 | tf_op jit(solution)/shard_map/ppermute | solution.py:442
  62.3 4.5 %collective-permute-start.30 = (f32[8,512]{1,0:T(8,128)S(1)}, f32[8,512]{1,0:T(8,128)S(1)}, u32[]{:S(2)}, u32[]{:S(2)}) collective-permute-start(f32[8,512]{1,0:T(8,128)S(1)} %get-tuple-element.148), channel_id=1, source_target_pairs={{0,1},{1,0},{2,3},{3,2},{4,5},{5,4},{6,7},{7,6},{8,9},{9,8},{10,11... | collective-permute-start | bytes 49160 | tf_op jit(solution)/shard_map/ppermute | solution.py:442
  62.3 4.5 %collective-permute-start.32 = (f32[8,512]{1,0:T(8,128)S(1)}, f32[8,512]{1,0:T(8,128)S(1)}, u32[]{:S(2)}, u32[]{:S(2)}) collective-permute-start(f32[8,512]{1,0:T(8,128)S(1)} %get-tuple-element.150), channel_id=1, source_target_pairs={{0,3},{1,2},{2,1},{3,0},{4,7},{5,6},{6,5},{7,4},{8,11},{9,10},{10,... | collective-permute-start | bytes 49160 | tf_op jit(solution)/shard_map/ppermute | solution.py:442
  64.2 8.1 %collective-permute-start.28 = (f32[3,16,512]{2,1,0:T(8,128)S(1)}, f32[3,16,512]{2,1,0:T(8,128)S(1)}, u32[]{:S(2)}, u32[]{:S(2)}) collective-permute-start(f32[3,16,512]{2,1,0:T(8,128)S(1)} %get-tuple-element.145), channel_id=1, source_target_pairs={{0,4},{4,0},{8,12},{12,8},{16,20},{20,16},{24,28},{28,24},{1,5},{5... | collective-permute-start | bytes 294920 | tf_op jit(solution)/shard_map/ppermute | solution.py:36
  64.8 7.5 %collective-permute-start.29 = (f32[3,16,512]{2,1,0:T(8,128)S(1)}, f32[3,16,512]{2,1,0:T(8,128)S(1)}, u32[]{:S(2)}, u32[]{:S(2)}) collective-permute-start(f32[3,16,512]{2,1,0:T(8,128)S(1)} %get-tuple-element.146), channel_id=1, source_target_pairs={{0,28},{4,8},{8,4},{12,16},{16,12},{20,24},{24,20},{28,0},{1,29},{... | collective-permute-start | bytes 294920 | tf_op jit(solution)/shard_map/ppermute | solution.py:36
  68.1 3.7 %collective-permute-start.34 = (f32[4,256]{1,0:T(4,128)S(1)}, f32[4,256]{1,0:T(4,128)S(1)}, u32[]{:S(2)}, u32[]{:S(2)}) collective-permute-start(f32[4,256]{1,0:T(4,128)S(1)} %get-tuple-element.153), channel_id=1, source_target_pairs={{0,2},{1,3},{2,0},{3,1},{4,6},{5,7},{6,4},{7,5},{8,10},{9,11},{10,... | collective-permute-start | bytes 12296 | tf_op jit(solution)/shard_map/ppermute | solution.py:442
  74.6 5.8 %collective-permute-start.36 = (f32[8,512]{1,0:T(8,128)S(1)}, f32[8,512]{1,0:T(8,128)S(1)}, u32[]{:S(2)}, u32[]{:S(2)}) collective-permute-start(f32[8,512]{1,0:T(8,128)S(1)} %get-tuple-element.160), channel_id=1, source_target_pairs={{0,1},{1,0},{2,3},{3,2},{4,5},{5,4},{6,7},{7,6},{8,9},{9,8},{10,11... | collective-permute-start | bytes 49160 | tf_op jit(solution)/shard_map/ppermute | solution.py:442
  74.8 5.6 %collective-permute-start.38 = (f32[8,512]{1,0:T(8,128)S(1)}, f32[8,512]{1,0:T(8,128)S(1)}, u32[]{:S(2)}, u32[]{:S(2)}) collective-permute-start(f32[8,512]{1,0:T(8,128)S(1)} %get-tuple-element.162), channel_id=1, source_target_pairs={{0,3},{1,2},{2,1},{3,0},{4,7},{5,6},{6,5},{7,4},{8,11},{9,10},{10,... | collective-permute-start | bytes 49160 | tf_op jit(solution)/shard_map/ppermute | solution.py:442
  75.8 4.6 %collective-permute-start.37 = (f32[4,256]{1,0:T(4,128)S(1)}, f32[4,256]{1,0:T(4,128)S(1)}, u32[]{:S(2)}, u32[]{:S(2)}) collective-permute-start(f32[4,256]{1,0:T(4,128)S(1)} %get-tuple-element.161), channel_id=1, source_target_pairs={{0,2},{1,3},{2,0},{3,1},{4,6},{5,7},{6,4},{7,5},{8,10},{9,11},{10,... | collective-permute-start | bytes 12296 | tf_op jit(solution)/shard_map/ppermute | solution.py:442
  76.8 3.6 %collective-permute-start.39 = (f32[1,256]{1,0:T(1,128)S(1)}, f32[1,256]{1,0:T(1,128)S(1)}, u32[]{:S(2)}, u32[]{:S(2)}) collective-permute-start(f32[1,256]{1,0:T(1,128)S(1)} %get-tuple-element.163.refs_4_), channel_id=1, source_target_pairs={{0,4},{4,0},{8,12},{12,8},{16,20},{20,16},{24,28},{28,24},{1,5},{5... | collective-permute-start | bytes 3080 | tf_op jit(solution)/shard_map/ppermute | solution.py:448
  80.9 6.9 %collective-permute-start.44 = (f32[1,256]{1,0:T(1,128)S(1)}, f32[1,256]{1,0:T(1,128)S(1)}, u32[]{:S(2)}, u32[]{:S(2)}) collective-permute-start(f32[1,256]{1,0:T(1,128)S(1)} %get-tuple-element.167.refs_0_), channel_id=1, source_target_pairs={{0,24},{4,28},{8,16},{12,20},{16,8},{20,12},{24,0},{28,4},{1,25},{... | collective-permute-start | bytes 3080 | tf_op jit(solution)/shard_map/ppermute | solution.py:448
  81.9 5.9 %collective-permute-start.43 = (f32[1,256]{1,0:T(1,128)S(1)}, f32[1,256]{1,0:T(1,128)S(1)}, u32[]{:S(2)}, u32[]{:S(2)}) collective-permute-start(f32[1,256]{1,0:T(1,128)S(1)} %get-tuple-element.167.refs_0_), channel_id=1, source_target_pairs={{0,16},{4,20},{8,24},{12,28},{16,0},{20,4},{24,8},{28,12},{1,17},{... | collective-permute-start | bytes 3080 | tf_op jit(solution)/shard_map/ppermute | solution.py:448
  83.0 4.8 %collective-permute-start.42 = (f32[1,256]{1,0:T(1,128)S(1)}, f32[1,256]{1,0:T(1,128)S(1)}, u32[]{:S(2)}, u32[]{:S(2)}) collective-permute-start(f32[1,256]{1,0:T(1,128)S(1)} %get-tuple-element.167.refs_0_), channel_id=1, source_target_pairs={{0,8},{4,12},{8,0},{12,4},{16,24},{20,28},{24,16},{28,20},{1,9},{5... | collective-permute-start | bytes 3080 | tf_op jit(solution)/shard_map/ppermute | solution.py:448
  85.3 8.3 %collective-permute-start.40 = (f32[3,16,512]{2,1,0:T(8,128)S(1)}, f32[3,16,512]{2,1,0:T(8,128)S(1)}, u32[]{:S(2)}, u32[]{:S(2)}) collective-permute-start(f32[3,16,512]{2,1,0:T(8,128)S(1)} %get-tuple-element.165), channel_id=1, source_target_pairs={{0,4},{4,0},{8,12},{12,8},{16,20},{20,16},{24,28},{28,24},{1,5},{5... | collective-permute-start | bytes 294920 | tf_op jit(solution)/shard_map/ppermute | solution.py:36
  85.3 8.2 %collective-permute-start.41 = (f32[3,16,512]{2,1,0:T(8,128)S(1)}, f32[3,16,512]{2,1,0:T(8,128)S(1)}, u32[]{:S(2)}, u32[]{:S(2)}) collective-permute-start(f32[3,16,512]{2,1,0:T(8,128)S(1)} %get-tuple-element.166), channel_id=1, source_target_pairs={{0,28},{4,8},{8,4},{12,16},{16,12},{20,24},{24,20},{28,0},{1,29},{... | collective-permute-start | bytes 294920 | tf_op jit(solution)/shard_map/ppermute | solution.py:36
  89.1 3.7 %collective-permute-start.46 = (f32[5,256]{1,0:T(8,128)S(1)}, f32[5,256]{1,0:T(8,128)S(1)}, u32[]{:S(2)}, u32[]{:S(2)}) collective-permute-start(f32[5,256]{1,0:T(8,128)S(1)} %get-tuple-element.170), channel_id=1, source_target_pairs={{0,2},{1,3},{2,0},{3,1},{4,6},{5,7},{6,4},{7,5},{8,10},{9,11},{10,... | collective-permute-start | bytes 15368 | tf_op jit(solution)/shard_map/ppermute | solution.py:442
  90.5 3.1 %collective-permute-start.47 = (f32[5,256]{1,0:T(8,128)S(1)}, f32[5,256]{1,0:T(8,128)S(1)}, u32[]{:S(2)}, u32[]{:S(2)}) collective-permute-start(f32[5,256]{1,0:T(8,128)S(1)} %get-tuple-element.171), channel_id=1, source_target_pairs={{0,3},{1,2},{2,1},{3,0},{4,7},{5,6},{6,5},{7,4},{8,11},{9,10},{10,... | collective-permute-start | bytes 15368 | tf_op jit(solution)/shard_map/ppermute | solution.py:442
  95.9 5.2 %collective-permute-start.51 = (f32[4,256]{1,0:T(4,128)S(1)}, f32[4,256]{1,0:T(4,128)S(1)}, u32[]{:S(2)}, u32[]{:S(2)}) collective-permute-start(f32[4,256]{1,0:T(4,128)S(1)} %get-tuple-element.182), channel_id=1, source_target_pairs={{0,2},{1,3},{2,0},{3,1},{4,6},{5,7},{6,4},{7,5},{8,10},{9,11},{10,... | collective-permute-start | bytes 12296 | tf_op jit(solution)/shard_map/ppermute | solution.py:442
  96.6 4.5 %collective-permute-start.50 = (f32[8,512]{1,0:T(8,128)S(1)}, f32[8,512]{1,0:T(8,128)S(1)}, u32[]{:S(2)}, u32[]{:S(2)}) collective-permute-start(f32[8,512]{1,0:T(8,128)S(1)} %get-tuple-element.181), channel_id=1, source_target_pairs={{0,1},{1,0},{2,3},{3,2},{4,5},{5,4},{6,7},{7,6},{8,9},{9,8},{10,11... | collective-permute-start | bytes 49160 | tf_op jit(solution)/shard_map/ppermute | solution.py:442
  96.6 4.5 %collective-permute-start.52 = (f32[8,512]{1,0:T(8,128)S(1)}, f32[8,512]{1,0:T(8,128)S(1)}, u32[]{:S(2)}, u32[]{:S(2)}) collective-permute-start(f32[8,512]{1,0:T(8,128)S(1)} %get-tuple-element.183), channel_id=1, source_target_pairs={{0,3},{1,2},{2,1},{3,0},{4,7},{5,6},{6,5},{7,4},{8,11},{9,10},{10,... | collective-permute-start | bytes 49160 | tf_op jit(solution)/shard_map/ppermute | solution.py:442
  98.5 8.1 %collective-permute-start.48 = (f32[3,16,512]{2,1,0:T(8,128)S(1)}, f32[3,16,512]{2,1,0:T(8,128)S(1)}, u32[]{:S(2)}, u32[]{:S(2)}) collective-permute-start(f32[3,16,512]{2,1,0:T(8,128)S(1)} %get-tuple-element.178), channel_id=1, source_target_pairs={{0,4},{4,0},{8,12},{12,8},{16,20},{20,16},{24,28},{28,24},{1,5},{5... | collective-permute-start | bytes 294920 | tf_op jit(solution)/shard_map/ppermute | solution.py:36
  99.2 7.4 %collective-permute-start.49 = (f32[3,16,512]{2,1,0:T(8,128)S(1)}, f32[3,16,512]{2,1,0:T(8,128)S(1)}, u32[]{:S(2)}, u32[]{:S(2)}) collective-permute-start(f32[3,16,512]{2,1,0:T(8,128)S(1)} %get-tuple-element.179), channel_id=1, source_target_pairs={{0,28},{4,8},{8,4},{12,16},{16,12},{20,24},{24,20},{28,0},{1,29},{... | collective-permute-start | bytes 294920 | tf_op jit(solution)/shard_map/ppermute | solution.py:36
  102.4 3.7 %collective-permute-start.54 = (f32[4,256]{1,0:T(4,128)S(1)}, f32[4,256]{1,0:T(4,128)S(1)}, u32[]{:S(2)}, u32[]{:S(2)}) collective-permute-start(f32[4,256]{1,0:T(4,128)S(1)} %get-tuple-element.186), channel_id=1, source_target_pairs={{0,2},{1,3},{2,0},{3,1},{4,6},{5,7},{6,4},{7,5},{8,10},{9,11},{10,... | collective-permute-start | bytes 12296 | tf_op jit(solution)/shard_map/ppermute | solution.py:442
  (18 other events, 42.3 us)

commit v4 on v3

--- a/solution.py
+++ b/solution.py
@@ -13,18 +13,21 @@
 VMEM = pl.BlockSpec(memory_space=pltpu.VMEM)
 SMEM = pl.BlockSpec(memory_space=pltpu.SMEM)
 LIMIT = 20 * 1024 * 1024
+START_LIMIT = 60 * 1024 * 1024
 SOLVE_FLOPS = 5_000_000_000
 NAMES = ("br", "bs", "bw", "bz", "rw", "rz", "sw", "sz", "ww", "wz", "zz")
 
 
-def call(kernel, outs, args, specs=None, scratch=(), flops=1_000_000, moved=1_000_000):
+def call(
+    kernel, outs, args, specs=None, scratch=(), flops=1_000_000, moved=1_000_000, limit=LIMIT
+):
     return pl.pallas_call(
         kernel,
         out_shape=[jax.ShapeDtypeStruct(shape, dtype) for shape, dtype in outs],
         in_specs=specs or [VMEM] * len(args),
         out_specs=[VMEM] * len(outs),
         scratch_shapes=list(scratch),
-        compiler_params=pltpu.CompilerParams(vmem_limit_bytes=LIMIT),
+        compiler_params=pltpu.CompilerParams(vmem_limit_bytes=limit),
         cost_estimate=pl.CostEstimate(flops=flops, bytes_accessed=moved, transcendentals=0),
     )(*args)
 
@@ -171,19 +174,13 @@
     return dot(jnp.concatenate([high, low], axis=0), place[:, part], True)
 
 
-def stencil_kernel(after, with_sums, vec, trans, diag, *refs):
-    refs = refs[after:]
-    if with_sums:
-        row, other, *refs = refs
-        refs, total = (*refs[:2], *refs[3:]), refs[2]
-        total[...] = row[...] + other[...]
+def stencil_kernel(vec, trans, diag, *refs):
     *faces, out, shifted = refs
     write_faces(Planes(vec), faces)
     inner_stencil(vec, trans, diag, shifted, out)
 
 
-def first_stencil_kernel(vec, trans, acc, face0, face1, out, diag, shifted):
-    write_faces(Planes(vec), (face0, face1))
+def first_stencil_kernel(vec, trans, acc, after, out, diag, shifted):
     for i in range(acc.shape[0]):
         for j in range(acc.shape[1]):
             total = acc[i, j]
@@ -197,11 +194,31 @@
     return k > 0 and k & (k + 1) == 0
 
 
-def message_shapes(groups, capacity, segb, lines, cells_z):
-    rows = -(-capacity // (cells_z // segb))
-    return [
-        (rows + lines, cells_z) if carries_face(k) else (capacity, segb) for k in range(groups)
-    ]
+def coupled_rows(k, capacity, segb, cells_z):
+    return -(-capacity // (cells_z // segb)) if carries_face(k) else capacity
+
+
+def message_shapes(groups, capacity, segb, lines, cells_z, with_sums):
+    out = []
+    for k in range(groups):
+        rows = coupled_rows(k, capacity, segb, cells_z) + with_sums
+        out.append((rows + lines, cells_z) if carries_face(k) else (rows, segb))
+    return out
+
+
+def share(count, groups):
+    return -(-count // groups)
+
+
+def share_swap(row, q):
+    count, groups = lax.axis_size("res"), lax.axis_size("grp")
+    pairs = []
+    for r in range(count):
+        for g in range(groups):
+            mask = g * share(count, groups) + q
+            mask = mask if 0 < mask < count else 1
+            pairs.append((r * groups + g, (r ^ mask) * groups + g))
+    return lax.ppermute(row, ("res", "grp"), pairs)
 
 
 def spot(message, slot, segb):
@@ -214,15 +231,15 @@
     g = lax.axis_index("grp")
     out = []
     for b in range(wells):
-        mine = owner[b, 0]
+        mine = owner[b]
         slot = jnp.int32(0)
         for c in range(b):
-            slot = slot + (owner[c, 0] == mine).astype(jnp.int32)
+            slot = slot + (owner[c] == mine).astype(jnp.int32)
         out.append(jnp.bitwise_xor(g, mine) * capacity + slot)
     return out
 
 
-def write_messages(vec, place, column, take, owner, capacity, messages):
+def write_messages(vec, place, column, take, owner, capacity, messages, sums=None):
     components, cells_x, cells_y, cells_z = vec.shape
     wells, segb = column.shape
     high, low = halves(vec[...].reshape(components * cells_x * cells_y, cells_z))
@@ -237,6 +254,9 @@
             block = jnp.where(slots == where[b] - k * capacity, coupled[b], block)
         for slot in range(capacity):
             message[spot(message, slot, segb)] = block[slot : slot + 1]
+        if sums is not None:
+            row = coupled_rows(k, capacity, segb, cells_z)
+            message[row : row + 1, 0:segb] = sums
         if carries_face(k):
             above = jnp.bitwise_xor(g, k) > g
             start = message.shape[0] - components * cells_x
@@ -249,8 +269,8 @@
                     )
 
 
-def solve_kernel(parts, groups, first, second, *refs):
-    sums, sent, back = refs[:parts], refs[parts : parts + groups], refs[parts + groups :]
+def solve_kernel(groups, first, second, *refs):
+    sent, back = refs[:groups], refs[groups:]
     g = lax.axis_index("grp")
     capacity, segb = first.shape[1], first.shape[2]
     for k in range(groups):
@@ -258,12 +278,29 @@
         for slot in range(capacity):
             coupled = sent[k][spot(sent[k], slot, segb)]
             back[k][slot : slot + 1] = solve_well(coupled, first[home, slot], second[home, slot])
-    if parts:
-        total = sums[0][...]
-        for ref in sums[1:]:
-            total = total + ref[...]
-        for k in range(groups):
-            back[k][capacity : capacity + 1] = total
+
+
+def group_sum_kernel(capacity, *refs):
+    *messages, out = refs
+    segb = out.shape[1]
+    total = jnp.zeros(out.shape, F32)
+    for k, message in enumerate(messages):
+        row = coupled_rows(k, capacity, segb, max(m.shape[1] for m in messages))
+        total = total + message[row : row + 1, 0:segb]
+    out[...] = total
+
+
+def append_kernel(groups, mine, *refs):
+    values, fetched, outs = refs[:groups], refs[groups:-groups], refs[-groups:]
+    count, g = lax.axis_size("res"), lax.axis_index("grp")
+    row = jnp.where(g == 0, mine[...], 0.0)
+    for q, ref in enumerate(fetched):
+        mask = g * len(fetched) + q
+        row = row + jnp.where((mask > 0) & (mask < count), ref[...], 0.0)
+    capacity = values[0].shape[0]
+    for value, out in zip(values, outs):
+        out[0:capacity] = value[...]
+        out[capacity : capacity + 1] = row
 
 
 def well_terms(values, place, column, give, owner, capacity, shape):
@@ -284,9 +321,20 @@
     return (total[:rows] + total[rows:]).reshape(shape)
 
 
-def start_kernel(groups, capacity, vec, completion, live, owner, take, give, place, column, take_out, give_out, *sends):
+def start_kernel(groups, capacity, *refs):
+    given, (place, column, take_out, give_out, *sends) = refs[:6], refs[6:-7]
+    held, sems = refs[-7:-1], refs[-1]
+    copies = [
+        pltpu.make_async_copy(src, dst, sems.at[n]) for n, (src, dst) in enumerate(zip(given, held))
+    ]
+    for copy in copies:
+        copy.start()
+    for copy in copies:
+        copy.wait()
+    vec, completion, live, owner, take, give = held
     components, cells_x, cells_y, cells_z = vec.shape
     wells, segb = completion.shape
+    write_faces(Planes(vec), sends[groups:])
     depth = lax.broadcasted_iota(jnp.int32, (cells_z, segb), 0)
     lanes = lax.broadcasted_iota(jnp.int32, (1, segb), 1)
     for b in range(wells):
@@ -299,7 +347,7 @@
         for i in range(components):
             take_out[i, b : b + 1] = take[i, b : b + 1] * is_open
             give_out[i, b : b + 1] = give[i, b : b + 1] * is_open
-    write_messages(vec, place, column, take_out, owner, capacity, sends)
+    write_messages(vec, place, column, take_out, owner, capacity, sends[:groups])
 
 
 def split_kernel(inverse, first, second):
@@ -324,8 +372,8 @@
         terms = halo_terms(self.halo, self.messages, self.trans)
         return lambda i, x: self.part[i, x] - wells[i, x] - terms(i, x)
 
-    def send(self, vec, sends):
-        write_messages(vec, self.place, self.column, self.take, self.owner, self.capacity, sends)
+    def send(self, vec, sends, sums=None):
+        write_messages(vec, self.place, self.column, self.take, self.owner, self.capacity, sends, sums)
 
 
 def apply_kernel(sizes, *refs):
@@ -369,14 +417,13 @@
             if not first_time:
                 s[i, x] = w[i, x] + s_rest[i, x]
                 z[i, x] = t[i, x] + z_rest[i, x]
-    sums, *sends = rest
-    row = local_sums((b, r, s, w, z), sums.shape[-1])
     if end:
+        sums = rest[0]
+        row = local_sums((b, r, s, w, z), sums.shape[-1])
         for d in range(sums.shape[0]):
             sums[d] = row
     else:
-        sums[...] = row
-        got.send(z, sends)
+        got.send(z, rest, local_sums((b, r, s, w, z), got.column.shape[1]))
 
 
 def coefficients(row):
@@ -444,22 +491,6 @@
     ]
 
 
-def over_res(row, mask):
-    return lax.ppermute(row, "res", [(i, i ^ mask) for i in range(lax.axis_size("res"))])
-
-
-def res_sums(row):
-    count, step = lax.axis_size("res"), 2
-    parts = [row]
-    while step < count:
-        many = min(4, count // step)
-        if len(parts) > 1:
-            row = functools.reduce(jnp.add, parts)
-        parts = [row] + [over_res(row, k * step) for k in range(1, many)]
-        step *= many
-    return parts
-
-
 def body(
     right_side,
     accumulation,
@@ -477,12 +508,16 @@
     capacity = inverse.shape[2]
     devices = lax.axis_size("res") * groups
     field = (right_side.shape, F32)
-    shapes = message_shapes(groups, capacity, segb, components * cells_x, cells_z)
-    send_outs = [(shape, F32) for shape in shapes]
+    lines = components * cells_x
+    plain, summed = [
+        [(shape, F32) for shape in message_shapes(groups, capacity, segb, lines, cells_z, extra)]
+        for extra in (0, 1)
+    ]
     face_outs = [((components, cells_y, cells_z), F32)] * 2
     trans = transmissibility
     take = jnp.moveaxis(cell_to_well, 1, 0)
     give = jnp.moveaxis(well_to_cell, 1, 0)
+    owner = owner.reshape(-1)
     b = right_side
     sizes = (groups, capacity)
 
@@ -494,82 +529,89 @@
             (take.shape, F32),
             (give.shape, F32),
         ]
-        + send_outs,
+        + plain
+        + face_outs,
         [b, completion, live_count, owner, take, give],
-        [VMEM, VMEM, SMEM, SMEM, VMEM, VMEM],
+        [pl.BlockSpec(memory_space=pltpu.HBM)] * 6,
+        scratch=[
+            pltpu.VMEM(b.shape, F32),
+            pltpu.VMEM(completion.shape, jnp.int32),
+            pltpu.SMEM(live_count.shape, jnp.int32),
+            pltpu.SMEM(owner.shape, jnp.int32),
+            pltpu.VMEM(take.shape, F32),
+            pltpu.VMEM(give.shape, F32),
+            pltpu.SemaphoreType.DMA((6,)),
+        ],
+        limit=START_LIMIT,
     )
     first, second = call(split_kernel, [(inverse.shape[1:], BF16)] * 2, [inverse[0]])
     shifted = [pltpu.VMEM((4,) + b.shape, F32)]
-
     cost = dict(scratch=shifted, flops=200_000_000, moved=4_000_000)
 
-    def finish(kernel, outs, vec, sends, extra, row=None):
-        messages = swapped(sends)
-        if vec is b:
-            *faces, part, diag_total = call(
-                first_stencil_kernel,
-                face_outs + [field, (accumulation.shape, F32)],
-                [b, trans, accumulation],
-                **cost,
-            )
-            diag.append(diag_total)
-        elif row is None:
-            *faces, part = call(
-                functools.partial(stencil_kernel, 0, False),
-                face_outs + [field],
-                [vec, trans, *diag],
-                **cost,
-            )
-        else:
-            *faces, row, part = call(
-                functools.partial(stencil_kernel, groups, True),
-                face_outs + [((1, segb), F32), field],
-                [vec, trans, *diag, *messages, row, over_res(row, 1)],
-                **cost,
-            )
-        sums = [] if row is None else res_sums(row)
+    def finish(kernel, outs, part, messages, faces, extra, with_sums=False):
         halo = exchange(faces)
         values = call(
-            functools.partial(solve_kernel, len(sums), groups),
-            [((capacity + (len(sums) > 0), segb), F32)] * groups,
-            [first, second, *sums, *messages],
+            functools.partial(solve_kernel, groups),
+            [((capacity, segb), F32)] * groups,
+            [first, second, *messages],
             flops=SOLVE_FLOPS,
             moved=4_000_000,
         )
+        if with_sums:
+            mine = call(
+                functools.partial(group_sum_kernel, capacity), [((1, segb), F32)], messages
+            )[0]
+            fetched = [share_swap(mine, q) for q in range(share(lax.axis_size("res"), groups))]
+            values = call(
+                functools.partial(append_kernel, groups),
+                [((capacity + 1, segb), F32)] * groups,
+                [mine, *values, *fetched],
+            )
         values = swapped(values)
         args = [part, trans, place, column, take, give, owner, *halo, *messages, *values, *extra]
         specs = [VMEM] * len(args)
         specs[6] = SMEM
         return call(kernel, outs, args, specs, flops=1_000_000_000, moved=8_000_000)
 
-    diag = []
+    def apply(kernel, outs, vec, sends, extra, with_sums=False):
+        messages = swapped(sends)
+        *faces, part = call(stencil_kernel, face_outs + [field], [vec, trans, diag], **cost)
+        return finish(kernel, outs, part, messages, faces, extra, with_sums)
+
+    messages, faces = swapped(sends[:groups]), sends[groups:]
+    part, diag = call(
+        first_stencil_kernel,
+        [field, (accumulation.shape, F32)],
+        [b, trans, accumulation, messages[1]],
+        **cost,
+    )
     w, *sends = finish(
-        functools.partial(apply_kernel, sizes), [field] + send_outs, b, sends, []
+        functools.partial(apply_kernel, sizes), [field] + plain, part, messages, faces, []
     )
     r, s, p, x = b, w, b, None
     for index in range(ITERS):
         start, end = index == 0, index + 1 == ITERS
-        tail = [((devices, 1, 128), F32)] if end else [((1, segb), F32)] + send_outs
+        tail = [((devices, 1, 128), F32)] if end else summed
         kernel = functools.partial(second_kernel, sizes, start, end)
         if start:
-            t, sums, *sends = finish(kernel, [field] + tail, w, sends, [b, r, w])
+            t, *sends = apply(kernel, [field] + tail, w, sends, [b, r, w])
             z = t
         else:
-            t, s, z, sums, *sends = finish(
+            t, s, z, *sends = apply(
                 kernel, [field] * 3 + tail, w, sends, [b, r, w, s_rest, z_rest]
             )
         if end:
             break
         more = [] if start else [s, z, p, x]
-        r, w, x, p, s_rest, z_rest, *sends = finish(
+        r, w, x, p, s_rest, z_rest, *sends = apply(
             functools.partial(third_kernel, sizes, start),
-            [field] * 6 + send_outs,
+            [field] * 6 + plain,
             z,
             sends,
             [r, w, t, *more],
-            sums,
+            True,
         )
-    sums = lax.all_to_all(sums, ("res", "grp"), split_axis=0, concat_axis=0, tiled=True)
+    sums = lax.all_to_all(sends[0], ("res", "grp"), split_axis=0, concat_axis=0, tiled=True)
     x, r = call(last_kernel, [field, field], [sums, r, w, s, z, p, x])
     return (x, r)
 

time: 121 us -> 111 us (0.917)
  local copies, waits for them, and re-layouts: 7.56 us -> 2.23 us
  waiting for transfers between devices: 22.1 us -> 17.2 us
  Pallas kernels: 26.9 us -> 28.2 us
    ppermute x8 -> x4, waiting for transfers between devices: 6.99 us -> 1.56 us  [share_swap(): return lax.ppermute(row, ('res', 'grp'), pairs)]
    unnamed x21 -> x20, local copies, waits for them, and re-layouts: 7.56 us -> 2.23 us
    ppermute x8 -> x4, starting transfers between devices: 9.06 us -> 4.18 us  [share_swap(): return lax.ppermute(row, ('res', 'grp'), pairs)]
    ppermute x36, starting transfers between devices: 25.9 us -> 30 us  [swapped(): lax.ppermute(messages[k], 'grp', [(i, i ^ k) for i in range(groups)])]
    pallas_call x21 -> x25, Pallas kernels: 26.9 us -> 28.2 us  [call(): pl.pallas_call(kernel, out_shape=[jax.ShapeDtypeStruct(shape, dtype) for...]
  transfers between devices with their start and end apart: 56 -> 52, of which waited for: 15 -> 18; matrix products, arithmetic and copies ran while one was open for 0% -> 0% of each run, Pallas kernels for 8% -> 10%
where the time goes in v4:
time: 111 us
  starting transfers between devices  51.4 us (46%)
  Pallas kernels  28.2 us (25%)
  waiting for transfers between devices  17.2 us (15%)
  blocking collectives  10.5 us (9%)
  local copies, waits for them, and re-layouts  2.23 us (2%)
    ppermute x36, starting transfers between devices, swapped(): lax.ppermute(messages[k], 'grp', [(i, i ^ k) for i in range(groups)])  30 us
    pallas_call x25, Pallas kernels, call(): pl.pallas_call(kernel, out_shape=[jax.ShapeDtypeStruct(shape, dtype) for...  28.2 us
    ppermute x12, starting transfers between devices, exchange(): lax.ppermute(face, 'res', pairs)  17.3 us
    ppermute x36, waiting for transfers between devices, swapped(): lax.ppermute(messages[k], 'grp', [(i, i ^ k) for i in range(groups)])  14.6 us
    all_to_all x1, blocking collectives, body(): lax.all_to_all(sends[0], ('res', 'grp'), split_axis=0, concat_axis=0, til...  10.5 us
    ppermute x4, starting transfers between devices, share_swap(): return lax.ppermute(row, ('res', 'grp'), pairs)  4.18 us
    unnamed x20, local copies, waits for them, and re-layouts  2.23 us
  transfers between devices with their start and end apart: 52, of which 18 were waited for; matrix products, arithmetic and copies ran while one was open for 0% of the time, Pallas kernels for 10%

profile of v4, /device:TPU:0, one launch (start us, length us, event | category | flops | bytes accessed | tf_op | source)
XLA Modules:
  0.0 110.5 jit_solution(13128754873744795163)
XLA Ops:
  0.6 3.2 %shard_map.104 = (bf16[512,2048]{1,0:T(8,128)(2,1)}, s32[8,256]{1,0:T(8,128)}, f32[3,8,256]{2,1,0:T(8,128)}, f32[3,8,256]{2,1,0:T(8,128)}, f32[4,256]{1,0:T(4,12...) custom-call(f32[3,2,16,512]{3,2,1,0:T(8,128)} %refs_17_.7, ...), custom_call_target="tpu_custom_call" | custom-call | flops 1000000 | bytes 1000000 | tf_op jit(solution)/shard_map/pallas_call | solution.py:24
  4.3 2.6 %collective-permute-start.4 = (f32[8,512]{1,0:T(8,128)}, f32[8,512]{1,0:T(8,128)S(1)}, u32[]{:S(2)}, u32[]{:S(2)}) collective-permute-start(f32[8,512]{1,0:T(8,128)} %get-tuple-element.113), channel_id=1, source_target_pairs={{0,3},{1,2},{2,1},{3,0},{4,7},{5,6},{6,5},{7,4},{8,11},{9,10},{10,... | collective-permute-start | bytes 49160 | tf_op jit(solution)/shard_map/ppermute | solution.py:489
  7.0 2.0 %collective-permute-start.1 = (f32[3,16,512]{2,1,0:T(8,128)}, f32[3,16,512]{2,1,0:T(8,128)S(1)}, u32[]{:S(2)}, u32[]{:S(2)}) collective-permute-start(f32[3,16,512]{2,1,0:T(8,128)} %get-tuple-element.109), channel_id=1, source_target_pairs={{0,4},{4,0},{8,12},{12,8},{16,20},{20,16},{24,28},{28,24},{1,5},{5... | collective-permute-start | bytes 294920 | tf_op jit(solution)/shard_map/ppermute | solution.py:39
  9.0 3.6 %collective-permute-start.2 = (f32[3,16,512]{2,1,0:T(8,128)}, f32[3,16,512]{2,1,0:T(8,128)S(1)}, u32[]{:S(2)}, u32[]{:S(2)}) collective-permute-start(f32[3,16,512]{2,1,0:T(8,128)} %get-tuple-element.110), channel_id=1, source_target_pairs={{0,28},{4,8},{8,4},{12,16},{16,12},{20,24},{24,20},{28,0},{1,29},{... | collective-permute-start | bytes 294920 | tf_op jit(solution)/shard_map/ppermute | solution.py:39
  12.5 2.2 %copy-done.3 = f32[1,4,4,256,256]{4,3,2,1,0:T(8,128)S(1)} copy-done((f32[1,4,4,256,256]{4,3,2,1,0:T(8,128)S(1)}, f32[1,4,4,256,256]{4,3,2,1,0:T(8,128)}, u32[]{:S(2)}) %copy-start.3) | copy-done | bytes 4194328
  15.5 1.2 %shard_map.107 = (f32[4,256]{1,0:T(4,128)S(1)}, f32[4,256]{1,0:T(4,128)S(1)}, f32[4,256]{1,0:T(4,128)S(1)}, f32[4,256]{1,0:T(4,128)S(1)}) custom-call(bf16[4,4,256,256]{3,2,1,0:T(8,128)(2,1)S(1)} %get-tuple-element.114.first, bf16[4,4,256,256]{3,2,1,0:T(8,128)(2,1)S(1)} %get-tuple-element.115.second, f32[4,256]{1,0:T(4,128)S(1)} %copy-done.9, ...), custom_call_target="tpu_custom_call" | custom-call | flops 5000000000 | bytes 4000000 | tf_op jit(solution)/shard_map/pallas_call | solution.py:24
  16.8 1.6 %collective-permute-start.6 = (f32[4,256]{1,0:T(4,128)S(1)}, f32[4,256]{1,0:T(4,128)S(1)}, u32[]{:S(2)}, u32[]{:S(2)}) collective-permute-start(f32[4,256]{1,0:T(4,128)S(1)} %get-tuple-element.118), channel_id=1, source_target_pairs={{0,2},{1,3},{2,0},{3,1},{4,6},{5,7},{6,4},{7,5},{8,10},{9,11},{10,... | collective-permute-start | bytes 12296 | tf_op jit(solution)/shard_map/ppermute | solution.py:489
  19.5 1.0 collective-permute-done.6.refs_15_
  20.4 1.0 collective-permute-done.7.refs_16_
  21.5 2.0 %shard_map.108 = (f32[3,2,16,512]{3,2,1,0:T(8,128)S(1)}, f32[4,256]{1,0:T(4,128)S(1)}, f32[8,512]{1,0:T(8,128)S(1)}, f32[4,256]{1,0:T(4,128)S(1)}, f32[8,512]{1,0:T(8,128)S(1)}) custom-call(f32[3,2,16,512]{3,2,1,0:T(8,128)S(1)} %get-tuple-element.104.refs_0_, f32[6,3,3,2,16,512]{5,4,3,2,1,0:T(8,128)S(1)} %copy-done, bf16[512,2048]{1,0:T(8,128)(2,1)S(1)} %copy-done.1, ...), custom_call_target="tpu_custom_call" | custom-call | flops 1000000000 | bytes 8000000 | tf_op jit(solution)/shard_map/pallas_call | solution.py:24
  24.2 1.6 %collective-permute-start.12 = (f32[8,512]{1,0:T(8,128)S(1)}, f32[8,512]{1,0:T(8,128)S(1)}, u32[]{:S(2)}, u32[]{:S(2)}) collective-permute-start(f32[8,512]{1,0:T(8,128)S(1)} %get-tuple-element.128), channel_id=1, source_target_pairs={{0,3},{1,2},{2,1},{3,0},{4,7},{5,6},{6,5},{7,4},{8,11},{9,10},{10,... | collective-permute-start | bytes 49160 | tf_op jit(solution)/shard_map/ppermute | solution.py:489
  26.3 1.9 %collective-permute-start.9 = (f32[3,16,512]{2,1,0:T(8,128)S(1)}, f32[3,16,512]{2,1,0:T(8,128)S(1)}, u32[]{:S(2)}, u32[]{:S(2)}) collective-permute-start(f32[3,16,512]{2,1,0:T(8,128)S(1)} %get-tuple-element.124), channel_id=1, source_target_pairs={{0,28},{4,8},{8,4},{12,16},{16,12},{20,24},{24,20},{28,0},{1,29},{... | collective-permute-start | bytes 294920 | tf_op jit(solution)/shard_map/ppermute | solution.py:39
  28.2 1.2 %shard_map.110 = (f32[4,256]{1,0:T(4,128)S(1)}, f32[4,256]{1,0:T(4,128)S(1)}, f32[4,256]{1,0:T(4,128)S(1)}, f32[4,256]{1,0:T(4,128)S(1)}) custom-call(bf16[4,4,256,256]{3,2,1,0:T(8,128)(2,1)S(1)} %get-tuple-element.114.first, bf16[4,4,256,256]{3,2,1,0:T(8,128)(2,1)S(1)} %get-tuple-element.115.second, f32[4,256]{1,0:T(4,128)S(1)} %get-tuple-element.125.refs_0_.refs_9_, ...), custom_call_target="tpu_custom_call" | custom-call | flops 5000000000 | bytes 4000000 | tf_op jit(solution)/shard_map/pallas_call | solution.py:24
  29.5 1.1 collective-permute-start.14
  31.4 1.8 %collective-permute-done.14.refs_15_ = f32[4,256]{1,0:T(4,128)S(1)} collective-permute-done((f32[4,256]{1,0:T(4,128)S(1)}, f32[4,256]{1,0:T(4,128)S(1)}, u32[]{:S(2)}, u32[]{:S(2)}) %collective-permute-start.14) | collective-permute-done | bytes 4128 | tf_op jit(solution)/shard_map/ppermute | solution.py:489
  33.8 2.1 %shard_map.111 = (f32[3,2,16,512]{3,2,1,0:T(8,128)S(1)}, f32[5,256]{1,0:T(8,128)S(1)}, f32[9,512]{1,0:T(8,128)S(1)}, f32[5,256]{1,0:T(8,128)S(1)}, f32[9,512]{1,0:T(8,128)S(1)}) custom-call(f32[3,2,16,512]{3,2,1,0:T(8,128)S(1)} %get-tuple-element.122.refs_0_, f32[6,3,3,2,16,512]{5,4,3,2,1,0:T(8,128)S(1)} %copy-done, bf16[512,2048]{1,0:T(8,128)(2,1)S(1)} %copy-done.1, ...), custom_call_target="tpu_custom_call" | custom-call | flops 1000000000 | bytes 8000000 | tf_op jit(solution)/shard_map/pallas_call | solution.py:24
  35.9 1.0 collective-permute-start.19
  36.9 1.3 %collective-permute-start.20 = (f32[9,512]{1,0:T(8,128)S(1)}, f32[9,512]{1,0:T(8,128)S(1)}, u32[]{:S(2)}, u32[]{:S(2)}) collective-permute-start(f32[9,512]{1,0:T(8,128)S(1)} %get-tuple-element.140), channel_id=1, source_target_pairs={{0,3},{1,2},{2,1},{3,0},{4,7},{5,6},{6,5},{7,4},{8,11},{9,10},{10,... | collective-permute-start | bytes 55304 | tf_op jit(solution)/shard_map/ppermute | solution.py:489
  38.7 2.4 %collective-permute-start.17 = (f32[3,16,512]{2,1,0:T(8,128)S(1)}, f32[3,16,512]{2,1,0:T(8,128)S(1)}, u32[]{:S(2)}, u32[]{:S(2)}) collective-permute-start(f32[3,16,512]{2,1,0:T(8,128)S(1)} %get-tuple-element.136), channel_id=1, source_target_pairs={{0,28},{4,8},{8,4},{12,16},{16,12},{20,24},{24,20},{28,0},{1,29},{... | collective-permute-start | bytes 294920 | tf_op jit(solution)/shard_map/ppermute | solution.py:39
  41.8 1.4 %collective-permute-start.21 = (f32[1,256]{1,0:T(1,128)S(1)}, f32[1,256]{1,0:T(1,128)S(1)}, u32[]{:S(2)}, u32[]{:S(2)}) collective-permute-start(f32[1,256]{1,0:T(1,128)S(1)} %shard_map.113.mine), channel_id=1, source_target_pairs={{0,4},{1,9},{2,18},{3,27},{4,0},{5,13},{6,22},{7,31},{8,12},{9,1},... | collective-permute-start | bytes 3080 | tf_op jit(solution)/shard_map/ppermute | solution.py:221
  43.2 1.2 %shard_map.114 = (f32[4,256]{1,0:T(4,128)S(1)}, f32[4,256]{1,0:T(4,128)S(1)}, f32[4,256]{1,0:T(4,128)S(1)}, f32[4,256]{1,0:T(4,128)S(1)}) custom-call(bf16[4,4,256,256]{3,2,1,0:T(8,128)(2,1)S(1)} %get-tuple-element.114.first, bf16[4,4,256,256]{3,2,1,0:T(8,128)(2,1)S(1)} %get-tuple-element.115.second, f32[5,256]{1,0:T(8,128)S(1)} %get-tuple-element.137.refs_0_.refs_9_, ...), custom_call_target="tpu_custom_call" | custom-call | flops 5000000000 | bytes 4000000 | tf_op jit(solution)/shard_map/pallas_call | solution.py:24
  45.5 3.6 %collective-permute-start.24 = (f32[5,256]{1,0:T(8,128)S(1)}, f32[5,256]{1,0:T(8,128)S(1)}, u32[]{:S(2)}, u32[]{:S(2)}) collective-permute-start(f32[5,256]{1,0:T(8,128)S(1)} %get-tuple-element.147), channel_id=1, source_target_pairs={{0,2},{1,3},{2,0},{3,1},{4,6},{5,7},{6,4},{7,5},{8,10},{9,11},{10,... | collective-permute-start | bytes 15368 | tf_op jit(solution)/shard_map/ppermute | solution.py:489
  49.2 1.6 %collective-permute-done.24.refs_15_ = f32[5,256]{1,0:T(8,128)S(1)} collective-permute-done((f32[5,256]{1,0:T(8,128)S(1)}, f32[5,256]{1,0:T(8,128)S(1)}, u32[]{:S(2)}, u32[]{:S(2)}) %collective-permute-start.24) | collective-permute-done | bytes 5152 | tf_op jit(solution)/shard_map/ppermute | solution.py:489
  50.8 1.4 %collective-permute-done.25.refs_16_ = f32[5,256]{1,0:T(8,128)S(1)} collective-permute-done((f32[5,256]{1,0:T(8,128)S(1)}, f32[5,256]{1,0:T(8,128)S(1)}, u32[]{:S(2)}, u32[]{:S(2)}) %collective-permute-start.25) | collective-permute-done | bytes 5152 | tf_op jit(solution)/shard_map/ppermute | solution.py:489
  52.2 2.2 %shard_map.116 = (f32[3,2,16,512]{3,2,1,0:T(8,128)S(1)}, f32[3,2,16,512]{3,2,1,0:T(8,128)S(1)}, f32[3,2,16,512]{3,2,1,0:T(8,128)S(1)}, f32[3,2,16,512]{3,2,1,0:T...) custom-call(f32[3,2,16,512]{3,2,1,0:T(8,128)S(1)} %get-tuple-element, ...), custom_call_target="tpu_custom_call" | custom-call | flops 1000000000 | bytes 8000000 | tf_op jit(solution)/shard_map/pallas_call | solution.py:24
  55.1 1.5 %collective-permute-start.30 = (f32[8,512]{1,0:T(8,128)S(1)}, f32[8,512]{1,0:T(8,128)S(1)}, u32[]{:S(2)}, u32[]{:S(2)}) collective-permute-start(f32[8,512]{1,0:T(8,128)S(1)} %get-tuple-element.156), channel_id=1, source_target_pairs={{0,3},{1,2},{2,1},{3,0},{4,7},{5,6},{6,5},{7,4},{8,11},{9,10},{10,... | collective-permute-start | bytes 49160 | tf_op jit(solution)/shard_map/ppermute | solution.py:489
  57.0 1.1 %collective-permute-start.26 = (f32[3,16,512]{2,1,0:T(8,128)S(1)}, f32[3,16,512]{2,1,0:T(8,128)S(1)}, u32[]{:S(2)}, u32[]{:S(2)}) collective-permute-start(f32[3,16,512]{2,1,0:T(8,128)S(1)} %get-tuple-element.151), channel_id=1, source_target_pairs={{0,4},{4,0},{8,12},{12,8},{16,20},{20,16},{24,28},{28,24},{1,5},{5... | collective-permute-start | bytes 294920 | tf_op jit(solution)/shard_map/ppermute | solution.py:39
  58.2 1.2 %collective-permute-start.27 = (f32[3,16,512]{2,1,0:T(8,128)S(1)}, f32[3,16,512]{2,1,0:T(8,128)S(1)}, u32[]{:S(2)}, u32[]{:S(2)}) collective-permute-start(f32[3,16,512]{2,1,0:T(8,128)S(1)} %get-tuple-element.152), channel_id=1, source_target_pairs={{0,28},{4,8},{8,4},{12,16},{16,12},{20,24},{24,20},{28,0},{1,29},{... | collective-permute-start | bytes 294920 | tf_op jit(solution)/shard_map/ppermute | solution.py:39
  59.4 1.2 %shard_map.118 = (f32[4,256]{1,0:T(4,128)S(1)}, f32[4,256]{1,0:T(4,128)S(1)}, f32[4,256]{1,0:T(4,128)S(1)}, f32[4,256]{1,0:T(4,128)S(1)}) custom-call(bf16[4,4,256,256]{3,2,1,0:T(8,128)(2,1)S(1)} %get-tuple-element.114.first, bf16[4,4,256,256]{3,2,1,0:T(8,128)(2,1)S(1)} %get-tuple-element.115.second, f32[4,256]{1,0:T(4,128)S(1)} %get-tuple-element.153.refs_0_.refs_9_, ...), custom_call_target="tpu_custom_call" | custom-call | flops 5000000000 | bytes 4000000 | tf_op jit(solution)/shard_map/pallas_call | solution.py:24
  61.6 1.0 collective-permute-start.33
  62.6 2.0 %collective-permute-done.32.refs_15_ = f32[4,256]{1,0:T(4,128)S(1)} collective-permute-done((f32[4,256]{1,0:T(4,128)S(1)}, f32[4,256]{1,0:T(4,128)S(1)}, u32[]{:S(2)}, u32[]{:S(2)}) %collective-permute-start.32) | collective-permute-done | bytes 4128 | tf_op jit(solution)/shard_map/ppermute | solution.py:489
  65.5 2.3 %shard_map.119 = (f32[3,2,16,512]{3,2,1,0:T(8,128)S(1)}, f32[3,2,16,512]{3,2,1,0:T(8,128)S(1)}, f32[3,2,16,512]{3,2,1,0:T(8,128)S(1)}, f32[5,256]{1,0:T(8,128)S(...) custom-call(f32[3,2,16,512]{3,2,1,0:T(8,128)S(1)} %get-tuple-element.150.refs_0_, ...), custom_call_target="tpu_custom_call" | custom-call | flops 1000000000 | bytes 8000000 | tf_op jit(solution)/shard_map/pallas_call | solution.py:24
  68.5 1.5 %collective-permute-start.38 = (f32[9,512]{1,0:T(8,128)S(1)}, f32[9,512]{1,0:T(8,128)S(1)}, u32[]{:S(2)}, u32[]{:S(2)}) collective-permute-start(f32[9,512]{1,0:T(8,128)S(1)} %get-tuple-element.171), channel_id=1, source_target_pairs={{0,3},{1,2},{2,1},{3,0},{4,7},{5,6},{6,5},{7,4},{8,11},{9,10},{10,... | collective-permute-start | bytes 55304 | tf_op jit(solution)/shard_map/ppermute | solution.py:489
  70.6 2.6 %collective-permute-start.35 = (f32[3,16,512]{2,1,0:T(8,128)S(1)}, f32[3,16,512]{2,1,0:T(8,128)S(1)}, u32[]{:S(2)}, u32[]{:S(2)}) collective-permute-start(f32[3,16,512]{2,1,0:T(8,128)S(1)} %get-tuple-element.167), channel_id=1, source_target_pairs={{0,28},{4,8},{8,4},{12,16},{16,12},{20,24},{24,20},{28,0},{1,29},{... | collective-permute-start | bytes 294920 | tf_op jit(solution)/shard_map/ppermute | solution.py:39
  73.3 2.0 %collective-permute-start.39 = (f32[1,256]{1,0:T(1,128)S(1)}, f32[1,256]{1,0:T(1,128)S(1)}, u32[]{:S(2)}, u32[]{:S(2)}) collective-permute-start(f32[1,256]{1,0:T(1,128)S(1)} %shard_map.121.mine), channel_id=1, source_target_pairs={{0,4},{1,9},{2,18},{3,27},{4,0},{5,13},{6,22},{7,31},{8,12},{9,1},... | collective-permute-start | bytes 3080 | tf_op jit(solution)/shard_map/ppermute | solution.py:221
  75.3 1.2 %shard_map.122 = (f32[4,256]{1,0:T(4,128)S(1)}, f32[4,256]{1,0:T(4,128)S(1)}, f32[4,256]{1,0:T(4,128)S(1)}, f32[4,256]{1,0:T(4,128)S(1)}) custom-call(bf16[4,4,256,256]{3,2,1,0:T(8,128)(2,1)S(1)} %get-tuple-element.114.first, bf16[4,4,256,256]{3,2,1,0:T(8,128)(2,1)S(1)} %get-tuple-element.115.second, f32[5,256]{1,0:T(8,128)S(1)} %get-tuple-element.168.refs_0_.refs_9_, ...), custom_call_target="tpu_custom_call" | custom-call | flops 5000000000 | bytes 4000000 | tf_op jit(solution)/shard_map/pallas_call | solution.py:24
  77.2 4.1 %collective-permute-start.42 = (f32[5,256]{1,0:T(8,128)S(1)}, f32[5,256]{1,0:T(8,128)S(1)}, u32[]{:S(2)}, u32[]{:S(2)}) collective-permute-start(f32[5,256]{1,0:T(8,128)S(1)} %get-tuple-element.178), channel_id=1, source_target_pairs={{0,2},{1,3},{2,0},{3,1},{4,6},{5,7},{6,4},{7,5},{8,10},{9,11},{10,... | collective-permute-start | bytes 15368 | tf_op jit(solution)/shard_map/ppermute | solution.py:489
  81.3 1.6 %collective-permute-done.42.refs_15_ = f32[5,256]{1,0:T(8,128)S(1)} collective-permute-done((f32[5,256]{1,0:T(8,128)S(1)}, f32[5,256]{1,0:T(8,128)S(1)}, u32[]{:S(2)}, u32[]{:S(2)}) %collective-permute-start.42) | collective-permute-done | bytes 5152 | tf_op jit(solution)/shard_map/ppermute | solution.py:489
  82.9 1.4 %collective-permute-done.43.refs_16_ = f32[5,256]{1,0:T(8,128)S(1)} collective-permute-done((f32[5,256]{1,0:T(8,128)S(1)}, f32[5,256]{1,0:T(8,128)S(1)}, u32[]{:S(2)}, u32[]{:S(2)}) %collective-permute-start.43) | collective-permute-done | bytes 5152 | tf_op jit(solution)/shard_map/ppermute | solution.py:489
  84.4 2.2 %shard_map.124 = (f32[3,2,16,512]{3,2,1,0:T(8,128)S(1)}, f32[3,2,16,512]{3,2,1,0:T(8,128)S(1)}, f32[3,2,16,512]{3,2,1,0:T(8,128)S(1)}, f32[3,2,16,512]{3,2,1,0:T...) custom-call(f32[3,2,16,512]{3,2,1,0:T(8,128)S(1)} %get-tuple-element, ...), custom_call_target="tpu_custom_call" | custom-call | flops 1000000000 | bytes 8000000 | tf_op jit(solution)/shard_map/pallas_call | solution.py:24
  87.2 1.5 %collective-permute-start.48 = (f32[8,512]{1,0:T(8,128)S(1)}, f32[8,512]{1,0:T(8,128)S(1)}, u32[]{:S(2)}, u32[]{:S(2)}) collective-permute-start(f32[8,512]{1,0:T(8,128)S(1)} %get-tuple-element.191), channel_id=1, source_target_pairs={{0,3},{1,2},{2,1},{3,0},{4,7},{5,6},{6,5},{7,4},{8,11},{9,10},{10,... | collective-permute-start | bytes 49160 | tf_op jit(solution)/shard_map/ppermute | solution.py:489
  89.3 2.0 %collective-permute-start.45 = (f32[3,16,512]{2,1,0:T(8,128)S(1)}, f32[3,16,512]{2,1,0:T(8,128)S(1)}, u32[]{:S(2)}, u32[]{:S(2)}) collective-permute-start(f32[3,16,512]{2,1,0:T(8,128)S(1)} %get-tuple-element.187), channel_id=1, source_target_pairs={{0,28},{4,8},{8,4},{12,16},{16,12},{20,24},{24,20},{28,0},{1,29},{... | collective-permute-start | bytes 294920 | tf_op jit(solution)/shard_map/ppermute | solution.py:39
  91.3 1.2 %shard_map.126 = (f32[4,256]{1,0:T(4,128)S(1)}, f32[4,256]{1,0:T(4,128)S(1)}, f32[4,256]{1,0:T(4,128)S(1)}, f32[4,256]{1,0:T(4,128)S(1)}) custom-call(bf16[4,4,256,256]{3,2,1,0:T(8,128)(2,1)S(1)} %get-tuple-element.114.first, bf16[4,4,256,256]{3,2,1,0:T(8,128)(2,1)S(1)} %get-tuple-element.115.second, f32[4,256]{1,0:T(4,128)S(1)} %get-tuple-element.188.refs_0_.refs_9_, ...), custom_call_target="tpu_custom_call" | custom-call | flops 5000000000 | bytes 4000000 | tf_op jit(solution)/shard_map/pallas_call | solution.py:24
  92.6 1.0 collective-permute-start.50
  94.5 1.8 %collective-permute-done.50.refs_15_ = f32[4,256]{1,0:T(4,128)S(1)} collective-permute-done((f32[4,256]{1,0:T(4,128)S(1)}, f32[4,256]{1,0:T(4,128)S(1)}, u32[]{:S(2)}, u32[]{:S(2)}) %collective-permute-start.50) | collective-permute-done | bytes 4128 | tf_op jit(solution)/shard_map/ppermute | solution.py:489
  96.8 2.3 %shard_map.127 = (f32[3,2,16,512]{3,2,1,0:T(8,128)}, f32[3,2,16,512]{3,2,1,0:T(8,128)S(1)}, f32[3,2,16,512]{3,2,1,0:T(8,128)S(1)}, f32[32,1,128]{2,1,0:T(1,128)S(1)}) custom-call(f32[3,2,16,512]{3,2,1,0:T(8,128)S(1)} %get-tuple-element.185.refs_0_, f32[6,3,3,2,16,512]{5,4,3,2,1,0:T(8,128)S(1)} %copy-done, bf16[512,2048]{1,0:T(8,128)(2,1)S(1)} %copy-done.1, ...), custom_call_target="tpu_custom_call" | custom-call | flops 1000000000 | bytes 8000000 | tf_op jit(solution)/shard_map/pallas_call | solution.py:24
  99.1 10.5 %all_to_all.5.sums = f32[32,1,128]{2,1,0:T(1,128)S(1)} all-to-all(f32[32,1,128]{2,1,0:T(1,128)S(1)} %get-tuple-element.199), channel_id=1, replica_groups=mesh['res'=8,'grp'=4] {'res','grp'}, dimensions={0} | all-to-all | bytes 32768 | tf_op jit(solution)/shard_map/all_to_all | solution.py:614
  109.6 0.9 shard_map.128
  (102 shorter events, 15.2 us)
Async XLA Ops:
  3.8 11.6 %collective-permute-start = (f32[8,512]{1,0:T(8,128)}, f32[8,512]{1,0:T(8,128)S(1)}, u32[]{:S(2)}, u32[]{:S(2)}) collective-permute-start(f32[8,512]{1,0:T(8,128)} %get-tuple-element.103), channel_id=1, source_target_pairs={{0,1},{1,0},{2,3},{3,2},{4,5},{5,4},{6,7},{7,6},{8,9},{9,8},{10,11... | collective-permute-start | bytes 49160 | tf_op jit(solution)/shard_map/ppermute | solution.py:489
  4.3 11.1 %collective-permute-start.4 = (f32[8,512]{1,0:T(8,128)}, f32[8,512]{1,0:T(8,128)S(1)}, u32[]{:S(2)}, u32[]{:S(2)}) collective-permute-start(f32[8,512]{1,0:T(8,128)} %get-tuple-element.113), channel_id=1, source_target_pairs={{0,3},{1,2},{2,1},{3,0},{4,7},{5,6},{6,5},{7,4},{8,11},{9,10},{10,... | collective-permute-start | bytes 49160 | tf_op jit(solution)/shard_map/ppermute | solution.py:489
  7.0 8.4 %collective-permute-start.3 = (f32[4,256]{1,0:T(4,128)}, f32[4,256]{1,0:T(4,128)S(1)}, u32[]{:S(2)}, u32[]{:S(2)}) collective-permute-start(f32[4,256]{1,0:T(4,128)} %get-tuple-element.112), channel_id=1, source_target_pairs={{0,2},{1,3},{2,0},{3,1},{4,6},{5,7},{6,4},{7,5},{8,10},{9,11},{10,... | collective-permute-start | bytes 12296 | tf_op jit(solution)/shard_map/ppermute | solution.py:489
  7.0 14.5 %collective-permute-start.1 = (f32[3,16,512]{2,1,0:T(8,128)}, f32[3,16,512]{2,1,0:T(8,128)S(1)}, u32[]{:S(2)}, u32[]{:S(2)}) collective-permute-start(f32[3,16,512]{2,1,0:T(8,128)} %get-tuple-element.109), channel_id=1, source_target_pairs={{0,4},{4,0},{8,12},{12,8},{16,20},{20,16},{24,28},{28,24},{1,5},{5... | collective-permute-start | bytes 294920 | tf_op jit(solution)/shard_map/ppermute | solution.py:39
  9.0 12.5 %collective-permute-start.2 = (f32[3,16,512]{2,1,0:T(8,128)}, f32[3,16,512]{2,1,0:T(8,128)S(1)}, u32[]{:S(2)}, u32[]{:S(2)}) collective-permute-start(f32[3,16,512]{2,1,0:T(8,128)} %get-tuple-element.110), channel_id=1, source_target_pairs={{0,28},{4,8},{8,4},{12,16},{16,12},{20,24},{24,20},{28,0},{1,29},{... | collective-permute-start | bytes 294920 | tf_op jit(solution)/shard_map/ppermute | solution.py:39
  16.8 3.7 %collective-permute-start.6 = (f32[4,256]{1,0:T(4,128)S(1)}, f32[4,256]{1,0:T(4,128)S(1)}, u32[]{:S(2)}, u32[]{:S(2)}) collective-permute-start(f32[4,256]{1,0:T(4,128)S(1)} %get-tuple-element.118), channel_id=1, source_target_pairs={{0,2},{1,3},{2,0},{3,1},{4,6},{5,7},{6,4},{7,5},{8,10},{9,11},{10,... | collective-permute-start | bytes 12296 | tf_op jit(solution)/shard_map/ppermute | solution.py:489
  18.4 3.1 %collective-permute-start.7 = (f32[4,256]{1,0:T(4,128)S(1)}, f32[4,256]{1,0:T(4,128)S(1)}, u32[]{:S(2)}, u32[]{:S(2)}) collective-permute-start(f32[4,256]{1,0:T(4,128)S(1)} %get-tuple-element.119), channel_id=1, source_target_pairs={{0,3},{1,2},{2,1},{3,0},{4,7},{5,6},{6,5},{7,4},{8,11},{9,10},{10,... | collective-permute-start | bytes 12296 | tf_op jit(solution)/shard_map/ppermute | solution.py:489
  23.6 4.6 %collective-permute-start.11 = (f32[4,256]{1,0:T(4,128)S(1)}, f32[4,256]{1,0:T(4,128)S(1)}, u32[]{:S(2)}, u32[]{:S(2)}) collective-permute-start(f32[4,256]{1,0:T(4,128)S(1)} %get-tuple-element.127), channel_id=1, source_target_pairs={{0,2},{1,3},{2,0},{3,1},{4,6},{5,7},{6,4},{7,5},{8,10},{9,11},{10,... | collective-permute-start | bytes 12296 | tf_op jit(solution)/shard_map/ppermute | solution.py:489
  24.2 4.0 %collective-permute-start.10 = (f32[8,512]{1,0:T(8,128)S(1)}, f32[8,512]{1,0:T(8,128)S(1)}, u32[]{:S(2)}, u32[]{:S(2)}) collective-permute-start(f32[8,512]{1,0:T(8,128)S(1)} %get-tuple-element.126), channel_id=1, source_target_pairs={{0,1},{1,0},{2,3},{3,2},{4,5},{5,4},{6,7},{7,6},{8,9},{9,8},{10,11... | collective-permute-start | bytes 49160 | tf_op jit(solution)/shard_map/ppermute | solution.py:489
  24.2 4.0 %collective-permute-start.12 = (f32[8,512]{1,0:T(8,128)S(1)}, f32[8,512]{1,0:T(8,128)S(1)}, u32[]{:S(2)}, u32[]{:S(2)}) collective-permute-start(f32[8,512]{1,0:T(8,128)S(1)} %get-tuple-element.128), channel_id=1, source_target_pairs={{0,3},{1,2},{2,1},{3,0},{4,7},{5,6},{6,5},{7,4},{8,11},{9,10},{10,... | collective-permute-start | bytes 49160 | tf_op jit(solution)/shard_map/ppermute | solution.py:489
  26.2 7.5 %collective-permute-start.8 = (f32[3,16,512]{2,1,0:T(8,128)S(1)}, f32[3,16,512]{2,1,0:T(8,128)S(1)}, u32[]{:S(2)}, u32[]{:S(2)}) collective-permute-start(f32[3,16,512]{2,1,0:T(8,128)S(1)} %get-tuple-element.123), channel_id=1, source_target_pairs={{0,4},{4,0},{8,12},{12,8},{16,20},{20,16},{24,28},{28,24},{1,5},{5... | collective-permute-start | bytes 294920 | tf_op jit(solution)/shard_map/ppermute | solution.py:39
  26.3 7.5 %collective-permute-start.9 = (f32[3,16,512]{2,1,0:T(8,128)S(1)}, f32[3,16,512]{2,1,0:T(8,128)S(1)}, u32[]{:S(2)}, u32[]{:S(2)}) collective-permute-start(f32[3,16,512]{2,1,0:T(8,128)S(1)} %get-tuple-element.124), channel_id=1, source_target_pairs={{0,28},{4,8},{8,4},{12,16},{16,12},{20,24},{24,20},{28,0},{1,29},{... | collective-permute-start | bytes 294920 | tf_op jit(solution)/shard_map/ppermute | solution.py:39
  29.5 3.7 %collective-permute-start.14 = (f32[4,256]{1,0:T(4,128)S(1)}, f32[4,256]{1,0:T(4,128)S(1)}, u32[]{:S(2)}, u32[]{:S(2)}) collective-permute-start(f32[4,256]{1,0:T(4,128)S(1)} %get-tuple-element.131), channel_id=1, source_target_pairs={{0,2},{1,3},{2,0},{3,1},{4,6},{5,7},{6,4},{7,5},{8,10},{9,11},{10,... | collective-permute-start | bytes 12296 | tf_op jit(solution)/shard_map/ppermute | solution.py:489
  30.6 3.1 %collective-permute-start.15 = (f32[4,256]{1,0:T(4,128)S(1)}, f32[4,256]{1,0:T(4,128)S(1)}, u32[]{:S(2)}, u32[]{:S(2)}) collective-permute-start(f32[4,256]{1,0:T(4,128)S(1)} %get-tuple-element.132), channel_id=1, source_target_pairs={{0,3},{1,2},{2,1},{3,0},{4,7},{5,6},{6,5},{7,4},{8,11},{9,10},{10,... | collective-permute-start | bytes 12296 | tf_op jit(solution)/shard_map/ppermute | solution.py:489
  35.9 5.2 %collective-permute-start.19 = (f32[5,256]{1,0:T(8,128)S(1)}, f32[5,256]{1,0:T(8,128)S(1)}, u32[]{:S(2)}, u32[]{:S(2)}) collective-permute-start(f32[5,256]{1,0:T(8,128)S(1)} %get-tuple-element.139), channel_id=1, source_target_pairs={{0,2},{1,3},{2,0},{3,1},{4,6},{5,7},{6,4},{7,5},{8,10},{9,11},{10,... | collective-permute-start | bytes 15368 | tf_op jit(solution)/shard_map/ppermute | solution.py:489
  36.9 4.2 %collective-permute-start.18 = (f32[9,512]{1,0:T(8,128)S(1)}, f32[9,512]{1,0:T(8,128)S(1)}, u32[]{:S(2)}, u32[]{:S(2)}) collective-permute-start(f32[9,512]{1,0:T(8,128)S(1)} %get-tuple-element.138), channel_id=1, source_target_pairs={{0,1},{1,0},{2,3},{3,2},{4,5},{5,4},{6,7},{7,6},{8,9},{9,8},{10,11... | collective-permute-start | bytes 55304 | tf_op jit(solution)/shard_map/ppermute | solution.py:489
  36.9 4.2 %collective-permute-start.20 = (f32[9,512]{1,0:T(8,128)S(1)}, f32[9,512]{1,0:T(8,128)S(1)}, u32[]{:S(2)}, u32[]{:S(2)}) collective-permute-start(f32[9,512]{1,0:T(8,128)S(1)} %get-tuple-element.140), channel_id=1, source_target_pairs={{0,3},{1,2},{2,1},{3,0},{4,7},{5,6},{6,5},{7,4},{8,11},{9,10},{10,... | collective-permute-start | bytes 55304 | tf_op jit(solution)/shard_map/ppermute | solution.py:489
  38.6 13.7 %collective-permute-start.16 = (f32[3,16,512]{2,1,0:T(8,128)S(1)}, f32[3,16,512]{2,1,0:T(8,128)S(1)}, u32[]{:S(2)}, u32[]{:S(2)}) collective-permute-start(f32[3,16,512]{2,1,0:T(8,128)S(1)} %get-tuple-element.135), channel_id=1, source_target_pairs={{0,4},{4,0},{8,12},{12,8},{16,20},{20,16},{24,28},{28,24},{1,5},{5... | collective-permute-start | bytes 294920 | tf_op jit(solution)/shard_map/ppermute | solution.py:39
  38.7 13.5 %collective-permute-start.17 = (f32[3,16,512]{2,1,0:T(8,128)S(1)}, f32[3,16,512]{2,1,0:T(8,128)S(1)}, u32[]{:S(2)}, u32[]{:S(2)}) collective-permute-start(f32[3,16,512]{2,1,0:T(8,128)S(1)} %get-tuple-element.136), channel_id=1, source_target_pairs={{0,28},{4,8},{8,4},{12,16},{16,12},{20,24},{24,20},{28,0},{1,29},{... | collective-permute-start | bytes 294920 | tf_op jit(solution)/shard_map/ppermute | solution.py:39
  41.1 3.7 %collective-permute-start.22 = (f32[1,256]{1,0:T(1,128)S(1)}, f32[1,256]{1,0:T(1,128)S(1)}, u32[]{:S(2)}, u32[]{:S(2)}) collective-permute-start(f32[1,256]{1,0:T(1,128)S(1)} %shard_map.113.mine), channel_id=1, source_target_pairs={{0,4},{1,13},{2,22},{3,31},{4,0},{5,9},{6,18},{7,27},{8,12},{9,5},... | collective-permute-start | bytes 3080 | tf_op jit(solution)/shard_map/ppermute | solution.py:221
  41.8 3.6 %collective-permute-start.21 = (f32[1,256]{1,0:T(1,128)S(1)}, f32[1,256]{1,0:T(1,128)S(1)}, u32[]{:S(2)}, u32[]{:S(2)}) collective-permute-start(f32[1,256]{1,0:T(1,128)S(1)} %shard_map.113.mine), channel_id=1, source_target_pairs={{0,4},{1,9},{2,18},{3,27},{4,0},{5,13},{6,22},{7,31},{8,12},{9,1},... | collective-permute-start | bytes 3080 | tf_op jit(solution)/shard_map/ppermute | solution.py:221
  45.4 3.8 %collective-permute-start.23 = (f32[5,256]{1,0:T(8,128)S(1)}, f32[5,256]{1,0:T(8,128)S(1)}, u32[]{:S(2)}, u32[]{:S(2)}) collective-permute-start(f32[5,256]{1,0:T(8,128)S(1)} %get-tuple-element.146), channel_id=1, source_target_pairs={{0,1},{1,0},{2,3},{3,2},{4,5},{5,4},{6,7},{7,6},{8,9},{9,8},{10,11... | collective-permute-start | bytes 15368 | tf_op jit(solution)/shard_map/ppermute | solution.py:489
  45.5 5.2 %collective-permute-start.24 = (f32[5,256]{1,0:T(8,128)S(1)}, f32[5,256]{1,0:T(8,128)S(1)}, u32[]{:S(2)}, u32[]{:S(2)}) collective-permute-start(f32[5,256]{1,0:T(8,128)S(1)} %get-tuple-element.147), channel_id=1, source_target_pairs={{0,2},{1,3},{2,0},{3,1},{4,6},{5,7},{6,4},{7,5},{8,10},{9,11},{10,... | collective-permute-start | bytes 15368 | tf_op jit(solution)/shard_map/ppermute | solution.py:489
  49.1 3.1 %collective-permute-start.25 = (f32[5,256]{1,0:T(8,128)S(1)}, f32[5,256]{1,0:T(8,128)S(1)}, u32[]{:S(2)}, u32[]{:S(2)}) collective-permute-start(f32[5,256]{1,0:T(8,128)S(1)} %get-tuple-element.148), channel_id=1, source_target_pairs={{0,3},{1,2},{2,1},{3,0},{4,7},{5,6},{6,5},{7,4},{8,11},{9,10},{10,... | collective-permute-start | bytes 15368 | tf_op jit(solution)/shard_map/ppermute | solution.py:489
  54.4 5.0 %collective-permute-start.29 = (f32[4,256]{1,0:T(4,128)S(1)}, f32[4,256]{1,0:T(4,128)S(1)}, u32[]{:S(2)}, u32[]{:S(2)}) collective-permute-start(f32[4,256]{1,0:T(4,128)S(1)} %get-tuple-element.155), channel_id=1, source_target_pairs={{0,2},{1,3},{2,0},{3,1},{4,6},{5,7},{6,4},{7,5},{8,10},{9,11},{10,... | collective-permute-start | bytes 12296 | tf_op jit(solution)/shard_map/ppermute | solution.py:489
  55.1 4.3 %collective-permute-start.28 = (f32[8,512]{1,0:T(8,128)S(1)}, f32[8,512]{1,0:T(8,128)S(1)}, u32[]{:S(2)}, u32[]{:S(2)}) collective-permute-start(f32[8,512]{1,0:T(8,128)S(1)} %get-tuple-element.154), channel_id=1, source_target_pairs={{0,1},{1,0},{2,3},{3,2},{4,5},{5,4},{6,7},{7,6},{8,9},{9,8},{10,11... | collective-permute-start | bytes 49160 | tf_op jit(solution)/shard_map/ppermute | solution.py:489
  55.1 4.3 %collective-permute-start.30 = (f32[8,512]{1,0:T(8,128)S(1)}, f32[8,512]{1,0:T(8,128)S(1)}, u32[]{:S(2)}, u32[]{:S(2)}) collective-permute-start(f32[8,512]{1,0:T(8,128)S(1)} %get-tuple-element.156), channel_id=1, source_target_pairs={{0,3},{1,2},{2,1},{3,0},{4,7},{5,6},{6,5},{7,4},{8,11},{9,10},{10,... | collective-permute-start | bytes 49160 | tf_op jit(solution)/shard_map/ppermute | solution.py:489
  57.0 7.6 %collective-permute-start.26 = (f32[3,16,512]{2,1,0:T(8,128)S(1)}, f32[3,16,512]{2,1,0:T(8,128)S(1)}, u32[]{:S(2)}, u32[]{:S(2)}) collective-permute-start(f32[3,16,512]{2,1,0:T(8,128)S(1)} %get-tuple-element.151), channel_id=1, source_target_pairs={{0,4},{4,0},{8,12},{12,8},{16,20},{20,16},{24,28},{28,24},{1,5},{5... | collective-permute-start | bytes 294920 | tf_op jit(solution)/shard_map/ppermute | solution.py:39
  58.2 7.3 %collective-permute-start.27 = (f32[3,16,512]{2,1,0:T(8,128)S(1)}, f32[3,16,512]{2,1,0:T(8,128)S(1)}, u32[]{:S(2)}, u32[]{:S(2)}) collective-permute-start(f32[3,16,512]{2,1,0:T(8,128)S(1)} %get-tuple-element.152), channel_id=1, source_target_pairs={{0,28},{4,8},{8,4},{12,16},{16,12},{20,24},{24,20},{28,0},{1,29},{... | collective-permute-start | bytes 294920 | tf_op jit(solution)/shard_map/ppermute | solution.py:39
  60.7 3.9 %collective-permute-start.32 = (f32[4,256]{1,0:T(4,128)S(1)}, f32[4,256]{1,0:T(4,128)S(1)}, u32[]{:S(2)}, u32[]{:S(2)}) collective-permute-start(f32[4,256]{1,0:T(4,128)S(1)} %get-tuple-element.159), channel_id=1, source_target_pairs={{0,2},{1,3},{2,0},{3,1},{4,6},{5,7},{6,4},{7,5},{8,10},{9,11},{10,... | collective-permute-start | bytes 12296 | tf_op jit(solution)/shard_map/ppermute | solution.py:489
  61.6 3.0 %collective-permute-start.33 = (f32[4,256]{1,0:T(4,128)S(1)}, f32[4,256]{1,0:T(4,128)S(1)}, u32[]{:S(2)}, u32[]{:S(2)}) collective-permute-start(f32[4,256]{1,0:T(4,128)S(1)} %get-tuple-element.160), channel_id=1, source_target_pairs={{0,3},{1,2},{2,1},{3,0},{4,7},{5,6},{6,5},{7,4},{8,11},{9,10},{10,... | collective-permute-start | bytes 12296 | tf_op jit(solution)/shard_map/ppermute | solution.py:489
  67.8 5.4 %collective-permute-start.37 = (f32[5,256]{1,0:T(8,128)S(1)}, f32[5,256]{1,0:T(8,128)S(1)}, u32[]{:S(2)}, u32[]{:S(2)}) collective-permute-start(f32[5,256]{1,0:T(8,128)S(1)} %get-tuple-element.170), channel_id=1, source_target_pairs={{0,2},{1,3},{2,0},{3,1},{4,6},{5,7},{6,4},{7,5},{8,10},{9,11},{10,... | collective-permute-start | bytes 15368 | tf_op jit(solution)/shard_map/ppermute | solution.py:489
  68.5 4.8 %collective-permute-start.36 = (f32[9,512]{1,0:T(8,128)S(1)}, f32[9,512]{1,0:T(8,128)S(1)}, u32[]{:S(2)}, u32[]{:S(2)}) collective-permute-start(f32[9,512]{1,0:T(8,128)S(1)} %get-tuple-element.169), channel_id=1, source_target_pairs={{0,1},{1,0},{2,3},{3,2},{4,5},{5,4},{6,7},{7,6},{8,9},{9,8},{10,11... | collective-permute-start | bytes 55304 | tf_op jit(solution)/shard_map/ppermute | solution.py:489
  68.5 4.8 %collective-permute-start.38 = (f32[9,512]{1,0:T(8,128)S(1)}, f32[9,512]{1,0:T(8,128)S(1)}, u32[]{:S(2)}, u32[]{:S(2)}) collective-permute-start(f32[9,512]{1,0:T(8,128)S(1)} %get-tuple-element.171), channel_id=1, source_target_pairs={{0,3},{1,2},{2,1},{3,0},{4,7},{5,6},{6,5},{7,4},{8,11},{9,10},{10,... | collective-permute-start | bytes 55304 | tf_op jit(solution)/shard_map/ppermute | solution.py:489
  70.4 13.9 %collective-permute-start.34 = (f32[3,16,512]{2,1,0:T(8,128)S(1)}, f32[3,16,512]{2,1,0:T(8,128)S(1)}, u32[]{:S(2)}, u32[]{:S(2)}) collective-permute-start(f32[3,16,512]{2,1,0:T(8,128)S(1)} %get-tuple-element.166), channel_id=1, source_target_pairs={{0,4},{4,0},{8,12},{12,8},{16,20},{20,16},{24,28},{28,24},{1,5},{5... | collective-permute-start | bytes 294920 | tf_op jit(solution)/shard_map/ppermute | solution.py:39
  70.6 13.8 %collective-permute-start.35 = (f32[3,16,512]{2,1,0:T(8,128)S(1)}, f32[3,16,512]{2,1,0:T(8,128)S(1)}, u32[]{:S(2)}, u32[]{:S(2)}) collective-permute-start(f32[3,16,512]{2,1,0:T(8,128)S(1)} %get-tuple-element.167), channel_id=1, source_target_pairs={{0,28},{4,8},{8,4},{12,16},{16,12},{20,24},{24,20},{28,0},{1,29},{... | collective-permute-start | bytes 294920 | tf_op jit(solution)/shard_map/ppermute | solution.py:39
  73.2 3.7 %collective-permute-start.40 = (f32[1,256]{1,0:T(1,128)S(1)}, f32[1,256]{1,0:T(1,128)S(1)}, u32[]{:S(2)}, u32[]{:S(2)}) collective-permute-start(f32[1,256]{1,0:T(1,128)S(1)} %shard_map.121.mine), channel_id=1, source_target_pairs={{0,4},{1,13},{2,22},{3,31},{4,0},{5,9},{6,18},{7,27},{8,12},{9,5},... | collective-permute-start | bytes 3080 | tf_op jit(solution)/shard_map/ppermute | solution.py:221
  73.3 3.7 %collective-permute-start.39 = (f32[1,256]{1,0:T(1,128)S(1)}, f32[1,256]{1,0:T(1,128)S(1)}, u32[]{:S(2)}, u32[]{:S(2)}) collective-permute-start(f32[1,256]{1,0:T(1,128)S(1)} %shard_map.121.mine), channel_id=1, source_target_pairs={{0,4},{1,9},{2,18},{3,27},{4,0},{5,13},{6,22},{7,31},{8,12},{9,1},... | collective-permute-start | bytes 3080 | tf_op jit(solution)/shard_map/ppermute | solution.py:221
  77.1 4.2 %collective-permute-start.41 = (f32[5,256]{1,0:T(8,128)S(1)}, f32[5,256]{1,0:T(8,128)S(1)}, u32[]{:S(2)}, u32[]{:S(2)}) collective-permute-start(f32[5,256]{1,0:T(8,128)S(1)} %get-tuple-element.177), channel_id=1, source_target_pairs={{0,1},{1,0},{2,3},{3,2},{4,5},{5,4},{6,7},{7,6},{8,9},{9,8},{10,11... | collective-permute-start | bytes 15368 | tf_op jit(solution)/shard_map/ppermute | solution.py:489
  77.2 5.7 %collective-permute-start.42 = (f32[5,256]{1,0:T(8,128)S(1)}, f32[5,256]{1,0:T(8,128)S(1)}, u32[]{:S(2)}, u32[]{:S(2)}) collective-permute-start(f32[5,256]{1,0:T(8,128)S(1)} %get-tuple-element.178), channel_id=1, source_target_pairs={{0,2},{1,3},{2,0},{3,1},{4,6},{5,7},{6,4},{7,5},{8,10},{9,11},{10,... | collective-permute-start | bytes 15368 | tf_op jit(solution)/shard_map/ppermute | solution.py:489
  81.3 3.1 %collective-permute-start.43 = (f32[5,256]{1,0:T(8,128)S(1)}, f32[5,256]{1,0:T(8,128)S(1)}, u32[]{:S(2)}, u32[]{:S(2)}) collective-permute-start(f32[5,256]{1,0:T(8,128)S(1)} %get-tuple-element.179), channel_id=1, source_target_pairs={{0,3},{1,2},{2,1},{3,0},{4,7},{5,6},{6,5},{7,4},{8,11},{9,10},{10,... | collective-permute-start | bytes 15368 | tf_op jit(solution)/shard_map/ppermute | solution.py:489
  86.6 4.8 %collective-permute-start.47 = (f32[4,256]{1,0:T(4,128)S(1)}, f32[4,256]{1,0:T(4,128)S(1)}, u32[]{:S(2)}, u32[]{:S(2)}) collective-permute-start(f32[4,256]{1,0:T(4,128)S(1)} %get-tuple-element.190), channel_id=1, source_target_pairs={{0,2},{1,3},{2,0},{3,1},{4,6},{5,7},{6,4},{7,5},{8,10},{9,11},{10,... | collective-permute-start | bytes 12296 | tf_op jit(solution)/shard_map/ppermute | solution.py:489
  87.2 4.1 %collective-permute-start.46 = (f32[8,512]{1,0:T(8,128)S(1)}, f32[8,512]{1,0:T(8,128)S(1)}, u32[]{:S(2)}, u32[]{:S(2)}) collective-permute-start(f32[8,512]{1,0:T(8,128)S(1)} %get-tuple-element.189), channel_id=1, source_target_pairs={{0,1},{1,0},{2,3},{3,2},{4,5},{5,4},{6,7},{7,6},{8,9},{9,8},{10,11... | collective-permute-start | bytes 49160 | tf_op jit(solution)/shard_map/ppermute | solution.py:489
  87.2 4.1 %collective-permute-start.48 = (f32[8,512]{1,0:T(8,128)S(1)}, f32[8,512]{1,0:T(8,128)S(1)}, u32[]{:S(2)}, u32[]{:S(2)}) collective-permute-start(f32[8,512]{1,0:T(8,128)S(1)} %get-tuple-element.191), channel_id=1, source_target_pairs={{0,3},{1,2},{2,1},{3,0},{4,7},{5,6},{6,5},{7,4},{8,11},{9,10},{10,... | collective-permute-start | bytes 49160 | tf_op jit(solution)/shard_map/ppermute | solution.py:489
  89.2 7.5 %collective-permute-start.44 = (f32[3,16,512]{2,1,0:T(8,128)S(1)}, f32[3,16,512]{2,1,0:T(8,128)S(1)}, u32[]{:S(2)}, u32[]{:S(2)}) collective-permute-start(f32[3,16,512]{2,1,0:T(8,128)S(1)} %get-tuple-element.186), channel_id=1, source_target_pairs={{0,4},{4,0},{8,12},{12,8},{16,20},{20,16},{24,28},{28,24},{1,5},{5... | collective-permute-start | bytes 294920 | tf_op jit(solution)/shard_map/ppermute | solution.py:39
  89.3 7.4 %collective-permute-start.45 = (f32[3,16,512]{2,1,0:T(8,128)S(1)}, f32[3,16,512]{2,1,0:T(8,128)S(1)}, u32[]{:S(2)}, u32[]{:S(2)}) collective-permute-start(f32[3,16,512]{2,1,0:T(8,128)S(1)} %get-tuple-element.187), channel_id=1, source_target_pairs={{0,28},{4,8},{8,4},{12,16},{16,12},{20,24},{24,20},{28,0},{1,29},{... | collective-permute-start | bytes 294920 | tf_op jit(solution)/shard_map/ppermute | solution.py:39
  92.6 3.7 %collective-permute-start.50 = (f32[4,256]{1,0:T(4,128)S(1)}, f32[4,256]{1,0:T(4,128)S(1)}, u32[]{:S(2)}, u32[]{:S(2)}) collective-permute-start(f32[4,256]{1,0:T(4,128)S(1)} %get-tuple-element.194), channel_id=1, source_target_pairs={{0,2},{1,3},{2,0},{3,1},{4,6},{5,7},{6,4},{7,5},{8,10},{9,11},{10,... | collective-permute-start | bytes 12296 | tf_op jit(solution)/shard_map/ppermute | solution.py:489
  93.6 3.1 %collective-permute-start.51 = (f32[4,256]{1,0:T(4,128)S(1)}, f32[4,256]{1,0:T(4,128)S(1)}, u32[]{:S(2)}, u32[]{:S(2)}) collective-permute-start(f32[4,256]{1,0:T(4,128)S(1)} %get-tuple-element.195), channel_id=1, source_target_pairs={{0,3},{1,2},{2,1},{3,0},{4,7},{5,6},{6,5},{7,4},{8,11},{9,10},{10,... | collective-permute-start | bytes 12296 | tf_op jit(solution)/shard_map/ppermute | solution.py:489
  (14 other events, 37.0 us)

commit v5 on v4

--- a/solution.py
+++ b/solution.py
@@ -154,24 +154,24 @@
     return coupled
 
 
-def solve_well(coupled, first, second):
+def solve_well(coupled, first, second, transposed=False):
     high = coupled.astype(BF16).astype(F32)
     low = coupled - high
     rows = lax.broadcasted_iota(jnp.int32, (16, coupled.shape[1]), 0)
     left = jnp.where(rows == 0, high, jnp.where(rows == 1, low, 0.0)).astype(BF16)
-    return jnp.sum(dot(left, first, True) + dot(left, second, True), axis=0, keepdims=True)
-
-
-def scatter_well(value, place, column, weight, rows, b):
+    total = dot(left, first, transposed) + dot(left, second, transposed)
+    return jnp.sum(total, axis=0, keepdims=True)
+
+
+def scatter_block(value, column, weight, rows, b):
     components, _, segb = weight.shape
     per = rows // components
-    part = slice(b * segb, (b + 1) * segb)
     here = lax.broadcasted_iota(jnp.int32, (per, segb), 0) == column[b : b + 1, :]
     blocks = [
         jnp.where(here, weight[i, b : b + 1] * value, 0.0) for i in range(components)
     ]
     high, low = halves(jnp.concatenate(blocks, axis=0))
-    return dot(jnp.concatenate([high, low], axis=0), place[:, part], True)
+    return jnp.concatenate([high, low], axis=0)
 
 
 def stencil_kernel(vec, trans, diag, *refs):
@@ -180,7 +180,8 @@
     inner_stencil(vec, trans, diag, shifted, out)
 
 
-def first_stencil_kernel(vec, trans, acc, after, out, diag, shifted):
+def first_stencil_kernel(vec, trans, acc, place, after, out, diag, placed, shifted):
+    placed[...] = place[...].T
     for i in range(acc.shape[0]):
         for j in range(acc.shape[1]):
             total = acc[i, j]
@@ -210,12 +211,16 @@
     return -(-count // groups)
 
 
+def share_mask(g, q, groups):
+    return q * groups + (g if q % 2 == 0 else groups - 1 - g)
+
+
 def share_swap(row, q):
     count, groups = lax.axis_size("res"), lax.axis_size("grp")
     pairs = []
     for r in range(count):
         for g in range(groups):
-            mask = g * share(count, groups) + q
+            mask = share_mask(g, q, groups)
             mask = mask if 0 < mask < count else 1
             pairs.append((r * groups + g, (r ^ mask) * groups + g))
     return lax.ppermute(row, ("res", "grp"), pairs)
@@ -269,15 +274,16 @@
                     )
 
 
-def solve_kernel(groups, first, second, *refs):
+def solve_kernel(groups, transposed, first, second, *refs):
     sent, back = refs[:groups], refs[groups:]
     g = lax.axis_index("grp")
-    capacity, segb = first.shape[1], first.shape[2]
+    capacity, segb = back[0].shape
     for k in range(groups):
         home = jnp.bitwise_xor(g, k)
         for slot in range(capacity):
             coupled = sent[k][spot(sent[k], slot, segb)]
-            back[k][slot : slot + 1] = solve_well(coupled, first[home, slot], second[home, slot])
+            value = solve_well(coupled, first[home, slot], second[home, slot], transposed)
+            back[k][slot : slot + 1] = value
 
 
 def group_sum_kernel(capacity, *refs):
@@ -295,7 +301,7 @@
     count, g = lax.axis_size("res"), lax.axis_index("grp")
     row = jnp.where(g == 0, mine[...], 0.0)
     for q, ref in enumerate(fetched):
-        mask = g * len(fetched) + q
+        mask = share_mask(g, q, groups)
         row = row + jnp.where((mask > 0) & (mask < count), ref[...], 0.0)
     capacity = values[0].shape[0]
     for value, out in zip(values, outs):
@@ -303,21 +309,21 @@
         out[capacity : capacity + 1] = row
 
 
-def well_terms(values, place, column, give, owner, capacity, shape):
+def well_terms(values, placed, column, give, owner, capacity, shape):
     components, cells_x, cells_y, cells_z = shape
     rows = components * cells_x * cells_y
     wells, segb = column.shape
     slots = lax.broadcasted_iota(jnp.int32, (capacity, segb), 0)
     where = places(owner, capacity, wells)
     values = [ref[0:capacity] for ref in values]
-    total = None
+    blocks = []
     for b in range(wells):
         value = jnp.zeros((capacity, segb), F32)
         for k, rows_of in enumerate(values):
             value = value + jnp.where(slots == where[b] - k * capacity, rows_of, 0.0)
         value = jnp.sum(value, axis=0, keepdims=True)
-        term = scatter_well(value, place, column, give, rows, b)
-        total = term if total is None else total + term
+        blocks.append(scatter_block(value, column, give, rows, b))
+    total = dot(jnp.concatenate(blocks, axis=1), placed[...])
     return (total[:rows] + total[rows:]).reshape(shape)
 
 
@@ -356,18 +362,26 @@
             first[h, slot], second[h, slot] = halves(inverse[h, slot])
 
 
+def turn_kernel(first, second, after, first_out, second_out):
+    for h in range(first.shape[0]):
+        for slot in range(first.shape[1]):
+            first_out[h, slot] = first[h, slot].T
+            second_out[h, slot] = second[h, slot].T
+
+
 class Arrived:
     def __init__(self, groups, capacity, refs):
         self.capacity, self.groups = capacity, groups
-        self.part, self.trans, self.place, self.column, self.take, self.give, self.owner = refs[:7]
-        self.halo = refs[7:9]
-        self.messages = refs[9 : 9 + groups]
-        self.values = refs[9 + groups : 9 + 2 * groups]
-        self.rest = refs[9 + 2 * groups :]
+        self.part, self.trans, self.place, self.placed, self.column = refs[:5]
+        self.take, self.give, self.owner = refs[5:8]
+        self.halo = refs[8:10]
+        self.messages = refs[10 : 10 + groups]
+        self.values = refs[10 + groups : 10 + 2 * groups]
+        self.rest = refs[10 + 2 * groups :]
 
     def result(self):
         wells = well_terms(
-            self.values, self.place, self.column, self.give, self.owner, self.capacity, self.part.shape
+            self.values, self.placed, self.column, self.give, self.owner, self.capacity, self.part.shape
         )
         terms = halo_terms(self.halo, self.messages, self.trans)
         return lambda i, x: self.part[i, x] - wells[i, x] - terms(i, x)
@@ -544,19 +558,20 @@
         ],
         limit=START_LIMIT,
     )
-    first, second = call(split_kernel, [(inverse.shape[1:], BF16)] * 2, [inverse[0]])
     shifted = [pltpu.VMEM((4,) + b.shape, F32)]
     cost = dict(scratch=shifted, flops=200_000_000, moved=4_000_000)
 
-    def finish(kernel, outs, part, messages, faces, extra, with_sums=False):
-        halo = exchange(faces)
-        values = call(
-            functools.partial(solve_kernel, groups),
+    def solve(transposed, given):
+        return call(
+            functools.partial(solve_kernel, groups, transposed),
             [((capacity, segb), F32)] * groups,
-            [first, second, *messages],
+            given,
             flops=SOLVE_FLOPS,
             moved=4_000_000,
         )
+
+    def finish(kernel, outs, part, messages, values, faces, extra, with_sums=False):
+        halo = exchange(faces)
         if with_sums:
             mine = call(
                 functools.partial(group_sum_kernel, capacity), [((1, segb), F32)], messages
@@ -568,25 +583,31 @@
                 [mine, *values, *fetched],
             )
         values = swapped(values)
-        args = [part, trans, place, column, take, give, owner, *halo, *messages, *values, *extra]
+        args = [part, trans, place, placed, column, take, give, owner]
+        args += [*halo, *messages, *values, *extra]
         specs = [VMEM] * len(args)
-        specs[6] = SMEM
+        specs[7] = SMEM
         return call(kernel, outs, args, specs, flops=1_000_000_000, moved=8_000_000)
 
     def apply(kernel, outs, vec, sends, extra, with_sums=False):
         messages = swapped(sends)
         *faces, part = call(stencil_kernel, face_outs + [field], [vec, trans, diag], **cost)
-        return finish(kernel, outs, part, messages, faces, extra, with_sums)
+        values = solve(False, [first, second, *messages])
+        return finish(kernel, outs, part, messages, values, faces, extra, with_sums)
 
     messages, faces = swapped(sends[:groups]), sends[groups:]
-    part, diag = call(
+    kept = [(inverse.shape[1:], BF16)] * 2
+    first, second = call(split_kernel, kept, [inverse[0]])
+    values = solve(True, [first, second, *messages])
+    part, diag, placed = call(
         first_stencil_kernel,
-        [field, (accumulation.shape, F32)],
-        [b, trans, accumulation, messages[1]],
+        [field, (accumulation.shape, F32), ((wells * segb, cells_z), BF16)],
+        [b, trans, accumulation, place, messages[1]],
         **cost,
     )
+    first, second = call(turn_kernel, kept, [first, second, values[0]])
     w, *sends = finish(
-        functools.partial(apply_kernel, sizes), [field] + plain, part, messages, faces, []
+        functools.partial(apply_kernel, sizes), [field] + plain, part, messages, values, faces, []
     )
     r, s, p, x = b, w, b, None
     for index in range(ITERS):

time: 111 us -> 110 us (level)
  waiting for transfers between devices: 17.2 us -> 19.9 us
  Pallas kernels: 28.2 us -> 25.7 us
    ppermute x4, waiting for transfers between devices: 1.56 us -> 7.03 us  [share_swap(): return lax.ppermute(row, ('res', 'grp'), pairs)]
    ppermute x36, starting transfers between devices: 30 us -> 25.8 us  [swapped(): lax.ppermute(messages[k], 'grp', [(i, i ^ k) for i in range(groups)])]
    ppermute x12, starting transfers between devices: 17.3 us -> 20.3 us  [exchange(): lax.ppermute(face, 'res', pairs)]
    pallas_call x25 -> x26, Pallas kernels: 28.2 us -> 25.7 us  [call(): pl.pallas_call(kernel, out_shape=[jax.ShapeDtypeStruct(shape, dtype) for...]
    ppermute x36, waiting for transfers between devices: 14.6 us -> 12.5 us  [swapped(): lax.ppermute(messages[k], 'grp', [(i, i ^ k) for i in range(groups)])]
  transfers between devices with their start and end apart: 52 -> 52, of which waited for: 18 -> 17; matrix products, arithmetic and copies ran while one was open for 0% -> 0% of each run, Pallas kernels for 10% -> 9%
where the time goes in v5:
time: 110 us
  starting transfers between devices  51.1 us (46%)
  Pallas kernels  25.7 us (23%)
  waiting for transfers between devices  19.9 us (18%)
  blocking collectives  10.2 us (9%)
  local copies, waits for them, and re-layouts  2.23 us (2%)
    ppermute x36, starting transfers between devices, swapped(): lax.ppermute(messages[k], 'grp', [(i, i ^ k) for i in range(groups)])  25.8 us
    pallas_call x26, Pallas kernels, call(): pl.pallas_call(kernel, out_shape=[jax.ShapeDtypeStruct(shape, dtype) for...  25.7 us
    ppermute x12, starting transfers between devices, exchange(): lax.ppermute(face, 'res', pairs)  20.3 us
    ppermute x36, waiting for transfers between devices, swapped(): lax.ppermute(messages[k], 'grp', [(i, i ^ k) for i in range(groups)])  12.5 us
    all_to_all x1, blocking collectives, body(): lax.all_to_all(sends[0], ('res', 'grp'), split_axis=0, concat_axis=0, til...  10.2 us
    ppermute x4, waiting for transfers between devices, share_swap(): return lax.ppermute(row, ('res', 'grp'), pairs)  7.03 us
    ppermute x4, starting transfers between devices, share_swap(): return lax.ppermute(row, ('res', 'grp'), pairs)  5 us
    unnamed x20, local copies, waits for them, and re-layouts  2.23 us
  transfers between devices with their start and end apart: 52, of which 17 were waited for; matrix products, arithmetic and copies ran while one was open for 0% of the time, Pallas kernels for 9%

profile of v5, /device:TPU:0, one launch (start us, length us, event | category | flops | bytes accessed | tf_op | source)
XLA Modules:
  0.0 110.2 jit_solution(6318758142926442932)
XLA Ops:
  0.6 3.2 %shard_map.104 = (bf16[512,2048]{1,0:T(8,128)(2,1)}, s32[8,256]{1,0:T(8,128)}, f32[3,8,256]{2,1,0:T(8,128)}, f32[3,8,256]{2,1,0:T(8,128)}, f32[4,256]{1,0:T(4,12...) custom-call(f32[3,2,16,512]{3,2,1,0:T(8,128)} %refs_18_.7, ...), custom_call_target="tpu_custom_call" | custom-call | flops 1000000 | bytes 1000000 | tf_op jit(solution)/shard_map/pallas_call | solution.py:24
  4.3 2.6 %collective-permute-start.4 = (f32[8,512]{1,0:T(8,128)}, f32[8,512]{1,0:T(8,128)S(1)}, u32[]{:S(2)}, u32[]{:S(2)}) collective-permute-start(f32[8,512]{1,0:T(8,128)} %get-tuple-element.117), channel_id=1, source_target_pairs={{0,3},{1,2},{2,1},{3,0},{4,7},{5,6},{6,5},{7,4},{8,11},{9,10},{10,... | collective-permute-start | bytes 49160 | tf_op jit(solution)/shard_map/ppermute | solution.py:503
  7.0 2.0 %collective-permute-start.1 = (f32[3,16,512]{2,1,0:T(8,128)}, f32[3,16,512]{2,1,0:T(8,128)S(1)}, u32[]{:S(2)}, u32[]{:S(2)}) collective-permute-start(f32[3,16,512]{2,1,0:T(8,128)} %get-tuple-element.113), channel_id=1, source_target_pairs={{0,4},{4,0},{8,12},{12,8},{16,20},{20,16},{24,28},{28,24},{1,5},{5... | collective-permute-start | bytes 294920 | tf_op jit(solution)/shard_map/ppermute | solution.py:39
  9.0 3.6 %collective-permute-start.2 = (f32[3,16,512]{2,1,0:T(8,128)}, f32[3,16,512]{2,1,0:T(8,128)S(1)}, u32[]{:S(2)}, u32[]{:S(2)}) collective-permute-start(f32[3,16,512]{2,1,0:T(8,128)} %get-tuple-element.114), channel_id=1, source_target_pairs={{0,28},{4,8},{8,4},{12,16},{16,12},{20,24},{24,20},{28,0},{1,29},{... | collective-permute-start | bytes 294920 | tf_op jit(solution)/shard_map/ppermute | solution.py:39
  12.5 2.2 %copy-done.3 = f32[1,4,4,256,256]{4,3,2,1,0:T(8,128)S(1)} copy-done((f32[1,4,4,256,256]{4,3,2,1,0:T(8,128)S(1)}, f32[1,4,4,256,256]{4,3,2,1,0:T(8,128)}, u32[]{:S(2)}) %copy-start.3) | copy-done | bytes 4194328
  15.5 1.2 %shard_map.107 = (f32[4,256]{1,0:T(4,128)S(1)}, f32[4,256]{1,0:T(4,128)S(1)}, f32[4,256]{1,0:T(4,128)S(1)}, f32[4,256]{1,0:T(4,128)S(1)}) custom-call(bf16[4,4,256,256]{3,2,1,0:T(8,128)(2,1)S(1)} %get-tuple-element.118.first, bf16[4,4,256,256]{3,2,1,0:T(8,128)(2,1)S(1)} %get-tuple-element.119.second, f32[4,256]{1,0:T(4,128)S(1)} %copy-done.9, ...), custom_call_target="tpu_custom_call" | custom-call | flops 5000000000 | bytes 4000000 | tf_op jit(solution)/shard_map/pallas_call | solution.py:24
  16.8 1.6 %collective-permute-start.6 = (f32[4,256]{1,0:T(4,128)S(1)}, f32[4,256]{1,0:T(4,128)S(1)}, u32[]{:S(2)}, u32[]{:S(2)}) collective-permute-start(f32[4,256]{1,0:T(4,128)S(1)} %get-tuple-element.122), channel_id=1, source_target_pairs={{0,2},{1,3},{2,0},{3,1},{4,6},{5,7},{6,4},{7,5},{8,10},{9,11},{10,... | collective-permute-start | bytes 12296 | tf_op jit(solution)/shard_map/ppermute | solution.py:503
  18.7 1.3 %shard_map.105 = (f32[3,2,16,512]{3,2,1,0:T(8,128)S(1)}, f32[3,3,2,16,512]{4,3,2,1,0:T(8,128)S(1)}, bf16[2048,512]{1,0:T(8,128)(2,1)S(1)}) custom-call(f32[3,2,16,512]{3,2,1,0:T(8,128)S(1)} %copy-done.2, f32[6,3,3,2,16,512]{5,4,3,2,1,0:T(8,128)S(1)} %copy-done, f32[3,3,2,16,512]{4,3,2,1,0:T(8,128)S(1)} %copy-done.6, bf16[512,2048]{1,0:T(8,128)(2,1)S(1)} %copy-done.1, ...), custom_call_target="tpu_custom_call" | custom-call | flops 200000000 | bytes 4000000 | tf_op jit(solution)/shard_map/pallas_call | solution.py:24
  20.0 1.1 %shard_map.110 = (bf16[4,4,256,256]{3,2,1,0:T(8,128)(2,1)S(1)}, bf16[4,4,256,256]{3,2,1,0:T(8,128)(2,1)S(1)}) custom-call(bf16[4,4,256,256]{3,2,1,0:T(8,128)(2,1)S(1)} %get-tuple-element.118.first, bf16[4,4,256,256]{3,2,1,0:T(8,128)(2,1)S(1)} %get-tuple-element.119.second, f32[4,256]{1,0:T(4,128)S(1)} %get-tuple-element.120.refs_14_.after), custom_call_target="tpu_custom_call" | custom-call | flops 1000000 | bytes 1000000 | tf_op jit(solution)/shard_map/pallas_call | solution.py:24
  21.4 1.8 %shard_map.108 = (f32[3,2,16,512]{3,2,1,0:T(8,128)S(1)}, f32[4,256]{1,0:T(4,128)S(1)}, f32[8,512]{1,0:T(8,128)S(1)}, f32[4,256]{1,0:T(4,128)S(1)}, f32[8,512]{1,0:T(8,128)S(1)}) custom-call(f32[3,2,16,512]{3,2,1,0:T(8,128)S(1)} %get-tuple-element.108.refs_0_, f32[6,3,3,2,16,512]{5,4,3,2,1,0:T(8,128)S(1)} %copy-done, bf16[512,2048]{1,0:T(8,128)(2,1)S(1)} %copy-done.1, ...), custom_call_target="tpu_custom_call" | custom-call | flops 1000000000 | bytes 8000000 | tf_op jit(solution)/shard_map/pallas_call | solution.py:24
  23.4 1.2 %collective-permute-start.12 = (f32[8,512]{1,0:T(8,128)S(1)}, f32[8,512]{1,0:T(8,128)S(1)}, u32[]{:S(2)}, u32[]{:S(2)}) collective-permute-start(f32[8,512]{1,0:T(8,128)S(1)} %get-tuple-element.132), channel_id=1, source_target_pairs={{0,3},{1,2},{2,1},{3,0},{4,7},{5,6},{6,5},{7,4},{8,11},{9,10},{10,... | collective-permute-start | bytes 49160 | tf_op jit(solution)/shard_map/ppermute | solution.py:503
  25.9 1.9 %collective-permute-start.9 = (f32[3,16,512]{2,1,0:T(8,128)S(1)}, f32[3,16,512]{2,1,0:T(8,128)S(1)}, u32[]{:S(2)}, u32[]{:S(2)}) collective-permute-start(f32[3,16,512]{2,1,0:T(8,128)S(1)} %get-tuple-element.128), channel_id=1, source_target_pairs={{0,28},{4,8},{8,4},{12,16},{16,12},{20,24},{24,20},{28,0},{1,29},{... | collective-permute-start | bytes 294920 | tf_op jit(solution)/shard_map/ppermute | solution.py:39
  29.1 0.9 collective-permute-start.14
  30.0 1.0 collective-permute-start.15
  30.9 1.8 %collective-permute-done.14.refs_16_ = f32[4,256]{1,0:T(4,128)S(1)} collective-permute-done((f32[4,256]{1,0:T(4,128)S(1)}, f32[4,256]{1,0:T(4,128)S(1)}, u32[]{:S(2)}, u32[]{:S(2)}) %collective-permute-start.14) | collective-permute-done | bytes 4128 | tf_op jit(solution)/shard_map/ppermute | solution.py:503
  33.3 1.9 %shard_map.112 = (f32[3,2,16,512]{3,2,1,0:T(8,128)S(1)}, f32[5,256]{1,0:T(8,128)S(1)}, f32[9,512]{1,0:T(8,128)S(1)}, f32[5,256]{1,0:T(8,128)S(1)}, f32[9,512]{1,0:T(8,128)S(1)}) custom-call(f32[3,2,16,512]{3,2,1,0:T(8,128)S(1)} %get-tuple-element.126.refs_0_, f32[6,3,3,2,16,512]{5,4,3,2,1,0:T(8,128)S(1)} %copy-done, bf16[512,2048]{1,0:T(8,128)(2,1)S(1)} %copy-done.1, ...), custom_call_target="tpu_custom_call" | custom-call | flops 1000000000 | bytes 8000000 | tf_op jit(solution)/shard_map/pallas_call | solution.py:24
  35.4 1.4 %collective-permute-start.20 = (f32[9,512]{1,0:T(8,128)S(1)}, f32[9,512]{1,0:T(8,128)S(1)}, u32[]{:S(2)}, u32[]{:S(2)}) collective-permute-start(f32[9,512]{1,0:T(8,128)S(1)} %get-tuple-element.146), channel_id=1, source_target_pairs={{0,3},{1,2},{2,1},{3,0},{4,7},{5,6},{6,5},{7,4},{8,11},{9,10},{10,... | collective-permute-start | bytes 55304 | tf_op jit(solution)/shard_map/ppermute | solution.py:503
  38.2 2.4 %collective-permute-start.17 = (f32[3,16,512]{2,1,0:T(8,128)S(1)}, f32[3,16,512]{2,1,0:T(8,128)S(1)}, u32[]{:S(2)}, u32[]{:S(2)}) collective-permute-start(f32[3,16,512]{2,1,0:T(8,128)S(1)} %get-tuple-element.142), channel_id=1, source_target_pairs={{0,28},{4,8},{8,4},{12,16},{16,12},{20,24},{24,20},{28,0},{1,29},{... | collective-permute-start | bytes 294920 | tf_op jit(solution)/shard_map/ppermute | solution.py:39
  41.3 1.8 %collective-permute-start.22 = (f32[1,256]{1,0:T(1,128)S(1)}, f32[1,256]{1,0:T(1,128)S(1)}, u32[]{:S(2)}, u32[]{:S(2)}) collective-permute-start(f32[1,256]{1,0:T(1,128)S(1)} %shard_map.114.mine), channel_id=1, source_target_pairs={{0,28},{1,25},{2,22},{3,19},{4,24},{5,29},{6,18},{7,23},{8,20},{9,... | collective-permute-start | bytes 3080 | tf_op jit(solution)/shard_map/ppermute | solution.py:226
  44.2 3.4 %collective-permute-done.22.refs_5_ = f32[1,256]{1,0:T(1,128)S(1)} collective-permute-done((f32[1,256]{1,0:T(1,128)S(1)}, f32[1,256]{1,0:T(1,128)S(1)}, u32[]{:S(2)}, u32[]{:S(2)}) %collective-permute-start.22) | collective-permute-done | bytes 1056 | tf_op jit(solution)/shard_map/ppermute | solution.py:226
  48.5 1.1 collective-permute-start.25
  49.5 1.9 %collective-permute-done.24.refs_16_ = f32[5,256]{1,0:T(8,128)S(1)} collective-permute-done((f32[5,256]{1,0:T(8,128)S(1)}, f32[5,256]{1,0:T(8,128)S(1)}, u32[]{:S(2)}, u32[]{:S(2)}) %collective-permute-start.24) | collective-permute-done | bytes 5152 | tf_op jit(solution)/shard_map/ppermute | solution.py:503
  51.5 1.9 %shard_map.117 = (f32[3,2,16,512]{3,2,1,0:T(8,128)S(1)}, f32[3,2,16,512]{3,2,1,0:T(8,128)S(1)}, f32[3,2,16,512]{3,2,1,0:T(8,128)S(1)}, f32[3,2,16,512]{3,2,1,0:T...) custom-call(f32[3,2,16,512]{3,2,1,0:T(8,128)S(1)} %get-tuple-element, ...), custom_call_target="tpu_custom_call" | custom-call | flops 1000000000 | bytes 8000000 | tf_op jit(solution)/shard_map/pallas_call | solution.py:24
  53.7 1.3 %collective-permute-start.30 = (f32[8,512]{1,0:T(8,128)S(1)}, f32[8,512]{1,0:T(8,128)S(1)}, u32[]{:S(2)}, u32[]{:S(2)}) collective-permute-start(f32[8,512]{1,0:T(8,128)S(1)} %get-tuple-element.162), channel_id=1, source_target_pairs={{0,3},{1,2},{2,1},{3,0},{4,7},{5,6},{6,5},{7,4},{8,11},{9,10},{10,... | collective-permute-start | bytes 49160 | tf_op jit(solution)/shard_map/ppermute | solution.py:503
  56.3 1.4 %collective-permute-start.26 = (f32[3,16,512]{2,1,0:T(8,128)S(1)}, f32[3,16,512]{2,1,0:T(8,128)S(1)}, u32[]{:S(2)}, u32[]{:S(2)}) collective-permute-start(f32[3,16,512]{2,1,0:T(8,128)S(1)} %get-tuple-element.157), channel_id=1, source_target_pairs={{0,4},{4,0},{8,12},{12,8},{16,20},{20,16},{24,28},{28,24},{1,5},{5... | collective-permute-start | bytes 294920 | tf_op jit(solution)/shard_map/ppermute | solution.py:39
  57.7 2.3 %collective-permute-start.27 = (f32[3,16,512]{2,1,0:T(8,128)S(1)}, f32[3,16,512]{2,1,0:T(8,128)S(1)}, u32[]{:S(2)}, u32[]{:S(2)}) collective-permute-start(f32[3,16,512]{2,1,0:T(8,128)S(1)} %get-tuple-element.158), channel_id=1, source_target_pairs={{0,28},{4,8},{8,4},{12,16},{16,12},{20,24},{24,20},{28,0},{1,29},{... | collective-permute-start | bytes 294920 | tf_op jit(solution)/shard_map/ppermute | solution.py:39
  60.8 1.5 %collective-permute-start.32 = (f32[4,256]{1,0:T(4,128)S(1)}, f32[4,256]{1,0:T(4,128)S(1)}, u32[]{:S(2)}, u32[]{:S(2)}) collective-permute-start(f32[4,256]{1,0:T(4,128)S(1)} %get-tuple-element.165), channel_id=1, source_target_pairs={{0,2},{1,3},{2,0},{3,1},{4,6},{5,7},{6,4},{7,5},{8,10},{9,11},{10,... | collective-permute-start | bytes 12296 | tf_op jit(solution)/shard_map/ppermute | solution.py:503
  62.7 1.8 %collective-permute-done.32.refs_16_ = f32[4,256]{1,0:T(4,128)S(1)} collective-permute-done((f32[4,256]{1,0:T(4,128)S(1)}, f32[4,256]{1,0:T(4,128)S(1)}, u32[]{:S(2)}, u32[]{:S(2)}) %collective-permute-start.32) | collective-permute-done | bytes 4128 | tf_op jit(solution)/shard_map/ppermute | solution.py:503
  64.5 0.8 collective-permute-done.33.refs_17_
  65.3 2.0 %shard_map.120 = (f32[3,2,16,512]{3,2,1,0:T(8,128)S(1)}, f32[3,2,16,512]{3,2,1,0:T(8,128)S(1)}, f32[3,2,16,512]{3,2,1,0:T(8,128)S(1)}, f32[5,256]{1,0:T(8,128)S(...) custom-call(f32[3,2,16,512]{3,2,1,0:T(8,128)S(1)} %get-tuple-element.156.refs_0_, ...), custom_call_target="tpu_custom_call" | custom-call | flops 1000000000 | bytes 8000000 | tf_op jit(solution)/shard_map/pallas_call | solution.py:24
  67.5 1.0 collective-permute-start.38
  68.5 1.0 collective-permute-start.37
  70.0 2.4 %collective-permute-start.35 = (f32[3,16,512]{2,1,0:T(8,128)S(1)}, f32[3,16,512]{2,1,0:T(8,128)S(1)}, u32[]{:S(2)}, u32[]{:S(2)}) collective-permute-start(f32[3,16,512]{2,1,0:T(8,128)S(1)} %get-tuple-element.173), channel_id=1, source_target_pairs={{0,28},{4,8},{8,4},{12,16},{16,12},{20,24},{24,20},{28,0},{1,29},{... | collective-permute-start | bytes 294920 | tf_op jit(solution)/shard_map/ppermute | solution.py:39
  72.5 2.4 %collective-permute-start.40 = (f32[1,256]{1,0:T(1,128)S(1)}, f32[1,256]{1,0:T(1,128)S(1)}, u32[]{:S(2)}, u32[]{:S(2)}) collective-permute-start(f32[1,256]{1,0:T(1,128)S(1)} %shard_map.122.mine), channel_id=1, source_target_pairs={{0,28},{1,25},{2,22},{3,19},{4,24},{5,29},{6,18},{7,23},{8,20},{9,... | collective-permute-start | bytes 3080 | tf_op jit(solution)/shard_map/ppermute | solution.py:226
  76.2 2.7 %collective-permute-done.40.refs_5_ = f32[1,256]{1,0:T(1,128)S(1)} collective-permute-done((f32[1,256]{1,0:T(1,128)S(1)}, f32[1,256]{1,0:T(1,128)S(1)}, u32[]{:S(2)}, u32[]{:S(2)}) %collective-permute-start.40) | collective-permute-done | bytes 1056 | tf_op jit(solution)/shard_map/ppermute | solution.py:226
  79.0 1.2 %collective-permute-start.42 = (f32[5,256]{1,0:T(8,128)S(1)}, f32[5,256]{1,0:T(8,128)S(1)}, u32[]{:S(2)}, u32[]{:S(2)}) collective-permute-start(f32[5,256]{1,0:T(8,128)S(1)} %get-tuple-element.184), channel_id=1, source_target_pairs={{0,2},{1,3},{2,0},{3,1},{4,6},{5,7},{6,4},{7,5},{8,10},{9,11},{10,... | collective-permute-start | bytes 15368 | tf_op jit(solution)/shard_map/ppermute | solution.py:503
  80.8 1.9 %collective-permute-done.42.refs_16_ = f32[5,256]{1,0:T(8,128)S(1)} collective-permute-done((f32[5,256]{1,0:T(8,128)S(1)}, f32[5,256]{1,0:T(8,128)S(1)}, u32[]{:S(2)}, u32[]{:S(2)}) %collective-permute-start.42) | collective-permute-done | bytes 5152 | tf_op jit(solution)/shard_map/ppermute | solution.py:503
  83.2 1.9 %shard_map.125 = (f32[3,2,16,512]{3,2,1,0:T(8,128)S(1)}, f32[3,2,16,512]{3,2,1,0:T(8,128)S(1)}, f32[3,2,16,512]{3,2,1,0:T(8,128)S(1)}, f32[3,2,16,512]{3,2,1,0:T...) custom-call(f32[3,2,16,512]{3,2,1,0:T(8,128)S(1)} %get-tuple-element, ...), custom_call_target="tpu_custom_call" | custom-call | flops 1000000000 | bytes 8000000 | tf_op jit(solution)/shard_map/pallas_call | solution.py:24
  85.4 0.8 collective-permute-start.48
  86.3 1.1 %collective-permute-start.47 = (f32[4,256]{1,0:T(4,128)S(1)}, f32[4,256]{1,0:T(4,128)S(1)}, u32[]{:S(2)}, u32[]{:S(2)}) collective-permute-start(f32[4,256]{1,0:T(4,128)S(1)} %get-tuple-element.196), channel_id=1, source_target_pairs={{0,2},{1,3},{2,0},{3,1},{4,6},{5,7},{6,4},{7,5},{8,10},{9,11},{10,... | collective-permute-start | bytes 12296 | tf_op jit(solution)/shard_map/ppermute | solution.py:503
  87.9 1.5 %collective-permute-start.44 = (f32[3,16,512]{2,1,0:T(8,128)S(1)}, f32[3,16,512]{2,1,0:T(8,128)S(1)}, u32[]{:S(2)}, u32[]{:S(2)}) collective-permute-start(f32[3,16,512]{2,1,0:T(8,128)S(1)} %get-tuple-element.192), channel_id=1, source_target_pairs={{0,4},{4,0},{8,12},{12,8},{16,20},{20,16},{24,28},{28,24},{1,5},{5... | collective-permute-start | bytes 294920 | tf_op jit(solution)/shard_map/ppermute | solution.py:39
  89.4 2.4 %collective-permute-start.45 = (f32[3,16,512]{2,1,0:T(8,128)S(1)}, f32[3,16,512]{2,1,0:T(8,128)S(1)}, u32[]{:S(2)}, u32[]{:S(2)}) collective-permute-start(f32[3,16,512]{2,1,0:T(8,128)S(1)} %get-tuple-element.193), channel_id=1, source_target_pairs={{0,28},{4,8},{8,4},{12,16},{16,12},{20,24},{24,20},{28,0},{1,29},{... | collective-permute-start | bytes 294920 | tf_op jit(solution)/shard_map/ppermute | solution.py:39
  92.5 1.5 %collective-permute-start.50 = (f32[4,256]{1,0:T(4,128)S(1)}, f32[4,256]{1,0:T(4,128)S(1)}, u32[]{:S(2)}, u32[]{:S(2)}) collective-permute-start(f32[4,256]{1,0:T(4,128)S(1)} %get-tuple-element.200), channel_id=1, source_target_pairs={{0,2},{1,3},{2,0},{3,1},{4,6},{5,7},{6,4},{7,5},{8,10},{9,11},{10,... | collective-permute-start | bytes 12296 | tf_op jit(solution)/shard_map/ppermute | solution.py:503
  94.4 1.8 %collective-permute-done.50.refs_16_ = f32[4,256]{1,0:T(4,128)S(1)} collective-permute-done((f32[4,256]{1,0:T(4,128)S(1)}, f32[4,256]{1,0:T(4,128)S(1)}, u32[]{:S(2)}, u32[]{:S(2)}) %collective-permute-start.50) | collective-permute-done | bytes 4128 | tf_op jit(solution)/shard_map/ppermute | solution.py:503
  96.2 0.8 collective-permute-done.51.refs_17_
  97.0 2.0 %shard_map.128 = (f32[3,2,16,512]{3,2,1,0:T(8,128)}, f32[3,2,16,512]{3,2,1,0:T(8,128)S(1)}, f32[3,2,16,512]{3,2,1,0:T(8,128)S(1)}, f32[32,1,128]{2,1,0:T(1,128)S(1)}) custom-call(f32[3,2,16,512]{3,2,1,0:T(8,128)S(1)} %get-tuple-element.191.refs_0_, f32[6,3,3,2,16,512]{5,4,3,2,1,0:T(8,128)S(1)} %copy-done, bf16[512,2048]{1,0:T(8,128)(2,1)S(1)} %copy-done.1, ...), custom_call_target="tpu_custom_call" | custom-call | flops 1000000000 | bytes 8000000 | tf_op jit(solution)/shard_map/pallas_call | solution.py:24
  99.0 10.2 %all_to_all.5.sums = f32[32,1,128]{2,1,0:T(1,128)S(1)} all-to-all(f32[32,1,128]{2,1,0:T(1,128)S(1)} %get-tuple-element.205), channel_id=1, replica_groups=mesh['res'=8,'grp'=4] {'res','grp'}, dimensions={0} | all-to-all | bytes 32768 | tf_op jit(solution)/shard_map/all_to_all | solution.py:635
  109.2 0.9 shard_map.129
  (103 shorter events, 17.5 us)
Async XLA Ops:
  3.8 11.6 %collective-permute-start = (f32[8,512]{1,0:T(8,128)}, f32[8,512]{1,0:T(8,128)S(1)}, u32[]{:S(2)}, u32[]{:S(2)}) collective-permute-start(f32[8,512]{1,0:T(8,128)} %get-tuple-element.107), channel_id=1, source_target_pairs={{0,1},{1,0},{2,3},{3,2},{4,5},{5,4},{6,7},{7,6},{8,9},{9,8},{10,11... | collective-permute-start | bytes 49160 | tf_op jit(solution)/shard_map/ppermute | solution.py:503
  4.3 11.1 %collective-permute-start.4 = (f32[8,512]{1,0:T(8,128)}, f32[8,512]{1,0:T(8,128)S(1)}, u32[]{:S(2)}, u32[]{:S(2)}) collective-permute-start(f32[8,512]{1,0:T(8,128)} %get-tuple-element.117), channel_id=1, source_target_pairs={{0,3},{1,2},{2,1},{3,0},{4,7},{5,6},{6,5},{7,4},{8,11},{9,10},{10,... | collective-permute-start | bytes 49160 | tf_op jit(solution)/shard_map/ppermute | solution.py:503
  7.0 8.4 %collective-permute-start.3 = (f32[4,256]{1,0:T(4,128)}, f32[4,256]{1,0:T(4,128)S(1)}, u32[]{:S(2)}, u32[]{:S(2)}) collective-permute-start(f32[4,256]{1,0:T(4,128)} %get-tuple-element.116), channel_id=1, source_target_pairs={{0,2},{1,3},{2,0},{3,1},{4,6},{5,7},{6,4},{7,5},{8,10},{9,11},{10,... | collective-permute-start | bytes 12296 | tf_op jit(solution)/shard_map/ppermute | solution.py:503
  7.0 14.4 %collective-permute-start.1 = (f32[3,16,512]{2,1,0:T(8,128)}, f32[3,16,512]{2,1,0:T(8,128)S(1)}, u32[]{:S(2)}, u32[]{:S(2)}) collective-permute-start(f32[3,16,512]{2,1,0:T(8,128)} %get-tuple-element.113), channel_id=1, source_target_pairs={{0,4},{4,0},{8,12},{12,8},{16,20},{20,16},{24,28},{28,24},{1,5},{5... | collective-permute-start | bytes 294920 | tf_op jit(solution)/shard_map/ppermute | solution.py:39
  9.0 12.4 %collective-permute-start.2 = (f32[3,16,512]{2,1,0:T(8,128)}, f32[3,16,512]{2,1,0:T(8,128)S(1)}, u32[]{:S(2)}, u32[]{:S(2)}) collective-permute-start(f32[3,16,512]{2,1,0:T(8,128)} %get-tuple-element.114), channel_id=1, source_target_pairs={{0,28},{4,8},{8,4},{12,16},{16,12},{20,24},{24,20},{28,0},{1,29},{... | collective-permute-start | bytes 294920 | tf_op jit(solution)/shard_map/ppermute | solution.py:39
  16.7 4.4 %collective-permute-start.5 = (f32[4,256]{1,0:T(4,128)S(1)}, f32[4,256]{1,0:T(4,128)S(1)}, u32[]{:S(2)}, u32[]{:S(2)}) collective-permute-start(f32[4,256]{1,0:T(4,128)S(1)} %get-tuple-element.121), channel_id=1, source_target_pairs={{0,1},{1,0},{2,3},{3,2},{4,5},{5,4},{6,7},{7,6},{8,9},{9,8},{10,11... | collective-permute-start | bytes 12296 | tf_op jit(solution)/shard_map/ppermute | solution.py:503
  16.8 4.3 %collective-permute-start.6 = (f32[4,256]{1,0:T(4,128)S(1)}, f32[4,256]{1,0:T(4,128)S(1)}, u32[]{:S(2)}, u32[]{:S(2)}) collective-permute-start(f32[4,256]{1,0:T(4,128)S(1)} %get-tuple-element.122), channel_id=1, source_target_pairs={{0,2},{1,3},{2,0},{3,1},{4,6},{5,7},{6,4},{7,5},{8,10},{9,11},{10,... | collective-permute-start | bytes 12296 | tf_op jit(solution)/shard_map/ppermute | solution.py:503
  18.4 3.0 %collective-permute-start.7 = (f32[4,256]{1,0:T(4,128)S(1)}, f32[4,256]{1,0:T(4,128)S(1)}, u32[]{:S(2)}, u32[]{:S(2)}) collective-permute-start(f32[4,256]{1,0:T(4,128)S(1)} %get-tuple-element.123), channel_id=1, source_target_pairs={{0,3},{1,2},{2,1},{3,0},{4,7},{5,6},{6,5},{7,4},{8,11},{9,10},{10,... | collective-permute-start | bytes 12296 | tf_op jit(solution)/shard_map/ppermute | solution.py:503
  23.2 5.1 %collective-permute-start.10 = (f32[8,512]{1,0:T(8,128)S(1)}, f32[8,512]{1,0:T(8,128)S(1)}, u32[]{:S(2)}, u32[]{:S(2)}) collective-permute-start(f32[8,512]{1,0:T(8,128)S(1)} %get-tuple-element.130), channel_id=1, source_target_pairs={{0,1},{1,0},{2,3},{3,2},{4,5},{5,4},{6,7},{7,6},{8,9},{9,8},{10,11... | collective-permute-start | bytes 49160 | tf_op jit(solution)/shard_map/ppermute | solution.py:503
  23.4 4.9 %collective-permute-start.12 = (f32[8,512]{1,0:T(8,128)S(1)}, f32[8,512]{1,0:T(8,128)S(1)}, u32[]{:S(2)}, u32[]{:S(2)}) collective-permute-start(f32[8,512]{1,0:T(8,128)S(1)} %get-tuple-element.132), channel_id=1, source_target_pairs={{0,3},{1,2},{2,1},{3,0},{4,7},{5,6},{6,5},{7,4},{8,11},{9,10},{10,... | collective-permute-start | bytes 49160 | tf_op jit(solution)/shard_map/ppermute | solution.py:503
  24.7 3.6 %collective-permute-start.11 = (f32[4,256]{1,0:T(4,128)S(1)}, f32[4,256]{1,0:T(4,128)S(1)}, u32[]{:S(2)}, u32[]{:S(2)}) collective-permute-start(f32[4,256]{1,0:T(4,128)S(1)} %get-tuple-element.131), channel_id=1, source_target_pairs={{0,2},{1,3},{2,0},{3,1},{4,6},{5,7},{6,4},{7,5},{8,10},{9,11},{10,... | collective-permute-start | bytes 12296 | tf_op jit(solution)/shard_map/ppermute | solution.py:503
  25.9 7.1 %collective-permute-start.8 = (f32[3,16,512]{2,1,0:T(8,128)S(1)}, f32[3,16,512]{2,1,0:T(8,128)S(1)}, u32[]{:S(2)}, u32[]{:S(2)}) collective-permute-start(f32[3,16,512]{2,1,0:T(8,128)S(1)} %get-tuple-element.127), channel_id=1, source_target_pairs={{0,4},{4,0},{8,12},{12,8},{16,20},{20,16},{24,28},{28,24},{1,5},{5... | collective-permute-start | bytes 294920 | tf_op jit(solution)/shard_map/ppermute | solution.py:39
  25.9 7.4 %collective-permute-start.9 = (f32[3,16,512]{2,1,0:T(8,128)S(1)}, f32[3,16,512]{2,1,0:T(8,128)S(1)}, u32[]{:S(2)}, u32[]{:S(2)}) collective-permute-start(f32[3,16,512]{2,1,0:T(8,128)S(1)} %get-tuple-element.128), channel_id=1, source_target_pairs={{0,28},{4,8},{8,4},{12,16},{16,12},{20,24},{24,20},{28,0},{1,29},{... | collective-permute-start | bytes 294920 | tf_op jit(solution)/shard_map/ppermute | solution.py:39
  29.0 1.9 %collective-permute-start.13 = (f32[4,256]{1,0:T(4,128)S(1)}, f32[4,256]{1,0:T(4,128)S(1)}, u32[]{:S(2)}, u32[]{:S(2)}) collective-permute-start(f32[4,256]{1,0:T(4,128)S(1)} %get-tuple-element.136), channel_id=1, source_target_pairs={{0,1},{1,0},{2,3},{3,2},{4,5},{5,4},{6,7},{7,6},{8,9},{9,8},{10,11... | collective-permute-start | bytes 12296 | tf_op jit(solution)/shard_map/ppermute | solution.py:503
  29.1 3.7 %collective-permute-start.14 = (f32[4,256]{1,0:T(4,128)S(1)}, f32[4,256]{1,0:T(4,128)S(1)}, u32[]{:S(2)}, u32[]{:S(2)}) collective-permute-start(f32[4,256]{1,0:T(4,128)S(1)} %get-tuple-element.137), channel_id=1, source_target_pairs={{0,2},{1,3},{2,0},{3,1},{4,6},{5,7},{6,4},{7,5},{8,10},{9,11},{10,... | collective-permute-start | bytes 12296 | tf_op jit(solution)/shard_map/ppermute | solution.py:503
  30.0 3.0 %collective-permute-start.15 = (f32[4,256]{1,0:T(4,128)S(1)}, f32[4,256]{1,0:T(4,128)S(1)}, u32[]{:S(2)}, u32[]{:S(2)}) collective-permute-start(f32[4,256]{1,0:T(4,128)S(1)} %get-tuple-element.138), channel_id=1, source_target_pairs={{0,3},{1,2},{2,1},{3,0},{4,7},{5,6},{6,5},{7,4},{8,11},{9,10},{10,... | collective-permute-start | bytes 12296 | tf_op jit(solution)/shard_map/ppermute | solution.py:503
  35.2 5.4 %collective-permute-start.18 = (f32[9,512]{1,0:T(8,128)S(1)}, f32[9,512]{1,0:T(8,128)S(1)}, u32[]{:S(2)}, u32[]{:S(2)}) collective-permute-start(f32[9,512]{1,0:T(8,128)S(1)} %get-tuple-element.144), channel_id=1, source_target_pairs={{0,1},{1,0},{2,3},{3,2},{4,5},{5,4},{6,7},{7,6},{8,9},{9,8},{10,11... | collective-permute-start | bytes 55304 | tf_op jit(solution)/shard_map/ppermute | solution.py:503
  35.4 5.2 %collective-permute-start.20 = (f32[9,512]{1,0:T(8,128)S(1)}, f32[9,512]{1,0:T(8,128)S(1)}, u32[]{:S(2)}, u32[]{:S(2)}) collective-permute-start(f32[9,512]{1,0:T(8,128)S(1)} %get-tuple-element.146), channel_id=1, source_target_pairs={{0,3},{1,2},{2,1},{3,0},{4,7},{5,6},{6,5},{7,4},{8,11},{9,10},{10,... | collective-permute-start | bytes 55304 | tf_op jit(solution)/shard_map/ppermute | solution.py:503
  36.8 3.7 %collective-permute-start.19 = (f32[5,256]{1,0:T(8,128)S(1)}, f32[5,256]{1,0:T(8,128)S(1)}, u32[]{:S(2)}, u32[]{:S(2)}) collective-permute-start(f32[5,256]{1,0:T(8,128)S(1)} %get-tuple-element.145), channel_id=1, source_target_pairs={{0,2},{1,3},{2,0},{3,1},{4,6},{5,7},{6,4},{7,5},{8,10},{9,11},{10,... | collective-permute-start | bytes 15368 | tf_op jit(solution)/shard_map/ppermute | solution.py:503
  37.8 13.7 %collective-permute-start.16 = (f32[3,16,512]{2,1,0:T(8,128)S(1)}, f32[3,16,512]{2,1,0:T(8,128)S(1)}, u32[]{:S(2)}, u32[]{:S(2)}) collective-permute-start(f32[3,16,512]{2,1,0:T(8,128)S(1)} %get-tuple-element.141), channel_id=1, source_target_pairs={{0,4},{4,0},{8,12},{12,8},{16,20},{20,16},{24,28},{28,24},{1,5},{5... | collective-permute-start | bytes 294920 | tf_op jit(solution)/shard_map/ppermute | solution.py:39
  38.2 13.3 %collective-permute-start.17 = (f32[3,16,512]{2,1,0:T(8,128)S(1)}, f32[3,16,512]{2,1,0:T(8,128)S(1)}, u32[]{:S(2)}, u32[]{:S(2)}) collective-permute-start(f32[3,16,512]{2,1,0:T(8,128)S(1)} %get-tuple-element.142), channel_id=1, source_target_pairs={{0,28},{4,8},{8,4},{12,16},{16,12},{20,24},{24,20},{28,0},{1,29},{... | collective-permute-start | bytes 294920 | tf_op jit(solution)/shard_map/ppermute | solution.py:39
  40.6 3.6 %collective-permute-start.21 = (f32[1,256]{1,0:T(1,128)S(1)}, f32[1,256]{1,0:T(1,128)S(1)}, u32[]{:S(2)}, u32[]{:S(2)}) collective-permute-start(f32[1,256]{1,0:T(1,128)S(1)} %shard_map.114.mine), channel_id=1, source_target_pairs={{0,4},{1,5},{2,10},{3,15},{4,0},{5,1},{6,14},{7,11},{8,12},{9,13},... | collective-permute-start | bytes 3080 | tf_op jit(solution)/shard_map/ppermute | solution.py:226
  41.3 6.3 %collective-permute-start.22 = (f32[1,256]{1,0:T(1,128)S(1)}, f32[1,256]{1,0:T(1,128)S(1)}, u32[]{:S(2)}, u32[]{:S(2)}) collective-permute-start(f32[1,256]{1,0:T(1,128)S(1)} %shard_map.114.mine), channel_id=1, source_target_pairs={{0,28},{1,25},{2,22},{3,19},{4,24},{5,29},{6,18},{7,23},{8,20},{9,... | collective-permute-start | bytes 3080 | tf_op jit(solution)/shard_map/ppermute | solution.py:226
  47.7 3.7 %collective-permute-start.24 = (f32[5,256]{1,0:T(8,128)S(1)}, f32[5,256]{1,0:T(8,128)S(1)}, u32[]{:S(2)}, u32[]{:S(2)}) collective-permute-start(f32[5,256]{1,0:T(8,128)S(1)} %get-tuple-element.153), channel_id=1, source_target_pairs={{0,2},{1,3},{2,0},{3,1},{4,6},{5,7},{6,4},{7,5},{8,10},{9,11},{10,... | collective-permute-start | bytes 15368 | tf_op jit(solution)/shard_map/ppermute | solution.py:503
  48.5 3.1 %collective-permute-start.25 = (f32[5,256]{1,0:T(8,128)S(1)}, f32[5,256]{1,0:T(8,128)S(1)}, u32[]{:S(2)}, u32[]{:S(2)}) collective-permute-start(f32[5,256]{1,0:T(8,128)S(1)} %get-tuple-element.154), channel_id=1, source_target_pairs={{0,3},{1,2},{2,1},{3,0},{4,7},{5,6},{6,5},{7,4},{8,11},{9,10},{10,... | collective-permute-start | bytes 15368 | tf_op jit(solution)/shard_map/ppermute | solution.py:503
  53.5 6.6 %collective-permute-start.28 = (f32[8,512]{1,0:T(8,128)S(1)}, f32[8,512]{1,0:T(8,128)S(1)}, u32[]{:S(2)}, u32[]{:S(2)}) collective-permute-start(f32[8,512]{1,0:T(8,128)S(1)} %get-tuple-element.160), channel_id=1, source_target_pairs={{0,1},{1,0},{2,3},{3,2},{4,5},{5,4},{6,7},{7,6},{8,9},{9,8},{10,11... | collective-permute-start | bytes 49160 | tf_op jit(solution)/shard_map/ppermute | solution.py:503
  53.7 6.3 %collective-permute-start.30 = (f32[8,512]{1,0:T(8,128)S(1)}, f32[8,512]{1,0:T(8,128)S(1)}, u32[]{:S(2)}, u32[]{:S(2)}) collective-permute-start(f32[8,512]{1,0:T(8,128)S(1)} %get-tuple-element.162), channel_id=1, source_target_pairs={{0,3},{1,2},{2,1},{3,0},{4,7},{5,6},{6,5},{7,4},{8,11},{9,10},{10,... | collective-permute-start | bytes 49160 | tf_op jit(solution)/shard_map/ppermute | solution.py:503
  55.0 5.0 %collective-permute-start.29 = (f32[4,256]{1,0:T(4,128)S(1)}, f32[4,256]{1,0:T(4,128)S(1)}, u32[]{:S(2)}, u32[]{:S(2)}) collective-permute-start(f32[4,256]{1,0:T(4,128)S(1)} %get-tuple-element.161), channel_id=1, source_target_pairs={{0,2},{1,3},{2,0},{3,1},{4,6},{5,7},{6,4},{7,5},{8,10},{9,11},{10,... | collective-permute-start | bytes 12296 | tf_op jit(solution)/shard_map/ppermute | solution.py:503
  56.3 9.0 %collective-permute-start.26 = (f32[3,16,512]{2,1,0:T(8,128)S(1)}, f32[3,16,512]{2,1,0:T(8,128)S(1)}, u32[]{:S(2)}, u32[]{:S(2)}) collective-permute-start(f32[3,16,512]{2,1,0:T(8,128)S(1)} %get-tuple-element.157), channel_id=1, source_target_pairs={{0,4},{4,0},{8,12},{12,8},{16,20},{20,16},{24,28},{28,24},{1,5},{5... | collective-permute-start | bytes 294920 | tf_op jit(solution)/shard_map/ppermute | solution.py:39
  57.7 7.6 %collective-permute-start.27 = (f32[3,16,512]{2,1,0:T(8,128)S(1)}, f32[3,16,512]{2,1,0:T(8,128)S(1)}, u32[]{:S(2)}, u32[]{:S(2)}) collective-permute-start(f32[3,16,512]{2,1,0:T(8,128)S(1)} %get-tuple-element.158), channel_id=1, source_target_pairs={{0,28},{4,8},{8,4},{12,16},{16,12},{20,24},{24,20},{28,0},{1,29},{... | collective-permute-start | bytes 294920 | tf_op jit(solution)/shard_map/ppermute | solution.py:39
  60.8 3.7 %collective-permute-start.32 = (f32[4,256]{1,0:T(4,128)S(1)}, f32[4,256]{1,0:T(4,128)S(1)}, u32[]{:S(2)}, u32[]{:S(2)}) collective-permute-start(f32[4,256]{1,0:T(4,128)S(1)} %get-tuple-element.165), channel_id=1, source_target_pairs={{0,2},{1,3},{2,0},{3,1},{4,6},{5,7},{6,4},{7,5},{8,10},{9,11},{10,... | collective-permute-start | bytes 12296 | tf_op jit(solution)/shard_map/ppermute | solution.py:503
  62.3 3.0 %collective-permute-start.33 = (f32[4,256]{1,0:T(4,128)S(1)}, f32[4,256]{1,0:T(4,128)S(1)}, u32[]{:S(2)}, u32[]{:S(2)}) collective-permute-start(f32[4,256]{1,0:T(4,128)S(1)} %get-tuple-element.166), channel_id=1, source_target_pairs={{0,3},{1,2},{2,1},{3,0},{4,7},{5,6},{6,5},{7,4},{8,11},{9,10},{10,... | collective-permute-start | bytes 12296 | tf_op jit(solution)/shard_map/ppermute | solution.py:503
  67.3 5.1 %collective-permute-start.36 = (f32[9,512]{1,0:T(8,128)S(1)}, f32[9,512]{1,0:T(8,128)S(1)}, u32[]{:S(2)}, u32[]{:S(2)}) collective-permute-start(f32[9,512]{1,0:T(8,128)S(1)} %get-tuple-element.175), channel_id=1, source_target_pairs={{0,1},{1,0},{2,3},{3,2},{4,5},{5,4},{6,7},{7,6},{8,9},{9,8},{10,11... | collective-permute-start | bytes 55304 | tf_op jit(solution)/shard_map/ppermute | solution.py:503
  67.5 4.9 %collective-permute-start.38 = (f32[9,512]{1,0:T(8,128)S(1)}, f32[9,512]{1,0:T(8,128)S(1)}, u32[]{:S(2)}, u32[]{:S(2)}) collective-permute-start(f32[9,512]{1,0:T(8,128)S(1)} %get-tuple-element.177), channel_id=1, source_target_pairs={{0,3},{1,2},{2,1},{3,0},{4,7},{5,6},{6,5},{7,4},{8,11},{9,10},{10,... | collective-permute-start | bytes 55304 | tf_op jit(solution)/shard_map/ppermute | solution.py:503
  68.5 3.9 %collective-permute-start.37 = (f32[5,256]{1,0:T(8,128)S(1)}, f32[5,256]{1,0:T(8,128)S(1)}, u32[]{:S(2)}, u32[]{:S(2)}) collective-permute-start(f32[5,256]{1,0:T(8,128)S(1)} %get-tuple-element.176), channel_id=1, source_target_pairs={{0,2},{1,3},{2,0},{3,1},{4,6},{5,7},{6,4},{7,5},{8,10},{9,11},{10,... | collective-permute-start | bytes 15368 | tf_op jit(solution)/shard_map/ppermute | solution.py:503
  69.9 13.3 %collective-permute-start.34 = (f32[3,16,512]{2,1,0:T(8,128)S(1)}, f32[3,16,512]{2,1,0:T(8,128)S(1)}, u32[]{:S(2)}, u32[]{:S(2)}) collective-permute-start(f32[3,16,512]{2,1,0:T(8,128)S(1)} %get-tuple-element.172), channel_id=1, source_target_pairs={{0,4},{4,0},{8,12},{12,8},{16,20},{20,16},{24,28},{28,24},{1,5},{5... | collective-permute-start | bytes 294920 | tf_op jit(solution)/shard_map/ppermute | solution.py:39
  70.0 13.2 %collective-permute-start.35 = (f32[3,16,512]{2,1,0:T(8,128)S(1)}, f32[3,16,512]{2,1,0:T(8,128)S(1)}, u32[]{:S(2)}, u32[]{:S(2)}) collective-permute-start(f32[3,16,512]{2,1,0:T(8,128)S(1)} %get-tuple-element.173), channel_id=1, source_target_pairs={{0,28},{4,8},{8,4},{12,16},{16,12},{20,24},{24,20},{28,0},{1,29},{... | collective-permute-start | bytes 294920 | tf_op jit(solution)/shard_map/ppermute | solution.py:39
  72.5 3.7 %collective-permute-start.39 = (f32[1,256]{1,0:T(1,128)S(1)}, f32[1,256]{1,0:T(1,128)S(1)}, u32[]{:S(2)}, u32[]{:S(2)}) collective-permute-start(f32[1,256]{1,0:T(1,128)S(1)} %shard_map.122.mine), channel_id=1, source_target_pairs={{0,4},{1,5},{2,10},{3,15},{4,0},{5,1},{6,14},{7,11},{8,12},{9,13},... | collective-permute-start | bytes 3080 | tf_op jit(solution)/shard_map/ppermute | solution.py:226
  72.5 6.3 %collective-permute-start.40 = (f32[1,256]{1,0:T(1,128)S(1)}, f32[1,256]{1,0:T(1,128)S(1)}, u32[]{:S(2)}, u32[]{:S(2)}) collective-permute-start(f32[1,256]{1,0:T(1,128)S(1)} %shard_map.122.mine), channel_id=1, source_target_pairs={{0,28},{1,25},{2,22},{3,19},{4,24},{5,29},{6,18},{7,23},{8,20},{9,... | collective-permute-start | bytes 3080 | tf_op jit(solution)/shard_map/ppermute | solution.py:226
  79.0 3.7 %collective-permute-start.42 = (f32[5,256]{1,0:T(8,128)S(1)}, f32[5,256]{1,0:T(8,128)S(1)}, u32[]{:S(2)}, u32[]{:S(2)}) collective-permute-start(f32[5,256]{1,0:T(8,128)S(1)} %get-tuple-element.184), channel_id=1, source_target_pairs={{0,2},{1,3},{2,0},{3,1},{4,6},{5,7},{6,4},{7,5},{8,10},{9,11},{10,... | collective-permute-start | bytes 15368 | tf_op jit(solution)/shard_map/ppermute | solution.py:503
  80.2 3.1 %collective-permute-start.43 = (f32[5,256]{1,0:T(8,128)S(1)}, f32[5,256]{1,0:T(8,128)S(1)}, u32[]{:S(2)}, u32[]{:S(2)}) collective-permute-start(f32[5,256]{1,0:T(8,128)S(1)} %get-tuple-element.185), channel_id=1, source_target_pairs={{0,3},{1,2},{2,1},{3,0},{4,7},{5,6},{6,5},{7,4},{8,11},{9,10},{10,... | collective-permute-start | bytes 15368 | tf_op jit(solution)/shard_map/ppermute | solution.py:503
  85.2 6.5 %collective-permute-start.46 = (f32[8,512]{1,0:T(8,128)S(1)}, f32[8,512]{1,0:T(8,128)S(1)}, u32[]{:S(2)}, u32[]{:S(2)}) collective-permute-start(f32[8,512]{1,0:T(8,128)S(1)} %get-tuple-element.195), channel_id=1, source_target_pairs={{0,1},{1,0},{2,3},{3,2},{4,5},{5,4},{6,7},{7,6},{8,9},{9,8},{10,11... | collective-permute-start | bytes 49160 | tf_op jit(solution)/shard_map/ppermute | solution.py:503
  85.4 6.3 %collective-permute-start.48 = (f32[8,512]{1,0:T(8,128)S(1)}, f32[8,512]{1,0:T(8,128)S(1)}, u32[]{:S(2)}, u32[]{:S(2)}) collective-permute-start(f32[8,512]{1,0:T(8,128)S(1)} %get-tuple-element.197), channel_id=1, source_target_pairs={{0,3},{1,2},{2,1},{3,0},{4,7},{5,6},{6,5},{7,4},{8,11},{9,10},{10,... | collective-permute-start | bytes 49160 | tf_op jit(solution)/shard_map/ppermute | solution.py:503
  86.3 5.5 %collective-permute-start.47 = (f32[4,256]{1,0:T(4,128)S(1)}, f32[4,256]{1,0:T(4,128)S(1)}, u32[]{:S(2)}, u32[]{:S(2)}) collective-permute-start(f32[4,256]{1,0:T(4,128)S(1)} %get-tuple-element.196), channel_id=1, source_target_pairs={{0,2},{1,3},{2,0},{3,1},{4,6},{5,7},{6,4},{7,5},{8,10},{9,11},{10,... | collective-permute-start | bytes 12296 | tf_op jit(solution)/shard_map/ppermute | solution.py:503
  87.9 9.1 %collective-permute-start.44 = (f32[3,16,512]{2,1,0:T(8,128)S(1)}, f32[3,16,512]{2,1,0:T(8,128)S(1)}, u32[]{:S(2)}, u32[]{:S(2)}) collective-permute-start(f32[3,16,512]{2,1,0:T(8,128)S(1)} %get-tuple-element.192), channel_id=1, source_target_pairs={{0,4},{4,0},{8,12},{12,8},{16,20},{20,16},{24,28},{28,24},{1,5},{5... | collective-permute-start | bytes 294920 | tf_op jit(solution)/shard_map/ppermute | solution.py:39
  89.4 7.6 %collective-permute-start.45 = (f32[3,16,512]{2,1,0:T(8,128)S(1)}, f32[3,16,512]{2,1,0:T(8,128)S(1)}, u32[]{:S(2)}, u32[]{:S(2)}) collective-permute-start(f32[3,16,512]{2,1,0:T(8,128)S(1)} %get-tuple-element.193), channel_id=1, source_target_pairs={{0,28},{4,8},{8,4},{12,16},{16,12},{20,24},{24,20},{28,0},{1,29},{... | collective-permute-start | bytes 294920 | tf_op jit(solution)/shard_map/ppermute | solution.py:39
  92.5 3.7 %collective-permute-start.50 = (f32[4,256]{1,0:T(4,128)S(1)}, f32[4,256]{1,0:T(4,128)S(1)}, u32[]{:S(2)}, u32[]{:S(2)}) collective-permute-start(f32[4,256]{1,0:T(4,128)S(1)} %get-tuple-element.200), channel_id=1, source_target_pairs={{0,2},{1,3},{2,0},{3,1},{4,6},{5,7},{6,4},{7,5},{8,10},{9,11},{10,... | collective-permute-start | bytes 12296 | tf_op jit(solution)/shard_map/ppermute | solution.py:503
  94.0 3.0 %collective-permute-start.51 = (f32[4,256]{1,0:T(4,128)S(1)}, f32[4,256]{1,0:T(4,128)S(1)}, u32[]{:S(2)}, u32[]{:S(2)}) collective-permute-start(f32[4,256]{1,0:T(4,128)S(1)} %get-tuple-element.201), channel_id=1, source_target_pairs={{0,3},{1,2},{2,1},{3,0},{4,7},{5,6},{6,5},{7,4},{8,11},{9,10},{10,... | collective-permute-start | bytes 12296 | tf_op jit(solution)/shard_map/ppermute | solution.py:503
  (14 other events, 29.4 us)

commit v6 on v5

--- a/solution.py
+++ b/solution.py
@@ -174,8 +174,8 @@
     return jnp.concatenate([high, low], axis=0)
 
 
-def stencil_kernel(vec, trans, diag, *refs):
-    *faces, out, shifted = refs
+def stencil_kernel(after, vec, trans, diag, *refs):
+    *faces, out, shifted = refs[after:]
     write_faces(Planes(vec), faces)
     inner_stencil(vec, trans, diag, shifted, out)
 
@@ -286,8 +286,8 @@
             back[k][slot : slot + 1] = value
 
 
-def group_sum_kernel(capacity, *refs):
-    *messages, out = refs
+def group_sum_kernel(capacity, after, *refs):
+    *messages, out = refs[after:]
     segb = out.shape[1]
     total = jnp.zeros(out.shape, F32)
     for k, message in enumerate(messages):
@@ -417,27 +417,14 @@
     return row
 
 
-def second_kernel(sizes, first_time, end, *refs):
+def second_kernel(sizes, *refs):
     got = Arrived(*sizes, refs)
-    if first_time:
-        b, r, w, t, *rest = got.rest
-        s, z = w, t
-    else:
-        b, r, w, s_rest, z_rest, t, s, z, *rest = got.rest
+    b, w, t, *sends = got.rest
     value = got.result()
     for i in range(t.shape[0]):
         for x in range(t.shape[1]):
             t[i, x] = value(i, x)
-            if not first_time:
-                s[i, x] = w[i, x] + s_rest[i, x]
-                z[i, x] = t[i, x] + z_rest[i, x]
-    if end:
-        sums = rest[0]
-        row = local_sums((b, r, s, w, z), sums.shape[-1])
-        for d in range(sums.shape[0]):
-            sums[d] = row
-    else:
-        got.send(z, rest, local_sums((b, r, s, w, z), got.column.shape[1]))
+    got.send(t, sends, local_sums((b, b, w, w, t), got.column.shape[1]))
 
 
 def coefficients(row):
@@ -454,14 +441,17 @@
     return alpha, omega, beta
 
 
-def third_kernel(sizes, first_time, *refs):
+def step_kernel(sizes, first_time, end, *refs):
     got = Arrived(*sizes, refs)
-    r, w, t, *rest = got.rest
     if first_time:
-        r_out, w_out, x_out, p_out, s_rest, z_rest, *sends = rest
-        s, z, p, x_in = w, t, r, None
+        r, w, t, v, *rest = got.rest
+        s, z, p, x_in, fix = w, t, r, None, None
+        b = r
     else:
-        s, z, p, x_in, r_out, w_out, x_out, p_out, s_rest, z_rest, *sends = rest
+        b, r, w, t, v, s, z, p, x_in, fix, *rest = got.rest
+    r_out, w_out, s_out, z_out, p_out, x_out, *rest = rest
+    if not end:
+        t_out, fix_out, *rest = rest
     value = got.result()
     last = slice(got.capacity, got.capacity + 1)
     row = got.values[0][last]
@@ -470,18 +460,32 @@
     alpha, omega, beta = coefficients(row)
     for i in range(r.shape[0]):
         for x in range(r.shape[1]):
-            v = value(i, x)
+            u = value(i, x)
+            e = v[i, x] if fix is None else v[i, x] - fix[i, x]
             q = r[i, x] - alpha * s[i, x]
             y = w[i, x] - alpha * z[i, x]
+            g = t[i, x] - alpha * v[i, x]
             new_r = q - omega * y
+            new_w = y - omega * g
+            new_t = g - omega * (e - alpha * u)
             r_out[i, x] = new_r
-            w_out[i, x] = y - omega * (t[i, x] - alpha * v)
+            w_out[i, x] = new_w
+            s_out[i, x] = new_w + beta * (s[i, x] - omega * z[i, x])
+            z_out[i, x] = new_t + beta * (z[i, x] - omega * v[i, x])
+            p_out[i, x] = new_r + beta * (p[i, x] - omega * s[i, x])
             step = alpha * p[i, x] + omega * q
             x_out[i, x] = step if x_in is None else x_in[i, x] + step
-            p_out[i, x] = new_r + beta * (p[i, x] - omega * s[i, x])
-            s_rest[i, x] = beta * (s[i, x] - omega * z[i, x])
-            z_rest[i, x] = beta * (z[i, x] - omega * v)
-    got.send(w_out, sends)
+            if not end:
+                t_out[i, x] = new_t
+                fix_out[i, x] = beta * (v[i, x] - omega * u)
+    vecs = (b, r_out, s_out, w_out, z_out)
+    if end:
+        sums = rest[0]
+        row = local_sums(vecs, sums.shape[-1])
+        for d in range(sums.shape[0]):
+            sums[d] = row
+    else:
+        got.send(z_out, rest, local_sums(vecs, got.column.shape[1]))
 
 
 def last_kernel(sums, r, w, s, z, p, x_in, x_out, r_out):
@@ -570,68 +574,67 @@
             moved=4_000_000,
         )
 
-    def finish(kernel, outs, part, messages, values, faces, extra, with_sums=False):
-        halo = exchange(faces)
-        if with_sums:
-            mine = call(
-                functools.partial(group_sum_kernel, capacity), [((1, segb), F32)], messages
-            )[0]
-            fetched = [share_swap(mine, q) for q in range(share(lax.axis_size("res"), groups))]
-            values = call(
-                functools.partial(append_kernel, groups),
-                [((capacity + 1, segb), F32)] * groups,
-                [mine, *values, *fetched],
-            )
-        values = swapped(values)
+    def finish(kernel, outs, part, messages, values, halo, extra):
         args = [part, trans, place, placed, column, take, give, owner]
         args += [*halo, *messages, *values, *extra]
         specs = [VMEM] * len(args)
         specs[7] = SMEM
         return call(kernel, outs, args, specs, flops=1_000_000_000, moved=8_000_000)
 
-    def apply(kernel, outs, vec, sends, extra, with_sums=False):
+    def apply(kernel, outs, vec, sends, extra, sums=None, with_sums=False):
         messages = swapped(sends)
-        *faces, part = call(stencil_kernel, face_outs + [field], [vec, trans, diag], **cost)
+        first_here = sums or []
+        *faces, part = call(
+            functools.partial(stencil_kernel, len(first_here)),
+            face_outs + [field],
+            [vec, trans, diag, *first_here],
+            **cost,
+        )
+        halo = exchange(faces)
         values = solve(False, [first, second, *messages])
-        return finish(kernel, outs, part, messages, values, faces, extra, with_sums)
-
-    messages, faces = swapped(sends[:groups]), sends[groups:]
+        if sums is not None:
+            values = call(
+                functools.partial(append_kernel, groups),
+                [((capacity + 1, segb), F32)] * groups,
+                [sums[0], *values, *sums[1:]],
+            )
+        values = swapped(values)
+        out = finish(kernel, outs, part, messages, values, halo, extra)
+        return (fetch(messages, [values[1], halo[0]]), out) if with_sums else out
+
+    def fetch(messages, after):
+        mine = call(
+            functools.partial(group_sum_kernel, capacity, len(after)),
+            [((1, segb), F32)],
+            [*after, *messages],
+        )[0]
+        return [mine] + [share_swap(mine, q) for q in range(share(lax.axis_size("res"), groups))]
+
     kept = [(inverse.shape[1:], BF16)] * 2
     first, second = call(split_kernel, kept, [inverse[0]])
-    values = solve(True, [first, second, *messages])
+    messages, halo = swapped(sends[:groups]), exchange(sends[groups:])
+    values = swapped(back := solve(True, [first, second, *messages]))
     part, diag, placed = call(
         first_stencil_kernel,
         [field, (accumulation.shape, F32), ((wells * segb, cells_z), BF16)],
         [b, trans, accumulation, place, messages[1]],
         **cost,
     )
-    first, second = call(turn_kernel, kept, [first, second, values[0]])
-    w, *sends = finish(
-        functools.partial(apply_kernel, sizes), [field] + plain, part, messages, values, faces, []
-    )
-    r, s, p, x = b, w, b, None
-    for index in range(ITERS):
-        start, end = index == 0, index + 1 == ITERS
-        tail = [((devices, 1, 128), F32)] if end else summed
-        kernel = functools.partial(second_kernel, sizes, start, end)
-        if start:
-            t, *sends = apply(kernel, [field] + tail, w, sends, [b, r, w])
-            z = t
-        else:
-            t, s, z, *sends = apply(
-                kernel, [field] * 3 + tail, w, sends, [b, r, w, s_rest, z_rest]
-            )
-        if end:
-            break
-        more = [] if start else [s, z, p, x]
-        r, w, x, p, s_rest, z_rest, *sends = apply(
-            functools.partial(third_kernel, sizes, start),
-            [field] * 6 + plain,
-            z,
-            sends,
-            [r, w, t, *more],
-            True,
+    first, second = call(turn_kernel, kept, [first, second, back[0]])
+    plainly = functools.partial(apply_kernel, sizes)
+    w, *sends = finish(plainly, [field] + plain, part, messages, values, halo, [])
+    t, *sends = apply(functools.partial(second_kernel, sizes), [field] + summed, w, sends, [b, w])
+    r, s, z, p, x, fix = b, w, t, b, None, None
+    for index in range(ITERS - 1):
+        start, end = index == 0, index + 2 == ITERS
+        sums, (v, *sends) = apply(plainly, [field] + plain, z, sends, [], None, True)
+        given = [r, w, t, v] if start else [b, r, w, t, v, s, z, p, x, fix]
+        tail = [((devices, 1, 128), F32)] if end else [field] * 2 + summed
+        r, w, s, z, p, x, *sends = apply(
+            functools.partial(step_kernel, sizes, start, end), [field] * 6 + tail, v, sends, given, sums
         )
+        if not end:
+            t, fix, *sends = sends
     sums = lax.all_to_all(sends[0], ("res", "grp"), split_axis=0, concat_axis=0, tiled=True)
     x, r = call(last_kernel, [field, field], [sums, r, w, s, z, p, x])
     return (x, r)

time: 110 us -> 99.2 us (0.902)
  waiting for transfers between devices: 19.9 us -> 8.02 us
  starting transfers between devices: 51.1 us -> 52.4 us
    ppermute x4, waiting for transfers between devices: 7.03 us -> 0.54 us  [share_swap(): return lax.ppermute(row, ('res', 'grp'), pairs)]
    ppermute x36, waiting for transfers between devices: 12.5 us -> 6.57 us  [swapped(): lax.ppermute(messages[k], 'grp', [(i, i ^ k) for i in range(groups)])]
  transfers between devices with their start and end apart: 52 -> 52, of which waited for: 17 -> 10; matrix products, arithmetic and copies ran while one was open for 0% -> 0% of each run, Pallas kernels for 9% -> 14%
where the time goes in v6:
time: 99.2 us; the launch traced here: 99 us
  starting transfers between devices  52.4 us (53%)
  Pallas kernels  25.2 us (25%)
  blocking collectives  10.1 us (10%)
  waiting for transfers between devices  8.02 us (8%)
  local copies, waits for them, and re-layouts  2.23 us (2%)
  between operations  1.05 us (1%)
    ppermute x36, starting transfers between devices, swapped(): lax.ppermute(messages[k], 'grp', [(i, i ^ k) for i in range(groups)])  25.8 us
    pallas_call x26, Pallas kernels, call(): pl.pallas_call(kernel, out_shape=[jax.ShapeDtypeStruct(shape, dtype) for...  25.2 us
    ppermute x12, starting transfers between devices, exchange(): lax.ppermute(face, 'res', pairs)  21 us
    all_to_all x1, blocking collectives, body(): lax.all_to_all(sends[0], ('res', 'grp'), split_axis=0, concat_axis=0, til...  10.1 us
    ppermute x36, waiting for transfers between devices, swapped(): lax.ppermute(messages[k], 'grp', [(i, i ^ k) for i in range(groups)])  6.57 us
    ppermute x4, starting transfers between devices, share_swap(): return lax.ppermute(row, ('res', 'grp'), pairs)  5.51 us
    unnamed x20, local copies, waits for them, and re-layouts  2.23 us
  transfers between devices with their start and end apart: 52, of which 10 were waited for; matrix products, arithmetic and copies ran while one was open for 0% of the time, Pallas kernels for 14%

profile of v6, /device:TPU:0, one launch (start us, length us, event | category | flops | bytes accessed | tf_op | source)
XLA Modules:
  0.0 99.0 jit_solution(1896053690763203874)
XLA Ops:
  0.6 3.2 %shard_map.104 = (bf16[512,2048]{1,0:T(8,128)(2,1)}, s32[8,256]{1,0:T(8,128)}, f32[3,8,256]{2,1,0:T(8,128)}, f32[3,8,256]{2,1,0:T(8,128)}, f32[4,256]{1,0:T(4,12...) custom-call(f32[3,2,16,512]{3,2,1,0:T(8,128)} %refs_18_.5, ...), custom_call_target="tpu_custom_call" | custom-call | flops 1000000 | bytes 1000000 | tf_op jit(solution)/shard_map/pallas_call | solution.py:24
  4.3 2.6 %collective-permute-start.4 = (f32[8,512]{1,0:T(8,128)}, f32[8,512]{1,0:T(8,128)S(1)}, u32[]{:S(2)}, u32[]{:S(2)}) collective-permute-start(f32[8,512]{1,0:T(8,128)} %get-tuple-element.116), channel_id=1, source_target_pairs={{0,3},{1,2},{2,1},{3,0},{4,7},{5,6},{6,5},{7,4},{8,11},{9,10},{10,... | collective-permute-start | bytes 49160 | tf_op jit(solution)/shard_map/ppermute | solution.py:507
  7.0 2.0 %collective-permute-start.1 = (f32[3,16,512]{2,1,0:T(8,128)}, f32[3,16,512]{2,1,0:T(8,128)S(1)}, u32[]{:S(2)}, u32[]{:S(2)}) collective-permute-start(f32[3,16,512]{2,1,0:T(8,128)} %get-tuple-element.112), channel_id=1, source_target_pairs={{0,4},{4,0},{8,12},{12,8},{16,20},{20,16},{24,28},{28,24},{1,5},{5... | collective-permute-start | bytes 294920 | tf_op jit(solution)/shard_map/ppermute | solution.py:39
  9.0 3.6 %collective-permute-start.2 = (f32[3,16,512]{2,1,0:T(8,128)}, f32[3,16,512]{2,1,0:T(8,128)S(1)}, u32[]{:S(2)}, u32[]{:S(2)}) collective-permute-start(f32[3,16,512]{2,1,0:T(8,128)} %get-tuple-element.113), channel_id=1, source_target_pairs={{0,28},{4,8},{8,4},{12,16},{16,12},{20,24},{24,20},{28,0},{1,29},{... | collective-permute-start | bytes 294920 | tf_op jit(solution)/shard_map/ppermute | solution.py:39
  12.5 2.2 %copy-done.3 = f32[1,4,4,256,256]{4,3,2,1,0:T(8,128)S(1)} copy-done((f32[1,4,4,256,256]{4,3,2,1,0:T(8,128)S(1)}, f32[1,4,4,256,256]{4,3,2,1,0:T(8,128)}, u32[]{:S(2)}) %copy-start.3) | copy-done | bytes 4194328
  15.5 1.2 %shard_map.107 = (f32[4,256]{1,0:T(4,128)S(1)}, f32[4,256]{1,0:T(4,128)S(1)}, f32[4,256]{1,0:T(4,128)S(1)}, f32[4,256]{1,0:T(4,128)S(1)}) custom-call(bf16[4,4,256,256]{3,2,1,0:T(8,128)(2,1)S(1)} %get-tuple-element.117.first, bf16[4,4,256,256]{3,2,1,0:T(8,128)(2,1)S(1)} %get-tuple-element.118.second, f32[4,256]{1,0:T(4,128)S(1)} %copy-done.9, ...), custom_call_target="tpu_custom_call" | custom-call | flops 5000000000 | bytes 4000000 | tf_op jit(solution)/shard_map/pallas_call | solution.py:24
  16.8 1.6 %collective-permute-start.6 = (f32[4,256]{1,0:T(4,128)S(1)}, f32[4,256]{1,0:T(4,128)S(1)}, u32[]{:S(2)}, u32[]{:S(2)}) collective-permute-start(f32[4,256]{1,0:T(4,128)S(1)} %get-tuple-element.121), channel_id=1, source_target_pairs={{0,2},{1,3},{2,0},{3,1},{4,6},{5,7},{6,4},{7,5},{8,10},{9,11},{10,... | collective-permute-start | bytes 12296 | tf_op jit(solution)/shard_map/ppermute | solution.py:507
  18.7 1.3 %shard_map.105 = (f32[3,2,16,512]{3,2,1,0:T(8,128)S(1)}, f32[3,3,2,16,512]{4,3,2,1,0:T(8,128)S(1)}, bf16[2048,512]{1,0:T(8,128)(2,1)S(1)}) custom-call(f32[3,2,16,512]{3,2,1,0:T(8,128)S(1)} %copy-done.2, f32[6,3,3,2,16,512]{5,4,3,2,1,0:T(8,128)S(1)} %copy-done, f32[3,3,2,16,512]{4,3,2,1,0:T(8,128)S(1)} %copy-done.6, bf16[512,2048]{1,0:T(8,128)(2,1)S(1)} %copy-done.1, ...), custom_call_target="tpu_custom_call" | custom-call | flops 200000000 | bytes 4000000 | tf_op jit(solution)/shard_map/pallas_call | solution.py:24
  20.0 1.1 %shard_map.110 = (bf16[4,4,256,256]{3,2,1,0:T(8,128)(2,1)S(1)}, bf16[4,4,256,256]{3,2,1,0:T(8,128)(2,1)S(1)}) custom-call(bf16[4,4,256,256]{3,2,1,0:T(8,128)(2,1)S(1)} %get-tuple-element.117.first, bf16[4,4,256,256]{3,2,1,0:T(8,128)(2,1)S(1)} %get-tuple-element.118.second, f32[4,256]{1,0:T(4,128)S(1)} %get-tuple-element.119.refs_14_.after), custom_call_target="tpu_custom_call" | custom-call | flops 1000000 | bytes 1000000 | tf_op jit(solution)/shard_map/pallas_call | solution.py:24
  21.4 1.8 %shard_map.108 = (f32[3,2,16,512]{3,2,1,0:T(8,128)S(1)}, f32[4,256]{1,0:T(4,128)S(1)}, f32[8,512]{1,0:T(8,128)S(1)}, f32[4,256]{1,0:T(4,128)S(1)}, f32[8,512]{1,0:T(8,128)S(1)}) custom-call(f32[3,2,16,512]{3,2,1,0:T(8,128)S(1)} %get-tuple-element.107.refs_0_, f32[6,3,3,2,16,512]{5,4,3,2,1,0:T(8,128)S(1)} %copy-done, bf16[512,2048]{1,0:T(8,128)(2,1)S(1)} %copy-done.1, ...), custom_call_target="tpu_custom_call" | custom-call | flops 1000000000 | bytes 8000000 | tf_op jit(solution)/shard_map/pallas_call | solution.py:24
  23.5 1.2 %collective-permute-start.12 = (f32[8,512]{1,0:T(8,128)S(1)}, f32[8,512]{1,0:T(8,128)S(1)}, u32[]{:S(2)}, u32[]{:S(2)}) collective-permute-start(f32[8,512]{1,0:T(8,128)S(1)} %get-tuple-element.131), channel_id=1, source_target_pairs={{0,3},{1,2},{2,1},{3,0},{4,7},{5,6},{6,5},{7,4},{8,11},{9,10},{10,... | collective-permute-start | bytes 49160 | tf_op jit(solution)/shard_map/ppermute | solution.py:507
  24.7 0.7 collective-permute-start.11
  25.9 1.9 %collective-permute-start.9 = (f32[3,16,512]{2,1,0:T(8,128)S(1)}, f32[3,16,512]{2,1,0:T(8,128)S(1)}, u32[]{:S(2)}, u32[]{:S(2)}) collective-permute-start(f32[3,16,512]{2,1,0:T(8,128)S(1)} %get-tuple-element.127), channel_id=1, source_target_pairs={{0,28},{4,8},{8,4},{12,16},{16,12},{20,24},{24,20},{28,0},{1,29},{... | collective-permute-start | bytes 294920 | tf_op jit(solution)/shard_map/ppermute | solution.py:39
  28.3 0.7 shard_map.111
  29.1 0.9 collective-permute-start.14
  30.0 0.9 collective-permute-start.15
  30.9 1.8 %collective-permute-done.14.refs_16_ = f32[4,256]{1,0:T(4,128)S(1)} collective-permute-done((f32[4,256]{1,0:T(4,128)S(1)}, f32[4,256]{1,0:T(4,128)S(1)}, u32[]{:S(2)}, u32[]{:S(2)}) %collective-permute-start.14) | collective-permute-done | bytes 4128 | tf_op jit(solution)/shard_map/ppermute | solution.py:507
  33.3 1.8 %shard_map.112 = (f32[3,2,16,512]{3,2,1,0:T(8,128)S(1)}, f32[5,256]{1,0:T(8,128)S(1)}, f32[9,512]{1,0:T(8,128)S(1)}, f32[5,256]{1,0:T(8,128)S(1)}, f32[9,512]{1,0:T(8,128)S(1)}) custom-call(f32[3,2,16,512]{3,2,1,0:T(8,128)S(1)} %get-tuple-element.125.refs_0_, f32[6,3,3,2,16,512]{5,4,3,2,1,0:T(8,128)S(1)} %copy-done, bf16[512,2048]{1,0:T(8,128)(2,1)S(1)} %copy-done.1, ...), custom_call_target="tpu_custom_call" | custom-call | flops 1000000000 | bytes 8000000 | tf_op jit(solution)/shard_map/pallas_call | solution.py:24
  35.3 1.4 %collective-permute-start.20 = (f32[9,512]{1,0:T(8,128)S(1)}, f32[9,512]{1,0:T(8,128)S(1)}, u32[]{:S(2)}, u32[]{:S(2)}) collective-permute-start(f32[9,512]{1,0:T(8,128)S(1)} %get-tuple-element.145), channel_id=1, source_target_pairs={{0,3},{1,2},{2,1},{3,0},{4,7},{5,6},{6,5},{7,4},{8,11},{9,10},{10,... | collective-permute-start | bytes 55304 | tf_op jit(solution)/shard_map/ppermute | solution.py:507
  38.1 2.4 %collective-permute-start.17 = (f32[3,16,512]{2,1,0:T(8,128)S(1)}, f32[3,16,512]{2,1,0:T(8,128)S(1)}, u32[]{:S(2)}, u32[]{:S(2)}) collective-permute-start(f32[3,16,512]{2,1,0:T(8,128)S(1)} %get-tuple-element.141), channel_id=1, source_target_pairs={{0,28},{4,8},{8,4},{12,16},{16,12},{20,24},{24,20},{28,0},{1,29},{... | collective-permute-start | bytes 294920 | tf_op jit(solution)/shard_map/ppermute | solution.py:39
  41.3 0.8 collective-permute-start.22
  42.1 1.1 %collective-permute-start.23 = (f32[4,256]{1,0:T(4,128)S(1)}, f32[4,256]{1,0:T(4,128)S(1)}, u32[]{:S(2)}, u32[]{:S(2)}) collective-permute-start(f32[4,256]{1,0:T(4,128)S(1)} %get-tuple-element.149), channel_id=1, source_target_pairs={{0,3},{1,2},{2,1},{3,0},{4,7},{5,6},{6,5},{7,4},{8,11},{9,10},{10,... | collective-permute-start | bytes 12296 | tf_op jit(solution)/shard_map/ppermute | solution.py:507
  43.2 0.7 collective-permute-start.24
  43.9 1.8 %collective-permute-start.25 = (f32[1,256]{1,0:T(1,128)S(1)}, f32[1,256]{1,0:T(1,128)S(1)}, u32[]{:S(2)}, u32[]{:S(2)}) collective-permute-start(f32[1,256]{1,0:T(1,128)S(1)} %shard_map.116.refs_0_.mine), channel_id=1, source_target_pairs={{0,28},{1,25},{2,22},{3,19},{4,24},{5,29},{6,18},{7,23},{8,20},{9,... | collective-permute-start | bytes 3080 | tf_op jit(solution)/shard_map/ppermute | solution.py:226
  45.7 1.8 %shard_map.115 = (f32[3,2,16,512]{3,2,1,0:T(8,128)S(1)}, f32[4,256]{1,0:T(4,128)S(1)}, f32[8,512]{1,0:T(8,128)S(1)}, f32[4,256]{1,0:T(4,128)S(1)}, f32[8,512]{1,0:T(8,128)S(1)}) custom-call(f32[3,2,16,512]{3,2,1,0:T(8,128)S(1)} %get-tuple-element.139.refs_0_, f32[6,3,3,2,16,512]{5,4,3,2,1,0:T(8,128)S(1)} %copy-done, bf16[512,2048]{1,0:T(8,128)(2,1)S(1)} %copy-done.1, ...), custom_call_target="tpu_custom_call" | custom-call | flops 1000000000 | bytes 8000000 | tf_op jit(solution)/shard_map/pallas_call | solution.py:24
  47.8 1.6 %collective-permute-start.30 = (f32[8,512]{1,0:T(8,128)S(1)}, f32[8,512]{1,0:T(8,128)S(1)}, u32[]{:S(2)}, u32[]{:S(2)}) collective-permute-start(f32[8,512]{1,0:T(8,128)S(1)} %get-tuple-element.157), channel_id=1, source_target_pairs={{0,3},{1,2},{2,1},{3,0},{4,7},{5,6},{6,5},{7,4},{8,11},{9,10},{10,... | collective-permute-start | bytes 49160 | tf_op jit(solution)/shard_map/ppermute | solution.py:507
  50.6 1.5 %collective-permute-start.26 = (f32[3,16,512]{2,1,0:T(8,128)S(1)}, f32[3,16,512]{2,1,0:T(8,128)S(1)}, u32[]{:S(2)}, u32[]{:S(2)}) collective-permute-start(f32[3,16,512]{2,1,0:T(8,128)S(1)} %get-tuple-element.152), channel_id=1, source_target_pairs={{0,4},{4,0},{8,12},{12,8},{16,20},{20,16},{24,28},{28,24},{1,5},{5... | collective-permute-start | bytes 294920 | tf_op jit(solution)/shard_map/ppermute | solution.py:39
  52.1 2.4 %collective-permute-start.27 = (f32[3,16,512]{2,1,0:T(8,128)S(1)}, f32[3,16,512]{2,1,0:T(8,128)S(1)}, u32[]{:S(2)}, u32[]{:S(2)}) collective-permute-start(f32[3,16,512]{2,1,0:T(8,128)S(1)} %get-tuple-element.153), channel_id=1, source_target_pairs={{0,28},{4,8},{8,4},{12,16},{16,12},{20,24},{24,20},{28,0},{1,29},{... | collective-permute-start | bytes 294920 | tf_op jit(solution)/shard_map/ppermute | solution.py:39
  54.5 0.9 shard_map.118
  55.6 1.8 %collective-permute-start.33 = (f32[5,256]{1,0:T(8,128)S(1)}, f32[5,256]{1,0:T(8,128)S(1)}, u32[]{:S(2)}, u32[]{:S(2)}) collective-permute-start(f32[5,256]{1,0:T(8,128)S(1)} %get-tuple-element.165), channel_id=1, source_target_pairs={{0,3},{1,2},{2,1},{3,0},{4,7},{5,6},{6,5},{7,4},{8,11},{9,10},{10,... | collective-permute-start | bytes 15368 | tf_op jit(solution)/shard_map/ppermute | solution.py:507
  57.3 1.9 %collective-permute-done.32.refs_16_ = f32[5,256]{1,0:T(8,128)S(1)} collective-permute-done((f32[5,256]{1,0:T(8,128)S(1)}, f32[5,256]{1,0:T(8,128)S(1)}, u32[]{:S(2)}, u32[]{:S(2)}) %collective-permute-start.32) | collective-permute-done | bytes 5152 | tf_op jit(solution)/shard_map/ppermute | solution.py:507
  59.4 2.2 %shard_map.120 = (f32[3,2,16,512]{3,2,1,0:T(8,128)S(1)}, f32[3,2,16,512]{3,2,1,0:T(8,128)S(1)}, f32[3,2,16,512]{3,2,1,0:T(8,128)S(1)}, f32[3,2,16,512]{3,2,1,0:T...) custom-call(f32[3,2,16,512]{3,2,1,0:T(8,128)S(1)} %get-tuple-element, ...), custom_call_target="tpu_custom_call" | custom-call | flops 1000000000 | bytes 8000000 | tf_op jit(solution)/shard_map/pallas_call | solution.py:24
  61.7 1.3 %collective-permute-start.38 = (f32[9,512]{1,0:T(8,128)S(1)}, f32[9,512]{1,0:T(8,128)S(1)}, u32[]{:S(2)}, u32[]{:S(2)}) collective-permute-start(f32[9,512]{1,0:T(8,128)S(1)} %get-tuple-element.173), channel_id=1, source_target_pairs={{0,3},{1,2},{2,1},{3,0},{4,7},{5,6},{6,5},{7,4},{8,11},{9,10},{10,... | collective-permute-start | bytes 55304 | tf_op jit(solution)/shard_map/ppermute | solution.py:507
  63.0 0.8 collective-permute-start.37
  64.4 3.0 %collective-permute-start.35 = (f32[3,16,512]{2,1,0:T(8,128)S(1)}, f32[3,16,512]{2,1,0:T(8,128)S(1)}, u32[]{:S(2)}, u32[]{:S(2)}) collective-permute-start(f32[3,16,512]{2,1,0:T(8,128)S(1)} %get-tuple-element.169), channel_id=1, source_target_pairs={{0,28},{4,8},{8,4},{12,16},{16,12},{20,24},{24,20},{28,0},{1,29},{... | collective-permute-start | bytes 294920 | tf_op jit(solution)/shard_map/ppermute | solution.py:39
  68.1 1.5 %collective-permute-start.40 = (f32[4,256]{1,0:T(4,128)S(1)}, f32[4,256]{1,0:T(4,128)S(1)}, u32[]{:S(2)}, u32[]{:S(2)}) collective-permute-start(f32[4,256]{1,0:T(4,128)S(1)} %get-tuple-element.176), channel_id=1, source_target_pairs={{0,2},{1,3},{2,0},{3,1},{4,6},{5,7},{6,4},{7,5},{8,10},{9,11},{10,... | collective-permute-start | bytes 12296 | tf_op jit(solution)/shard_map/ppermute | solution.py:507
  70.0 0.7 collective-permute-start.42
  70.8 2.3 %collective-permute-start.43 = (f32[1,256]{1,0:T(1,128)S(1)}, f32[1,256]{1,0:T(1,128)S(1)}, u32[]{:S(2)}, u32[]{:S(2)}) collective-permute-start(f32[1,256]{1,0:T(1,128)S(1)} %shard_map.124.refs_0_.mine), channel_id=1, source_target_pairs={{0,28},{1,25},{2,22},{3,19},{4,24},{5,29},{6,18},{7,23},{8,20},{9,... | collective-permute-start | bytes 3080 | tf_op jit(solution)/shard_map/ppermute | solution.py:226
  73.0 1.8 %shard_map.123 = (f32[3,2,16,512]{3,2,1,0:T(8,128)S(1)}, f32[4,256]{1,0:T(4,128)S(1)}, f32[8,512]{1,0:T(8,128)S(1)}, f32[4,256]{1,0:T(4,128)S(1)}, f32[8,512]{1,0:T(8,128)S(1)}) custom-call(f32[3,2,16,512]{3,2,1,0:T(8,128)S(1)} %get-tuple-element.167.refs_0_, f32[6,3,3,2,16,512]{5,4,3,2,1,0:T(8,128)S(1)} %copy-done, bf16[512,2048]{1,0:T(8,128)(2,1)S(1)} %copy-done.1, ...), custom_call_target="tpu_custom_call" | custom-call | flops 1000000000 | bytes 8000000 | tf_op jit(solution)/shard_map/pallas_call | solution.py:24
  74.9 0.9 collective-permute-start.48
  75.8 1.2 %collective-permute-start.47 = (f32[4,256]{1,0:T(4,128)S(1)}, f32[4,256]{1,0:T(4,128)S(1)}, u32[]{:S(2)}, u32[]{:S(2)}) collective-permute-start(f32[4,256]{1,0:T(4,128)S(1)} %get-tuple-element.184), channel_id=1, source_target_pairs={{0,2},{1,3},{2,0},{3,1},{4,6},{5,7},{6,4},{7,5},{8,10},{9,11},{10,... | collective-permute-start | bytes 12296 | tf_op jit(solution)/shard_map/ppermute | solution.py:507
  77.5 1.4 %collective-permute-start.44 = (f32[3,16,512]{2,1,0:T(8,128)S(1)}, f32[3,16,512]{2,1,0:T(8,128)S(1)}, u32[]{:S(2)}, u32[]{:S(2)}) collective-permute-start(f32[3,16,512]{2,1,0:T(8,128)S(1)} %get-tuple-element.180), channel_id=1, source_target_pairs={{0,4},{4,0},{8,12},{12,8},{16,20},{20,16},{24,28},{28,24},{1,5},{5... | collective-permute-start | bytes 294920 | tf_op jit(solution)/shard_map/ppermute | solution.py:39
  78.9 2.5 %collective-permute-start.45 = (f32[3,16,512]{2,1,0:T(8,128)S(1)}, f32[3,16,512]{2,1,0:T(8,128)S(1)}, u32[]{:S(2)}, u32[]{:S(2)}) collective-permute-start(f32[3,16,512]{2,1,0:T(8,128)S(1)} %get-tuple-element.181), channel_id=1, source_target_pairs={{0,28},{4,8},{8,4},{12,16},{16,12},{20,24},{24,20},{28,0},{1,29},{... | collective-permute-start | bytes 294920 | tf_op jit(solution)/shard_map/ppermute | solution.py:39
  82.6 1.4 %collective-permute-start.51 = (f32[5,256]{1,0:T(8,128)S(1)}, f32[5,256]{1,0:T(8,128)S(1)}, u32[]{:S(2)}, u32[]{:S(2)}) collective-permute-start(f32[5,256]{1,0:T(8,128)S(1)} %get-tuple-element.193), channel_id=1, source_target_pairs={{0,3},{1,2},{2,1},{3,0},{4,7},{5,6},{6,5},{7,4},{8,11},{9,10},{10,... | collective-permute-start | bytes 15368 | tf_op jit(solution)/shard_map/ppermute | solution.py:507
  84.0 1.9 %collective-permute-done.50.refs_16_ = f32[5,256]{1,0:T(8,128)S(1)} collective-permute-done((f32[5,256]{1,0:T(8,128)S(1)}, f32[5,256]{1,0:T(8,128)S(1)}, u32[]{:S(2)}, u32[]{:S(2)}) %collective-permute-start.50) | collective-permute-done | bytes 5152 | tf_op jit(solution)/shard_map/ppermute | solution.py:507
  86.2 1.7 %shard_map.128 = (f32[3,2,16,512]{3,2,1,0:T(8,128)S(1)}, f32[3,2,16,512]{3,2,1,0:T(8,128)S(1)}, f32[3,2,16,512]{3,2,1,0:T(8,128)S(1)}, f32[3,2,16,512]{3,2,1,0:T...) custom-call(f32[3,2,16,512]{3,2,1,0:T(8,128)S(1)} %get-tuple-element.179.refs_0, ...), custom_call_target="tpu_custom_call" | custom-call | flops 1000000000 | bytes 8000000 | tf_op jit(solution)/shard_map/pallas_call | solution.py:24
  87.9 10.1 %all_to_all.5.sums = f32[32,1,128]{2,1,0:T(1,128)S(1)} all-to-all(f32[32,1,128]{2,1,0:T(1,128)S(1)} %get-tuple-element.201), channel_id=1, replica_groups=mesh['res'=8,'grp'=4] {'res','grp'}, dimensions={0} | all-to-all | bytes 32768 | tf_op jit(solution)/shard_map/all_to_all | solution.py:638
  98.0 0.9 shard_map.129
  (103 shorter events, 12.0 us)
Async XLA Ops:
  3.8 11.6 %collective-permute-start = (f32[8,512]{1,0:T(8,128)}, f32[8,512]{1,0:T(8,128)S(1)}, u32[]{:S(2)}, u32[]{:S(2)}) collective-permute-start(f32[8,512]{1,0:T(8,128)} %get-tuple-element.106), channel_id=1, source_target_pairs={{0,1},{1,0},{2,3},{3,2},{4,5},{5,4},{6,7},{7,6},{8,9},{9,8},{10,11... | collective-permute-start | bytes 49160 | tf_op jit(solution)/shard_map/ppermute | solution.py:507
  4.3 11.1 %collective-permute-start.4 = (f32[8,512]{1,0:T(8,128)}, f32[8,512]{1,0:T(8,128)S(1)}, u32[]{:S(2)}, u32[]{:S(2)}) collective-permute-start(f32[8,512]{1,0:T(8,128)} %get-tuple-element.116), channel_id=1, source_target_pairs={{0,3},{1,2},{2,1},{3,0},{4,7},{5,6},{6,5},{7,4},{8,11},{9,10},{10,... | collective-permute-start | bytes 49160 | tf_op jit(solution)/shard_map/ppermute | solution.py:507
  7.0 8.4 %collective-permute-start.3 = (f32[4,256]{1,0:T(4,128)}, f32[4,256]{1,0:T(4,128)S(1)}, u32[]{:S(2)}, u32[]{:S(2)}) collective-permute-start(f32[4,256]{1,0:T(4,128)} %get-tuple-element.115), channel_id=1, source_target_pairs={{0,2},{1,3},{2,0},{3,1},{4,6},{5,7},{6,4},{7,5},{8,10},{9,11},{10,... | collective-permute-start | bytes 12296 | tf_op jit(solution)/shard_map/ppermute | solution.py:507
  7.0 14.4 %collective-permute-start.1 = (f32[3,16,512]{2,1,0:T(8,128)}, f32[3,16,512]{2,1,0:T(8,128)S(1)}, u32[]{:S(2)}, u32[]{:S(2)}) collective-permute-start(f32[3,16,512]{2,1,0:T(8,128)} %get-tuple-element.112), channel_id=1, source_target_pairs={{0,4},{4,0},{8,12},{12,8},{16,20},{20,16},{24,28},{28,24},{1,5},{5... | collective-permute-start | bytes 294920 | tf_op jit(solution)/shard_map/ppermute | solution.py:39
  9.0 12.4 %collective-permute-start.2 = (f32[3,16,512]{2,1,0:T(8,128)}, f32[3,16,512]{2,1,0:T(8,128)S(1)}, u32[]{:S(2)}, u32[]{:S(2)}) collective-permute-start(f32[3,16,512]{2,1,0:T(8,128)} %get-tuple-element.113), channel_id=1, source_target_pairs={{0,28},{4,8},{8,4},{12,16},{16,12},{20,24},{24,20},{28,0},{1,29},{... | collective-permute-start | bytes 294920 | tf_op jit(solution)/shard_map/ppermute | solution.py:39
  16.7 4.4 %collective-permute-start.5 = (f32[4,256]{1,0:T(4,128)S(1)}, f32[4,256]{1,0:T(4,128)S(1)}, u32[]{:S(2)}, u32[]{:S(2)}) collective-permute-start(f32[4,256]{1,0:T(4,128)S(1)} %get-tuple-element.120), channel_id=1, source_target_pairs={{0,1},{1,0},{2,3},{3,2},{4,5},{5,4},{6,7},{7,6},{8,9},{9,8},{10,11... | collective-permute-start | bytes 12296 | tf_op jit(solution)/shard_map/ppermute | solution.py:507
  16.8 4.3 %collective-permute-start.6 = (f32[4,256]{1,0:T(4,128)S(1)}, f32[4,256]{1,0:T(4,128)S(1)}, u32[]{:S(2)}, u32[]{:S(2)}) collective-permute-start(f32[4,256]{1,0:T(4,128)S(1)} %get-tuple-element.121), channel_id=1, source_target_pairs={{0,2},{1,3},{2,0},{3,1},{4,6},{5,7},{6,4},{7,5},{8,10},{9,11},{10,... | collective-permute-start | bytes 12296 | tf_op jit(solution)/shard_map/ppermute | solution.py:507
  18.4 3.0 %collective-permute-start.7 = (f32[4,256]{1,0:T(4,128)S(1)}, f32[4,256]{1,0:T(4,128)S(1)}, u32[]{:S(2)}, u32[]{:S(2)}) collective-permute-start(f32[4,256]{1,0:T(4,128)S(1)} %get-tuple-element.122), channel_id=1, source_target_pairs={{0,3},{1,2},{2,1},{3,0},{4,7},{5,6},{6,5},{7,4},{8,11},{9,10},{10,... | collective-permute-start | bytes 12296 | tf_op jit(solution)/shard_map/ppermute | solution.py:507
  23.2 5.1 %collective-permute-start.10 = (f32[8,512]{1,0:T(8,128)S(1)}, f32[8,512]{1,0:T(8,128)S(1)}, u32[]{:S(2)}, u32[]{:S(2)}) collective-permute-start(f32[8,512]{1,0:T(8,128)S(1)} %get-tuple-element.129), channel_id=1, source_target_pairs={{0,1},{1,0},{2,3},{3,2},{4,5},{5,4},{6,7},{7,6},{8,9},{9,8},{10,11... | collective-permute-start | bytes 49160 | tf_op jit(solution)/shard_map/ppermute | solution.py:507
  23.5 4.8 %collective-permute-start.12 = (f32[8,512]{1,0:T(8,128)S(1)}, f32[8,512]{1,0:T(8,128)S(1)}, u32[]{:S(2)}, u32[]{:S(2)}) collective-permute-start(f32[8,512]{1,0:T(8,128)S(1)} %get-tuple-element.131), channel_id=1, source_target_pairs={{0,3},{1,2},{2,1},{3,0},{4,7},{5,6},{6,5},{7,4},{8,11},{9,10},{10,... | collective-permute-start | bytes 49160 | tf_op jit(solution)/shard_map/ppermute | solution.py:507
  24.7 3.6 %collective-permute-start.11 = (f32[4,256]{1,0:T(4,128)S(1)}, f32[4,256]{1,0:T(4,128)S(1)}, u32[]{:S(2)}, u32[]{:S(2)}) collective-permute-start(f32[4,256]{1,0:T(4,128)S(1)} %get-tuple-element.130), channel_id=1, source_target_pairs={{0,2},{1,3},{2,0},{3,1},{4,6},{5,7},{6,4},{7,5},{8,10},{9,11},{10,... | collective-permute-start | bytes 12296 | tf_op jit(solution)/shard_map/ppermute | solution.py:507
  25.9 7.2 %collective-permute-start.8 = (f32[3,16,512]{2,1,0:T(8,128)S(1)}, f32[3,16,512]{2,1,0:T(8,128)S(1)}, u32[]{:S(2)}, u32[]{:S(2)}) collective-permute-start(f32[3,16,512]{2,1,0:T(8,128)S(1)} %get-tuple-element.126), channel_id=1, source_target_pairs={{0,4},{4,0},{8,12},{12,8},{16,20},{20,16},{24,28},{28,24},{1,5},{5... | collective-permute-start | bytes 294920 | tf_op jit(solution)/shard_map/ppermute | solution.py:39
  25.9 7.4 %collective-permute-start.9 = (f32[3,16,512]{2,1,0:T(8,128)S(1)}, f32[3,16,512]{2,1,0:T(8,128)S(1)}, u32[]{:S(2)}, u32[]{:S(2)}) collective-permute-start(f32[3,16,512]{2,1,0:T(8,128)S(1)} %get-tuple-element.127), channel_id=1, source_target_pairs={{0,28},{4,8},{8,4},{12,16},{16,12},{20,24},{24,20},{28,0},{1,29},{... | collective-permute-start | bytes 294920 | tf_op jit(solution)/shard_map/ppermute | solution.py:39
  29.0 1.9 %collective-permute-start.13 = (f32[4,256]{1,0:T(4,128)S(1)}, f32[4,256]{1,0:T(4,128)S(1)}, u32[]{:S(2)}, u32[]{:S(2)}) collective-permute-start(f32[4,256]{1,0:T(4,128)S(1)} %get-tuple-element.135), channel_id=1, source_target_pairs={{0,1},{1,0},{2,3},{3,2},{4,5},{5,4},{6,7},{7,6},{8,9},{9,8},{10,11... | collective-permute-start | bytes 12296 | tf_op jit(solution)/shard_map/ppermute | solution.py:507
  29.1 3.7 %collective-permute-start.14 = (f32[4,256]{1,0:T(4,128)S(1)}, f32[4,256]{1,0:T(4,128)S(1)}, u32[]{:S(2)}, u32[]{:S(2)}) collective-permute-start(f32[4,256]{1,0:T(4,128)S(1)} %get-tuple-element.136), channel_id=1, source_target_pairs={{0,2},{1,3},{2,0},{3,1},{4,6},{5,7},{6,4},{7,5},{8,10},{9,11},{10,... | collective-permute-start | bytes 12296 | tf_op jit(solution)/shard_map/ppermute | solution.py:507
  30.0 3.0 %collective-permute-start.15 = (f32[4,256]{1,0:T(4,128)S(1)}, f32[4,256]{1,0:T(4,128)S(1)}, u32[]{:S(2)}, u32[]{:S(2)}) collective-permute-start(f32[4,256]{1,0:T(4,128)S(1)} %get-tuple-element.137), channel_id=1, source_target_pairs={{0,3},{1,2},{2,1},{3,0},{4,7},{5,6},{6,5},{7,4},{8,11},{9,10},{10,... | collective-permute-start | bytes 12296 | tf_op jit(solution)/shard_map/ppermute | solution.py:507
  35.2 5.4 %collective-permute-start.18 = (f32[9,512]{1,0:T(8,128)S(1)}, f32[9,512]{1,0:T(8,128)S(1)}, u32[]{:S(2)}, u32[]{:S(2)}) collective-permute-start(f32[9,512]{1,0:T(8,128)S(1)} %get-tuple-element.143), channel_id=1, source_target_pairs={{0,1},{1,0},{2,3},{3,2},{4,5},{5,4},{6,7},{7,6},{8,9},{9,8},{10,11... | collective-permute-start | bytes 55304 | tf_op jit(solution)/shard_map/ppermute | solution.py:507
  35.3 5.2 %collective-permute-start.20 = (f32[9,512]{1,0:T(8,128)S(1)}, f32[9,512]{1,0:T(8,128)S(1)}, u32[]{:S(2)}, u32[]{:S(2)}) collective-permute-start(f32[9,512]{1,0:T(8,128)S(1)} %get-tuple-element.145), channel_id=1, source_target_pairs={{0,3},{1,2},{2,1},{3,0},{4,7},{5,6},{6,5},{7,4},{8,11},{9,10},{10,... | collective-permute-start | bytes 55304 | tf_op jit(solution)/shard_map/ppermute | solution.py:507
  36.8 3.7 %collective-permute-start.19 = (f32[5,256]{1,0:T(8,128)S(1)}, f32[5,256]{1,0:T(8,128)S(1)}, u32[]{:S(2)}, u32[]{:S(2)}) collective-permute-start(f32[5,256]{1,0:T(8,128)S(1)} %get-tuple-element.144), channel_id=1, source_target_pairs={{0,2},{1,3},{2,0},{3,1},{4,6},{5,7},{6,4},{7,5},{8,10},{9,11},{10,... | collective-permute-start | bytes 15368 | tf_op jit(solution)/shard_map/ppermute | solution.py:507
  37.8 5.4 %collective-permute-start.16 = (f32[3,16,512]{2,1,0:T(8,128)S(1)}, f32[3,16,512]{2,1,0:T(8,128)S(1)}, u32[]{:S(2)}, u32[]{:S(2)}) collective-permute-start(f32[3,16,512]{2,1,0:T(8,128)S(1)} %get-tuple-element.140), channel_id=1, source_target_pairs={{0,4},{4,0},{8,12},{12,8},{16,20},{20,16},{24,28},{28,24},{1,5},{5... | collective-permute-start | bytes 294920 | tf_op jit(solution)/shard_map/ppermute | solution.py:39
  38.1 7.5 %collective-permute-start.17 = (f32[3,16,512]{2,1,0:T(8,128)S(1)}, f32[3,16,512]{2,1,0:T(8,128)S(1)}, u32[]{:S(2)}, u32[]{:S(2)}) collective-permute-start(f32[3,16,512]{2,1,0:T(8,128)S(1)} %get-tuple-element.141), channel_id=1, source_target_pairs={{0,28},{4,8},{8,4},{12,16},{16,12},{20,24},{24,20},{28,0},{1,29},{... | collective-permute-start | bytes 294920 | tf_op jit(solution)/shard_map/ppermute | solution.py:39
  41.3 4.4 %collective-permute-start.22 = (f32[4,256]{1,0:T(4,128)S(1)}, f32[4,256]{1,0:T(4,128)S(1)}, u32[]{:S(2)}, u32[]{:S(2)}) collective-permute-start(f32[4,256]{1,0:T(4,128)S(1)} %get-tuple-element.148), channel_id=1, source_target_pairs={{0,2},{1,3},{2,0},{3,1},{4,6},{5,7},{6,4},{7,5},{8,10},{9,11},{10,... | collective-permute-start | bytes 12296 | tf_op jit(solution)/shard_map/ppermute | solution.py:507
  42.1 3.6 %collective-permute-start.23 = (f32[4,256]{1,0:T(4,128)S(1)}, f32[4,256]{1,0:T(4,128)S(1)}, u32[]{:S(2)}, u32[]{:S(2)}) collective-permute-start(f32[4,256]{1,0:T(4,128)S(1)} %get-tuple-element.149), channel_id=1, source_target_pairs={{0,3},{1,2},{2,1},{3,0},{4,7},{5,6},{6,5},{7,4},{8,11},{9,10},{10,... | collective-permute-start | bytes 12296 | tf_op jit(solution)/shard_map/ppermute | solution.py:507
  43.2 6.5 %collective-permute-start.24 = (f32[1,256]{1,0:T(1,128)S(1)}, f32[1,256]{1,0:T(1,128)S(1)}, u32[]{:S(2)}, u32[]{:S(2)}) collective-permute-start(f32[1,256]{1,0:T(1,128)S(1)} %shard_map.116.refs_0_.mine), channel_id=1, source_target_pairs={{0,4},{1,5},{2,10},{3,15},{4,0},{5,1},{6,14},{7,11},{8,12},{9,13},... | collective-permute-start | bytes 3080 | tf_op jit(solution)/shard_map/ppermute | solution.py:226
  43.9 6.3 %collective-permute-start.25 = (f32[1,256]{1,0:T(1,128)S(1)}, f32[1,256]{1,0:T(1,128)S(1)}, u32[]{:S(2)}, u32[]{:S(2)}) collective-permute-start(f32[1,256]{1,0:T(1,128)S(1)} %shard_map.116.refs_0_.mine), channel_id=1, source_target_pairs={{0,28},{1,25},{2,22},{3,19},{4,24},{5,29},{6,18},{7,23},{8,20},{9,... | collective-permute-start | bytes 3080 | tf_op jit(solution)/shard_map/ppermute | solution.py:226
  47.4 7.1 %collective-permute-start.28 = (f32[8,512]{1,0:T(8,128)S(1)}, f32[8,512]{1,0:T(8,128)S(1)}, u32[]{:S(2)}, u32[]{:S(2)}) collective-permute-start(f32[8,512]{1,0:T(8,128)S(1)} %get-tuple-element.155), channel_id=1, source_target_pairs={{0,1},{1,0},{2,3},{3,2},{4,5},{5,4},{6,7},{7,6},{8,9},{9,8},{10,11... | collective-permute-start | bytes 49160 | tf_op jit(solution)/shard_map/ppermute | solution.py:507
  47.8 6.7 %collective-permute-start.30 = (f32[8,512]{1,0:T(8,128)S(1)}, f32[8,512]{1,0:T(8,128)S(1)}, u32[]{:S(2)}, u32[]{:S(2)}) collective-permute-start(f32[8,512]{1,0:T(8,128)S(1)} %get-tuple-element.157), channel_id=1, source_target_pairs={{0,3},{1,2},{2,1},{3,0},{4,7},{5,6},{6,5},{7,4},{8,11},{9,10},{10,... | collective-permute-start | bytes 49160 | tf_op jit(solution)/shard_map/ppermute | solution.py:507
  49.4 5.1 %collective-permute-start.29 = (f32[4,256]{1,0:T(4,128)S(1)}, f32[4,256]{1,0:T(4,128)S(1)}, u32[]{:S(2)}, u32[]{:S(2)}) collective-permute-start(f32[4,256]{1,0:T(4,128)S(1)} %get-tuple-element.156), channel_id=1, source_target_pairs={{0,2},{1,3},{2,0},{3,1},{4,6},{5,7},{6,4},{7,5},{8,10},{9,11},{10,... | collective-permute-start | bytes 12296 | tf_op jit(solution)/shard_map/ppermute | solution.py:507
  50.6 8.6 %collective-permute-start.26 = (f32[3,16,512]{2,1,0:T(8,128)S(1)}, f32[3,16,512]{2,1,0:T(8,128)S(1)}, u32[]{:S(2)}, u32[]{:S(2)}) collective-permute-start(f32[3,16,512]{2,1,0:T(8,128)S(1)} %get-tuple-element.152), channel_id=1, source_target_pairs={{0,4},{4,0},{8,12},{12,8},{16,20},{20,16},{24,28},{28,24},{1,5},{5... | collective-permute-start | bytes 294920 | tf_op jit(solution)/shard_map/ppermute | solution.py:39
  52.1 7.3 %collective-permute-start.27 = (f32[3,16,512]{2,1,0:T(8,128)S(1)}, f32[3,16,512]{2,1,0:T(8,128)S(1)}, u32[]{:S(2)}, u32[]{:S(2)}) collective-permute-start(f32[3,16,512]{2,1,0:T(8,128)S(1)} %get-tuple-element.153), channel_id=1, source_target_pairs={{0,28},{4,8},{8,4},{12,16},{16,12},{20,24},{24,20},{28,0},{1,29},{... | collective-permute-start | bytes 294920 | tf_op jit(solution)/shard_map/ppermute | solution.py:39
  55.5 3.7 %collective-permute-start.32 = (f32[5,256]{1,0:T(8,128)S(1)}, f32[5,256]{1,0:T(8,128)S(1)}, u32[]{:S(2)}, u32[]{:S(2)}) collective-permute-start(f32[5,256]{1,0:T(8,128)S(1)} %get-tuple-element.164), channel_id=1, source_target_pairs={{0,2},{1,3},{2,0},{3,1},{4,6},{5,7},{6,4},{7,5},{8,10},{9,11},{10,... | collective-permute-start | bytes 15368 | tf_op jit(solution)/shard_map/ppermute | solution.py:507
  55.6 3.6 %collective-permute-start.33 = (f32[5,256]{1,0:T(8,128)S(1)}, f32[5,256]{1,0:T(8,128)S(1)}, u32[]{:S(2)}, u32[]{:S(2)}) collective-permute-start(f32[5,256]{1,0:T(8,128)S(1)} %get-tuple-element.165), channel_id=1, source_target_pairs={{0,3},{1,2},{2,1},{3,0},{4,7},{5,6},{6,5},{7,4},{8,11},{9,10},{10,... | collective-permute-start | bytes 15368 | tf_op jit(solution)/shard_map/ppermute | solution.py:507
  61.7 5.7 %collective-permute-start.36 = (f32[9,512]{1,0:T(8,128)S(1)}, f32[9,512]{1,0:T(8,128)S(1)}, u32[]{:S(2)}, u32[]{:S(2)}) collective-permute-start(f32[9,512]{1,0:T(8,128)S(1)} %get-tuple-element.171), channel_id=1, source_target_pairs={{0,1},{1,0},{2,3},{3,2},{4,5},{5,4},{6,7},{7,6},{8,9},{9,8},{10,11... | collective-permute-start | bytes 55304 | tf_op jit(solution)/shard_map/ppermute | solution.py:507
  61.7 5.6 %collective-permute-start.38 = (f32[9,512]{1,0:T(8,128)S(1)}, f32[9,512]{1,0:T(8,128)S(1)}, u32[]{:S(2)}, u32[]{:S(2)}) collective-permute-start(f32[9,512]{1,0:T(8,128)S(1)} %get-tuple-element.173), channel_id=1, source_target_pairs={{0,3},{1,2},{2,1},{3,0},{4,7},{5,6},{6,5},{7,4},{8,11},{9,10},{10,... | collective-permute-start | bytes 55304 | tf_op jit(solution)/shard_map/ppermute | solution.py:507
  63.0 4.3 %collective-permute-start.37 = (f32[5,256]{1,0:T(8,128)S(1)}, f32[5,256]{1,0:T(8,128)S(1)}, u32[]{:S(2)}, u32[]{:S(2)}) collective-permute-start(f32[5,256]{1,0:T(8,128)S(1)} %get-tuple-element.172), channel_id=1, source_target_pairs={{0,2},{1,3},{2,0},{3,1},{4,6},{5,7},{6,4},{7,5},{8,10},{9,11},{10,... | collective-permute-start | bytes 15368 | tf_op jit(solution)/shard_map/ppermute | solution.py:507
  64.3 5.7 %collective-permute-start.34 = (f32[3,16,512]{2,1,0:T(8,128)S(1)}, f32[3,16,512]{2,1,0:T(8,128)S(1)}, u32[]{:S(2)}, u32[]{:S(2)}) collective-permute-start(f32[3,16,512]{2,1,0:T(8,128)S(1)} %get-tuple-element.168), channel_id=1, source_target_pairs={{0,4},{4,0},{8,12},{12,8},{16,20},{20,16},{24,28},{28,24},{1,5},{5... | collective-permute-start | bytes 294920 | tf_op jit(solution)/shard_map/ppermute | solution.py:39
  64.4 8.7 %collective-permute-start.35 = (f32[3,16,512]{2,1,0:T(8,128)S(1)}, f32[3,16,512]{2,1,0:T(8,128)S(1)}, u32[]{:S(2)}, u32[]{:S(2)}) collective-permute-start(f32[3,16,512]{2,1,0:T(8,128)S(1)} %get-tuple-element.169), channel_id=1, source_target_pairs={{0,28},{4,8},{8,4},{12,16},{16,12},{20,24},{24,20},{28,0},{1,29},{... | collective-permute-start | bytes 294920 | tf_op jit(solution)/shard_map/ppermute | solution.py:39
  68.1 4.9 %collective-permute-start.40 = (f32[4,256]{1,0:T(4,128)S(1)}, f32[4,256]{1,0:T(4,128)S(1)}, u32[]{:S(2)}, u32[]{:S(2)}) collective-permute-start(f32[4,256]{1,0:T(4,128)S(1)} %get-tuple-element.176), channel_id=1, source_target_pairs={{0,2},{1,3},{2,0},{3,1},{4,6},{5,7},{6,4},{7,5},{8,10},{9,11},{10,... | collective-permute-start | bytes 12296 | tf_op jit(solution)/shard_map/ppermute | solution.py:507
  69.6 3.5 %collective-permute-start.41 = (f32[4,256]{1,0:T(4,128)S(1)}, f32[4,256]{1,0:T(4,128)S(1)}, u32[]{:S(2)}, u32[]{:S(2)}) collective-permute-start(f32[4,256]{1,0:T(4,128)S(1)} %get-tuple-element.177), channel_id=1, source_target_pairs={{0,3},{1,2},{2,1},{3,0},{4,7},{5,6},{6,5},{7,4},{8,11},{9,10},{10,... | collective-permute-start | bytes 12296 | tf_op jit(solution)/shard_map/ppermute | solution.py:507
  70.0 7.0 %collective-permute-start.42 = (f32[1,256]{1,0:T(1,128)S(1)}, f32[1,256]{1,0:T(1,128)S(1)}, u32[]{:S(2)}, u32[]{:S(2)}) collective-permute-start(f32[1,256]{1,0:T(1,128)S(1)} %shard_map.124.refs_0_.mine), channel_id=1, source_target_pairs={{0,4},{1,5},{2,10},{3,15},{4,0},{5,1},{6,14},{7,11},{8,12},{9,13},... | collective-permute-start | bytes 3080 | tf_op jit(solution)/shard_map/ppermute | solution.py:226
  70.8 6.3 %collective-permute-start.43 = (f32[1,256]{1,0:T(1,128)S(1)}, f32[1,256]{1,0:T(1,128)S(1)}, u32[]{:S(2)}, u32[]{:S(2)}) collective-permute-start(f32[1,256]{1,0:T(1,128)S(1)} %shard_map.124.refs_0_.mine), channel_id=1, source_target_pairs={{0,28},{1,25},{2,22},{3,19},{4,24},{5,29},{6,18},{7,23},{8,20},{9,... | collective-permute-start | bytes 3080 | tf_op jit(solution)/shard_map/ppermute | solution.py:226
  74.8 6.5 %collective-permute-start.46 = (f32[8,512]{1,0:T(8,128)S(1)}, f32[8,512]{1,0:T(8,128)S(1)}, u32[]{:S(2)}, u32[]{:S(2)}) collective-permute-start(f32[8,512]{1,0:T(8,128)S(1)} %get-tuple-element.183), channel_id=1, source_target_pairs={{0,1},{1,0},{2,3},{3,2},{4,5},{5,4},{6,7},{7,6},{8,9},{9,8},{10,11... | collective-permute-start | bytes 49160 | tf_op jit(solution)/shard_map/ppermute | solution.py:507
  74.9 6.5 %collective-permute-start.48 = (f32[8,512]{1,0:T(8,128)S(1)}, f32[8,512]{1,0:T(8,128)S(1)}, u32[]{:S(2)}, u32[]{:S(2)}) collective-permute-start(f32[8,512]{1,0:T(8,128)S(1)} %get-tuple-element.185), channel_id=1, source_target_pairs={{0,3},{1,2},{2,1},{3,0},{4,7},{5,6},{6,5},{7,4},{8,11},{9,10},{10,... | collective-permute-start | bytes 49160 | tf_op jit(solution)/shard_map/ppermute | solution.py:507
  75.8 5.5 %collective-permute-start.47 = (f32[4,256]{1,0:T(4,128)S(1)}, f32[4,256]{1,0:T(4,128)S(1)}, u32[]{:S(2)}, u32[]{:S(2)}) collective-permute-start(f32[4,256]{1,0:T(4,128)S(1)} %get-tuple-element.184), channel_id=1, source_target_pairs={{0,2},{1,3},{2,0},{3,1},{4,6},{5,7},{6,4},{7,5},{8,10},{9,11},{10,... | collective-permute-start | bytes 12296 | tf_op jit(solution)/shard_map/ppermute | solution.py:507
  77.5 8.4 %collective-permute-start.44 = (f32[3,16,512]{2,1,0:T(8,128)S(1)}, f32[3,16,512]{2,1,0:T(8,128)S(1)}, u32[]{:S(2)}, u32[]{:S(2)}) collective-permute-start(f32[3,16,512]{2,1,0:T(8,128)S(1)} %get-tuple-element.180), channel_id=1, source_target_pairs={{0,4},{4,0},{8,12},{12,8},{16,20},{20,16},{24,28},{28,24},{1,5},{5... | collective-permute-start | bytes 294920 | tf_op jit(solution)/shard_map/ppermute | solution.py:39
  78.9 7.3 %collective-permute-start.45 = (f32[3,16,512]{2,1,0:T(8,128)S(1)}, f32[3,16,512]{2,1,0:T(8,128)S(1)}, u32[]{:S(2)}, u32[]{:S(2)}) collective-permute-start(f32[3,16,512]{2,1,0:T(8,128)S(1)} %get-tuple-element.181), channel_id=1, source_target_pairs={{0,28},{4,8},{8,4},{12,16},{16,12},{20,24},{24,20},{28,0},{1,29},{... | collective-permute-start | bytes 294920 | tf_op jit(solution)/shard_map/ppermute | solution.py:39
  82.1 3.7 %collective-permute-start.50 = (f32[5,256]{1,0:T(8,128)S(1)}, f32[5,256]{1,0:T(8,128)S(1)}, u32[]{:S(2)}, u32[]{:S(2)}) collective-permute-start(f32[5,256]{1,0:T(8,128)S(1)} %get-tuple-element.192), channel_id=1, source_target_pairs={{0,2},{1,3},{2,0},{3,1},{4,6},{5,7},{6,4},{7,5},{8,10},{9,11},{10,... | collective-permute-start | bytes 15368 | tf_op jit(solution)/shard_map/ppermute | solution.py:507
  82.6 3.2 %collective-permute-start.51 = (f32[5,256]{1,0:T(8,128)S(1)}, f32[5,256]{1,0:T(8,128)S(1)}, u32[]{:S(2)}, u32[]{:S(2)}) collective-permute-start(f32[5,256]{1,0:T(8,128)S(1)} %get-tuple-element.193), channel_id=1, source_target_pairs={{0,3},{1,2},{2,1},{3,0},{4,7},{5,6},{6,5},{7,4},{8,11},{9,10},{10,... | collective-permute-start | bytes 15368 | tf_op jit(solution)/shard_map/ppermute | solution.py:507
  (14 other events, 29.4 us)

commit v7 on v6

--- a/solution.py
+++ b/solution.py
@@ -33,10 +33,19 @@
 
 
 def exchange(faces):
-    count = lax.axis_size("res")
+    count, groups = lax.axis_size("res"), lax.axis_size("grp")
     first = [(i, i ^ 1) for i in range(count)]
-    second = [(i, (i + 1 if i % 2 else i - 1) % count) for i in range(count)]
-    return [lax.ppermute(face, "res", pairs) for face, pairs in zip(faces, (first, second))]
+    second = []
+    for r in range(count):
+        for g in range(groups):
+            other, line = (r + 1 if r % 2 else r - 1), g
+            if not 0 <= other < count:
+                other, line = r, g ^ 1
+            second.append((r * groups + g, other * groups + line))
+    return [
+        lax.ppermute(faces[0], "res", first),
+        lax.ppermute(faces[1], ("res", "grp"), second),
+    ]
 
 
 def is_even(axis):
@@ -176,12 +185,19 @@
 
 def stencil_kernel(after, vec, trans, diag, *refs):
     *faces, out, shifted = refs[after:]
-    write_faces(Planes(vec), faces)
+    if faces:
+        write_faces(Planes(vec), faces)
     inner_stencil(vec, trans, diag, shifted, out)
 
 
-def first_stencil_kernel(vec, trans, acc, place, after, out, diag, placed, shifted):
+def first_stencil_kernel(
+    vec, trans, acc, place, first, second, after, out, diag, placed, first_out, second_out, shifted
+):
     placed[...] = place[...].T
+    for h in range(first.shape[0]):
+        for slot in range(first.shape[1]):
+            first_out[h, slot] = first[h, slot].T
+            second_out[h, slot] = second[h, slot].T
     for i in range(acc.shape[0]):
         for j in range(acc.shape[1]):
             total = acc[i, j]
@@ -362,13 +378,6 @@
             first[h, slot], second[h, slot] = halves(inverse[h, slot])
 
 
-def turn_kernel(first, second, after, first_out, second_out):
-    for h in range(first.shape[0]):
-        for slot in range(first.shape[1]):
-            first_out[h, slot] = first[h, slot].T
-            second_out[h, slot] = second[h, slot].T
-
-
 class Arrived:
     def __init__(self, groups, capacity, refs):
         self.capacity, self.groups = capacity, groups
@@ -387,6 +396,9 @@
         return lambda i, x: self.part[i, x] - wells[i, x] - terms(i, x)
 
     def send(self, vec, sends, sums=None):
+        sends, faces = sends[: self.groups], sends[self.groups :]
+        if faces:
+            write_faces(Planes(vec), faces)
         write_messages(vec, self.place, self.column, self.take, self.owner, self.capacity, sends, sums)
 
 
@@ -582,16 +594,16 @@
         return call(kernel, outs, args, specs, flops=1_000_000_000, moved=8_000_000)
 
     def apply(kernel, outs, vec, sends, extra, sums=None, with_sums=False):
-        messages = swapped(sends)
-        first_here = sums or []
-        *faces, part = call(
+        messages, faces = swapped(sends[:groups]), sends[groups:]
+        values = solve(False, [first, second, *messages])
+        first_here = values[:1] if faces else sums
+        *made, part = call(
             functools.partial(stencil_kernel, len(first_here)),
-            face_outs + [field],
+            ([] if faces else face_outs) + [field],
             [vec, trans, diag, *first_here],
             **cost,
         )
-        halo = exchange(faces)
-        values = solve(False, [first, second, *messages])
+        halo = exchange(faces or made)
         if sums is not None:
             values = call(
                 functools.partial(append_kernel, groups),
@@ -614,22 +626,23 @@
     first, second = call(split_kernel, kept, [inverse[0]])
     messages, halo = swapped(sends[:groups]), exchange(sends[groups:])
     values = swapped(back := solve(True, [first, second, *messages]))
-    part, diag, placed = call(
+    part, diag, placed, first, second = call(
         first_stencil_kernel,
-        [field, (accumulation.shape, F32), ((wells * segb, cells_z), BF16)],
-        [b, trans, accumulation, place, messages[1]],
+        [field, (accumulation.shape, F32), ((wells * segb, cells_z), BF16)] + kept,
+        [b, trans, accumulation, place, first, second, back[0]],
         **cost,
     )
-    first, second = call(turn_kernel, kept, [first, second, back[0]])
     plainly = functools.partial(apply_kernel, sizes)
-    w, *sends = finish(plainly, [field] + plain, part, messages, values, halo, [])
-    t, *sends = apply(functools.partial(second_kernel, sizes), [field] + summed, w, sends, [b, w])
+    w, *sends = finish(plainly, [field] + plain + face_outs, part, messages, values, halo, [])
+    t, *sends = apply(
+        functools.partial(second_kernel, sizes), [field] + summed + face_outs, w, sends, [b, w]
+    )
     r, s, z, p, x, fix = b, w, t, b, None, None
     for index in range(ITERS - 1):
         start, end = index == 0, index + 2 == ITERS
         sums, (v, *sends) = apply(plainly, [field] + plain, z, sends, [], None, True)
         given = [r, w, t, v] if start else [b, r, w, t, v, s, z, p, x, fix]
-        tail = [((devices, 1, 128), F32)] if end else [field] * 2 + summed
+        tail = [((devices, 1, 128), F32)] if end else [field] * 2 + summed + face_outs
         r, w, s, z, p, x, *sends = apply(
             functools.partial(step_kernel, sizes, start, end), [field] * 6 + tail, v, sends, given, sums
         )

time: 99.2 us -> 96.5 us (0.973)
  starting transfers between devices: 52.4 us -> 45.1 us
  waiting for transfers between devices: 8.02 us -> 13.4 us
    ppermute x12, starting transfers between devices: 21 us -> 8.86 us  [the longest x6 8.78 us: exchange(): lax.ppermute(faces[0], 'res', first)]
    ppermute x36, waiting for transfers between devices: 6.57 us -> 12.2 us  [swapped(): lax.ppermute(messages[k], 'grp', [(i, i ^ k) for i in range(groups)])]
    ppermute x4, starting transfers between devices: 5.51 us -> 9.87 us  [share_swap(): return lax.ppermute(row, ('res', 'grp'), pairs)]
    pallas_call x26 -> x25, Pallas kernels: 25.2 us -> 25.1 us  [call(): pl.pallas_call(kernel, out_shape=[jax.ShapeDtypeStruct(shape, dtype) for...]
  transfers between devices with their start and end apart: 52 -> 52, of which waited for: 10 -> 14; matrix products, arithmetic and copies ran while one was open for 0% -> 0% of each run, Pallas kernels for 14% -> 14%
where the time goes in v7:
time: 96.5 us; the launch traced here: 96.3 us
  starting transfers between devices  45.1 us (47%)
  Pallas kernels  25.1 us (26%)
  waiting for transfers between devices  13.4 us (14%)
  blocking collectives  9.51 us (10%)
  local copies, waits for them, and re-layouts  2.23 us (2%)
  between operations  1.04 us (1%)
    ppermute x36, starting transfers between devices, swapped(): lax.ppermute(messages[k], 'grp', [(i, i ^ k) for i in range(groups)])  26.4 us
    pallas_call x25, Pallas kernels, call(): pl.pallas_call(kernel, out_shape=[jax.ShapeDtypeStruct(shape, dtype) for...  25.1 us
    ppermute x36, waiting for transfers between devices, swapped(): lax.ppermute(messages[k], 'grp', [(i, i ^ k) for i in range(groups)])  12.2 us
    ppermute x4, starting transfers between devices, share_swap(): return lax.ppermute(row, ('res', 'grp'), pairs)  9.87 us
    all_to_all x1, blocking collectives, body(): lax.all_to_all(sends[0], ('res', 'grp'), split_axis=0, concat_axis=0, til...  9.51 us
    ppermute x6, starting transfers between devices, exchange(): lax.ppermute(faces[0], 'res', first)  8.78 us
    unnamed x20, local copies, waits for them, and re-layouts  2.23 us
  transfers between devices with their start and end apart: 52, of which 14 were waited for; matrix products, arithmetic and copies ran while one was open for 0% of the time, Pallas kernels for 14%

profile of v7, /device:TPU:0, one launch (start us, length us, event | category | flops | bytes accessed | tf_op | source)
XLA Modules:
  0.0 96.3 jit_solution(15403720828489047884)
XLA Ops:
  0.6 3.2 %shard_map.104 = (bf16[512,2048]{1,0:T(8,128)(2,1)}, s32[8,256]{1,0:T(8,128)}, f32[3,8,256]{2,1,0:T(8,128)}, f32[3,8,256]{2,1,0:T(8,128)}, f32[4,256]{1,0:T(4,12...) custom-call(f32[3,2,16,512]{3,2,1,0:T(8,128)} %refs_18_.5, ...), custom_call_target="tpu_custom_call" | custom-call | flops 1000000 | bytes 1000000 | tf_op jit(solution)/shard_map/pallas_call | solution.py:24
  4.3 2.6 %collective-permute-start.2 = (f32[8,512]{1,0:T(8,128)}, f32[8,512]{1,0:T(8,128)S(1)}, u32[]{:S(2)}, u32[]{:S(2)}) collective-permute-start(f32[8,512]{1,0:T(8,128)} %get-tuple-element.108), channel_id=1, source_target_pairs={{0,3},{1,2},{2,1},{3,0},{4,7},{5,6},{6,5},{7,4},{8,11},{9,10},{10,... | collective-permute-start | bytes 49160 | tf_op jit(solution)/shard_map/ppermute | solution.py:519
  7.0 2.0 %collective-permute-start.3 = (f32[3,16,512]{2,1,0:T(8,128)}, f32[3,16,512]{2,1,0:T(8,128)S(1)}, u32[]{:S(2)}, u32[]{:S(2)}) collective-permute-start(f32[3,16,512]{2,1,0:T(8,128)} %get-tuple-element.115), channel_id=1, source_target_pairs={{0,4},{4,0},{8,12},{12,8},{16,20},{20,16},{24,28},{28,24},{1,5},{5... | collective-permute-start | bytes 294920 | tf_op jit(solution)/shard_map/ppermute | solution.py:46
  9.0 2.2 %copy-done.3 = f32[1,4,4,256,256]{4,3,2,1,0:T(8,128)S(1)} copy-done((f32[1,4,4,256,256]{4,3,2,1,0:T(8,128)S(1)}, f32[1,4,4,256,256]{4,3,2,1,0:T(8,128)}, u32[]{:S(2)}) %copy-start.3) | copy-done | bytes 4194328
  11.9 1.2 %shard_map.106 = (f32[4,256]{1,0:T(4,128)S(1)}, f32[4,256]{1,0:T(4,128)S(1)}, f32[4,256]{1,0:T(4,128)S(1)}, f32[4,256]{1,0:T(4,128)S(1)}) custom-call(bf16[4,4,256,256]{3,2,1,0:T(8,128)(2,1)S(1)} %get-tuple-element.103.first, bf16[4,4,256,256]{3,2,1,0:T(8,128)(2,1)S(1)} %get-tuple-element.104.second, f32[4,256]{1,0:T(4,128)S(1)} %copy-done.9, ...), custom_call_target="tpu_custom_call" | custom-call | flops 5000000000 | bytes 4000000 | tf_op jit(solution)/shard_map/pallas_call | solution.py:24
  13.7 1.5 %collective-permute-start.6 = (f32[4,256]{1,0:T(4,128)S(1)}, f32[4,256]{1,0:T(4,128)S(1)}, u32[]{:S(2)}, u32[]{:S(2)}) collective-permute-start(f32[4,256]{1,0:T(4,128)S(1)} %get-tuple-element.118), channel_id=1, source_target_pairs={{0,2},{1,3},{2,0},{3,1},{4,6},{5,7},{6,4},{7,5},{8,10},{9,11},{10,... | collective-permute-start | bytes 12296 | tf_op jit(solution)/shard_map/ppermute | solution.py:519
  15.3 2.3 %shard_map.107 = (f32[3,2,16,512]{3,2,1,0:T(8,128)S(1)}, f32[3,3,2,16,512]{4,3,2,1,0:T(8,128)S(1)}, bf16[2048,512]{1,0:T(8,128)(2,1)S(1)}, bf16[4,4,256,256]{3,2...) custom-call(f32[3,2,16,512]{3,2,1,0:T(8,128)S(1)} %copy-done.2, f32[6,3,3,2,16,512]{5,4,3,2,1,0:T(8,128)S(1)} %copy-done, ...), custom_call_target="tpu_custom_call" | custom-call | flops 200000000 | bytes 4000000 | tf_op jit(solution)/shard_map/pallas_call | solution.py:24
  18.3 1.8 %shard_map.108 = (f32[3,2,16,512]{3,2,1,0:T(8,128)S(1)}, f32[4,256]{1,0:T(4,128)S(1)}, f32[8,512]{1,0:T(8,128)S(1)}, f32[4,256]{1,0:T(4,128)S(1)}, f32[8,512]{1,...) custom-call(f32[3,2,16,512]{3,2,1,0:T(8,128)S(1)} %get-tuple-element.110.refs_0_, ...), custom_call_target="tpu_custom_call" | custom-call | flops 1000000000 | bytes 8000000 | tf_op jit(solution)/shard_map/pallas_call | solution.py:24
  20.2 1.1 %collective-permute-start.10 = (f32[8,512]{1,0:T(8,128)S(1)}, f32[8,512]{1,0:T(8,128)S(1)}, u32[]{:S(2)}, u32[]{:S(2)}) collective-permute-start(f32[8,512]{1,0:T(8,128)S(1)} %get-tuple-element.127), channel_id=1, source_target_pairs={{0,3},{1,2},{2,1},{3,0},{4,7},{5,6},{6,5},{7,4},{8,11},{9,10},{10,... | collective-permute-start | bytes 49160 | tf_op jit(solution)/shard_map/ppermute | solution.py:519
  21.4 0.9 collective-permute-start.9
  22.3 2.6 %collective-permute-start.11 = (f32[3,16,512]{2,1,0:T(8,128)S(1)}, f32[3,16,512]{2,1,0:T(8,128)S(1)}, u32[]{:S(2)}, u32[]{:S(2)}) collective-permute-start(f32[3,16,512]{2,1,0:T(8,128)S(1)} %get-tuple-element.129), channel_id=1, source_target_pairs={{0,4},{4,0},{8,12},{12,8},{16,20},{20,16},{24,28},{28,24},{1,5},{5... | collective-permute-start | bytes 294920 | tf_op jit(solution)/shard_map/ppermute | solution.py:46
  25.0 0.7 shard_map.109
  26.2 1.2 %collective-permute-start.14 = (f32[4,256]{1,0:T(4,128)S(1)}, f32[4,256]{1,0:T(4,128)S(1)}, u32[]{:S(2)}, u32[]{:S(2)}) collective-permute-start(f32[4,256]{1,0:T(4,128)S(1)} %get-tuple-element.132), channel_id=1, source_target_pairs={{0,2},{1,3},{2,0},{3,1},{4,6},{5,7},{6,4},{7,5},{8,10},{9,11},{10,... | collective-permute-start | bytes 12296 | tf_op jit(solution)/shard_map/ppermute | solution.py:519
  28.0 1.7 %collective-permute-done.14.refs_16_ = f32[4,256]{1,0:T(4,128)S(1)} collective-permute-done((f32[4,256]{1,0:T(4,128)S(1)}, f32[4,256]{1,0:T(4,128)S(1)}, u32[]{:S(2)}, u32[]{:S(2)}) %collective-permute-start.14) | collective-permute-done | bytes 4128 | tf_op jit(solution)/shard_map/ppermute | solution.py:519
  30.4 1.8 %shard_map.111 = (f32[3,2,16,512]{3,2,1,0:T(8,128)S(1)}, f32[5,256]{1,0:T(8,128)S(1)}, f32[9,512]{1,0:T(8,128)S(1)}, f32[5,256]{1,0:T(8,128)S(1)}, f32[9,512]{1,...) custom-call(f32[3,2,16,512]{3,2,1,0:T(8,128)S(1)} %shard_map.110.refs_0_, ...), custom_call_target="tpu_custom_call" | custom-call | flops 1000000000 | bytes 8000000 | tf_op jit(solution)/shard_map/pallas_call | solution.py:24
  32.4 0.9 collective-permute-start.18
  33.3 1.2 %collective-permute-start.17 = (f32[5,256]{1,0:T(8,128)S(1)}, f32[5,256]{1,0:T(8,128)S(1)}, u32[]{:S(2)}, u32[]{:S(2)}) collective-permute-start(f32[5,256]{1,0:T(8,128)S(1)} %get-tuple-element.137), channel_id=1, source_target_pairs={{0,2},{1,3},{2,0},{3,1},{4,6},{5,7},{6,4},{7,5},{8,10},{9,11},{10,... | collective-permute-start | bytes 15368 | tf_op jit(solution)/shard_map/ppermute | solution.py:519
  34.5 2.6 %collective-permute-start.19 = (f32[3,16,512]{2,1,0:T(8,128)S(1)}, f32[3,16,512]{2,1,0:T(8,128)S(1)}, u32[]{:S(2)}, u32[]{:S(2)}) collective-permute-start(f32[3,16,512]{2,1,0:T(8,128)S(1)} %get-tuple-element.140), channel_id=1, source_target_pairs={{0,4},{4,0},{8,12},{12,8},{16,20},{20,16},{24,28},{28,24},{1,5},{5... | collective-permute-start | bytes 294920 | tf_op jit(solution)/shard_map/ppermute | solution.py:46
  37.1 0.7 shard_map.112
  38.3 0.8 collective-permute-start.22
  40.2 1.1 %collective-permute-done.19.refs_8_.refs_1_ = f32[3,16,512]{2,1,0:T(8,128)S(1)} collective-permute-done((f32[3,16,512]{2,1,0:T(8,128)S(1)}, f32[3,16,512]{2,1,0:T(8,128)S(1)}, u32[]{:S(2)}, u32[]{:S(2)}) %collective-permute-start.19) | collective-permute-done | bytes 98336 | tf_op jit(solution)/shard_map/ppermute | solution.py:46
  41.3 2.0 %collective-permute-start.25 = (f32[1,256]{1,0:T(1,128)S(1)}, f32[1,256]{1,0:T(1,128)S(1)}, u32[]{:S(2)}, u32[]{:S(2)}) collective-permute-start(f32[1,256]{1,0:T(1,128)S(1)} %shard_map.115.refs_0_.mine), channel_id=1, source_target_pairs={{0,28},{1,25},{2,22},{3,19},{4,24},{5,29},{6,18},{7,23},{8,20},{9,... | collective-permute-start | bytes 3080 | tf_op jit(solution)/shard_map/ppermute | solution.py:242
  43.3 2.4 %collective-permute-start.24 = (f32[1,256]{1,0:T(1,128)S(1)}, f32[1,256]{1,0:T(1,128)S(1)}, u32[]{:S(2)}, u32[]{:S(2)}) collective-permute-start(f32[1,256]{1,0:T(1,128)S(1)} %shard_map.115.refs_0_.mine), channel_id=1, source_target_pairs={{0,4},{1,5},{2,10},{3,15},{4,0},{5,1},{6,14},{7,11},{8,12},{9,13},... | collective-permute-start | bytes 3080 | tf_op jit(solution)/shard_map/ppermute | solution.py:242
  45.7 1.8 %shard_map.114 = (f32[3,2,16,512]{3,2,1,0:T(8,128)S(1)}, f32[4,256]{1,0:T(4,128)S(1)}, f32[8,512]{1,0:T(8,128)S(1)}, f32[4,256]{1,0:T(4,128)S(1)}, f32[8,512]{1,0:T(8,128)S(1)}) custom-call(f32[3,2,16,512]{3,2,1,0:T(8,128)S(1)} %shard_map.113.refs_0_, f32[6,3,3,2,16,512]{5,4,3,2,1,0:T(8,128)S(1)} %copy-done, bf16[512,2048]{1,0:T(8,128)(2,1)S(1)} %copy-done.1, ...), custom_call_target="tpu_custom_call" | custom-call | flops 1000000000 | bytes 8000000 | tf_op jit(solution)/shard_map/pallas_call | solution.py:24
  47.5 0.7 collective-permute-start.29
  48.2 1.5 %collective-permute-start.30 = (f32[8,512]{1,0:T(8,128)S(1)}, f32[8,512]{1,0:T(8,128)S(1)}, u32[]{:S(2)}, u32[]{:S(2)}) collective-permute-start(f32[8,512]{1,0:T(8,128)S(1)} %get-tuple-element.152), channel_id=1, source_target_pairs={{0,3},{1,2},{2,1},{3,0},{4,7},{5,6},{6,5},{7,4},{8,11},{9,10},{10,... | collective-permute-start | bytes 49160 | tf_op jit(solution)/shard_map/ppermute | solution.py:519
  51.4 0.8 shard_map.117
  52.8 1.4 %collective-permute-start.32 = (f32[5,256]{1,0:T(8,128)S(1)}, f32[5,256]{1,0:T(8,128)S(1)}, u32[]{:S(2)}, u32[]{:S(2)}) collective-permute-start(f32[5,256]{1,0:T(8,128)S(1)} %get-tuple-element.159), channel_id=1, source_target_pairs={{0,2},{1,3},{2,0},{3,1},{4,6},{5,7},{6,4},{7,5},{8,10},{9,11},{10,... | collective-permute-start | bytes 15368 | tf_op jit(solution)/shard_map/ppermute | solution.py:519
  54.2 2.2 %collective-permute-done.32.refs_16_ = f32[5,256]{1,0:T(8,128)S(1)} collective-permute-done((f32[5,256]{1,0:T(8,128)S(1)}, f32[5,256]{1,0:T(8,128)S(1)}, u32[]{:S(2)}, u32[]{:S(2)}) %collective-permute-start.32) | collective-permute-done | bytes 5152 | tf_op jit(solution)/shard_map/ppermute | solution.py:519
  56.5 0.9 collective-permute-done.33.refs_17_
  57.3 2.2 %shard_map.119 = (f32[3,2,16,512]{3,2,1,0:T(8,128)S(1)}, f32[3,2,16,512]{3,2,1,0:T(8,128)S(1)}, f32[3,2,16,512]{3,2,1,0:T(8,128)S(1)}, f32[3,2,16,512]{3,2,1,0:T...) custom-call(f32[3,2,16,512]{3,2,1,0:T(8,128)S(1)} %get-tuple-element, ...), custom_call_target="tpu_custom_call" | custom-call | flops 1000000000 | bytes 8000000 | tf_op jit(solution)/shard_map/pallas_call | solution.py:24
  59.7 0.7 collective-permute-start.36
  60.5 1.3 %collective-permute-start.35 = (f32[5,256]{1,0:T(8,128)S(1)}, f32[5,256]{1,0:T(8,128)S(1)}, u32[]{:S(2)}, u32[]{:S(2)}) collective-permute-start(f32[5,256]{1,0:T(8,128)S(1)} %get-tuple-element.164), channel_id=1, source_target_pairs={{0,2},{1,3},{2,0},{3,1},{4,6},{5,7},{6,4},{7,5},{8,10},{9,11},{10,... | collective-permute-start | bytes 15368 | tf_op jit(solution)/shard_map/ppermute | solution.py:519
  61.8 1.2 %collective-permute-start.37 = (f32[3,16,512]{2,1,0:T(8,128)S(1)}, f32[3,16,512]{2,1,0:T(8,128)S(1)}, u32[]{:S(2)}, u32[]{:S(2)}) collective-permute-start(f32[3,16,512]{2,1,0:T(8,128)S(1)} %get-tuple-element.167), channel_id=1, source_target_pairs={{0,4},{4,0},{8,12},{12,8},{16,20},{20,16},{24,28},{28,24},{1,5},{5... | collective-permute-start | bytes 294920 | tf_op jit(solution)/shard_map/ppermute | solution.py:46
  63.0 1.1 %collective-permute-done.35.refs_2_.refs_12_.refs_4_ = f32[5,256]{1,0:T(8,128)S(1)} collective-permute-done((f32[5,256]{1,0:T(8,128)S(1)}, f32[5,256]{1,0:T(8,128)S(1)}, u32[]{:S(2)}, u32[]{:S(2)}) %collective-permute-start.35) | collective-permute-done | bytes 5152 | tf_op jit(solution)/shard_map/ppermute | solution.py:519
  64.9 1.4 %collective-permute-start.40 = (f32[4,256]{1,0:T(4,128)S(1)}, f32[4,256]{1,0:T(4,128)S(1)}, u32[]{:S(2)}, u32[]{:S(2)}) collective-permute-start(f32[4,256]{1,0:T(4,128)S(1)} %get-tuple-element.170), channel_id=1, source_target_pairs={{0,2},{1,3},{2,0},{3,1},{4,6},{5,7},{6,4},{7,5},{8,10},{9,11},{10,... | collective-permute-start | bytes 12296 | tf_op jit(solution)/shard_map/ppermute | solution.py:519
  67.3 3.0 %collective-permute-start.43 = (f32[1,256]{1,0:T(1,128)S(1)}, f32[1,256]{1,0:T(1,128)S(1)}, u32[]{:S(2)}, u32[]{:S(2)}) collective-permute-start(f32[1,256]{1,0:T(1,128)S(1)} %shard_map.123.refs_0_.mine), channel_id=1, source_target_pairs={{0,28},{1,25},{2,22},{3,19},{4,24},{5,29},{6,18},{7,23},{8,20},{9,... | collective-permute-start | bytes 3080 | tf_op jit(solution)/shard_map/ppermute | solution.py:242
  70.3 2.4 %collective-permute-start.42 = (f32[1,256]{1,0:T(1,128)S(1)}, f32[1,256]{1,0:T(1,128)S(1)}, u32[]{:S(2)}, u32[]{:S(2)}) collective-permute-start(f32[1,256]{1,0:T(1,128)S(1)} %shard_map.123.refs_0_.mine), channel_id=1, source_target_pairs={{0,4},{1,5},{2,10},{3,15},{4,0},{5,1},{6,14},{7,11},{8,12},{9,13},... | collective-permute-start | bytes 3080 | tf_op jit(solution)/shard_map/ppermute | solution.py:242
  72.7 1.7 %shard_map.122 = (f32[3,2,16,512]{3,2,1,0:T(8,128)S(1)}, f32[4,256]{1,0:T(4,128)S(1)}, f32[8,512]{1,0:T(8,128)S(1)}, f32[4,256]{1,0:T(4,128)S(1)}, f32[8,512]{1,0:T(8,128)S(1)}) custom-call(f32[3,2,16,512]{3,2,1,0:T(8,128)S(1)} %shard_map.121.refs_0_, f32[6,3,3,2,16,512]{5,4,3,2,1,0:T(8,128)S(1)} %copy-done, bf16[512,2048]{1,0:T(8,128)(2,1)S(1)} %copy-done.1, ...), custom_call_target="tpu_custom_call" | custom-call | flops 1000000000 | bytes 8000000 | tf_op jit(solution)/shard_map/pallas_call | solution.py:24
  74.6 2.0 %collective-permute-start.48 = (f32[8,512]{1,0:T(8,128)S(1)}, f32[8,512]{1,0:T(8,128)S(1)}, u32[]{:S(2)}, u32[]{:S(2)}) collective-permute-start(f32[8,512]{1,0:T(8,128)S(1)} %get-tuple-element.179), channel_id=1, source_target_pairs={{0,3},{1,2},{2,1},{3,0},{4,7},{5,6},{6,5},{7,4},{8,11},{9,10},{10,... | collective-permute-start | bytes 49160 | tf_op jit(solution)/shard_map/ppermute | solution.py:519
  77.3 0.9 collective-permute-done.47.refs_2_.refs_12_
  78.2 0.7 shard_map.125
  79.1 1.9 %collective-permute-start.50 = (f32[5,256]{1,0:T(8,128)S(1)}, f32[5,256]{1,0:T(8,128)S(1)}, u32[]{:S(2)}, u32[]{:S(2)}) collective-permute-start(f32[5,256]{1,0:T(8,128)S(1)} %get-tuple-element.186), channel_id=1, source_target_pairs={{0,2},{1,3},{2,0},{3,1},{4,6},{5,7},{6,4},{7,5},{8,10},{9,11},{10,... | collective-permute-start | bytes 15368 | tf_op jit(solution)/shard_map/ppermute | solution.py:519
  81.0 1.7 %collective-permute-done.50.refs_16_ = f32[5,256]{1,0:T(8,128)S(1)} collective-permute-done((f32[5,256]{1,0:T(8,128)S(1)}, f32[5,256]{1,0:T(8,128)S(1)}, u32[]{:S(2)}, u32[]{:S(2)}) %collective-permute-start.50) | collective-permute-done | bytes 5152 | tf_op jit(solution)/shard_map/ppermute | solution.py:519
  82.8 1.4 %collective-permute-done.51.refs_17_ = f32[5,256]{1,0:T(8,128)S(1)} collective-permute-done((f32[5,256]{1,0:T(8,128)S(1)}, f32[5,256]{1,0:T(8,128)S(1)}, u32[]{:S(2)}, u32[]{:S(2)}) %collective-permute-start.51) | collective-permute-done | bytes 5152 | tf_op jit(solution)/shard_map/ppermute | solution.py:519
  84.2 1.7 %shard_map.127 = (f32[3,2,16,512]{3,2,1,0:T(8,128)S(1)}, f32[3,2,16,512]{3,2,1,0:T(8,128)S(1)}, f32[3,2,16,512]{3,2,1,0:T(8,128)S(1)}, f32[3,2,16,512]{3,2,1,0:T...) custom-call(f32[3,2,16,512]{3,2,1,0:T(8,128)S(1)} %get-tuple-element.173.refs_0, ...), custom_call_target="tpu_custom_call" | custom-call | flops 1000000000 | bytes 8000000 | tf_op jit(solution)/shard_map/pallas_call | solution.py:24
  85.9 9.5 %all_to_all.5.sums = f32[32,1,128]{2,1,0:T(1,128)S(1)} all-to-all(f32[32,1,128]{2,1,0:T(1,128)S(1)} %get-tuple-element.195), channel_id=1, replica_groups=mesh['res'=8,'grp'=4] {'res','grp'}, dimensions={0} | all-to-all | bytes 32768 | tf_op jit(solution)/shard_map/all_to_all | solution.py:651
  95.4 0.9 shard_map.128
  (102 shorter events, 11.5 us)
Async XLA Ops:
  3.8 8.0 %collective-permute-start = (f32[8,512]{1,0:T(8,128)}, f32[8,512]{1,0:T(8,128)S(1)}, u32[]{:S(2)}, u32[]{:S(2)}) collective-permute-start(f32[8,512]{1,0:T(8,128)} %get-tuple-element.106), channel_id=1, source_target_pairs={{0,1},{1,0},{2,3},{3,2},{4,5},{5,4},{6,7},{7,6},{8,9},{9,8},{10,11... | collective-permute-start | bytes 49160 | tf_op jit(solution)/shard_map/ppermute | solution.py:519
  4.3 7.5 %collective-permute-start.2 = (f32[8,512]{1,0:T(8,128)}, f32[8,512]{1,0:T(8,128)S(1)}, u32[]{:S(2)}, u32[]{:S(2)}) collective-permute-start(f32[8,512]{1,0:T(8,128)} %get-tuple-element.108), channel_id=1, source_target_pairs={{0,3},{1,2},{2,1},{3,0},{4,7},{5,6},{6,5},{7,4},{8,11},{9,10},{10,... | collective-permute-start | bytes 49160 | tf_op jit(solution)/shard_map/ppermute | solution.py:519
  7.0 4.8 %collective-permute-start.1 = (f32[4,256]{1,0:T(4,128)}, f32[4,256]{1,0:T(4,128)S(1)}, u32[]{:S(2)}, u32[]{:S(2)}) collective-permute-start(f32[4,256]{1,0:T(4,128)} %get-tuple-element.107), channel_id=1, source_target_pairs={{0,2},{1,3},{2,0},{3,1},{4,6},{5,7},{6,4},{7,5},{8,10},{9,11},{10,... | collective-permute-start | bytes 12296 | tf_op jit(solution)/shard_map/ppermute | solution.py:519
  7.0 11.3 %collective-permute-start.3 = (f32[3,16,512]{2,1,0:T(8,128)}, f32[3,16,512]{2,1,0:T(8,128)S(1)}, u32[]{:S(2)}, u32[]{:S(2)}) collective-permute-start(f32[3,16,512]{2,1,0:T(8,128)} %get-tuple-element.115), channel_id=1, source_target_pairs={{0,4},{4,0},{8,12},{12,8},{16,20},{20,16},{24,28},{28,24},{1,5},{5... | collective-permute-start | bytes 294920 | tf_op jit(solution)/shard_map/ppermute | solution.py:46
  9.0 9.3 %collective-permute-start.4 = (f32[3,16,512]{2,1,0:T(8,128)}, f32[3,16,512]{2,1,0:T(8,128)S(1)}, u32[]{:S(2)}, u32[]{:S(2)}) collective-permute-start(f32[3,16,512]{2,1,0:T(8,128)} %get-tuple-element.116), channel_id=1, source_target_pairs={{0,1},{1,0},{2,3},{3,2},{4,8},{5,9},{6,10},{7,11},{8,4},{9,5},{10,... | collective-permute-start | bytes 294920 | tf_op jit(solution)/shard_map/ppermute | solution.py:47
  13.1 4.5 %collective-permute-start.5 = (f32[4,256]{1,0:T(4,128)S(1)}, f32[4,256]{1,0:T(4,128)S(1)}, u32[]{:S(2)}, u32[]{:S(2)}) collective-permute-start(f32[4,256]{1,0:T(4,128)S(1)} %get-tuple-element.117), channel_id=1, source_target_pairs={{0,1},{1,0},{2,3},{3,2},{4,5},{5,4},{6,7},{7,6},{8,9},{9,8},{10,11... | collective-permute-start | bytes 12296 | tf_op jit(solution)/shard_map/ppermute | solution.py:519
  13.7 3.9 %collective-permute-start.6 = (f32[4,256]{1,0:T(4,128)S(1)}, f32[4,256]{1,0:T(4,128)S(1)}, u32[]{:S(2)}, u32[]{:S(2)}) collective-permute-start(f32[4,256]{1,0:T(4,128)S(1)} %get-tuple-element.118), channel_id=1, source_target_pairs={{0,2},{1,3},{2,0},{3,1},{4,6},{5,7},{6,4},{7,5},{8,10},{9,11},{10,... | collective-permute-start | bytes 12296 | tf_op jit(solution)/shard_map/ppermute | solution.py:519
  15.2 3.1 %collective-permute-start.7 = (f32[4,256]{1,0:T(4,128)S(1)}, f32[4,256]{1,0:T(4,128)S(1)}, u32[]{:S(2)}, u32[]{:S(2)}) collective-permute-start(f32[4,256]{1,0:T(4,128)S(1)} %get-tuple-element.119), channel_id=1, source_target_pairs={{0,3},{1,2},{2,1},{3,0},{4,7},{5,6},{6,5},{7,4},{8,11},{9,10},{10,... | collective-permute-start | bytes 12296 | tf_op jit(solution)/shard_map/ppermute | solution.py:519
  20.1 4.9 %collective-permute-start.8 = (f32[8,512]{1,0:T(8,128)S(1)}, f32[8,512]{1,0:T(8,128)S(1)}, u32[]{:S(2)}, u32[]{:S(2)}) collective-permute-start(f32[8,512]{1,0:T(8,128)S(1)} %get-tuple-element.125), channel_id=1, source_target_pairs={{0,1},{1,0},{2,3},{3,2},{4,5},{5,4},{6,7},{7,6},{8,9},{9,8},{10,11... | collective-permute-start | bytes 49160 | tf_op jit(solution)/shard_map/ppermute | solution.py:519
  20.2 4.7 %collective-permute-start.10 = (f32[8,512]{1,0:T(8,128)S(1)}, f32[8,512]{1,0:T(8,128)S(1)}, u32[]{:S(2)}, u32[]{:S(2)}) collective-permute-start(f32[8,512]{1,0:T(8,128)S(1)} %get-tuple-element.127), channel_id=1, source_target_pairs={{0,3},{1,2},{2,1},{3,0},{4,7},{5,6},{6,5},{7,4},{8,11},{9,10},{10,... | collective-permute-start | bytes 49160 | tf_op jit(solution)/shard_map/ppermute | solution.py:519
  21.4 3.6 %collective-permute-start.9 = (f32[4,256]{1,0:T(4,128)S(1)}, f32[4,256]{1,0:T(4,128)S(1)}, u32[]{:S(2)}, u32[]{:S(2)}) collective-permute-start(f32[4,256]{1,0:T(4,128)S(1)} %get-tuple-element.126), channel_id=1, source_target_pairs={{0,2},{1,3},{2,0},{3,1},{4,6},{5,7},{6,4},{7,5},{8,10},{9,11},{10,... | collective-permute-start | bytes 12296 | tf_op jit(solution)/shard_map/ppermute | solution.py:519
  22.3 8.1 %collective-permute-start.11 = (f32[3,16,512]{2,1,0:T(8,128)S(1)}, f32[3,16,512]{2,1,0:T(8,128)S(1)}, u32[]{:S(2)}, u32[]{:S(2)}) collective-permute-start(f32[3,16,512]{2,1,0:T(8,128)S(1)} %get-tuple-element.129), channel_id=1, source_target_pairs={{0,4},{4,0},{8,12},{12,8},{16,20},{20,16},{24,28},{28,24},{1,5},{5... | collective-permute-start | bytes 294920 | tf_op jit(solution)/shard_map/ppermute | solution.py:46
  24.9 5.5 %collective-permute-start.12 = (f32[3,16,512]{2,1,0:T(8,128)S(1)}, f32[3,16,512]{2,1,0:T(8,128)S(1)}, u32[]{:S(2)}, u32[]{:S(2)}) collective-permute-start(f32[3,16,512]{2,1,0:T(8,128)S(1)} %get-tuple-element.130), channel_id=1, source_target_pairs={{0,1},{1,0},{2,3},{3,2},{4,8},{5,9},{6,10},{7,11},{8,4},{9,5},{10,... | collective-permute-start | bytes 294920 | tf_op jit(solution)/shard_map/ppermute | solution.py:47
  26.2 3.6 %collective-permute-start.14 = (f32[4,256]{1,0:T(4,128)S(1)}, f32[4,256]{1,0:T(4,128)S(1)}, u32[]{:S(2)}, u32[]{:S(2)}) collective-permute-start(f32[4,256]{1,0:T(4,128)S(1)} %get-tuple-element.132), channel_id=1, source_target_pairs={{0,2},{1,3},{2,0},{3,1},{4,6},{5,7},{6,4},{7,5},{8,10},{9,11},{10,... | collective-permute-start | bytes 12296 | tf_op jit(solution)/shard_map/ppermute | solution.py:519
  27.4 3.1 %collective-permute-start.15 = (f32[4,256]{1,0:T(4,128)S(1)}, f32[4,256]{1,0:T(4,128)S(1)}, u32[]{:S(2)}, u32[]{:S(2)}) collective-permute-start(f32[4,256]{1,0:T(4,128)S(1)} %get-tuple-element.133), channel_id=1, source_target_pairs={{0,3},{1,2},{2,1},{3,0},{4,7},{5,6},{6,5},{7,4},{8,11},{9,10},{10,... | collective-permute-start | bytes 12296 | tf_op jit(solution)/shard_map/ppermute | solution.py:519
  32.3 4.8 %collective-permute-start.16 = (f32[9,512]{1,0:T(8,128)S(1)}, f32[9,512]{1,0:T(8,128)S(1)}, u32[]{:S(2)}, u32[]{:S(2)}) collective-permute-start(f32[9,512]{1,0:T(8,128)S(1)} %get-tuple-element.136), channel_id=1, source_target_pairs={{0,1},{1,0},{2,3},{3,2},{4,5},{5,4},{6,7},{7,6},{8,9},{9,8},{10,11... | collective-permute-start | bytes 55304 | tf_op jit(solution)/shard_map/ppermute | solution.py:519
  32.4 4.7 %collective-permute-start.18 = (f32[9,512]{1,0:T(8,128)S(1)}, f32[9,512]{1,0:T(8,128)S(1)}, u32[]{:S(2)}, u32[]{:S(2)}) collective-permute-start(f32[9,512]{1,0:T(8,128)S(1)} %get-tuple-element.138), channel_id=1, source_target_pairs={{0,3},{1,2},{2,1},{3,0},{4,7},{5,6},{6,5},{7,4},{8,11},{9,10},{10,... | collective-permute-start | bytes 55304 | tf_op jit(solution)/shard_map/ppermute | solution.py:519
  33.3 3.8 %collective-permute-start.17 = (f32[5,256]{1,0:T(8,128)S(1)}, f32[5,256]{1,0:T(8,128)S(1)}, u32[]{:S(2)}, u32[]{:S(2)}) collective-permute-start(f32[5,256]{1,0:T(8,128)S(1)} %get-tuple-element.137), channel_id=1, source_target_pairs={{0,2},{1,3},{2,0},{3,1},{4,6},{5,7},{6,4},{7,5},{8,10},{9,11},{10,... | collective-permute-start | bytes 15368 | tf_op jit(solution)/shard_map/ppermute | solution.py:519
  34.5 6.8 %collective-permute-start.19 = (f32[3,16,512]{2,1,0:T(8,128)S(1)}, f32[3,16,512]{2,1,0:T(8,128)S(1)}, u32[]{:S(2)}, u32[]{:S(2)}) collective-permute-start(f32[3,16,512]{2,1,0:T(8,128)S(1)} %get-tuple-element.140), channel_id=1, source_target_pairs={{0,4},{4,0},{8,12},{12,8},{16,20},{20,16},{24,28},{28,24},{1,5},{5... | collective-permute-start | bytes 294920 | tf_op jit(solution)/shard_map/ppermute | solution.py:46
  37.1 8.6 %collective-permute-start.20 = (f32[3,16,512]{2,1,0:T(8,128)S(1)}, f32[3,16,512]{2,1,0:T(8,128)S(1)}, u32[]{:S(2)}, u32[]{:S(2)}) collective-permute-start(f32[3,16,512]{2,1,0:T(8,128)S(1)} %get-tuple-element.141), channel_id=1, source_target_pairs={{0,1},{1,0},{2,3},{3,2},{4,8},{5,9},{6,10},{7,11},{8,4},{9,5},{10,... | collective-permute-start | bytes 294920 | tf_op jit(solution)/shard_map/ppermute | solution.py:47
  37.8 2.4 %collective-permute-start.21 = (f32[4,256]{1,0:T(4,128)S(1)}, f32[4,256]{1,0:T(4,128)S(1)}, u32[]{:S(2)}, u32[]{:S(2)}) collective-permute-start(f32[4,256]{1,0:T(4,128)S(1)} %get-tuple-element.142), channel_id=1, source_target_pairs={{0,1},{1,0},{2,3},{3,2},{4,5},{5,4},{6,7},{7,6},{8,9},{9,8},{10,11... | collective-permute-start | bytes 12296 | tf_op jit(solution)/shard_map/ppermute | solution.py:519
  38.3 7.4 %collective-permute-start.22 = (f32[4,256]{1,0:T(4,128)S(1)}, f32[4,256]{1,0:T(4,128)S(1)}, u32[]{:S(2)}, u32[]{:S(2)}) collective-permute-start(f32[4,256]{1,0:T(4,128)S(1)} %get-tuple-element.143), channel_id=1, source_target_pairs={{0,2},{1,3},{2,0},{3,1},{4,6},{5,7},{6,4},{7,5},{8,10},{9,11},{10,... | collective-permute-start | bytes 12296 | tf_op jit(solution)/shard_map/ppermute | solution.py:519
  39.2 6.5 %collective-permute-start.23 = (f32[4,256]{1,0:T(4,128)S(1)}, f32[4,256]{1,0:T(4,128)S(1)}, u32[]{:S(2)}, u32[]{:S(2)}) collective-permute-start(f32[4,256]{1,0:T(4,128)S(1)} %get-tuple-element.144), channel_id=1, source_target_pairs={{0,3},{1,2},{2,1},{3,0},{4,7},{5,6},{6,5},{7,4},{8,11},{9,10},{10,... | collective-permute-start | bytes 12296 | tf_op jit(solution)/shard_map/ppermute | solution.py:519
  41.3 8.4 %collective-permute-start.25 = (f32[1,256]{1,0:T(1,128)S(1)}, f32[1,256]{1,0:T(1,128)S(1)}, u32[]{:S(2)}, u32[]{:S(2)}) collective-permute-start(f32[1,256]{1,0:T(1,128)S(1)} %shard_map.115.refs_0_.mine), channel_id=1, source_target_pairs={{0,28},{1,25},{2,22},{3,19},{4,24},{5,29},{6,18},{7,23},{8,20},{9,... | collective-permute-start | bytes 3080 | tf_op jit(solution)/shard_map/ppermute | solution.py:242
  43.3 6.4 %collective-permute-start.24 = (f32[1,256]{1,0:T(1,128)S(1)}, f32[1,256]{1,0:T(1,128)S(1)}, u32[]{:S(2)}, u32[]{:S(2)}) collective-permute-start(f32[1,256]{1,0:T(1,128)S(1)} %shard_map.115.refs_0_.mine), channel_id=1, source_target_pairs={{0,4},{1,5},{2,10},{3,15},{4,0},{5,1},{6,14},{7,11},{8,12},{9,13},... | collective-permute-start | bytes 3080 | tf_op jit(solution)/shard_map/ppermute | solution.py:242
  47.5 3.7 %collective-permute-start.29 = (f32[4,256]{1,0:T(4,128)S(1)}, f32[4,256]{1,0:T(4,128)S(1)}, u32[]{:S(2)}, u32[]{:S(2)}) collective-permute-start(f32[4,256]{1,0:T(4,128)S(1)} %get-tuple-element.151), channel_id=1, source_target_pairs={{0,2},{1,3},{2,0},{3,1},{4,6},{5,7},{6,4},{7,5},{8,10},{9,11},{10,... | collective-permute-start | bytes 12296 | tf_op jit(solution)/shard_map/ppermute | solution.py:519
  48.2 3.0 %collective-permute-start.28 = (f32[8,512]{1,0:T(8,128)S(1)}, f32[8,512]{1,0:T(8,128)S(1)}, u32[]{:S(2)}, u32[]{:S(2)}) collective-permute-start(f32[8,512]{1,0:T(8,128)S(1)} %get-tuple-element.150), channel_id=1, source_target_pairs={{0,1},{1,0},{2,3},{3,2},{4,5},{5,4},{6,7},{7,6},{8,9},{9,8},{10,11... | collective-permute-start | bytes 49160 | tf_op jit(solution)/shard_map/ppermute | solution.py:519
  48.2 3.2 %collective-permute-start.30 = (f32[8,512]{1,0:T(8,128)S(1)}, f32[8,512]{1,0:T(8,128)S(1)}, u32[]{:S(2)}, u32[]{:S(2)}) collective-permute-start(f32[8,512]{1,0:T(8,128)S(1)} %get-tuple-element.152), channel_id=1, source_target_pairs={{0,3},{1,2},{2,1},{3,0},{4,7},{5,6},{6,5},{7,4},{8,11},{9,10},{10,... | collective-permute-start | bytes 49160 | tf_op jit(solution)/shard_map/ppermute | solution.py:519
  50.1 7.2 %collective-permute-start.26 = (f32[3,16,512]{2,1,0:T(8,128)S(1)}, f32[3,16,512]{2,1,0:T(8,128)S(1)}, u32[]{:S(2)}, u32[]{:S(2)}) collective-permute-start(f32[3,16,512]{2,1,0:T(8,128)S(1)} %get-tuple-element.147), channel_id=1, source_target_pairs={{0,4},{4,0},{8,12},{12,8},{16,20},{20,16},{24,28},{28,24},{1,5},{5... | collective-permute-start | bytes 294920 | tf_op jit(solution)/shard_map/ppermute | solution.py:46
  50.5 6.8 %collective-permute-start.27 = (f32[3,16,512]{2,1,0:T(8,128)S(1)}, f32[3,16,512]{2,1,0:T(8,128)S(1)}, u32[]{:S(2)}, u32[]{:S(2)}) collective-permute-start(f32[3,16,512]{2,1,0:T(8,128)S(1)} %get-tuple-element.148), channel_id=1, source_target_pairs={{0,1},{1,0},{2,3},{3,2},{4,8},{5,9},{6,10},{7,11},{8,4},{9,5},{10,... | collective-permute-start | bytes 294920 | tf_op jit(solution)/shard_map/ppermute | solution.py:47
  52.8 3.7 %collective-permute-start.32 = (f32[5,256]{1,0:T(8,128)S(1)}, f32[5,256]{1,0:T(8,128)S(1)}, u32[]{:S(2)}, u32[]{:S(2)}) collective-permute-start(f32[5,256]{1,0:T(8,128)S(1)} %get-tuple-element.159), channel_id=1, source_target_pairs={{0,2},{1,3},{2,0},{3,1},{4,6},{5,7},{6,4},{7,5},{8,10},{9,11},{10,... | collective-permute-start | bytes 15368 | tf_op jit(solution)/shard_map/ppermute | solution.py:519
  54.2 3.1 %collective-permute-start.33 = (f32[5,256]{1,0:T(8,128)S(1)}, f32[5,256]{1,0:T(8,128)S(1)}, u32[]{:S(2)}, u32[]{:S(2)}) collective-permute-start(f32[5,256]{1,0:T(8,128)S(1)} %get-tuple-element.160), channel_id=1, source_target_pairs={{0,3},{1,2},{2,1},{3,0},{4,7},{5,6},{6,5},{7,4},{8,11},{9,10},{10,... | collective-permute-start | bytes 15368 | tf_op jit(solution)/shard_map/ppermute | solution.py:519
  59.6 4.5 %collective-permute-start.34 = (f32[9,512]{1,0:T(8,128)S(1)}, f32[9,512]{1,0:T(8,128)S(1)}, u32[]{:S(2)}, u32[]{:S(2)}) collective-permute-start(f32[9,512]{1,0:T(8,128)S(1)} %get-tuple-element.163), channel_id=1, source_target_pairs={{0,1},{1,0},{2,3},{3,2},{4,5},{5,4},{6,7},{7,6},{8,9},{9,8},{10,11... | collective-permute-start | bytes 55304 | tf_op jit(solution)/shard_map/ppermute | solution.py:519
  59.7 4.4 %collective-permute-start.36 = (f32[9,512]{1,0:T(8,128)S(1)}, f32[9,512]{1,0:T(8,128)S(1)}, u32[]{:S(2)}, u32[]{:S(2)}) collective-permute-start(f32[9,512]{1,0:T(8,128)S(1)} %get-tuple-element.165), channel_id=1, source_target_pairs={{0,3},{1,2},{2,1},{3,0},{4,7},{5,6},{6,5},{7,4},{8,11},{9,10},{10,... | collective-permute-start | bytes 55304 | tf_op jit(solution)/shard_map/ppermute | solution.py:519
  60.5 3.7 %collective-permute-start.35 = (f32[5,256]{1,0:T(8,128)S(1)}, f32[5,256]{1,0:T(8,128)S(1)}, u32[]{:S(2)}, u32[]{:S(2)}) collective-permute-start(f32[5,256]{1,0:T(8,128)S(1)} %get-tuple-element.164), channel_id=1, source_target_pairs={{0,2},{1,3},{2,0},{3,1},{4,6},{5,7},{6,4},{7,5},{8,10},{9,11},{10,... | collective-permute-start | bytes 15368 | tf_op jit(solution)/shard_map/ppermute | solution.py:519
  61.8 5.5 %collective-permute-start.37 = (f32[3,16,512]{2,1,0:T(8,128)S(1)}, f32[3,16,512]{2,1,0:T(8,128)S(1)}, u32[]{:S(2)}, u32[]{:S(2)}) collective-permute-start(f32[3,16,512]{2,1,0:T(8,128)S(1)} %get-tuple-element.167), channel_id=1, source_target_pairs={{0,4},{4,0},{8,12},{12,8},{16,20},{20,16},{24,28},{28,24},{1,5},{5... | collective-permute-start | bytes 294920 | tf_op jit(solution)/shard_map/ppermute | solution.py:46
  63.0 9.7 %collective-permute-start.38 = (f32[3,16,512]{2,1,0:T(8,128)S(1)}, f32[3,16,512]{2,1,0:T(8,128)S(1)}, u32[]{:S(2)}, u32[]{:S(2)}) collective-permute-start(f32[3,16,512]{2,1,0:T(8,128)S(1)} %get-tuple-element.168), channel_id=1, source_target_pairs={{0,1},{1,0},{2,3},{3,2},{4,8},{5,9},{6,10},{7,11},{8,4},{9,5},{10,... | collective-permute-start | bytes 294920 | tf_op jit(solution)/shard_map/ppermute | solution.py:47
  64.9 7.8 %collective-permute-start.40 = (f32[4,256]{1,0:T(4,128)S(1)}, f32[4,256]{1,0:T(4,128)S(1)}, u32[]{:S(2)}, u32[]{:S(2)}) collective-permute-start(f32[4,256]{1,0:T(4,128)S(1)} %get-tuple-element.170), channel_id=1, source_target_pairs={{0,2},{1,3},{2,0},{3,1},{4,6},{5,7},{6,4},{7,5},{8,10},{9,11},{10,... | collective-permute-start | bytes 12296 | tf_op jit(solution)/shard_map/ppermute | solution.py:519
  66.3 6.4 %collective-permute-start.41 = (f32[4,256]{1,0:T(4,128)S(1)}, f32[4,256]{1,0:T(4,128)S(1)}, u32[]{:S(2)}, u32[]{:S(2)}) collective-permute-start(f32[4,256]{1,0:T(4,128)S(1)} %get-tuple-element.171), channel_id=1, source_target_pairs={{0,3},{1,2},{2,1},{3,0},{4,7},{5,6},{6,5},{7,4},{8,11},{9,10},{10,... | collective-permute-start | bytes 12296 | tf_op jit(solution)/shard_map/ppermute | solution.py:519
  67.3 9.4 %collective-permute-start.43 = (f32[1,256]{1,0:T(1,128)S(1)}, f32[1,256]{1,0:T(1,128)S(1)}, u32[]{:S(2)}, u32[]{:S(2)}) collective-permute-start(f32[1,256]{1,0:T(1,128)S(1)} %shard_map.123.refs_0_.mine), channel_id=1, source_target_pairs={{0,28},{1,25},{2,22},{3,19},{4,24},{5,29},{6,18},{7,23},{8,20},{9,... | collective-permute-start | bytes 3080 | tf_op jit(solution)/shard_map/ppermute | solution.py:242
  70.3 6.4 %collective-permute-start.42 = (f32[1,256]{1,0:T(1,128)S(1)}, f32[1,256]{1,0:T(1,128)S(1)}, u32[]{:S(2)}, u32[]{:S(2)}) collective-permute-start(f32[1,256]{1,0:T(1,128)S(1)} %shard_map.123.refs_0_.mine), channel_id=1, source_target_pairs={{0,4},{1,5},{2,10},{3,15},{4,0},{5,1},{6,14},{7,11},{8,12},{9,13},... | collective-permute-start | bytes 3080 | tf_op jit(solution)/shard_map/ppermute | solution.py:242
  74.5 3.7 %collective-permute-start.47 = (f32[4,256]{1,0:T(4,128)S(1)}, f32[4,256]{1,0:T(4,128)S(1)}, u32[]{:S(2)}, u32[]{:S(2)}) collective-permute-start(f32[4,256]{1,0:T(4,128)S(1)} %get-tuple-element.178), channel_id=1, source_target_pairs={{0,2},{1,3},{2,0},{3,1},{4,6},{5,7},{6,4},{7,5},{8,10},{9,11},{10,... | collective-permute-start | bytes 12296 | tf_op jit(solution)/shard_map/ppermute | solution.py:519
  74.6 3.6 %collective-permute-start.46 = (f32[8,512]{1,0:T(8,128)S(1)}, f32[8,512]{1,0:T(8,128)S(1)}, u32[]{:S(2)}, u32[]{:S(2)}) collective-permute-start(f32[8,512]{1,0:T(8,128)S(1)} %get-tuple-element.177), channel_id=1, source_target_pairs={{0,1},{1,0},{2,3},{3,2},{4,5},{5,4},{6,7},{7,6},{8,9},{9,8},{10,11... | collective-permute-start | bytes 49160 | tf_op jit(solution)/shard_map/ppermute | solution.py:519
  74.6 3.5 %collective-permute-start.48 = (f32[8,512]{1,0:T(8,128)S(1)}, f32[8,512]{1,0:T(8,128)S(1)}, u32[]{:S(2)}, u32[]{:S(2)}) collective-permute-start(f32[8,512]{1,0:T(8,128)S(1)} %get-tuple-element.179), channel_id=1, source_target_pairs={{0,3},{1,2},{2,1},{3,0},{4,7},{5,6},{6,5},{7,4},{8,11},{9,10},{10,... | collective-permute-start | bytes 49160 | tf_op jit(solution)/shard_map/ppermute | solution.py:519
  77.1 7.0 %collective-permute-start.44 = (f32[3,16,512]{2,1,0:T(8,128)S(1)}, f32[3,16,512]{2,1,0:T(8,128)S(1)}, u32[]{:S(2)}, u32[]{:S(2)}) collective-permute-start(f32[3,16,512]{2,1,0:T(8,128)S(1)} %get-tuple-element.174), channel_id=1, source_target_pairs={{0,4},{4,0},{8,12},{12,8},{16,20},{20,16},{24,28},{28,24},{1,5},{5... | collective-permute-start | bytes 294920 | tf_op jit(solution)/shard_map/ppermute | solution.py:46
  77.2 7.0 %collective-permute-start.45 = (f32[3,16,512]{2,1,0:T(8,128)S(1)}, f32[3,16,512]{2,1,0:T(8,128)S(1)}, u32[]{:S(2)}, u32[]{:S(2)}) collective-permute-start(f32[3,16,512]{2,1,0:T(8,128)S(1)} %get-tuple-element.175), channel_id=1, source_target_pairs={{0,1},{1,0},{2,3},{3,2},{4,8},{5,9},{6,10},{7,11},{8,4},{9,5},{10,... | collective-permute-start | bytes 294920 | tf_op jit(solution)/shard_map/ppermute | solution.py:47
  79.1 3.7 %collective-permute-start.50 = (f32[5,256]{1,0:T(8,128)S(1)}, f32[5,256]{1,0:T(8,128)S(1)}, u32[]{:S(2)}, u32[]{:S(2)}) collective-permute-start(f32[5,256]{1,0:T(8,128)S(1)} %get-tuple-element.186), channel_id=1, source_target_pairs={{0,2},{1,3},{2,0},{3,1},{4,6},{5,7},{6,4},{7,5},{8,10},{9,11},{10,... | collective-permute-start | bytes 15368 | tf_op jit(solution)/shard_map/ppermute | solution.py:519
  81.0 3.1 %collective-permute-start.51 = (f32[5,256]{1,0:T(8,128)S(1)}, f32[5,256]{1,0:T(8,128)S(1)}, u32[]{:S(2)}, u32[]{:S(2)}) collective-permute-start(f32[5,256]{1,0:T(8,128)S(1)} %get-tuple-element.187), channel_id=1, source_target_pairs={{0,3},{1,2},{2,1},{3,0},{4,7},{5,6},{6,5},{7,4},{8,11},{9,10},{10,... | collective-permute-start | bytes 15368 | tf_op jit(solution)/shard_map/ppermute | solution.py:519
  (14 other events, 37.3 us)

commit v8 on v7

--- a/solution.py
+++ b/solution.py
@@ -183,10 +183,7 @@
     return jnp.concatenate([high, low], axis=0)
 
 
-def stencil_kernel(after, vec, trans, diag, *refs):
-    *faces, out, shifted = refs[after:]
-    if faces:
-        write_faces(Planes(vec), faces)
+def stencil_kernel(vec, trans, diag, after, out, shifted):
     inner_stencil(vec, trans, diag, shifted, out)
 
 
@@ -223,23 +220,22 @@
     return out
 
 
-def share(count, groups):
-    return -(-count // groups)
-
-
-def share_mask(g, q, groups):
-    return q * groups + (g if q % 2 == 0 else groups - 1 - g)
-
-
-def share_swap(row, q):
+def near_fetch(row):
     count, groups = lax.axis_size("res"), lax.axis_size("grp")
     pairs = []
     for r in range(count):
         for g in range(groups):
-            mask = share_mask(g, q, groups)
-            mask = mask if 0 < mask < count else 1
+            mask = g if 0 < g < count else 1
             pairs.append((r * groups + g, (r ^ mask) * groups + g))
     return lax.ppermute(row, ("res", "grp"), pairs)
+
+
+def far_fetch(row):
+    count, groups = lax.axis_size("res"), lax.axis_size("grp")
+    return [
+        lax.ppermute(row, "res", [(r, r ^ mask) for r in range(count)])
+        for mask in range(groups, count, groups)
+    ]
 
 
 def spot(message, slot, segb):
@@ -303,26 +299,13 @@
 
 
 def group_sum_kernel(capacity, after, *refs):
-    *messages, out = refs[after:]
+    *messages, out = refs
     segb = out.shape[1]
     total = jnp.zeros(out.shape, F32)
     for k, message in enumerate(messages):
         row = coupled_rows(k, capacity, segb, max(m.shape[1] for m in messages))
         total = total + message[row : row + 1, 0:segb]
     out[...] = total
-
-
-def append_kernel(groups, mine, *refs):
-    values, fetched, outs = refs[:groups], refs[groups:-groups], refs[-groups:]
-    count, g = lax.axis_size("res"), lax.axis_index("grp")
-    row = jnp.where(g == 0, mine[...], 0.0)
-    for q, ref in enumerate(fetched):
-        mask = share_mask(g, q, groups)
-        row = row + jnp.where((mask > 0) & (mask < count), ref[...], 0.0)
-    capacity = values[0].shape[0]
-    for value, out in zip(values, outs):
-        out[0:capacity] = value[...]
-        out[capacity : capacity + 1] = row
 
 
 def well_terms(values, placed, column, give, owner, capacity, shape):
@@ -404,27 +387,38 @@
 
 def apply_kernel(sizes, *refs):
     got = Arrived(*sizes, refs)
+    row = None
+    if len(got.rest) > 1 + sizes[0] + 2:
+        mine, fetched, *got.rest = got.rest
+        g = lax.axis_index("grp")
+        row = jnp.where(g < lax.axis_size("res"), fetched[...], 0.0)
+        row = jnp.where(g == 0, mine[...], row)
     out, *sends = got.rest
     value = got.result()
     for i in range(out.shape[0]):
         for x in range(out.shape[1]):
             out[i, x] = value(i, x)
-    got.send(out, sends)
+    got.send(out, sends, row)
 
 
 def local_sums(vecs, width):
     b, r, s, w, z = vecs
     table = {"b": b, "r": r, "s": s, "w": w, "z": z}
+    known = {}
     lanes = lax.broadcasted_iota(jnp.int32, (1, width), 1)
     row = jnp.zeros((1, width), F32)
     for k, name in enumerate(NAMES):
         left, right = table[name[0]], table[name[1]]
-        total = None
-        for i in range(b.shape[0]):
-            for x in range(b.shape[1]):
-                term = left[i, x] * right[i, x]
-                total = term if total is None else total + term
-        total = jnp.sum(jnp.sum(total, axis=0, keepdims=True), axis=1, keepdims=True)
+        pair = id(left), id(right)
+        if pair not in known:
+            total = None
+            for i in range(b.shape[0]):
+                for x in range(b.shape[1]):
+                    term = left[i, x] * right[i, x]
+                    total = term if total is None else total + term
+            total = jnp.sum(total, axis=0, keepdims=True)
+            known[pair] = jnp.sum(total, axis=1, keepdims=True)
+        total = known[pair]
         row = jnp.where(lanes == k, total, row)
     return row
 
@@ -453,8 +447,9 @@
     return alpha, omega, beta
 
 
-def step_kernel(sizes, first_time, end, *refs):
+def step_kernel(sizes, parts, first_time, end, *refs):
     got = Arrived(*sizes, refs)
+    sums, got.rest = got.rest[:parts], got.rest[parts:]
     if first_time:
         r, w, t, v, *rest = got.rest
         s, z, p, x_in, fix = w, t, r, None, None
@@ -465,10 +460,9 @@
     if not end:
         t_out, fix_out, *rest = rest
     value = got.result()
-    last = slice(got.capacity, got.capacity + 1)
-    row = got.values[0][last]
-    for ref in got.values[1:]:
-        row = row + ref[last]
+    row = sums[0][...]
+    for ref in sums[1:]:
+        row = row + ref[...]
     alpha, omega, beta = coefficients(row)
     for i in range(r.shape[0]):
         for x in range(r.shape[1]):
@@ -593,34 +587,19 @@
         specs[7] = SMEM
         return call(kernel, outs, args, specs, flops=1_000_000_000, moved=8_000_000)
 
-    def apply(kernel, outs, vec, sends, extra, sums=None, with_sums=False):
+    def apply(kernel, outs, vec, sends, extra, then=None):
         messages, faces = swapped(sends[:groups]), sends[groups:]
-        values = solve(False, [first, second, *messages])
-        first_here = values[:1] if faces else sums
-        *made, part = call(
-            functools.partial(stencil_kernel, len(first_here)),
-            ([] if faces else face_outs) + [field],
-            [vec, trans, diag, *first_here],
-            **cost,
-        )
-        halo = exchange(faces or made)
-        if sums is not None:
-            values = call(
-                functools.partial(append_kernel, groups),
-                [((capacity + 1, segb), F32)] * groups,
-                [sums[0], *values, *sums[1:]],
-            )
-        values = swapped(values)
-        out = finish(kernel, outs, part, messages, values, halo, extra)
-        return (fetch(messages, [values[1], halo[0]]), out) if with_sums else out
-
-    def fetch(messages, after):
-        mine = call(
-            functools.partial(group_sum_kernel, capacity, len(after)),
-            [((1, segb), F32)],
-            [*after, *messages],
-        )[0]
-        return [mine] + [share_swap(mine, q) for q in range(share(lax.axis_size("res"), groups))]
+        back = solve(False, [first, second, *messages])
+        part = call(stencil_kernel, [field], [vec, trans, diag, back[0]], **cost)[0]
+        halo, values = exchange(faces), swapped(back)
+        if then is not None:
+            mine = call(
+                functools.partial(group_sum_kernel, capacity),
+                [((1, segb), F32)],
+                [values[1], *messages],
+            )[0]
+            extra = [mine, *then(mine), *extra]
+        return finish(kernel, outs, part, messages, values, halo, extra)
 
     kept = [(inverse.shape[1:], BF16)] * 2
     first, second = call(split_kernel, kept, [inverse[0]])
@@ -638,14 +617,16 @@
         functools.partial(second_kernel, sizes), [field] + summed + face_outs, w, sends, [b, w]
     )
     r, s, z, p, x, fix = b, w, t, b, None, None
+    parts = 1 + len(range(groups, lax.axis_size("res"), groups))
     for index in range(ITERS - 1):
         start, end = index == 0, index + 2 == ITERS
-        sums, (v, *sends) = apply(plainly, [field] + plain, z, sends, [], None, True)
+        v, *sends = apply(
+            plainly, [field] + summed + face_outs, z, sends, [], lambda row: [near_fetch(row)]
+        )
         given = [r, w, t, v] if start else [b, r, w, t, v, s, z, p, x, fix]
         tail = [((devices, 1, 128), F32)] if end else [field] * 2 + summed + face_outs
-        r, w, s, z, p, x, *sends = apply(
-            functools.partial(step_kernel, sizes, start, end), [field] * 6 + tail, v, sends, given, sums
-        )
+        kernel = functools.partial(step_kernel, sizes, parts, start, end)
+        r, w, s, z, p, x, *sends = apply(kernel, [field] * 6 + tail, v, sends, given, far_fetch)
         if not end:
             t, fix, *sends = sends
     sums = lax.all_to_all(sends[0], ("res", "grp"), split_axis=0, concat_axis=0, tiled=True)

time: 96.5 us -> 99.3 us (1.029)
  starting transfers between devices: 45.1 us -> 48.8 us
  waiting for transfers between devices: 13.4 us -> 10.8 us
  blocking collectives: 9.51 us -> 11.3 us
    ppermute x36, waiting for transfers between devices: 12.2 us -> 4.75 us  [swapped(): lax.ppermute(messages[k], 'grp', [(i, i ^ k) for i in range(groups)])]
    ppermute x4, waiting for transfers between devices: 0.01 us -> 6.03 us  [the longest x2 3.82 us: far_fetch(): lax.ppermute(row, 'res', [(r, r ^ mask) for r in range(count)])]
    ppermute x6, starting transfers between devices: 8.78 us -> 13.4 us  [exchange(): lax.ppermute(faces[0], 'res', first)]
    all_to_all x1, blocking collectives: 9.51 us -> 11.3 us  [body(): lax.all_to_all(sends[0], ('res', 'grp'), split_axis=0, concat_axis=0, til...]
    ppermute x6, waiting for transfers between devices: 1.16 us -> 0.02 us  [exchange(): lax.ppermute(faces[0], 'res', first)]
  transfers between devices with their start and end apart: 52 -> 52, of which waited for: 14 -> 13; matrix products, arithmetic and copies ran while one was open for 0% -> 0% of each run, Pallas kernels for 14% -> 10%
where the time goes in v8:
time: 99.3 us; the launch traced here: 99.1 us
  starting transfers between devices  48.8 us (49%)
  Pallas kernels  24.8 us (25%)
  blocking collectives  11.3 us (11%)
  waiting for transfers between devices  10.8 us (11%)
  local copies, waits for them, and re-layouts  2.23 us (2%)
  between operations  1.04 us (1%)
    ppermute x36, starting transfers between devices, swapped(): lax.ppermute(messages[k], 'grp', [(i, i ^ k) for i in range(groups)])  26.3 us
    pallas_call x25, Pallas kernels, call(): pl.pallas_call(kernel, out_shape=[jax.ShapeDtypeStruct(shape, dtype) for...  24.8 us
    ppermute x6, starting transfers between devices, exchange(): lax.ppermute(faces[0], 'res', first)  13.4 us
    all_to_all x1, blocking collectives, body(): lax.all_to_all(sends[0], ('res', 'grp'), split_axis=0, concat_axis=0, til...  11.3 us
    ppermute x2, starting transfers between devices, near_fetch(): return lax.ppermute(row, ('res', 'grp'), pairs)  5.11 us
    ppermute x36, waiting for transfers between devices, swapped(): lax.ppermute(messages[k], 'grp', [(i, i ^ k) for i in range(groups)])  4.75 us
    ppermute x2, starting transfers between devices, far_fetch(): lax.ppermute(row, 'res', [(r, r ^ mask) for r in range(count)])  4.09 us
    ppermute x2, waiting for transfers between devices, far_fetch(): lax.ppermute(row, 'res', [(r, r ^ mask) for r in range(count)])  3.82 us
  transfers between devices with their start and end apart: 52, of which 13 were waited for; matrix products, arithmetic and copies ran while one was open for 0% of the time, Pallas kernels for 10%

profile of v8, /device:TPU:0, one launch (start us, length us, event | category | flops | bytes accessed | tf_op | source)
XLA Modules:
  0.0 99.1 jit_solution(2398399088590853806)
XLA Ops:
  0.6 3.2 %shard_map.104 = (bf16[512,2048]{1,0:T(8,128)(2,1)}, s32[8,256]{1,0:T(8,128)}, f32[3,8,256]{2,1,0:T(8,128)}, f32[3,8,256]{2,1,0:T(8,128)}, f32[4,256]{1,0:T(4,12...) custom-call(f32[3,2,16,512]{3,2,1,0:T(8,128)} %refs_20_.3, ...), custom_call_target="tpu_custom_call" | custom-call | flops 1000000 | bytes 1000000 | tf_op jit(solution)/shard_map/pallas_call | solution.py:24
  4.3 2.6 %collective-permute-start.2 = (f32[8,512]{1,0:T(8,128)}, f32[8,512]{1,0:T(8,128)S(1)}, u32[]{:S(2)}, u32[]{:S(2)}) collective-permute-start(f32[8,512]{1,0:T(8,128)} %get-tuple-element.98), channel_id=1, source_target_pairs={{0,3},{1,2},{2,1},{3,0},{4,7},{5,6},{6,5},{7,4},{8,11},{9,10},{10,... | collective-permute-start | bytes 49160 | tf_op jit(solution)/shard_map/ppermute | solution.py:513
  7.0 2.0 %collective-permute-start.3 = (f32[3,16,512]{2,1,0:T(8,128)}, f32[3,16,512]{2,1,0:T(8,128)S(1)}, u32[]{:S(2)}, u32[]{:S(2)}) collective-permute-start(f32[3,16,512]{2,1,0:T(8,128)} %get-tuple-element.105), channel_id=1, source_target_pairs={{0,4},{4,0},{8,12},{12,8},{16,20},{20,16},{24,28},{28,24},{1,5},{5... | collective-permute-start | bytes 294920 | tf_op jit(solution)/shard_map/ppermute | solution.py:46
  9.0 2.2 %copy-done.3 = f32[1,4,4,256,256]{4,3,2,1,0:T(8,128)S(1)} copy-done((f32[1,4,4,256,256]{4,3,2,1,0:T(8,128)S(1)}, f32[1,4,4,256,256]{4,3,2,1,0:T(8,128)}, u32[]{:S(2)}) %copy-start.3) | copy-done | bytes 4194328
  11.9 1.2 %shard_map.106 = (f32[4,256]{1,0:T(4,128)S(1)}, f32[4,256]{1,0:T(4,128)S(1)}, f32[4,256]{1,0:T(4,128)S(1)}, f32[4,256]{1,0:T(4,128)S(1)}) custom-call(bf16[4,4,256,256]{3,2,1,0:T(8,128)(2,1)S(1)} %get-tuple-element.93.first, bf16[4,4,256,256]{3,2,1,0:T(8,128)(2,1)S(1)} %get-tuple-element.94.second, f32[4,256]{1,0:T(4,128)S(1)} %copy-done.9, ...), custom_call_target="tpu_custom_call" | custom-call | flops 5000000000 | bytes 4000000 | tf_op jit(solution)/shard_map/pallas_call | solution.py:24
  13.7 1.5 %collective-permute-start.6 = (f32[4,256]{1,0:T(4,128)S(1)}, f32[4,256]{1,0:T(4,128)S(1)}, u32[]{:S(2)}, u32[]{:S(2)}) collective-permute-start(f32[4,256]{1,0:T(4,128)S(1)} %get-tuple-element.108), channel_id=1, source_target_pairs={{0,2},{1,3},{2,0},{3,1},{4,6},{5,7},{6,4},{7,5},{8,10},{9,11},{10,... | collective-permute-start | bytes 12296 | tf_op jit(solution)/shard_map/ppermute | solution.py:513
  15.3 2.3 %shard_map.107 = (f32[3,2,16,512]{3,2,1,0:T(8,128)S(1)}, f32[3,3,2,16,512]{4,3,2,1,0:T(8,128)S(1)}, bf16[2048,512]{1,0:T(8,128)(2,1)S(1)}, bf16[4,4,256,256]{3,2...) custom-call(f32[3,2,16,512]{3,2,1,0:T(8,128)S(1)} %copy-done.2, f32[6,3,3,2,16,512]{5,4,3,2,1,0:T(8,128)S(1)} %copy-done, ...), custom_call_target="tpu_custom_call" | custom-call | flops 200000000 | bytes 4000000 | tf_op jit(solution)/shard_map/pallas_call | solution.py:24
  18.3 1.8 %shard_map.108 = (f32[3,2,16,512]{3,2,1,0:T(8,128)S(1)}, f32[4,256]{1,0:T(4,128)S(1)}, f32[8,512]{1,0:T(8,128)S(1)}, f32[4,256]{1,0:T(4,128)S(1)}, f32[8,512]{1,...) custom-call(f32[3,2,16,512]{3,2,1,0:T(8,128)S(1)} %get-tuple-element.100.refs_0_, ...), custom_call_target="tpu_custom_call" | custom-call | flops 1000000000 | bytes 8000000 | tf_op jit(solution)/shard_map/pallas_call | solution.py:24
  20.2 1.1 %collective-permute-start.10 = (f32[8,512]{1,0:T(8,128)S(1)}, f32[8,512]{1,0:T(8,128)S(1)}, u32[]{:S(2)}, u32[]{:S(2)}) collective-permute-start(f32[8,512]{1,0:T(8,128)S(1)} %get-tuple-element.117), channel_id=1, source_target_pairs={{0,3},{1,2},{2,1},{3,0},{4,7},{5,6},{6,5},{7,4},{8,11},{9,10},{10,... | collective-permute-start | bytes 49160 | tf_op jit(solution)/shard_map/ppermute | solution.py:513
  21.4 0.9 collective-permute-start.9
  22.3 2.6 %collective-permute-start.11 = (f32[3,16,512]{2,1,0:T(8,128)S(1)}, f32[3,16,512]{2,1,0:T(8,128)S(1)}, u32[]{:S(2)}, u32[]{:S(2)}) collective-permute-start(f32[3,16,512]{2,1,0:T(8,128)S(1)} %get-tuple-element.119), channel_id=1, source_target_pairs={{0,4},{4,0},{8,12},{12,8},{16,20},{20,16},{24,28},{28,24},{1,5},{5... | collective-permute-start | bytes 294920 | tf_op jit(solution)/shard_map/ppermute | solution.py:46
  25.0 0.7 shard_map.109
  26.2 1.2 %collective-permute-start.14 = (f32[4,256]{1,0:T(4,128)S(1)}, f32[4,256]{1,0:T(4,128)S(1)}, u32[]{:S(2)}, u32[]{:S(2)}) collective-permute-start(f32[4,256]{1,0:T(4,128)S(1)} %get-tuple-element.122), channel_id=1, source_target_pairs={{0,2},{1,3},{2,0},{3,1},{4,6},{5,7},{6,4},{7,5},{8,10},{9,11},{10,... | collective-permute-start | bytes 12296 | tf_op jit(solution)/shard_map/ppermute | solution.py:513
  28.0 1.7 %collective-permute-done.14.refs_16_ = f32[4,256]{1,0:T(4,128)S(1)} collective-permute-done((f32[4,256]{1,0:T(4,128)S(1)}, f32[4,256]{1,0:T(4,128)S(1)}, u32[]{:S(2)}, u32[]{:S(2)}) %collective-permute-start.14) | collective-permute-done | bytes 4128 | tf_op jit(solution)/shard_map/ppermute | solution.py:513
  30.4 1.8 %shard_map.111 = (f32[3,2,16,512]{3,2,1,0:T(8,128)S(1)}, f32[5,256]{1,0:T(8,128)S(1)}, f32[9,512]{1,0:T(8,128)S(1)}, f32[5,256]{1,0:T(8,128)S(1)}, f32[9,512]{1,...) custom-call(f32[3,2,16,512]{3,2,1,0:T(8,128)S(1)} %shard_map.110.refs_0_, ...), custom_call_target="tpu_custom_call" | custom-call | flops 1000000000 | bytes 8000000 | tf_op jit(solution)/shard_map/pallas_call | solution.py:24
  32.4 0.9 collective-permute-start.18
  33.3 1.2 %collective-permute-start.17 = (f32[5,256]{1,0:T(8,128)S(1)}, f32[5,256]{1,0:T(8,128)S(1)}, u32[]{:S(2)}, u32[]{:S(2)}) collective-permute-start(f32[5,256]{1,0:T(8,128)S(1)} %get-tuple-element.127), channel_id=1, source_target_pairs={{0,2},{1,3},{2,0},{3,1},{4,6},{5,7},{6,4},{7,5},{8,10},{9,11},{10,... | collective-permute-start | bytes 15368 | tf_op jit(solution)/shard_map/ppermute | solution.py:513
  34.5 2.6 %collective-permute-start.19 = (f32[3,16,512]{2,1,0:T(8,128)S(1)}, f32[3,16,512]{2,1,0:T(8,128)S(1)}, u32[]{:S(2)}, u32[]{:S(2)}) collective-permute-start(f32[3,16,512]{2,1,0:T(8,128)S(1)} %get-tuple-element.130), channel_id=1, source_target_pairs={{0,4},{4,0},{8,12},{12,8},{16,20},{20,16},{24,28},{28,24},{1,5},{5... | collective-permute-start | bytes 294920 | tf_op jit(solution)/shard_map/ppermute | solution.py:46
  37.1 0.7 shard_map.112
  38.3 0.8 collective-permute-start.22
  39.8 3.0 %collective-permute-start.24 = (f32[1,256]{1,0:T(1,128)S(1)}, f32[1,256]{1,0:T(1,128)S(1)}, u32[]{:S(2)}, u32[]{:S(2)}) collective-permute-start(f32[1,256]{1,0:T(1,128)S(1)} %shard_map.114.refs_18_), channel_id=1, source_target_pairs={{0,4},{1,5},{2,10},{3,15},{4,0},{5,1},{6,14},{7,11},{8,12},{9,13},... | collective-permute-start | bytes 3080 | tf_op jit(solution)/shard_map/ppermute | solution.py:230
  43.2 1.1 %collective-permute-done.24.refs_19_ = f32[1,256]{1,0:T(1,128)S(1)} collective-permute-done((f32[1,256]{1,0:T(1,128)S(1)}, f32[1,256]{1,0:T(1,128)S(1)}, u32[]{:S(2)}, u32[]{:S(2)}) %collective-permute-start.24) | collective-permute-done | bytes 1056 | tf_op jit(solution)/shard_map/ppermute | solution.py:230
  44.4 1.7 %shard_map.115 = (f32[3,2,16,512]{3,2,1,0:T(8,128)S(1)}, f32[5,256]{1,0:T(8,128)S(1)}, f32[9,512]{1,0:T(8,128)S(1)}, f32[5,256]{1,0:T(8,128)S(1)}, f32[9,512]{1,...) custom-call(f32[3,2,16,512]{3,2,1,0:T(8,128)S(1)} %shard_map.113.refs_0_, ...), custom_call_target="tpu_custom_call" | custom-call | flops 1000000000 | bytes 8000000 | tf_op jit(solution)/shard_map/pallas_call | solution.py:24
  46.2 0.8 collective-permute-start.27
  47.0 1.4 %collective-permute-start.26 = (f32[5,256]{1,0:T(8,128)S(1)}, f32[5,256]{1,0:T(8,128)S(1)}, u32[]{:S(2)}, u32[]{:S(2)}) collective-permute-start(f32[5,256]{1,0:T(8,128)S(1)} %get-tuple-element.138), channel_id=1, source_target_pairs={{0,2},{1,3},{2,0},{3,1},{4,6},{5,7},{6,4},{7,5},{8,10},{9,11},{10,... | collective-permute-start | bytes 15368 | tf_op jit(solution)/shard_map/ppermute | solution.py:513
  48.3 2.0 %collective-permute-start.28 = (f32[3,16,512]{2,1,0:T(8,128)S(1)}, f32[3,16,512]{2,1,0:T(8,128)S(1)}, u32[]{:S(2)}, u32[]{:S(2)}) collective-permute-start(f32[3,16,512]{2,1,0:T(8,128)S(1)} %get-tuple-element.141), channel_id=1, source_target_pairs={{0,4},{4,0},{8,12},{12,8},{16,20},{20,16},{24,28},{28,24},{1,5},{5... | collective-permute-start | bytes 294920 | tf_op jit(solution)/shard_map/ppermute | solution.py:46
  50.6 0.7 shard_map.116
  51.8 1.2 %collective-permute-start.31 = (f32[4,256]{1,0:T(4,128)S(1)}, f32[4,256]{1,0:T(4,128)S(1)}, u32[]{:S(2)}, u32[]{:S(2)}) collective-permute-start(f32[4,256]{1,0:T(4,128)S(1)} %get-tuple-element.144), channel_id=1, source_target_pairs={{0,2},{1,3},{2,0},{3,1},{4,6},{5,7},{6,4},{7,5},{8,10},{9,11},{10,... | collective-permute-start | bytes 12296 | tf_op jit(solution)/shard_map/ppermute | solution.py:513
  53.4 2.0 %collective-permute-start.33 = (f32[1,256]{1,0:T(1,128)S(1)}, f32[1,256]{1,0:T(1,128)S(1)}, u32[]{:S(2)}, u32[]{:S(2)}) collective-permute-start(f32[1,256]{1,0:T(1,128)S(1)} %shard_map.118.refs_18_), channel_id=1, source_target_pairs={{0,16},{4,20},{8,24},{12,28},{16,0},{20,4},{24,8},{28,12},{1,17},{... | collective-permute-start | bytes 3080 | tf_op jit(solution)/shard_map/ppermute | solution.py:236
  56.0 1.9 %collective-permute-done.33.refs_19_ = f32[1,256]{1,0:T(1,128)S(1)} collective-permute-done((f32[1,256]{1,0:T(1,128)S(1)}, f32[1,256]{1,0:T(1,128)S(1)}, u32[]{:S(2)}, u32[]{:S(2)}) %collective-permute-start.33) | collective-permute-done | bytes 1056 | tf_op jit(solution)/shard_map/ppermute | solution.py:236
  57.9 2.2 %shard_map.119 = (f32[3,2,16,512]{3,2,1,0:T(8,128)S(1)}, f32[3,2,16,512]{3,2,1,0:T(8,128)S(1)}, f32[3,2,16,512]{3,2,1,0:T(8,128)S(1)}, f32[3,2,16,512]{3,2,1,0:T...) custom-call(f32[3,2,16,512]{3,2,1,0:T(8,128)S(1)} %shard_map.117.ref, ...), custom_call_target="tpu_custom_call" | custom-call | flops 1000000000 | bytes 8000000 | tf_op jit(solution)/shard_map/pallas_call | solution.py:24
  60.2 1.5 %collective-permute-start.36 = (f32[9,512]{1,0:T(8,128)S(1)}, f32[9,512]{1,0:T(8,128)S(1)}, u32[]{:S(2)}, u32[]{:S(2)}) collective-permute-start(f32[9,512]{1,0:T(8,128)S(1)} %get-tuple-element.150), channel_id=1, source_target_pairs={{0,3},{1,2},{2,1},{3,0},{4,7},{5,6},{6,5},{7,4},{8,11},{9,10},{10,... | collective-permute-start | bytes 55304 | tf_op jit(solution)/shard_map/ppermute | solution.py:513
  62.4 2.2 %collective-permute-start.37 = (f32[3,16,512]{2,1,0:T(8,128)S(1)}, f32[3,16,512]{2,1,0:T(8,128)S(1)}, u32[]{:S(2)}, u32[]{:S(2)}) collective-permute-start(f32[3,16,512]{2,1,0:T(8,128)S(1)} %get-tuple-element.152), channel_id=1, source_target_pairs={{0,4},{4,0},{8,12},{12,8},{16,20},{20,16},{24,28},{28,24},{1,5},{5... | collective-permute-start | bytes 294920 | tf_op jit(solution)/shard_map/ppermute | solution.py:46
  64.6 0.8 collective-permute-done.35.refs_2_.refs_12_
  66.2 0.9 collective-permute-start.40
  67.1 1.0 collective-permute-start.41
  68.0 2.1 %collective-permute-start.42 = (f32[1,256]{1,0:T(1,128)S(1)}, f32[1,256]{1,0:T(1,128)S(1)}, u32[]{:S(2)}, u32[]{:S(2)}) collective-permute-start(f32[1,256]{1,0:T(1,128)S(1)} %shard_map.122.refs_18_), channel_id=1, source_target_pairs={{0,4},{1,5},{2,10},{3,15},{4,0},{5,1},{6,14},{7,11},{8,12},{9,13},... | collective-permute-start | bytes 3080 | tf_op jit(solution)/shard_map/ppermute | solution.py:230
  70.6 1.1 %collective-permute-done.42.refs_19_ = f32[1,256]{1,0:T(1,128)S(1)} collective-permute-done((f32[1,256]{1,0:T(1,128)S(1)}, f32[1,256]{1,0:T(1,128)S(1)}, u32[]{:S(2)}, u32[]{:S(2)}) %collective-permute-start.42) | collective-permute-done | bytes 1056 | tf_op jit(solution)/shard_map/ppermute | solution.py:230
  71.7 1.7 %shard_map.123 = (f32[3,2,16,512]{3,2,1,0:T(8,128)S(1)}, f32[5,256]{1,0:T(8,128)S(1)}, f32[9,512]{1,0:T(8,128)S(1)}, f32[5,256]{1,0:T(8,128)S(1)}, f32[9,512]{1,...) custom-call(f32[3,2,16,512]{3,2,1,0:T(8,128)S(1)} %shard_map.121.refs_0_, ...), custom_call_target="tpu_custom_call" | custom-call | flops 1000000000 | bytes 8000000 | tf_op jit(solution)/shard_map/pallas_call | solution.py:24
  73.5 0.8 collective-permute-start.45
  74.3 1.4 %collective-permute-start.44 = (f32[5,256]{1,0:T(8,128)S(1)}, f32[5,256]{1,0:T(8,128)S(1)}, u32[]{:S(2)}, u32[]{:S(2)}) collective-permute-start(f32[5,256]{1,0:T(8,128)S(1)} %get-tuple-element.160), channel_id=1, source_target_pairs={{0,2},{1,3},{2,0},{3,1},{4,6},{5,7},{6,4},{7,5},{8,10},{9,11},{10,... | collective-permute-start | bytes 15368 | tf_op jit(solution)/shard_map/ppermute | solution.py:513
  75.6 2.0 %collective-permute-start.46 = (f32[3,16,512]{2,1,0:T(8,128)S(1)}, f32[3,16,512]{2,1,0:T(8,128)S(1)}, u32[]{:S(2)}, u32[]{:S(2)}) collective-permute-start(f32[3,16,512]{2,1,0:T(8,128)S(1)} %get-tuple-element.163), channel_id=1, source_target_pairs={{0,4},{4,0},{8,12},{12,8},{16,20},{20,16},{24,28},{28,24},{1,5},{5... | collective-permute-start | bytes 294920 | tf_op jit(solution)/shard_map/ppermute | solution.py:46
  78.9 1.2 %collective-permute-start.49 = (f32[4,256]{1,0:T(4,128)S(1)}, f32[4,256]{1,0:T(4,128)S(1)}, u32[]{:S(2)}, u32[]{:S(2)}) collective-permute-start(f32[4,256]{1,0:T(4,128)S(1)} %get-tuple-element.166), channel_id=1, source_target_pairs={{0,2},{1,3},{2,0},{3,1},{4,6},{5,7},{6,4},{7,5},{8,10},{9,11},{10,... | collective-permute-start | bytes 12296 | tf_op jit(solution)/shard_map/ppermute | solution.py:513
  80.5 2.0 %collective-permute-start.51 = (f32[1,256]{1,0:T(1,128)S(1)}, f32[1,256]{1,0:T(1,128)S(1)}, u32[]{:S(2)}, u32[]{:S(2)}) collective-permute-start(f32[1,256]{1,0:T(1,128)S(1)} %shard_map.126.refs_18_), channel_id=1, source_target_pairs={{0,16},{4,20},{8,24},{12,28},{16,0},{20,4},{24,8},{28,12},{1,17},{... | collective-permute-start | bytes 3080 | tf_op jit(solution)/shard_map/ppermute | solution.py:236
  83.2 1.9 %collective-permute-done.51.refs_19_ = f32[1,256]{1,0:T(1,128)S(1)} collective-permute-done((f32[1,256]{1,0:T(1,128)S(1)}, f32[1,256]{1,0:T(1,128)S(1)}, u32[]{:S(2)}, u32[]{:S(2)}) %collective-permute-start.51) | collective-permute-done | bytes 1056 | tf_op jit(solution)/shard_map/ppermute | solution.py:236
  85.1 1.7 %shard_map.127 = (f32[3,2,16,512]{3,2,1,0:T(8,128)S(1)}, f32[3,2,16,512]{3,2,1,0:T(8,128)S(1)}, f32[3,2,16,512]{3,2,1,0:T(8,128)S(1)}, f32[3,2,16,512]{3,2,1,0:T...) custom-call(f32[3,2,16,512]{3,2,1,0:T(8,128)S(1)} %shard_map.125.refs_0_, ...), custom_call_target="tpu_custom_call" | custom-call | flops 1000000000 | bytes 8000000 | tf_op jit(solution)/shard_map/pallas_call | solution.py:24
  86.8 11.3 %all_to_all.5.sums = f32[32,1,128]{2,1,0:T(1,128)S(1)} all-to-all(f32[32,1,128]{2,1,0:T(1,128)S(1)} %get-tuple-element.175), channel_id=1, replica_groups=mesh['res'=8,'grp'=4] {'res','grp'}, dimensions={0} | all-to-all | bytes 32768 | tf_op jit(solution)/shard_map/all_to_all | solution.py:632
  98.1 0.9 shard_map.128
  (102 shorter events, 12.3 us)
Async XLA Ops:
  3.8 8.0 %collective-permute-start = (f32[8,512]{1,0:T(8,128)}, f32[8,512]{1,0:T(8,128)S(1)}, u32[]{:S(2)}, u32[]{:S(2)}) collective-permute-start(f32[8,512]{1,0:T(8,128)} %get-tuple-element.96), channel_id=1, source_target_pairs={{0,1},{1,0},{2,3},{3,2},{4,5},{5,4},{6,7},{7,6},{8,9},{9,8},{10,11... | collective-permute-start | bytes 49160 | tf_op jit(solution)/shard_map/ppermute | solution.py:513
  4.3 7.5 %collective-permute-start.2 = (f32[8,512]{1,0:T(8,128)}, f32[8,512]{1,0:T(8,128)S(1)}, u32[]{:S(2)}, u32[]{:S(2)}) collective-permute-start(f32[8,512]{1,0:T(8,128)} %get-tuple-element.98), channel_id=1, source_target_pairs={{0,3},{1,2},{2,1},{3,0},{4,7},{5,6},{6,5},{7,4},{8,11},{9,10},{10,... | collective-permute-start | bytes 49160 | tf_op jit(solution)/shard_map/ppermute | solution.py:513
  7.0 4.8 %collective-permute-start.1 = (f32[4,256]{1,0:T(4,128)}, f32[4,256]{1,0:T(4,128)S(1)}, u32[]{:S(2)}, u32[]{:S(2)}) collective-permute-start(f32[4,256]{1,0:T(4,128)} %get-tuple-element.97), channel_id=1, source_target_pairs={{0,2},{1,3},{2,0},{3,1},{4,6},{5,7},{6,4},{7,5},{8,10},{9,11},{10,... | collective-permute-start | bytes 12296 | tf_op jit(solution)/shard_map/ppermute | solution.py:513
  7.0 11.3 %collective-permute-start.3 = (f32[3,16,512]{2,1,0:T(8,128)}, f32[3,16,512]{2,1,0:T(8,128)S(1)}, u32[]{:S(2)}, u32[]{:S(2)}) collective-permute-start(f32[3,16,512]{2,1,0:T(8,128)} %get-tuple-element.105), channel_id=1, source_target_pairs={{0,4},{4,0},{8,12},{12,8},{16,20},{20,16},{24,28},{28,24},{1,5},{5... | collective-permute-start | bytes 294920 | tf_op jit(solution)/shard_map/ppermute | solution.py:46
  9.0 9.3 %collective-permute-start.4 = (f32[3,16,512]{2,1,0:T(8,128)}, f32[3,16,512]{2,1,0:T(8,128)S(1)}, u32[]{:S(2)}, u32[]{:S(2)}) collective-permute-start(f32[3,16,512]{2,1,0:T(8,128)} %get-tuple-element.106), channel_id=1, source_target_pairs={{0,1},{1,0},{2,3},{3,2},{4,8},{5,9},{6,10},{7,11},{8,4},{9,5},{10,... | collective-permute-start | bytes 294920 | tf_op jit(solution)/shard_map/ppermute | solution.py:47
  13.1 4.5 %collective-permute-start.5 = (f32[4,256]{1,0:T(4,128)S(1)}, f32[4,256]{1,0:T(4,128)S(1)}, u32[]{:S(2)}, u32[]{:S(2)}) collective-permute-start(f32[4,256]{1,0:T(4,128)S(1)} %get-tuple-element.107), channel_id=1, source_target_pairs={{0,1},{1,0},{2,3},{3,2},{4,5},{5,4},{6,7},{7,6},{8,9},{9,8},{10,11... | collective-permute-start | bytes 12296 | tf_op jit(solution)/shard_map/ppermute | solution.py:513
  13.7 3.9 %collective-permute-start.6 = (f32[4,256]{1,0:T(4,128)S(1)}, f32[4,256]{1,0:T(4,128)S(1)}, u32[]{:S(2)}, u32[]{:S(2)}) collective-permute-start(f32[4,256]{1,0:T(4,128)S(1)} %get-tuple-element.108), channel_id=1, source_target_pairs={{0,2},{1,3},{2,0},{3,1},{4,6},{5,7},{6,4},{7,5},{8,10},{9,11},{10,... | collective-permute-start | bytes 12296 | tf_op jit(solution)/shard_map/ppermute | solution.py:513
  15.2 3.1 %collective-permute-start.7 = (f32[4,256]{1,0:T(4,128)S(1)}, f32[4,256]{1,0:T(4,128)S(1)}, u32[]{:S(2)}, u32[]{:S(2)}) collective-permute-start(f32[4,256]{1,0:T(4,128)S(1)} %get-tuple-element.109), channel_id=1, source_target_pairs={{0,3},{1,2},{2,1},{3,0},{4,7},{5,6},{6,5},{7,4},{8,11},{9,10},{10,... | collective-permute-start | bytes 12296 | tf_op jit(solution)/shard_map/ppermute | solution.py:513
  20.1 4.9 %collective-permute-start.8 = (f32[8,512]{1,0:T(8,128)S(1)}, f32[8,512]{1,0:T(8,128)S(1)}, u32[]{:S(2)}, u32[]{:S(2)}) collective-permute-start(f32[8,512]{1,0:T(8,128)S(1)} %get-tuple-element.115), channel_id=1, source_target_pairs={{0,1},{1,0},{2,3},{3,2},{4,5},{5,4},{6,7},{7,6},{8,9},{9,8},{10,11... | collective-permute-start | bytes 49160 | tf_op jit(solution)/shard_map/ppermute | solution.py:513
  20.2 4.7 %collective-permute-start.10 = (f32[8,512]{1,0:T(8,128)S(1)}, f32[8,512]{1,0:T(8,128)S(1)}, u32[]{:S(2)}, u32[]{:S(2)}) collective-permute-start(f32[8,512]{1,0:T(8,128)S(1)} %get-tuple-element.117), channel_id=1, source_target_pairs={{0,3},{1,2},{2,1},{3,0},{4,7},{5,6},{6,5},{7,4},{8,11},{9,10},{10,... | collective-permute-start | bytes 49160 | tf_op jit(solution)/shard_map/ppermute | solution.py:513
  21.4 3.6 %collective-permute-start.9 = (f32[4,256]{1,0:T(4,128)S(1)}, f32[4,256]{1,0:T(4,128)S(1)}, u32[]{:S(2)}, u32[]{:S(2)}) collective-permute-start(f32[4,256]{1,0:T(4,128)S(1)} %get-tuple-element.116), channel_id=1, source_target_pairs={{0,2},{1,3},{2,0},{3,1},{4,6},{5,7},{6,4},{7,5},{8,10},{9,11},{10,... | collective-permute-start | bytes 12296 | tf_op jit(solution)/shard_map/ppermute | solution.py:513
  22.3 8.1 %collective-permute-start.11 = (f32[3,16,512]{2,1,0:T(8,128)S(1)}, f32[3,16,512]{2,1,0:T(8,128)S(1)}, u32[]{:S(2)}, u32[]{:S(2)}) collective-permute-start(f32[3,16,512]{2,1,0:T(8,128)S(1)} %get-tuple-element.119), channel_id=1, source_target_pairs={{0,4},{4,0},{8,12},{12,8},{16,20},{20,16},{24,28},{28,24},{1,5},{5... | collective-permute-start | bytes 294920 | tf_op jit(solution)/shard_map/ppermute | solution.py:46
  24.9 5.5 %collective-permute-start.12 = (f32[3,16,512]{2,1,0:T(8,128)S(1)}, f32[3,16,512]{2,1,0:T(8,128)S(1)}, u32[]{:S(2)}, u32[]{:S(2)}) collective-permute-start(f32[3,16,512]{2,1,0:T(8,128)S(1)} %get-tuple-element.120), channel_id=1, source_target_pairs={{0,1},{1,0},{2,3},{3,2},{4,8},{5,9},{6,10},{7,11},{8,4},{9,5},{10,... | collective-permute-start | bytes 294920 | tf_op jit(solution)/shard_map/ppermute | solution.py:47
  25.7 2.3 %collective-permute-start.13 = (f32[4,256]{1,0:T(4,128)S(1)}, f32[4,256]{1,0:T(4,128)S(1)}, u32[]{:S(2)}, u32[]{:S(2)}) collective-permute-start(f32[4,256]{1,0:T(4,128)S(1)} %get-tuple-element.121), channel_id=1, source_target_pairs={{0,1},{1,0},{2,3},{3,2},{4,5},{5,4},{6,7},{7,6},{8,9},{9,8},{10,11... | collective-permute-start | bytes 12296 | tf_op jit(solution)/shard_map/ppermute | solution.py:513
  26.2 3.6 %collective-permute-start.14 = (f32[4,256]{1,0:T(4,128)S(1)}, f32[4,256]{1,0:T(4,128)S(1)}, u32[]{:S(2)}, u32[]{:S(2)}) collective-permute-start(f32[4,256]{1,0:T(4,128)S(1)} %get-tuple-element.122), channel_id=1, source_target_pairs={{0,2},{1,3},{2,0},{3,1},{4,6},{5,7},{6,4},{7,5},{8,10},{9,11},{10,... | collective-permute-start | bytes 12296 | tf_op jit(solution)/shard_map/ppermute | solution.py:513
  27.4 3.1 %collective-permute-start.15 = (f32[4,256]{1,0:T(4,128)S(1)}, f32[4,256]{1,0:T(4,128)S(1)}, u32[]{:S(2)}, u32[]{:S(2)}) collective-permute-start(f32[4,256]{1,0:T(4,128)S(1)} %get-tuple-element.123), channel_id=1, source_target_pairs={{0,3},{1,2},{2,1},{3,0},{4,7},{5,6},{6,5},{7,4},{8,11},{9,10},{10,... | collective-permute-start | bytes 12296 | tf_op jit(solution)/shard_map/ppermute | solution.py:513
  32.3 4.8 %collective-permute-start.16 = (f32[9,512]{1,0:T(8,128)S(1)}, f32[9,512]{1,0:T(8,128)S(1)}, u32[]{:S(2)}, u32[]{:S(2)}) collective-permute-start(f32[9,512]{1,0:T(8,128)S(1)} %get-tuple-element.126), channel_id=1, source_target_pairs={{0,1},{1,0},{2,3},{3,2},{4,5},{5,4},{6,7},{7,6},{8,9},{9,8},{10,11... | collective-permute-start | bytes 55304 | tf_op jit(solution)/shard_map/ppermute | solution.py:513
  32.4 4.7 %collective-permute-start.18 = (f32[9,512]{1,0:T(8,128)S(1)}, f32[9,512]{1,0:T(8,128)S(1)}, u32[]{:S(2)}, u32[]{:S(2)}) collective-permute-start(f32[9,512]{1,0:T(8,128)S(1)} %get-tuple-element.128), channel_id=1, source_target_pairs={{0,3},{1,2},{2,1},{3,0},{4,7},{5,6},{6,5},{7,4},{8,11},{9,10},{10,... | collective-permute-start | bytes 55304 | tf_op jit(solution)/shard_map/ppermute | solution.py:513
  33.3 3.8 %collective-permute-start.17 = (f32[5,256]{1,0:T(8,128)S(1)}, f32[5,256]{1,0:T(8,128)S(1)}, u32[]{:S(2)}, u32[]{:S(2)}) collective-permute-start(f32[5,256]{1,0:T(8,128)S(1)} %get-tuple-element.127), channel_id=1, source_target_pairs={{0,2},{1,3},{2,0},{3,1},{4,6},{5,7},{6,4},{7,5},{8,10},{9,11},{10,... | collective-permute-start | bytes 15368 | tf_op jit(solution)/shard_map/ppermute | solution.py:513
  34.5 9.9 %collective-permute-start.19 = (f32[3,16,512]{2,1,0:T(8,128)S(1)}, f32[3,16,512]{2,1,0:T(8,128)S(1)}, u32[]{:S(2)}, u32[]{:S(2)}) collective-permute-start(f32[3,16,512]{2,1,0:T(8,128)S(1)} %get-tuple-element.130), channel_id=1, source_target_pairs={{0,4},{4,0},{8,12},{12,8},{16,20},{20,16},{24,28},{28,24},{1,5},{5... | collective-permute-start | bytes 294920 | tf_op jit(solution)/shard_map/ppermute | solution.py:46
  37.1 7.3 %collective-permute-start.20 = (f32[3,16,512]{2,1,0:T(8,128)S(1)}, f32[3,16,512]{2,1,0:T(8,128)S(1)}, u32[]{:S(2)}, u32[]{:S(2)}) collective-permute-start(f32[3,16,512]{2,1,0:T(8,128)S(1)} %get-tuple-element.131), channel_id=1, source_target_pairs={{0,1},{1,0},{2,3},{3,2},{4,8},{5,9},{6,10},{7,11},{8,4},{9,5},{10,... | collective-permute-start | bytes 294920 | tf_op jit(solution)/shard_map/ppermute | solution.py:47
  38.3 4.9 %collective-permute-start.22 = (f32[4,256]{1,0:T(4,128)S(1)}, f32[4,256]{1,0:T(4,128)S(1)}, u32[]{:S(2)}, u32[]{:S(2)}) collective-permute-start(f32[4,256]{1,0:T(4,128)S(1)} %get-tuple-element.133), channel_id=1, source_target_pairs={{0,2},{1,3},{2,0},{3,1},{4,6},{5,7},{6,4},{7,5},{8,10},{9,11},{10,... | collective-permute-start | bytes 12296 | tf_op jit(solution)/shard_map/ppermute | solution.py:513
  39.2 4.1 %collective-permute-start.23 = (f32[4,256]{1,0:T(4,128)S(1)}, f32[4,256]{1,0:T(4,128)S(1)}, u32[]{:S(2)}, u32[]{:S(2)}) collective-permute-start(f32[4,256]{1,0:T(4,128)S(1)} %get-tuple-element.134), channel_id=1, source_target_pairs={{0,3},{1,2},{2,1},{3,0},{4,7},{5,6},{6,5},{7,4},{8,11},{9,10},{10,... | collective-permute-start | bytes 12296 | tf_op jit(solution)/shard_map/ppermute | solution.py:513
  39.8 4.6 %collective-permute-start.24 = (f32[1,256]{1,0:T(1,128)S(1)}, f32[1,256]{1,0:T(1,128)S(1)}, u32[]{:S(2)}, u32[]{:S(2)}) collective-permute-start(f32[1,256]{1,0:T(1,128)S(1)} %shard_map.114.refs_18_), channel_id=1, source_target_pairs={{0,4},{1,5},{2,10},{3,15},{4,0},{5,1},{6,14},{7,11},{8,12},{9,13},... | collective-permute-start | bytes 3080 | tf_op jit(solution)/shard_map/ppermute | solution.py:230
  46.1 4.5 %collective-permute-start.25 = (f32[9,512]{1,0:T(8,128)S(1)}, f32[9,512]{1,0:T(8,128)S(1)}, u32[]{:S(2)}, u32[]{:S(2)}) collective-permute-start(f32[9,512]{1,0:T(8,128)S(1)} %get-tuple-element.137), channel_id=1, source_target_pairs={{0,1},{1,0},{2,3},{3,2},{4,5},{5,4},{6,7},{7,6},{8,9},{9,8},{10,11... | collective-permute-start | bytes 55304 | tf_op jit(solution)/shard_map/ppermute | solution.py:513
  46.2 4.4 %collective-permute-start.27 = (f32[9,512]{1,0:T(8,128)S(1)}, f32[9,512]{1,0:T(8,128)S(1)}, u32[]{:S(2)}, u32[]{:S(2)}) collective-permute-start(f32[9,512]{1,0:T(8,128)S(1)} %get-tuple-element.139), channel_id=1, source_target_pairs={{0,3},{1,2},{2,1},{3,0},{4,7},{5,6},{6,5},{7,4},{8,11},{9,10},{10,... | collective-permute-start | bytes 55304 | tf_op jit(solution)/shard_map/ppermute | solution.py:513
  47.0 3.7 %collective-permute-start.26 = (f32[5,256]{1,0:T(8,128)S(1)}, f32[5,256]{1,0:T(8,128)S(1)}, u32[]{:S(2)}, u32[]{:S(2)}) collective-permute-start(f32[5,256]{1,0:T(8,128)S(1)} %get-tuple-element.138), channel_id=1, source_target_pairs={{0,2},{1,3},{2,0},{3,1},{4,6},{5,7},{6,4},{7,5},{8,10},{9,11},{10,... | collective-permute-start | bytes 15368 | tf_op jit(solution)/shard_map/ppermute | solution.py:513
  48.3 9.6 %collective-permute-start.28 = (f32[3,16,512]{2,1,0:T(8,128)S(1)}, f32[3,16,512]{2,1,0:T(8,128)S(1)}, u32[]{:S(2)}, u32[]{:S(2)}) collective-permute-start(f32[3,16,512]{2,1,0:T(8,128)S(1)} %get-tuple-element.141), channel_id=1, source_target_pairs={{0,4},{4,0},{8,12},{12,8},{16,20},{20,16},{24,28},{28,24},{1,5},{5... | collective-permute-start | bytes 294920 | tf_op jit(solution)/shard_map/ppermute | solution.py:46
  50.4 7.6 %collective-permute-start.29 = (f32[3,16,512]{2,1,0:T(8,128)S(1)}, f32[3,16,512]{2,1,0:T(8,128)S(1)}, u32[]{:S(2)}, u32[]{:S(2)}) collective-permute-start(f32[3,16,512]{2,1,0:T(8,128)S(1)} %get-tuple-element.142), channel_id=1, source_target_pairs={{0,1},{1,0},{2,3},{3,2},{4,8},{5,9},{6,10},{7,11},{8,4},{9,5},{10,... | collective-permute-start | bytes 294920 | tf_op jit(solution)/shard_map/ppermute | solution.py:47
  51.8 4.1 %collective-permute-start.31 = (f32[4,256]{1,0:T(4,128)S(1)}, f32[4,256]{1,0:T(4,128)S(1)}, u32[]{:S(2)}, u32[]{:S(2)}) collective-permute-start(f32[4,256]{1,0:T(4,128)S(1)} %get-tuple-element.144), channel_id=1, source_target_pairs={{0,2},{1,3},{2,0},{3,1},{4,6},{5,7},{6,4},{7,5},{8,10},{9,11},{10,... | collective-permute-start | bytes 12296 | tf_op jit(solution)/shard_map/ppermute | solution.py:513
  53.0 3.0 %collective-permute-start.32 = (f32[4,256]{1,0:T(4,128)S(1)}, f32[4,256]{1,0:T(4,128)S(1)}, u32[]{:S(2)}, u32[]{:S(2)}) collective-permute-start(f32[4,256]{1,0:T(4,128)S(1)} %get-tuple-element.145), channel_id=1, source_target_pairs={{0,3},{1,2},{2,1},{3,0},{4,7},{5,6},{6,5},{7,4},{8,11},{9,10},{10,... | collective-permute-start | bytes 12296 | tf_op jit(solution)/shard_map/ppermute | solution.py:513
  53.4 4.5 %collective-permute-start.33 = (f32[1,256]{1,0:T(1,128)S(1)}, f32[1,256]{1,0:T(1,128)S(1)}, u32[]{:S(2)}, u32[]{:S(2)}) collective-permute-start(f32[1,256]{1,0:T(1,128)S(1)} %shard_map.118.refs_18_), channel_id=1, source_target_pairs={{0,16},{4,20},{8,24},{12,28},{16,0},{20,4},{24,8},{28,12},{1,17},{... | collective-permute-start | bytes 3080 | tf_op jit(solution)/shard_map/ppermute | solution.py:236
  60.2 5.2 %collective-permute-start.34 = (f32[9,512]{1,0:T(8,128)S(1)}, f32[9,512]{1,0:T(8,128)S(1)}, u32[]{:S(2)}, u32[]{:S(2)}) collective-permute-start(f32[9,512]{1,0:T(8,128)S(1)} %get-tuple-element.148), channel_id=1, source_target_pairs={{0,1},{1,0},{2,3},{3,2},{4,5},{5,4},{6,7},{7,6},{8,9},{9,8},{10,11... | collective-permute-start | bytes 55304 | tf_op jit(solution)/shard_map/ppermute | solution.py:513
  60.2 5.2 %collective-permute-start.36 = (f32[9,512]{1,0:T(8,128)S(1)}, f32[9,512]{1,0:T(8,128)S(1)}, u32[]{:S(2)}, u32[]{:S(2)}) collective-permute-start(f32[9,512]{1,0:T(8,128)S(1)} %get-tuple-element.150), channel_id=1, source_target_pairs={{0,3},{1,2},{2,1},{3,0},{4,7},{5,6},{6,5},{7,4},{8,11},{9,10},{10,... | collective-permute-start | bytes 55304 | tf_op jit(solution)/shard_map/ppermute | solution.py:513
  61.8 3.7 %collective-permute-start.35 = (f32[5,256]{1,0:T(8,128)S(1)}, f32[5,256]{1,0:T(8,128)S(1)}, u32[]{:S(2)}, u32[]{:S(2)}) collective-permute-start(f32[5,256]{1,0:T(8,128)S(1)} %get-tuple-element.149), channel_id=1, source_target_pairs={{0,2},{1,3},{2,0},{3,1},{4,6},{5,7},{6,4},{7,5},{8,10},{9,11},{10,... | collective-permute-start | bytes 15368 | tf_op jit(solution)/shard_map/ppermute | solution.py:513
  62.4 9.3 %collective-permute-start.37 = (f32[3,16,512]{2,1,0:T(8,128)S(1)}, f32[3,16,512]{2,1,0:T(8,128)S(1)}, u32[]{:S(2)}, u32[]{:S(2)}) collective-permute-start(f32[3,16,512]{2,1,0:T(8,128)S(1)} %get-tuple-element.152), channel_id=1, source_target_pairs={{0,4},{4,0},{8,12},{12,8},{16,20},{20,16},{24,28},{28,24},{1,5},{5... | collective-permute-start | bytes 294920 | tf_op jit(solution)/shard_map/ppermute | solution.py:46
  64.6 7.1 %collective-permute-start.38 = (f32[3,16,512]{2,1,0:T(8,128)S(1)}, f32[3,16,512]{2,1,0:T(8,128)S(1)}, u32[]{:S(2)}, u32[]{:S(2)}) collective-permute-start(f32[3,16,512]{2,1,0:T(8,128)S(1)} %get-tuple-element.153), channel_id=1, source_target_pairs={{0,1},{1,0},{2,3},{3,2},{4,8},{5,9},{6,10},{7,11},{8,4},{9,5},{10,... | collective-permute-start | bytes 294920 | tf_op jit(solution)/shard_map/ppermute | solution.py:47
  66.2 4.4 %collective-permute-start.40 = (f32[4,256]{1,0:T(4,128)S(1)}, f32[4,256]{1,0:T(4,128)S(1)}, u32[]{:S(2)}, u32[]{:S(2)}) collective-permute-start(f32[4,256]{1,0:T(4,128)S(1)} %get-tuple-element.155), channel_id=1, source_target_pairs={{0,2},{1,3},{2,0},{3,1},{4,6},{5,7},{6,4},{7,5},{8,10},{9,11},{10,... | collective-permute-start | bytes 12296 | tf_op jit(solution)/shard_map/ppermute | solution.py:513
  67.1 3.5 %collective-permute-start.41 = (f32[4,256]{1,0:T(4,128)S(1)}, f32[4,256]{1,0:T(4,128)S(1)}, u32[]{:S(2)}, u32[]{:S(2)}) collective-permute-start(f32[4,256]{1,0:T(4,128)S(1)} %get-tuple-element.156), channel_id=1, source_target_pairs={{0,3},{1,2},{2,1},{3,0},{4,7},{5,6},{6,5},{7,4},{8,11},{9,10},{10,... | collective-permute-start | bytes 12296 | tf_op jit(solution)/shard_map/ppermute | solution.py:513
  68.0 3.6 %collective-permute-start.42 = (f32[1,256]{1,0:T(1,128)S(1)}, f32[1,256]{1,0:T(1,128)S(1)}, u32[]{:S(2)}, u32[]{:S(2)}) collective-permute-start(f32[1,256]{1,0:T(1,128)S(1)} %shard_map.122.refs_18_), channel_id=1, source_target_pairs={{0,4},{1,5},{2,10},{3,15},{4,0},{5,1},{6,14},{7,11},{8,12},{9,13},... | collective-permute-start | bytes 3080 | tf_op jit(solution)/shard_map/ppermute | solution.py:230
  73.4 4.5 %collective-permute-start.43 = (f32[9,512]{1,0:T(8,128)S(1)}, f32[9,512]{1,0:T(8,128)S(1)}, u32[]{:S(2)}, u32[]{:S(2)}) collective-permute-start(f32[9,512]{1,0:T(8,128)S(1)} %get-tuple-element.159), channel_id=1, source_target_pairs={{0,1},{1,0},{2,3},{3,2},{4,5},{5,4},{6,7},{7,6},{8,9},{9,8},{10,11... | collective-permute-start | bytes 55304 | tf_op jit(solution)/shard_map/ppermute | solution.py:513
  73.5 4.4 %collective-permute-start.45 = (f32[9,512]{1,0:T(8,128)S(1)}, f32[9,512]{1,0:T(8,128)S(1)}, u32[]{:S(2)}, u32[]{:S(2)}) collective-permute-start(f32[9,512]{1,0:T(8,128)S(1)} %get-tuple-element.161), channel_id=1, source_target_pairs={{0,3},{1,2},{2,1},{3,0},{4,7},{5,6},{6,5},{7,4},{8,11},{9,10},{10,... | collective-permute-start | bytes 55304 | tf_op jit(solution)/shard_map/ppermute | solution.py:513
  74.3 3.7 %collective-permute-start.44 = (f32[5,256]{1,0:T(8,128)S(1)}, f32[5,256]{1,0:T(8,128)S(1)}, u32[]{:S(2)}, u32[]{:S(2)}) collective-permute-start(f32[5,256]{1,0:T(8,128)S(1)} %get-tuple-element.160), channel_id=1, source_target_pairs={{0,2},{1,3},{2,0},{3,1},{4,6},{5,7},{6,4},{7,5},{8,10},{9,11},{10,... | collective-permute-start | bytes 15368 | tf_op jit(solution)/shard_map/ppermute | solution.py:513
  75.6 9.4 %collective-permute-start.46 = (f32[3,16,512]{2,1,0:T(8,128)S(1)}, f32[3,16,512]{2,1,0:T(8,128)S(1)}, u32[]{:S(2)}, u32[]{:S(2)}) collective-permute-start(f32[3,16,512]{2,1,0:T(8,128)S(1)} %get-tuple-element.163), channel_id=1, source_target_pairs={{0,4},{4,0},{8,12},{12,8},{16,20},{20,16},{24,28},{28,24},{1,5},{5... | collective-permute-start | bytes 294920 | tf_op jit(solution)/shard_map/ppermute | solution.py:46
  77.7 7.4 %collective-permute-start.47 = (f32[3,16,512]{2,1,0:T(8,128)S(1)}, f32[3,16,512]{2,1,0:T(8,128)S(1)}, u32[]{:S(2)}, u32[]{:S(2)}) collective-permute-start(f32[3,16,512]{2,1,0:T(8,128)S(1)} %get-tuple-element.164), channel_id=1, source_target_pairs={{0,1},{1,0},{2,3},{3,2},{4,8},{5,9},{6,10},{7,11},{8,4},{9,5},{10,... | collective-permute-start | bytes 294920 | tf_op jit(solution)/shard_map/ppermute | solution.py:47
  78.9 4.1 %collective-permute-start.49 = (f32[4,256]{1,0:T(4,128)S(1)}, f32[4,256]{1,0:T(4,128)S(1)}, u32[]{:S(2)}, u32[]{:S(2)}) collective-permute-start(f32[4,256]{1,0:T(4,128)S(1)} %get-tuple-element.166), channel_id=1, source_target_pairs={{0,2},{1,3},{2,0},{3,1},{4,6},{5,7},{6,4},{7,5},{8,10},{9,11},{10,... | collective-permute-start | bytes 12296 | tf_op jit(solution)/shard_map/ppermute | solution.py:513
  80.1 3.0 %collective-permute-start.50 = (f32[4,256]{1,0:T(4,128)S(1)}, f32[4,256]{1,0:T(4,128)S(1)}, u32[]{:S(2)}, u32[]{:S(2)}) collective-permute-start(f32[4,256]{1,0:T(4,128)S(1)} %get-tuple-element.167), channel_id=1, source_target_pairs={{0,3},{1,2},{2,1},{3,0},{4,7},{5,6},{6,5},{7,4},{8,11},{9,10},{10,... | collective-permute-start | bytes 12296 | tf_op jit(solution)/shard_map/ppermute | solution.py:513
  80.5 4.5 %collective-permute-start.51 = (f32[1,256]{1,0:T(1,128)S(1)}, f32[1,256]{1,0:T(1,128)S(1)}, u32[]{:S(2)}, u32[]{:S(2)}) collective-permute-start(f32[1,256]{1,0:T(1,128)S(1)} %shard_map.126.refs_18_), channel_id=1, source_target_pairs={{0,16},{4,20},{8,24},{12,28},{16,0},{20,4},{24,8},{28,12},{1,17},{... | collective-permute-start | bytes 3080 | tf_op jit(solution)/shard_map/ppermute | solution.py:236
  (14 other events, 36.4 us)

commit v9 on v7

--- a/solution.py
+++ b/solution.py
@@ -290,16 +290,32 @@
                     )
 
 
-def solve_kernel(groups, transposed, first, second, *refs):
-    sent, back = refs[:groups], refs[groups:]
+def solve_slots(groups, sent, back, product):
     g = lax.axis_index("grp")
     capacity, segb = back[0].shape
     for k in range(groups):
         home = jnp.bitwise_xor(g, k)
         for slot in range(capacity):
             coupled = sent[k][spot(sent[k], slot, segb)]
-            value = solve_well(coupled, first[home, slot], second[home, slot], transposed)
-            back[k][slot : slot + 1] = value
+            back[k][slot : slot + 1] = product(coupled, home, slot)
+
+
+def solve_kernel(groups, first, second, *refs):
+    def product(coupled, home, slot):
+        return solve_well(coupled, first[home, slot], second[home, slot])
+
+    solve_slots(groups, refs[:groups], refs[groups:], product)
+
+
+def first_solve_kernel(groups, inverse, *refs):
+    *back, first, second = refs[groups:]
+
+    def product(coupled, home, slot):
+        high, low = halves(inverse[home, slot])
+        first[home, slot], second[home, slot] = high, low
+        return solve_well(coupled, high, low, True)
+
+    solve_slots(groups, refs[:groups], back, product)
 
 
 def group_sum_kernel(capacity, after, *refs):
@@ -343,9 +359,17 @@
     return (total[:rows] + total[rows:]).reshape(shape)
 
 
+def write_place(level, cells_z, place):
+    wells, segb = level.shape
+    depth = lax.broadcasted_iota(jnp.int32, (cells_z, segb), 0)
+    for b in range(wells):
+        hit = depth == level[b : b + 1, :]
+        place[:, b * segb : (b + 1) * segb] = jnp.where(hit, 1.0, 0.0).astype(BF16)
+
+
 def start_kernel(groups, capacity, *refs):
-    given, (place, column, take_out, give_out, *sends) = refs[:6], refs[6:-7]
-    held, sems = refs[-7:-1], refs[-1]
+    given, (column, level, take_out, give_out, *sends) = refs[:6], refs[6:-8]
+    place, held, sems = refs[-8], refs[-7:-1], refs[-1]
     copies = [
         pltpu.make_async_copy(src, dst, sems.at[n]) for n, (src, dst) in enumerate(zip(given, held))
     ]
@@ -356,26 +380,21 @@
     vec, completion, live, owner, take, give = held
     components, cells_x, cells_y, cells_z = vec.shape
     wells, segb = completion.shape
-    write_faces(Planes(vec), sends[groups:])
-    depth = lax.broadcasted_iota(jnp.int32, (cells_z, segb), 0)
     lanes = lax.broadcasted_iota(jnp.int32, (1, segb), 1)
+    column[...] = completion[...] // cells_z
+    level[...] = lax.rem(completion[...], cells_z)
+    write_place(level, cells_z, place)
     for b in range(wells):
-        cell = completion[b : b + 1, :]
-        row = cell // cells_z
-        column[b : b + 1, :] = row
-        hit = depth == cell - row * cells_z
-        place[:, b * segb : (b + 1) * segb] = jnp.where(hit, 1.0, 0.0).astype(BF16)
         is_open = (lanes < live[b]).astype(F32)
         for i in range(components):
             take_out[i, b : b + 1] = take[i, b : b + 1] * is_open
             give_out[i, b : b + 1] = give[i, b : b + 1] * is_open
-    write_messages(vec, place, column, take_out, owner, capacity, sends[:groups])
-
-
-def split_kernel(inverse, first, second):
-    for h in range(inverse.shape[0]):
-        for slot in range(inverse.shape[1]):
-            first[h, slot], second[h, slot] = halves(inverse[h, slot])
+    write_messages(vec, place, column, take_out, owner, capacity, sends)
+
+
+def place_kernel(vec, level, place, *faces):
+    write_faces(Planes(vec), faces)
+    write_place(level, vec.shape[3], place)
 
 
 class Arrived:
@@ -551,19 +570,13 @@
     b = right_side
     sizes = (groups, capacity)
 
-    place, column, take, give, *sends = call(
+    column, level, take, give, *sends = call(
         functools.partial(start_kernel, groups, capacity),
-        [
-            ((cells_z, wells * segb), BF16),
-            (completion.shape, jnp.int32),
-            (take.shape, F32),
-            (give.shape, F32),
-        ]
-        + plain
-        + face_outs,
+        [(completion.shape, jnp.int32)] * 2 + [(take.shape, F32), (give.shape, F32)] + plain,
         [b, completion, live_count, owner, take, give],
         [pl.BlockSpec(memory_space=pltpu.HBM)] * 6,
         scratch=[
+            pltpu.VMEM((cells_z, wells * segb), BF16),
             pltpu.VMEM(b.shape, F32),
             pltpu.VMEM(completion.shape, jnp.int32),
             pltpu.SMEM(live_count.shape, jnp.int32),
@@ -577,14 +590,12 @@
     shifted = [pltpu.VMEM((4,) + b.shape, F32)]
     cost = dict(scratch=shifted, flops=200_000_000, moved=4_000_000)
 
-    def solve(transposed, given):
-        return call(
-            functools.partial(solve_kernel, groups, transposed),
-            [((capacity, segb), F32)] * groups,
-            given,
-            flops=SOLVE_FLOPS,
-            moved=4_000_000,
-        )
+    messages_back = [((capacity, segb), F32)] * groups
+    kept = [(inverse.shape[1:], BF16)] * 2
+
+    def solve(kernel, outs, given):
+        kernel = functools.partial(kernel, groups)
+        return call(kernel, outs, given, flops=SOLVE_FLOPS, moved=4_000_000)
 
     def finish(kernel, outs, part, messages, values, halo, extra):
         args = [part, trans, place, placed, column, take, give, owner]
@@ -595,7 +606,7 @@
 
     def apply(kernel, outs, vec, sends, extra, sums=None, with_sums=False):
         messages, faces = swapped(sends[:groups]), sends[groups:]
-        values = solve(False, [first, second, *messages])
+        values = solve(solve_kernel, messages_back, [first, second, *messages])
         first_here = values[:1] if faces else sums
         *made, part = call(
             functools.partial(stencil_kernel, len(first_here)),
@@ -622,10 +633,16 @@
         )[0]
         return [mine] + [share_swap(mine, q) for q in range(share(lax.axis_size("res"), groups))]
 
-    kept = [(inverse.shape[1:], BF16)] * 2
-    first, second = call(split_kernel, kept, [inverse[0]])
-    messages, halo = swapped(sends[:groups]), exchange(sends[groups:])
-    values = swapped(back := solve(True, [first, second, *messages]))
+    messages = swapped(sends)
+    place, *faces = call(
+        place_kernel,
+        [((cells_z, wells * segb), BF16)] + face_outs,
+        [b, level],
+        flops=SOLVE_FLOPS,
+    )
+    halo = exchange(faces)
+    *back, first, second = solve(first_solve_kernel, messages_back + kept, [inverse[0], *messages])
+    values = swapped(back)
     part, diag, placed, first, second = call(
         first_stencil_kernel,
         [field, (accumulation.shape, F32), ((wells * segb, cells_z), BF16)] + kept,

time: 96.5 us -> 95 us (0.984)
  Pallas kernels: 25.1 us -> 23.9 us
    pallas_call x25, Pallas kernels: 25.1 us -> 23.9 us  [call(): pl.pallas_call(kernel, out_shape=[jax.ShapeDtypeStruct(shape, dtype) for...]
    unnamed x20 -> x22, local copies, waits for them, and re-layouts: 2.23 us -> 1.67 us
where the time goes in v9:
time: 95 us; the launch traced here: 94.8 us
  starting transfers between devices  45.2 us (48%)
  Pallas kernels  23.9 us (25%)
  waiting for transfers between devices  13.3 us (14%)
  blocking collectives  9.68 us (10%)
  local copies, waits for them, and re-layouts  1.67 us (2%)
  between operations  1.03 us (1%)
    ppermute x36, starting transfers between devices, swapped(): lax.ppermute(messages[k], 'grp', [(i, i ^ k) for i in range(groups)])  26.4 us
    pallas_call x25, Pallas kernels, call(): pl.pallas_call(kernel, out_shape=[jax.ShapeDtypeStruct(shape, dtype) for...  23.9 us
    ppermute x36, waiting for transfers between devices, swapped(): lax.ppermute(messages[k], 'grp', [(i, i ^ k) for i in range(groups)])  12 us
    ppermute x4, starting transfers between devices, share_swap(): return lax.ppermute(row, ('res', 'grp'), pairs)  9.69 us
    all_to_all x1, blocking collectives, body(): lax.all_to_all(sends[0], ('res', 'grp'), split_axis=0, concat_axis=0, til...  9.68 us
    ppermute x6, starting transfers between devices, exchange(): lax.ppermute(faces[0], 'res', first)  8.97 us
  transfers between devices with their start and end apart: 52, of which 14 were waited for; matrix products, arithmetic and copies ran while one was open for 0% of the time, Pallas kernels for 14%

profile of v9, /device:TPU:0, one launch (start us, length us, event | category | flops | bytes accessed | tf_op | source)
XLA Modules:
  0.0 94.8 jit_solution(5474320666512716676)
XLA Ops:
  0.6 2.4 %shard_map.104 = (s32[8,256]{1,0:T(8,128)}, s32[8,256]{1,0:T(8,128)}, f32[3,8,256]{2,1,0:T(8,128)}, f32[3,8,256]{2,1,0:T(8,128)}, f32[4,256]{1,0:T(4,128)}, /*in...) custom-call(f32[3,2,16,512]{3,2,1,0:T(8,128)} %refs_18_.5, s32[8,256]{1,0:T(8,128)} %refs_1_.7, s32[8]{0:T(128)} %refs_2_.1, ...), custom_call_target="tpu_custom_call" | custom-call | flops 1000000 | bytes 1000000 | tf_op jit(solution)/shard_map/pallas_call | solution.py:24
  3.0 3.0 %collective-permute-start.1 = (f32[4,256]{1,0:T(4,128)}, f32[4,256]{1,0:T(4,128)S(1)}, u32[]{:S(2)}, u32[]{:S(2)}) collective-permute-start(f32[4,256]{1,0:T(4,128)} %get-tuple-element.107), channel_id=1, source_target_pairs={{0,2},{1,3},{2,0},{3,1},{4,6},{5,7},{6,4},{7,5},{8,10},{9,11},{10,... | collective-permute-start | bytes 12296 | tf_op jit(solution)/shard_map/ppermute | solution.py:538
  6.3 0.9 copy-done.1
  7.2 0.7 copy-done.10
  8.3 2.0 %collective-permute-start.3 = (f32[3,16,512]{2,1,0:T(8,128)S(1)}, f32[3,16,512]{2,1,0:T(8,128)S(1)}, u32[]{:S(2)}, u32[]{:S(2)}) collective-permute-start(f32[3,16,512]{2,1,0:T(8,128)S(1)} %get-tuple-element.117), channel_id=1, source_target_pairs={{0,4},{4,0},{8,12},{12,8},{16,20},{20,16},{24,28},{28,24},{1,5},{5... | collective-permute-start | bytes 294920 | tf_op jit(solution)/shard_map/ppermute | solution.py:46
  10.3 1.3 %shard_map.106 = (f32[4,256]{1,0:T(4,128)S(1)}, f32[4,256]{1,0:T(4,128)S(1)}, f32[4,256]{1,0:T(4,128)S(1)}, f32[4,256]{1,0:T(4,128)S(1)}, bf16[4,4,256,256]{3,2,...) custom-call(f32[4,4,256,256]{3,2,1,0:T(8,128)S(1)} %bitcast.11, f32[4,256]{1,0:T(4,128)S(1)} %copy-done.8, ...), custom_call_target="tpu_custom_call" | custom-call | flops 5000000000 | bytes 4000000 | tf_op jit(solution)/shard_map/pallas_call | solution.py:24
  12.2 1.5 %collective-permute-start.6 = (f32[4,256]{1,0:T(4,128)S(1)}, f32[4,256]{1,0:T(4,128)S(1)}, u32[]{:S(2)}, u32[]{:S(2)}) collective-permute-start(f32[4,256]{1,0:T(4,128)S(1)} %get-tuple-element.120), channel_id=1, source_target_pairs={{0,2},{1,3},{2,0},{3,1},{4,6},{5,7},{6,4},{7,5},{8,10},{9,11},{10,... | collective-permute-start | bytes 12296 | tf_op jit(solution)/shard_map/ppermute | solution.py:538
  13.8 2.3 %shard_map.107 = (f32[3,2,16,512]{3,2,1,0:T(8,128)S(1)}, f32[3,3,2,16,512]{4,3,2,1,0:T(8,128)S(1)}, bf16[2048,512]{1,0:T(8,128)(2,1)S(1)}, bf16[4,4,256,256]{3,2...) custom-call(f32[3,2,16,512]{3,2,1,0:T(8,128)S(1)} %copy-done.2, f32[6,3,3,2,16,512]{5,4,3,2,1,0:T(8,128)S(1)} %copy-done, ...), custom_call_target="tpu_custom_call" | custom-call | flops 200000000 | bytes 4000000 | tf_op jit(solution)/shard_map/pallas_call | solution.py:24
  16.8 1.8 %shard_map.108 = (f32[3,2,16,512]{3,2,1,0:T(8,128)S(1)}, f32[4,256]{1,0:T(4,128)S(1)}, f32[8,512]{1,0:T(8,128)S(1)}, f32[4,256]{1,0:T(4,128)S(1)}, f32[8,512]{1,...) custom-call(f32[3,2,16,512]{3,2,1,0:T(8,128)S(1)} %get-tuple-element.112.refs_0_, ...), custom_call_target="tpu_custom_call" | custom-call | flops 1000000000 | bytes 8000000 | tf_op jit(solution)/shard_map/pallas_call | solution.py:24
  18.8 1.1 %collective-permute-start.10 = (f32[8,512]{1,0:T(8,128)S(1)}, f32[8,512]{1,0:T(8,128)S(1)}, u32[]{:S(2)}, u32[]{:S(2)}) collective-permute-start(f32[8,512]{1,0:T(8,128)S(1)} %get-tuple-element.129), channel_id=1, source_target_pairs={{0,3},{1,2},{2,1},{3,0},{4,7},{5,6},{6,5},{7,4},{8,11},{9,10},{10,... | collective-permute-start | bytes 49160 | tf_op jit(solution)/shard_map/ppermute | solution.py:538
  19.9 0.9 %collective-permute-start.9 = (f32[4,256]{1,0:T(4,128)S(1)}, f32[4,256]{1,0:T(4,128)S(1)}, u32[]{:S(2)}, u32[]{:S(2)}) collective-permute-start(f32[4,256]{1,0:T(4,128)S(1)} %get-tuple-element.128), channel_id=1, source_target_pairs={{0,2},{1,3},{2,0},{3,1},{4,6},{5,7},{6,4},{7,5},{8,10},{9,11},{10,... | collective-permute-start | bytes 12296 | tf_op jit(solution)/shard_map/ppermute | solution.py:538
  20.8 2.6 %collective-permute-start.11 = (f32[3,16,512]{2,1,0:T(8,128)S(1)}, f32[3,16,512]{2,1,0:T(8,128)S(1)}, u32[]{:S(2)}, u32[]{:S(2)}) collective-permute-start(f32[3,16,512]{2,1,0:T(8,128)S(1)} %get-tuple-element.131), channel_id=1, source_target_pairs={{0,4},{4,0},{8,12},{12,8},{16,20},{20,16},{24,28},{28,24},{1,5},{5... | collective-permute-start | bytes 294920 | tf_op jit(solution)/shard_map/ppermute | solution.py:46
  23.5 0.7 shard_map.109
  24.7 1.2 %collective-permute-start.14 = (f32[4,256]{1,0:T(4,128)S(1)}, f32[4,256]{1,0:T(4,128)S(1)}, u32[]{:S(2)}, u32[]{:S(2)}) collective-permute-start(f32[4,256]{1,0:T(4,128)S(1)} %get-tuple-element.134), channel_id=1, source_target_pairs={{0,2},{1,3},{2,0},{3,1},{4,6},{5,7},{6,4},{7,5},{8,10},{9,11},{10,... | collective-permute-start | bytes 12296 | tf_op jit(solution)/shard_map/ppermute | solution.py:538
  26.5 1.7 %collective-permute-done.14.refs_16_ = f32[4,256]{1,0:T(4,128)S(1)} collective-permute-done((f32[4,256]{1,0:T(4,128)S(1)}, f32[4,256]{1,0:T(4,128)S(1)}, u32[]{:S(2)}, u32[]{:S(2)}) %collective-permute-start.14) | collective-permute-done | bytes 4128 | tf_op jit(solution)/shard_map/ppermute | solution.py:538
  28.9 1.8 %shard_map.111 = (f32[3,2,16,512]{3,2,1,0:T(8,128)S(1)}, f32[5,256]{1,0:T(8,128)S(1)}, f32[9,512]{1,0:T(8,128)S(1)}, f32[5,256]{1,0:T(8,128)S(1)}, f32[9,512]{1,...) custom-call(f32[3,2,16,512]{3,2,1,0:T(8,128)S(1)} %shard_map.110.refs_0_, ...), custom_call_target="tpu_custom_call" | custom-call | flops 1000000000 | bytes 8000000 | tf_op jit(solution)/shard_map/pallas_call | solution.py:24
  30.9 0.9 collective-permute-start.18
  31.8 1.2 %collective-permute-start.17 = (f32[5,256]{1,0:T(8,128)S(1)}, f32[5,256]{1,0:T(8,128)S(1)}, u32[]{:S(2)}, u32[]{:S(2)}) collective-permute-start(f32[5,256]{1,0:T(8,128)S(1)} %get-tuple-element.139), channel_id=1, source_target_pairs={{0,2},{1,3},{2,0},{3,1},{4,6},{5,7},{6,4},{7,5},{8,10},{9,11},{10,... | collective-permute-start | bytes 15368 | tf_op jit(solution)/shard_map/ppermute | solution.py:538
  33.0 2.6 %collective-permute-start.19 = (f32[3,16,512]{2,1,0:T(8,128)S(1)}, f32[3,16,512]{2,1,0:T(8,128)S(1)}, u32[]{:S(2)}, u32[]{:S(2)}) collective-permute-start(f32[3,16,512]{2,1,0:T(8,128)S(1)} %get-tuple-element.142), channel_id=1, source_target_pairs={{0,4},{4,0},{8,12},{12,8},{16,20},{20,16},{24,28},{28,24},{1,5},{5... | collective-permute-start | bytes 294920 | tf_op jit(solution)/shard_map/ppermute | solution.py:46
  35.6 0.7 shard_map.112
  36.8 0.8 collective-permute-start.22
  38.7 1.1 %collective-permute-done.19.refs_8_.refs_1_ = f32[3,16,512]{2,1,0:T(8,128)S(1)} collective-permute-done((f32[3,16,512]{2,1,0:T(8,128)S(1)}, f32[3,16,512]{2,1,0:T(8,128)S(1)}, u32[]{:S(2)}, u32[]{:S(2)}) %collective-permute-start.19) | collective-permute-done | bytes 98336 | tf_op jit(solution)/shard_map/ppermute | solution.py:46
  39.8 2.8 %collective-permute-start.25 = (f32[1,256]{1,0:T(1,128)S(1)}, f32[1,256]{1,0:T(1,128)S(1)}, u32[]{:S(2)}, u32[]{:S(2)}) collective-permute-start(f32[1,256]{1,0:T(1,128)S(1)} %shard_map.115.refs_0_.mine), channel_id=1, source_target_pairs={{0,28},{1,25},{2,22},{3,19},{4,24},{5,29},{6,18},{7,23},{8,20},{9,... | collective-permute-start | bytes 3080 | tf_op jit(solution)/shard_map/ppermute | solution.py:242
  42.6 1.6 %collective-permute-start.24 = (f32[1,256]{1,0:T(1,128)S(1)}, f32[1,256]{1,0:T(1,128)S(1)}, u32[]{:S(2)}, u32[]{:S(2)}) collective-permute-start(f32[1,256]{1,0:T(1,128)S(1)} %shard_map.115.refs_0_.mine), channel_id=1, source_target_pairs={{0,4},{1,5},{2,10},{3,15},{4,0},{5,1},{6,14},{7,11},{8,12},{9,13},... | collective-permute-start | bytes 3080 | tf_op jit(solution)/shard_map/ppermute | solution.py:242
  44.2 1.7 %shard_map.114 = (f32[3,2,16,512]{3,2,1,0:T(8,128)S(1)}, f32[4,256]{1,0:T(4,128)S(1)}, f32[8,512]{1,0:T(8,128)S(1)}, f32[4,256]{1,0:T(4,128)S(1)}, f32[8,512]{1,0:T(8,128)S(1)}) custom-call(f32[3,2,16,512]{3,2,1,0:T(8,128)S(1)} %shard_map.113.refs_0_, f32[6,3,3,2,16,512]{5,4,3,2,1,0:T(8,128)S(1)} %copy-done, ...), custom_call_target="tpu_custom_call" | custom-call | flops 1000000000 | bytes 8000000 | tf_op jit(solution)/shard_map/pallas_call | solution.py:24
  46.0 0.7 collective-permute-start.29
  46.7 1.5 %collective-permute-start.30 = (f32[8,512]{1,0:T(8,128)S(1)}, f32[8,512]{1,0:T(8,128)S(1)}, u32[]{:S(2)}, u32[]{:S(2)}) collective-permute-start(f32[8,512]{1,0:T(8,128)S(1)} %get-tuple-element.154), channel_id=1, source_target_pairs={{0,3},{1,2},{2,1},{3,0},{4,7},{5,6},{6,5},{7,4},{8,11},{9,10},{10,... | collective-permute-start | bytes 49160 | tf_op jit(solution)/shard_map/ppermute | solution.py:538
  51.1 1.4 %collective-permute-start.32 = (f32[5,256]{1,0:T(8,128)S(1)}, f32[5,256]{1,0:T(8,128)S(1)}, u32[]{:S(2)}, u32[]{:S(2)}) collective-permute-start(f32[5,256]{1,0:T(8,128)S(1)} %get-tuple-element.161), channel_id=1, source_target_pairs={{0,2},{1,3},{2,0},{3,1},{4,6},{5,7},{6,4},{7,5},{8,10},{9,11},{10,... | collective-permute-start | bytes 15368 | tf_op jit(solution)/shard_map/ppermute | solution.py:538
  52.6 2.2 %collective-permute-done.32.refs_16_ = f32[5,256]{1,0:T(8,128)S(1)} collective-permute-done((f32[5,256]{1,0:T(8,128)S(1)}, f32[5,256]{1,0:T(8,128)S(1)}, u32[]{:S(2)}, u32[]{:S(2)}) %collective-permute-start.32) | collective-permute-done | bytes 5152 | tf_op jit(solution)/shard_map/ppermute | solution.py:538
  54.8 0.9 collective-permute-done.33.refs_17_
  55.7 2.2 %shard_map.119 = (f32[3,2,16,512]{3,2,1,0:T(8,128)S(1)}, f32[3,2,16,512]{3,2,1,0:T(8,128)S(1)}, f32[3,2,16,512]{3,2,1,0:T(8,128)S(1)}, f32[3,2,16,512]{3,2,1,0:T...) custom-call(f32[3,2,16,512]{3,2,1,0:T(8,128)S(1)} %get-tuple-element, ...), custom_call_target="tpu_custom_call" | custom-call | flops 1000000000 | bytes 8000000 | tf_op jit(solution)/shard_map/pallas_call | solution.py:24
  58.0 0.7 collective-permute-start.36
  58.8 1.3 %collective-permute-start.35 = (f32[5,256]{1,0:T(8,128)S(1)}, f32[5,256]{1,0:T(8,128)S(1)}, u32[]{:S(2)}, u32[]{:S(2)}) collective-permute-start(f32[5,256]{1,0:T(8,128)S(1)} %get-tuple-element.166), channel_id=1, source_target_pairs={{0,2},{1,3},{2,0},{3,1},{4,6},{5,7},{6,4},{7,5},{8,10},{9,11},{10,... | collective-permute-start | bytes 15368 | tf_op jit(solution)/shard_map/ppermute | solution.py:538
  60.1 1.4 %collective-permute-start.37 = (f32[3,16,512]{2,1,0:T(8,128)S(1)}, f32[3,16,512]{2,1,0:T(8,128)S(1)}, u32[]{:S(2)}, u32[]{:S(2)}) collective-permute-start(f32[3,16,512]{2,1,0:T(8,128)S(1)} %get-tuple-element.169), channel_id=1, source_target_pairs={{0,4},{4,0},{8,12},{12,8},{16,20},{20,16},{24,28},{28,24},{1,5},{5... | collective-permute-start | bytes 294920 | tf_op jit(solution)/shard_map/ppermute | solution.py:46
  61.5 1.0 %collective-permute-done.35.refs_2_.refs_12_.refs_4_ = f32[5,256]{1,0:T(8,128)S(1)} collective-permute-done((f32[5,256]{1,0:T(8,128)S(1)}, f32[5,256]{1,0:T(8,128)S(1)}, u32[]{:S(2)}, u32[]{:S(2)}) %collective-permute-start.35) | collective-permute-done | bytes 5152 | tf_op jit(solution)/shard_map/ppermute | solution.py:538
  62.4 0.7 shard_map.120
  63.2 1.4 %collective-permute-start.40 = (f32[4,256]{1,0:T(4,128)S(1)}, f32[4,256]{1,0:T(4,128)S(1)}, u32[]{:S(2)}, u32[]{:S(2)}) collective-permute-start(f32[4,256]{1,0:T(4,128)S(1)} %get-tuple-element.172), channel_id=1, source_target_pairs={{0,2},{1,3},{2,0},{3,1},{4,6},{5,7},{6,4},{7,5},{8,10},{9,11},{10,... | collective-permute-start | bytes 12296 | tf_op jit(solution)/shard_map/ppermute | solution.py:538
  65.7 2.8 %collective-permute-start.43 = (f32[1,256]{1,0:T(1,128)S(1)}, f32[1,256]{1,0:T(1,128)S(1)}, u32[]{:S(2)}, u32[]{:S(2)}) collective-permute-start(f32[1,256]{1,0:T(1,128)S(1)} %shard_map.123.refs_0_.mine), channel_id=1, source_target_pairs={{0,28},{1,25},{2,22},{3,19},{4,24},{5,29},{6,18},{7,23},{8,20},{9,... | collective-permute-start | bytes 3080 | tf_op jit(solution)/shard_map/ppermute | solution.py:242
  68.6 2.4 %collective-permute-start.42 = (f32[1,256]{1,0:T(1,128)S(1)}, f32[1,256]{1,0:T(1,128)S(1)}, u32[]{:S(2)}, u32[]{:S(2)}) collective-permute-start(f32[1,256]{1,0:T(1,128)S(1)} %shard_map.123.refs_0_.mine), channel_id=1, source_target_pairs={{0,4},{1,5},{2,10},{3,15},{4,0},{5,1},{6,14},{7,11},{8,12},{9,13},... | collective-permute-start | bytes 3080 | tf_op jit(solution)/shard_map/ppermute | solution.py:242
  71.0 1.8 %shard_map.122 = (f32[3,2,16,512]{3,2,1,0:T(8,128)S(1)}, f32[4,256]{1,0:T(4,128)S(1)}, f32[8,512]{1,0:T(8,128)S(1)}, f32[4,256]{1,0:T(4,128)S(1)}, f32[8,512]{1,0:T(8,128)S(1)}) custom-call(f32[3,2,16,512]{3,2,1,0:T(8,128)S(1)} %shard_map.121.refs_0_, f32[6,3,3,2,16,512]{5,4,3,2,1,0:T(8,128)S(1)} %copy-done, ...), custom_call_target="tpu_custom_call" | custom-call | flops 1000000000 | bytes 8000000 | tf_op jit(solution)/shard_map/pallas_call | solution.py:24
  73.0 2.0 %collective-permute-start.48 = (f32[8,512]{1,0:T(8,128)S(1)}, f32[8,512]{1,0:T(8,128)S(1)}, u32[]{:S(2)}, u32[]{:S(2)}) collective-permute-start(f32[8,512]{1,0:T(8,128)S(1)} %get-tuple-element.181), channel_id=1, source_target_pairs={{0,3},{1,2},{2,1},{3,0},{4,7},{5,6},{6,5},{7,4},{8,11},{9,10},{10,... | collective-permute-start | bytes 49160 | tf_op jit(solution)/shard_map/ppermute | solution.py:538
  75.6 0.9 collective-permute-done.47.refs_2_.refs_12_
  77.4 1.9 %collective-permute-start.50 = (f32[5,256]{1,0:T(8,128)S(1)}, f32[5,256]{1,0:T(8,128)S(1)}, u32[]{:S(2)}, u32[]{:S(2)}) collective-permute-start(f32[5,256]{1,0:T(8,128)S(1)} %get-tuple-element.188), channel_id=1, source_target_pairs={{0,2},{1,3},{2,0},{3,1},{4,6},{5,7},{6,4},{7,5},{8,10},{9,11},{10,... | collective-permute-start | bytes 15368 | tf_op jit(solution)/shard_map/ppermute | solution.py:538
  79.3 1.7 %collective-permute-done.50.refs_16_ = f32[5,256]{1,0:T(8,128)S(1)} collective-permute-done((f32[5,256]{1,0:T(8,128)S(1)}, f32[5,256]{1,0:T(8,128)S(1)}, u32[]{:S(2)}, u32[]{:S(2)}) %collective-permute-start.50) | collective-permute-done | bytes 5152 | tf_op jit(solution)/shard_map/ppermute | solution.py:538
  81.1 1.4 %collective-permute-done.51.refs_17_ = f32[5,256]{1,0:T(8,128)S(1)} collective-permute-done((f32[5,256]{1,0:T(8,128)S(1)}, f32[5,256]{1,0:T(8,128)S(1)}, u32[]{:S(2)}, u32[]{:S(2)}) %collective-permute-start.51) | collective-permute-done | bytes 5152 | tf_op jit(solution)/shard_map/ppermute | solution.py:538
  82.5 1.7 %shard_map.127 = (f32[3,2,16,512]{3,2,1,0:T(8,128)S(1)}, f32[3,2,16,512]{3,2,1,0:T(8,128)S(1)}, f32[3,2,16,512]{3,2,1,0:T(8,128)S(1)}, f32[3,2,16,512]{3,2,1,0:T...) custom-call(f32[3,2,16,512]{3,2,1,0:T(8,128)S(1)} %get-tuple-element.175.refs_0, ...), custom_call_target="tpu_custom_call" | custom-call | flops 1000000000 | bytes 8000000 | tf_op jit(solution)/shard_map/pallas_call | solution.py:24
  84.2 9.7 %all_to_all.5.sums = f32[32,1,128]{2,1,0:T(1,128)S(1)} all-to-all(f32[32,1,128]{2,1,0:T(1,128)S(1)} %get-tuple-element.197), channel_id=1, replica_groups=mesh['res'=8,'grp'=4] {'res','grp'}, dimensions={0} | all-to-all | bytes 32768 | tf_op jit(solution)/shard_map/all_to_all | solution.py:668
  93.9 0.9 shard_map.128
  (104 shorter events, 11.7 us)
Async XLA Ops:
  3.0 7.2 %collective-permute-start.1 = (f32[4,256]{1,0:T(4,128)}, f32[4,256]{1,0:T(4,128)S(1)}, u32[]{:S(2)}, u32[]{:S(2)}) collective-permute-start(f32[4,256]{1,0:T(4,128)} %get-tuple-element.107), channel_id=1, source_target_pairs={{0,2},{1,3},{2,0},{3,1},{4,6},{5,7},{6,4},{7,5},{8,10},{9,11},{10,... | collective-permute-start | bytes 12296 | tf_op jit(solution)/shard_map/ppermute | solution.py:538
  6.1 4.2 %collective-permute-start = (f32[8,512]{1,0:T(8,128)}, f32[8,512]{1,0:T(8,128)S(1)}, u32[]{:S(2)}, u32[]{:S(2)}) collective-permute-start(f32[8,512]{1,0:T(8,128)} %get-tuple-element.106), channel_id=1, source_target_pairs={{0,1},{1,0},{2,3},{3,2},{4,5},{5,4},{6,7},{7,6},{8,9},{9,8},{10,11... | collective-permute-start | bytes 49160 | tf_op jit(solution)/shard_map/ppermute | solution.py:538
  6.1 4.2 %collective-permute-start.2 = (f32[8,512]{1,0:T(8,128)}, f32[8,512]{1,0:T(8,128)S(1)}, u32[]{:S(2)}, u32[]{:S(2)}) collective-permute-start(f32[8,512]{1,0:T(8,128)} %get-tuple-element.108), channel_id=1, source_target_pairs={{0,3},{1,2},{2,1},{3,0},{4,7},{5,6},{6,5},{7,4},{8,11},{9,10},{10,... | collective-permute-start | bytes 49160 | tf_op jit(solution)/shard_map/ppermute | solution.py:538
  8.3 8.5 %collective-permute-start.3 = (f32[3,16,512]{2,1,0:T(8,128)S(1)}, f32[3,16,512]{2,1,0:T(8,128)S(1)}, u32[]{:S(2)}, u32[]{:S(2)}) collective-permute-start(f32[3,16,512]{2,1,0:T(8,128)S(1)} %get-tuple-element.117), channel_id=1, source_target_pairs={{0,4},{4,0},{8,12},{12,8},{16,20},{20,16},{24,28},{28,24},{1,5},{5... | collective-permute-start | bytes 294920 | tf_op jit(solution)/shard_map/ppermute | solution.py:46
  10.3 6.5 %collective-permute-start.4 = (f32[3,16,512]{2,1,0:T(8,128)S(1)}, f32[3,16,512]{2,1,0:T(8,128)S(1)}, u32[]{:S(2)}, u32[]{:S(2)}) collective-permute-start(f32[3,16,512]{2,1,0:T(8,128)S(1)} %get-tuple-element.118), channel_id=1, source_target_pairs={{0,1},{1,0},{2,3},{3,2},{4,8},{5,9},{6,10},{7,11},{8,4},{9,5},{10,... | collective-permute-start | bytes 294920 | tf_op jit(solution)/shard_map/ppermute | solution.py:47
  11.7 4.5 %collective-permute-start.5 = (f32[4,256]{1,0:T(4,128)S(1)}, f32[4,256]{1,0:T(4,128)S(1)}, u32[]{:S(2)}, u32[]{:S(2)}) collective-permute-start(f32[4,256]{1,0:T(4,128)S(1)} %get-tuple-element.119), channel_id=1, source_target_pairs={{0,1},{1,0},{2,3},{3,2},{4,5},{5,4},{6,7},{7,6},{8,9},{9,8},{10,11... | collective-permute-start | bytes 12296 | tf_op jit(solution)/shard_map/ppermute | solution.py:538
  12.2 3.9 %collective-permute-start.6 = (f32[4,256]{1,0:T(4,128)S(1)}, f32[4,256]{1,0:T(4,128)S(1)}, u32[]{:S(2)}, u32[]{:S(2)}) collective-permute-start(f32[4,256]{1,0:T(4,128)S(1)} %get-tuple-element.120), channel_id=1, source_target_pairs={{0,2},{1,3},{2,0},{3,1},{4,6},{5,7},{6,4},{7,5},{8,10},{9,11},{10,... | collective-permute-start | bytes 12296 | tf_op jit(solution)/shard_map/ppermute | solution.py:538
  13.8 3.0 %collective-permute-start.7 = (f32[4,256]{1,0:T(4,128)S(1)}, f32[4,256]{1,0:T(4,128)S(1)}, u32[]{:S(2)}, u32[]{:S(2)}) collective-permute-start(f32[4,256]{1,0:T(4,128)S(1)} %get-tuple-element.121), channel_id=1, source_target_pairs={{0,3},{1,2},{2,1},{3,0},{4,7},{5,6},{6,5},{7,4},{8,11},{9,10},{10,... | collective-permute-start | bytes 12296 | tf_op jit(solution)/shard_map/ppermute | solution.py:538
  18.6 4.9 %collective-permute-start.8 = (f32[8,512]{1,0:T(8,128)S(1)}, f32[8,512]{1,0:T(8,128)S(1)}, u32[]{:S(2)}, u32[]{:S(2)}) collective-permute-start(f32[8,512]{1,0:T(8,128)S(1)} %get-tuple-element.127), channel_id=1, source_target_pairs={{0,1},{1,0},{2,3},{3,2},{4,5},{5,4},{6,7},{7,6},{8,9},{9,8},{10,11... | collective-permute-start | bytes 49160 | tf_op jit(solution)/shard_map/ppermute | solution.py:538
  18.8 4.7 %collective-permute-start.10 = (f32[8,512]{1,0:T(8,128)S(1)}, f32[8,512]{1,0:T(8,128)S(1)}, u32[]{:S(2)}, u32[]{:S(2)}) collective-permute-start(f32[8,512]{1,0:T(8,128)S(1)} %get-tuple-element.129), channel_id=1, source_target_pairs={{0,3},{1,2},{2,1},{3,0},{4,7},{5,6},{6,5},{7,4},{8,11},{9,10},{10,... | collective-permute-start | bytes 49160 | tf_op jit(solution)/shard_map/ppermute | solution.py:538
  19.9 3.6 %collective-permute-start.9 = (f32[4,256]{1,0:T(4,128)S(1)}, f32[4,256]{1,0:T(4,128)S(1)}, u32[]{:S(2)}, u32[]{:S(2)}) collective-permute-start(f32[4,256]{1,0:T(4,128)S(1)} %get-tuple-element.128), channel_id=1, source_target_pairs={{0,2},{1,3},{2,0},{3,1},{4,6},{5,7},{6,4},{7,5},{8,10},{9,11},{10,... | collective-permute-start | bytes 12296 | tf_op jit(solution)/shard_map/ppermute | solution.py:538
  20.8 8.1 %collective-permute-start.11 = (f32[3,16,512]{2,1,0:T(8,128)S(1)}, f32[3,16,512]{2,1,0:T(8,128)S(1)}, u32[]{:S(2)}, u32[]{:S(2)}) collective-permute-start(f32[3,16,512]{2,1,0:T(8,128)S(1)} %get-tuple-element.131), channel_id=1, source_target_pairs={{0,4},{4,0},{8,12},{12,8},{16,20},{20,16},{24,28},{28,24},{1,5},{5... | collective-permute-start | bytes 294920 | tf_op jit(solution)/shard_map/ppermute | solution.py:46
  23.4 5.5 %collective-permute-start.12 = (f32[3,16,512]{2,1,0:T(8,128)S(1)}, f32[3,16,512]{2,1,0:T(8,128)S(1)}, u32[]{:S(2)}, u32[]{:S(2)}) collective-permute-start(f32[3,16,512]{2,1,0:T(8,128)S(1)} %get-tuple-element.132), channel_id=1, source_target_pairs={{0,1},{1,0},{2,3},{3,2},{4,8},{5,9},{6,10},{7,11},{8,4},{9,5},{10,... | collective-permute-start | bytes 294920 | tf_op jit(solution)/shard_map/ppermute | solution.py:47
  24.7 3.6 %collective-permute-start.14 = (f32[4,256]{1,0:T(4,128)S(1)}, f32[4,256]{1,0:T(4,128)S(1)}, u32[]{:S(2)}, u32[]{:S(2)}) collective-permute-start(f32[4,256]{1,0:T(4,128)S(1)} %get-tuple-element.134), channel_id=1, source_target_pairs={{0,2},{1,3},{2,0},{3,1},{4,6},{5,7},{6,4},{7,5},{8,10},{9,11},{10,... | collective-permute-start | bytes 12296 | tf_op jit(solution)/shard_map/ppermute | solution.py:538
  25.9 3.1 %collective-permute-start.15 = (f32[4,256]{1,0:T(4,128)S(1)}, f32[4,256]{1,0:T(4,128)S(1)}, u32[]{:S(2)}, u32[]{:S(2)}) collective-permute-start(f32[4,256]{1,0:T(4,128)S(1)} %get-tuple-element.135), channel_id=1, source_target_pairs={{0,3},{1,2},{2,1},{3,0},{4,7},{5,6},{6,5},{7,4},{8,11},{9,10},{10,... | collective-permute-start | bytes 12296 | tf_op jit(solution)/shard_map/ppermute | solution.py:538
  30.8 4.8 %collective-permute-start.16 = (f32[9,512]{1,0:T(8,128)S(1)}, f32[9,512]{1,0:T(8,128)S(1)}, u32[]{:S(2)}, u32[]{:S(2)}) collective-permute-start(f32[9,512]{1,0:T(8,128)S(1)} %get-tuple-element.138), channel_id=1, source_target_pairs={{0,1},{1,0},{2,3},{3,2},{4,5},{5,4},{6,7},{7,6},{8,9},{9,8},{10,11... | collective-permute-start | bytes 55304 | tf_op jit(solution)/shard_map/ppermute | solution.py:538
  30.9 4.6 %collective-permute-start.18 = (f32[9,512]{1,0:T(8,128)S(1)}, f32[9,512]{1,0:T(8,128)S(1)}, u32[]{:S(2)}, u32[]{:S(2)}) collective-permute-start(f32[9,512]{1,0:T(8,128)S(1)} %get-tuple-element.140), channel_id=1, source_target_pairs={{0,3},{1,2},{2,1},{3,0},{4,7},{5,6},{6,5},{7,4},{8,11},{9,10},{10,... | collective-permute-start | bytes 55304 | tf_op jit(solution)/shard_map/ppermute | solution.py:538
  31.8 3.8 %collective-permute-start.17 = (f32[5,256]{1,0:T(8,128)S(1)}, f32[5,256]{1,0:T(8,128)S(1)}, u32[]{:S(2)}, u32[]{:S(2)}) collective-permute-start(f32[5,256]{1,0:T(8,128)S(1)} %get-tuple-element.139), channel_id=1, source_target_pairs={{0,2},{1,3},{2,0},{3,1},{4,6},{5,7},{6,4},{7,5},{8,10},{9,11},{10,... | collective-permute-start | bytes 15368 | tf_op jit(solution)/shard_map/ppermute | solution.py:538
  33.0 6.8 %collective-permute-start.19 = (f32[3,16,512]{2,1,0:T(8,128)S(1)}, f32[3,16,512]{2,1,0:T(8,128)S(1)}, u32[]{:S(2)}, u32[]{:S(2)}) collective-permute-start(f32[3,16,512]{2,1,0:T(8,128)S(1)} %get-tuple-element.142), channel_id=1, source_target_pairs={{0,4},{4,0},{8,12},{12,8},{16,20},{20,16},{24,28},{28,24},{1,5},{5... | collective-permute-start | bytes 294920 | tf_op jit(solution)/shard_map/ppermute | solution.py:46
  35.6 8.6 %collective-permute-start.20 = (f32[3,16,512]{2,1,0:T(8,128)S(1)}, f32[3,16,512]{2,1,0:T(8,128)S(1)}, u32[]{:S(2)}, u32[]{:S(2)}) collective-permute-start(f32[3,16,512]{2,1,0:T(8,128)S(1)} %get-tuple-element.143), channel_id=1, source_target_pairs={{0,1},{1,0},{2,3},{3,2},{4,8},{5,9},{6,10},{7,11},{8,4},{9,5},{10,... | collective-permute-start | bytes 294920 | tf_op jit(solution)/shard_map/ppermute | solution.py:47
  36.3 2.4 %collective-permute-start.21 = (f32[4,256]{1,0:T(4,128)S(1)}, f32[4,256]{1,0:T(4,128)S(1)}, u32[]{:S(2)}, u32[]{:S(2)}) collective-permute-start(f32[4,256]{1,0:T(4,128)S(1)} %get-tuple-element.144), channel_id=1, source_target_pairs={{0,1},{1,0},{2,3},{3,2},{4,5},{5,4},{6,7},{7,6},{8,9},{9,8},{10,11... | collective-permute-start | bytes 12296 | tf_op jit(solution)/shard_map/ppermute | solution.py:538
  36.8 7.4 %collective-permute-start.22 = (f32[4,256]{1,0:T(4,128)S(1)}, f32[4,256]{1,0:T(4,128)S(1)}, u32[]{:S(2)}, u32[]{:S(2)}) collective-permute-start(f32[4,256]{1,0:T(4,128)S(1)} %get-tuple-element.145), channel_id=1, source_target_pairs={{0,2},{1,3},{2,0},{3,1},{4,6},{5,7},{6,4},{7,5},{8,10},{9,11},{10,... | collective-permute-start | bytes 12296 | tf_op jit(solution)/shard_map/ppermute | solution.py:538
  37.7 6.5 %collective-permute-start.23 = (f32[4,256]{1,0:T(4,128)S(1)}, f32[4,256]{1,0:T(4,128)S(1)}, u32[]{:S(2)}, u32[]{:S(2)}) collective-permute-start(f32[4,256]{1,0:T(4,128)S(1)} %get-tuple-element.146), channel_id=1, source_target_pairs={{0,3},{1,2},{2,1},{3,0},{4,7},{5,6},{6,5},{7,4},{8,11},{9,10},{10,... | collective-permute-start | bytes 12296 | tf_op jit(solution)/shard_map/ppermute | solution.py:538
  39.8 8.4 %collective-permute-start.25 = (f32[1,256]{1,0:T(1,128)S(1)}, f32[1,256]{1,0:T(1,128)S(1)}, u32[]{:S(2)}, u32[]{:S(2)}) collective-permute-start(f32[1,256]{1,0:T(1,128)S(1)} %shard_map.115.refs_0_.mine), channel_id=1, source_target_pairs={{0,28},{1,25},{2,22},{3,19},{4,24},{5,29},{6,18},{7,23},{8,20},{9,... | collective-permute-start | bytes 3080 | tf_op jit(solution)/shard_map/ppermute | solution.py:242
  42.6 5.6 %collective-permute-start.24 = (f32[1,256]{1,0:T(1,128)S(1)}, f32[1,256]{1,0:T(1,128)S(1)}, u32[]{:S(2)}, u32[]{:S(2)}) collective-permute-start(f32[1,256]{1,0:T(1,128)S(1)} %shard_map.115.refs_0_.mine), channel_id=1, source_target_pairs={{0,4},{1,5},{2,10},{3,15},{4,0},{5,1},{6,14},{7,11},{8,12},{9,13},... | collective-permute-start | bytes 3080 | tf_op jit(solution)/shard_map/ppermute | solution.py:242
  46.0 3.7 %collective-permute-start.29 = (f32[4,256]{1,0:T(4,128)S(1)}, f32[4,256]{1,0:T(4,128)S(1)}, u32[]{:S(2)}, u32[]{:S(2)}) collective-permute-start(f32[4,256]{1,0:T(4,128)S(1)} %get-tuple-element.153), channel_id=1, source_target_pairs={{0,2},{1,3},{2,0},{3,1},{4,6},{5,7},{6,4},{7,5},{8,10},{9,11},{10,... | collective-permute-start | bytes 12296 | tf_op jit(solution)/shard_map/ppermute | solution.py:538
  46.7 3.0 %collective-permute-start.28 = (f32[8,512]{1,0:T(8,128)S(1)}, f32[8,512]{1,0:T(8,128)S(1)}, u32[]{:S(2)}, u32[]{:S(2)}) collective-permute-start(f32[8,512]{1,0:T(8,128)S(1)} %get-tuple-element.152), channel_id=1, source_target_pairs={{0,1},{1,0},{2,3},{3,2},{4,5},{5,4},{6,7},{7,6},{8,9},{9,8},{10,11... | collective-permute-start | bytes 49160 | tf_op jit(solution)/shard_map/ppermute | solution.py:538
  46.7 3.2 %collective-permute-start.30 = (f32[8,512]{1,0:T(8,128)S(1)}, f32[8,512]{1,0:T(8,128)S(1)}, u32[]{:S(2)}, u32[]{:S(2)}) collective-permute-start(f32[8,512]{1,0:T(8,128)S(1)} %get-tuple-element.154), channel_id=1, source_target_pairs={{0,3},{1,2},{2,1},{3,0},{4,7},{5,6},{6,5},{7,4},{8,11},{9,10},{10,... | collective-permute-start | bytes 49160 | tf_op jit(solution)/shard_map/ppermute | solution.py:538
  48.6 7.0 %collective-permute-start.26 = (f32[3,16,512]{2,1,0:T(8,128)S(1)}, f32[3,16,512]{2,1,0:T(8,128)S(1)}, u32[]{:S(2)}, u32[]{:S(2)}) collective-permute-start(f32[3,16,512]{2,1,0:T(8,128)S(1)} %get-tuple-element.149), channel_id=1, source_target_pairs={{0,4},{4,0},{8,12},{12,8},{16,20},{20,16},{24,28},{28,24},{1,5},{5... | collective-permute-start | bytes 294920 | tf_op jit(solution)/shard_map/ppermute | solution.py:46
  49.1 6.6 %collective-permute-start.27 = (f32[3,16,512]{2,1,0:T(8,128)S(1)}, f32[3,16,512]{2,1,0:T(8,128)S(1)}, u32[]{:S(2)}, u32[]{:S(2)}) collective-permute-start(f32[3,16,512]{2,1,0:T(8,128)S(1)} %get-tuple-element.150), channel_id=1, source_target_pairs={{0,1},{1,0},{2,3},{3,2},{4,8},{5,9},{6,10},{7,11},{8,4},{9,5},{10,... | collective-permute-start | bytes 294920 | tf_op jit(solution)/shard_map/ppermute | solution.py:47
  51.1 3.7 %collective-permute-start.32 = (f32[5,256]{1,0:T(8,128)S(1)}, f32[5,256]{1,0:T(8,128)S(1)}, u32[]{:S(2)}, u32[]{:S(2)}) collective-permute-start(f32[5,256]{1,0:T(8,128)S(1)} %get-tuple-element.161), channel_id=1, source_target_pairs={{0,2},{1,3},{2,0},{3,1},{4,6},{5,7},{6,4},{7,5},{8,10},{9,11},{10,... | collective-permute-start | bytes 15368 | tf_op jit(solution)/shard_map/ppermute | solution.py:538
  52.5 3.1 %collective-permute-start.33 = (f32[5,256]{1,0:T(8,128)S(1)}, f32[5,256]{1,0:T(8,128)S(1)}, u32[]{:S(2)}, u32[]{:S(2)}) collective-permute-start(f32[5,256]{1,0:T(8,128)S(1)} %get-tuple-element.162), channel_id=1, source_target_pairs={{0,3},{1,2},{2,1},{3,0},{4,7},{5,6},{6,5},{7,4},{8,11},{9,10},{10,... | collective-permute-start | bytes 15368 | tf_op jit(solution)/shard_map/ppermute | solution.py:538
  57.9 4.5 %collective-permute-start.34 = (f32[9,512]{1,0:T(8,128)S(1)}, f32[9,512]{1,0:T(8,128)S(1)}, u32[]{:S(2)}, u32[]{:S(2)}) collective-permute-start(f32[9,512]{1,0:T(8,128)S(1)} %get-tuple-element.165), channel_id=1, source_target_pairs={{0,1},{1,0},{2,3},{3,2},{4,5},{5,4},{6,7},{7,6},{8,9},{9,8},{10,11... | collective-permute-start | bytes 55304 | tf_op jit(solution)/shard_map/ppermute | solution.py:538
  58.0 4.4 %collective-permute-start.36 = (f32[9,512]{1,0:T(8,128)S(1)}, f32[9,512]{1,0:T(8,128)S(1)}, u32[]{:S(2)}, u32[]{:S(2)}) collective-permute-start(f32[9,512]{1,0:T(8,128)S(1)} %get-tuple-element.167), channel_id=1, source_target_pairs={{0,3},{1,2},{2,1},{3,0},{4,7},{5,6},{6,5},{7,4},{8,11},{9,10},{10,... | collective-permute-start | bytes 55304 | tf_op jit(solution)/shard_map/ppermute | solution.py:538
  58.8 3.7 %collective-permute-start.35 = (f32[5,256]{1,0:T(8,128)S(1)}, f32[5,256]{1,0:T(8,128)S(1)}, u32[]{:S(2)}, u32[]{:S(2)}) collective-permute-start(f32[5,256]{1,0:T(8,128)S(1)} %get-tuple-element.166), channel_id=1, source_target_pairs={{0,2},{1,3},{2,0},{3,1},{4,6},{5,7},{6,4},{7,5},{8,10},{9,11},{10,... | collective-permute-start | bytes 15368 | tf_op jit(solution)/shard_map/ppermute | solution.py:538
  60.1 5.6 %collective-permute-start.37 = (f32[3,16,512]{2,1,0:T(8,128)S(1)}, f32[3,16,512]{2,1,0:T(8,128)S(1)}, u32[]{:S(2)}, u32[]{:S(2)}) collective-permute-start(f32[3,16,512]{2,1,0:T(8,128)S(1)} %get-tuple-element.169), channel_id=1, source_target_pairs={{0,4},{4,0},{8,12},{12,8},{16,20},{20,16},{24,28},{28,24},{1,5},{5... | collective-permute-start | bytes 294920 | tf_op jit(solution)/shard_map/ppermute | solution.py:46
  61.5 9.6 %collective-permute-start.38 = (f32[3,16,512]{2,1,0:T(8,128)S(1)}, f32[3,16,512]{2,1,0:T(8,128)S(1)}, u32[]{:S(2)}, u32[]{:S(2)}) collective-permute-start(f32[3,16,512]{2,1,0:T(8,128)S(1)} %get-tuple-element.170), channel_id=1, source_target_pairs={{0,1},{1,0},{2,3},{3,2},{4,8},{5,9},{6,10},{7,11},{8,4},{9,5},{10,... | collective-permute-start | bytes 294920 | tf_op jit(solution)/shard_map/ppermute | solution.py:47
  63.2 7.8 %collective-permute-start.40 = (f32[4,256]{1,0:T(4,128)S(1)}, f32[4,256]{1,0:T(4,128)S(1)}, u32[]{:S(2)}, u32[]{:S(2)}) collective-permute-start(f32[4,256]{1,0:T(4,128)S(1)} %get-tuple-element.172), channel_id=1, source_target_pairs={{0,2},{1,3},{2,0},{3,1},{4,6},{5,7},{6,4},{7,5},{8,10},{9,11},{10,... | collective-permute-start | bytes 12296 | tf_op jit(solution)/shard_map/ppermute | solution.py:538
  64.6 6.4 %collective-permute-start.41 = (f32[4,256]{1,0:T(4,128)S(1)}, f32[4,256]{1,0:T(4,128)S(1)}, u32[]{:S(2)}, u32[]{:S(2)}) collective-permute-start(f32[4,256]{1,0:T(4,128)S(1)} %get-tuple-element.173), channel_id=1, source_target_pairs={{0,3},{1,2},{2,1},{3,0},{4,7},{5,6},{6,5},{7,4},{8,11},{9,10},{10,... | collective-permute-start | bytes 12296 | tf_op jit(solution)/shard_map/ppermute | solution.py:538
  65.7 9.3 %collective-permute-start.43 = (f32[1,256]{1,0:T(1,128)S(1)}, f32[1,256]{1,0:T(1,128)S(1)}, u32[]{:S(2)}, u32[]{:S(2)}) collective-permute-start(f32[1,256]{1,0:T(1,128)S(1)} %shard_map.123.refs_0_.mine), channel_id=1, source_target_pairs={{0,28},{1,25},{2,22},{3,19},{4,24},{5,29},{6,18},{7,23},{8,20},{9,... | collective-permute-start | bytes 3080 | tf_op jit(solution)/shard_map/ppermute | solution.py:242
  68.6 6.4 %collective-permute-start.42 = (f32[1,256]{1,0:T(1,128)S(1)}, f32[1,256]{1,0:T(1,128)S(1)}, u32[]{:S(2)}, u32[]{:S(2)}) collective-permute-start(f32[1,256]{1,0:T(1,128)S(1)} %shard_map.123.refs_0_.mine), channel_id=1, source_target_pairs={{0,4},{1,5},{2,10},{3,15},{4,0},{5,1},{6,14},{7,11},{8,12},{9,13},... | collective-permute-start | bytes 3080 | tf_op jit(solution)/shard_map/ppermute | solution.py:242
  72.8 3.7 %collective-permute-start.47 = (f32[4,256]{1,0:T(4,128)S(1)}, f32[4,256]{1,0:T(4,128)S(1)}, u32[]{:S(2)}, u32[]{:S(2)}) collective-permute-start(f32[4,256]{1,0:T(4,128)S(1)} %get-tuple-element.180), channel_id=1, source_target_pairs={{0,2},{1,3},{2,0},{3,1},{4,6},{5,7},{6,4},{7,5},{8,10},{9,11},{10,... | collective-permute-start | bytes 12296 | tf_op jit(solution)/shard_map/ppermute | solution.py:538
  72.9 3.6 %collective-permute-start.46 = (f32[8,512]{1,0:T(8,128)S(1)}, f32[8,512]{1,0:T(8,128)S(1)}, u32[]{:S(2)}, u32[]{:S(2)}) collective-permute-start(f32[8,512]{1,0:T(8,128)S(1)} %get-tuple-element.179), channel_id=1, source_target_pairs={{0,1},{1,0},{2,3},{3,2},{4,5},{5,4},{6,7},{7,6},{8,9},{9,8},{10,11... | collective-permute-start | bytes 49160 | tf_op jit(solution)/shard_map/ppermute | solution.py:538
  73.0 3.5 %collective-permute-start.48 = (f32[8,512]{1,0:T(8,128)S(1)}, f32[8,512]{1,0:T(8,128)S(1)}, u32[]{:S(2)}, u32[]{:S(2)}) collective-permute-start(f32[8,512]{1,0:T(8,128)S(1)} %get-tuple-element.181), channel_id=1, source_target_pairs={{0,3},{1,2},{2,1},{3,0},{4,7},{5,6},{6,5},{7,4},{8,11},{9,10},{10,... | collective-permute-start | bytes 49160 | tf_op jit(solution)/shard_map/ppermute | solution.py:538
  75.5 7.0 %collective-permute-start.44 = (f32[3,16,512]{2,1,0:T(8,128)S(1)}, f32[3,16,512]{2,1,0:T(8,128)S(1)}, u32[]{:S(2)}, u32[]{:S(2)}) collective-permute-start(f32[3,16,512]{2,1,0:T(8,128)S(1)} %get-tuple-element.176), channel_id=1, source_target_pairs={{0,4},{4,0},{8,12},{12,8},{16,20},{20,16},{24,28},{28,24},{1,5},{5... | collective-permute-start | bytes 294920 | tf_op jit(solution)/shard_map/ppermute | solution.py:46
  75.5 7.0 %collective-permute-start.45 = (f32[3,16,512]{2,1,0:T(8,128)S(1)}, f32[3,16,512]{2,1,0:T(8,128)S(1)}, u32[]{:S(2)}, u32[]{:S(2)}) collective-permute-start(f32[3,16,512]{2,1,0:T(8,128)S(1)} %get-tuple-element.177), channel_id=1, source_target_pairs={{0,1},{1,0},{2,3},{3,2},{4,8},{5,9},{6,10},{7,11},{8,4},{9,5},{10,... | collective-permute-start | bytes 294920 | tf_op jit(solution)/shard_map/ppermute | solution.py:47
  77.4 3.7 %collective-permute-start.50 = (f32[5,256]{1,0:T(8,128)S(1)}, f32[5,256]{1,0:T(8,128)S(1)}, u32[]{:S(2)}, u32[]{:S(2)}) collective-permute-start(f32[5,256]{1,0:T(8,128)S(1)} %get-tuple-element.188), channel_id=1, source_target_pairs={{0,2},{1,3},{2,0},{3,1},{4,6},{5,7},{6,4},{7,5},{8,10},{9,11},{10,... | collective-permute-start | bytes 15368 | tf_op jit(solution)/shard_map/ppermute | solution.py:538
  79.3 3.1 %collective-permute-start.51 = (f32[5,256]{1,0:T(8,128)S(1)}, f32[5,256]{1,0:T(8,128)S(1)}, u32[]{:S(2)}, u32[]{:S(2)}) collective-permute-start(f32[5,256]{1,0:T(8,128)S(1)} %get-tuple-element.189), channel_id=1, source_target_pairs={{0,3},{1,2},{2,1},{3,0},{4,7},{5,6},{6,5},{7,4},{8,11},{9,10},{10,... | collective-permute-start | bytes 15368 | tf_op jit(solution)/shard_map/ppermute | solution.py:538
  (15 other events, 37.7 us)

commit v10 on v9

--- a/solution.py
+++ b/solution.py
@@ -607,7 +607,7 @@
     def apply(kernel, outs, vec, sends, extra, sums=None, with_sums=False):
         messages, faces = swapped(sends[:groups]), sends[groups:]
         values = solve(solve_kernel, messages_back, [first, second, *messages])
-        first_here = values[:1] if faces else sums
+        first_here = values[:1] if faces else sums or []
         *made, part = call(
             functools.partial(stencil_kernel, len(first_here)),
             ([] if faces else face_outs) + [field],
@@ -623,15 +623,20 @@
             )
         values = swapped(values)
         out = finish(kernel, outs, part, messages, values, halo, extra)
-        return (fetch(messages, [values[1], halo[0]]), out) if with_sums else out
-
-    def fetch(messages, after):
-        mine = call(
-            functools.partial(group_sum_kernel, capacity, len(after)),
-            [((1, segb), F32)],
-            [*after, *messages],
-        )[0]
-        return [mine] + [share_swap(mine, q) for q in range(share(lax.axis_size("res"), groups))]
+        return (fetch(messages, values[1], halo[0]), out) if with_sums else out
+
+    def fetch(messages, early, late):
+        count = share(lax.axis_size("res"), groups)
+        out = []
+        for q in reversed(range(count)):
+            after = [early] if q + 1 == count else [early, late]
+            mine = call(
+                functools.partial(group_sum_kernel, capacity, len(after)),
+                [((1, segb), F32)],
+                [*after, *messages],
+            )[0]
+            out.insert(0, share_swap(mine, q))
+        return [mine] + out
 
     messages = swapped(sends)
     place, *faces = call(
@@ -650,7 +655,7 @@
         **cost,
     )
     plainly = functools.partial(apply_kernel, sizes)
-    w, *sends = finish(plainly, [field] + plain + face_outs, part, messages, values, halo, [])
+    w, *sends = finish(plainly, [field] + plain, part, messages, values, halo, [])
     t, *sends = apply(
         functools.partial(second_kernel, sizes), [field] + summed + face_outs, w, sends, [b, w]
     )

time: 95 us -> 93.8 us (0.987)
  waiting for transfers between devices: 13.3 us -> 11.3 us
    ppermute x6, waiting for transfers between devices: 1.33 us -> 0.02 us  [exchange(): lax.ppermute(faces[0], 'res', first)]
    ppermute x6, starting transfers between devices: 8.97 us -> 10.1 us  [exchange(): lax.ppermute(faces[0], 'res', first)]
    pallas_call x25 -> x27, Pallas kernels: 23.9 us -> 24 us  [call(): pl.pallas_call(kernel, out_shape=[jax.ShapeDtypeStruct(shape, dtype) for...]
  transfers between devices with their start and end apart: 52 -> 52, of which waited for: 14 -> 11; matrix products, arithmetic and copies ran while one was open for 0% -> 0% of each run, Pallas kernels for 14% -> 14%
where the time goes in v10:
time: 93.8 us; the launch traced here: 93.5 us
  starting transfers between devices  45.7 us (49%)
  Pallas kernels  24 us (26%)
  waiting for transfers between devices  11.3 us (12%)
  blocking collectives  9.82 us (10%)
  local copies, waits for them, and re-layouts  1.67 us (2%)
  between operations  1.02 us (1%)
    ppermute x36, starting transfers between devices, swapped(): lax.ppermute(messages[k], 'grp', [(i, i ^ k) for i in range(groups)])  26.5 us
    pallas_call x27, Pallas kernels, call(): pl.pallas_call(kernel, out_shape=[jax.ShapeDtypeStruct(shape, dtype) for...  24 us
    ppermute x36, waiting for transfers between devices, swapped(): lax.ppermute(messages[k], 'grp', [(i, i ^ k) for i in range(groups)])  11.3 us
    ppermute x6, starting transfers between devices, exchange(): lax.ppermute(faces[0], 'res', first)  10.1 us
    all_to_all x1, blocking collectives, body(): lax.all_to_all(sends[0], ('res', 'grp'), split_axis=0, concat_axis=0, til...  9.82 us
    ppermute x4, starting transfers between devices, share_swap(): return lax.ppermute(row, ('res', 'grp'), pairs)  9.18 us
  transfers between devices with their start and end apart: 52, of which 11 were waited for; matrix products, arithmetic and copies ran while one was open for 0% of the time, Pallas kernels for 14%

profile of v10, /device:TPU:0, one launch (start us, length us, event | category | flops | bytes accessed | tf_op | source)
XLA Modules:
  0.0 93.5 jit_solution(14345616670347686612)
XLA Ops:
  0.6 2.4 %shard_map.104 = (s32[8,256]{1,0:T(8,128)}, s32[8,256]{1,0:T(8,128)}, f32[3,8,256]{2,1,0:T(8,128)}, f32[3,8,256]{2,1,0:T(8,128)}, f32[4,256]{1,0:T(4,128)}, /*in...) custom-call(f32[3,2,16,512]{3,2,1,0:T(8,128)} %refs_18_.5, s32[8,256]{1,0:T(8,128)} %refs_1_.7, s32[8]{0:T(128)} %refs_2_.1, ...), custom_call_target="tpu_custom_call" | custom-call | flops 1000000 | bytes 1000000 | tf_op jit(solution)/shard_map/pallas_call | solution.py:24
  3.0 3.0 %collective-permute-start.1 = (f32[4,256]{1,0:T(4,128)}, f32[4,256]{1,0:T(4,128)S(1)}, u32[]{:S(2)}, u32[]{:S(2)}) collective-permute-start(f32[4,256]{1,0:T(4,128)} %get-tuple-element.108), channel_id=1, source_target_pairs={{0,2},{1,3},{2,0},{3,1},{4,6},{5,7},{6,4},{7,5},{8,10},{9,11},{10,... | collective-permute-start | bytes 12296 | tf_op jit(solution)/shard_map/ppermute | solution.py:538
  6.3 0.9 copy-done.1
  7.2 0.7 copy-done.10
  8.3 2.0 %collective-permute-start.3 = (f32[3,16,512]{2,1,0:T(8,128)S(1)}, f32[3,16,512]{2,1,0:T(8,128)S(1)}, u32[]{:S(2)}, u32[]{:S(2)}) collective-permute-start(f32[3,16,512]{2,1,0:T(8,128)S(1)} %get-tuple-element.118), channel_id=1, source_target_pairs={{0,4},{4,0},{8,12},{12,8},{16,20},{20,16},{24,28},{28,24},{1,5},{5... | collective-permute-start | bytes 294920 | tf_op jit(solution)/shard_map/ppermute | solution.py:46
  10.3 1.3 %shard_map.106 = (f32[4,256]{1,0:T(4,128)S(1)}, f32[4,256]{1,0:T(4,128)S(1)}, f32[4,256]{1,0:T(4,128)S(1)}, f32[4,256]{1,0:T(4,128)S(1)}, bf16[4,4,256,256]{3,2,...) custom-call(f32[4,4,256,256]{3,2,1,0:T(8,128)S(1)} %bitcast.11, f32[4,256]{1,0:T(4,128)S(1)} %copy-done.8, ...), custom_call_target="tpu_custom_call" | custom-call | flops 5000000000 | bytes 4000000 | tf_op jit(solution)/shard_map/pallas_call | solution.py:24
  12.2 1.5 %collective-permute-start.6 = (f32[4,256]{1,0:T(4,128)S(1)}, f32[4,256]{1,0:T(4,128)S(1)}, u32[]{:S(2)}, u32[]{:S(2)}) collective-permute-start(f32[4,256]{1,0:T(4,128)S(1)} %get-tuple-element.121), channel_id=1, source_target_pairs={{0,2},{1,3},{2,0},{3,1},{4,6},{5,7},{6,4},{7,5},{8,10},{9,11},{10,... | collective-permute-start | bytes 12296 | tf_op jit(solution)/shard_map/ppermute | solution.py:538
  13.8 2.3 %shard_map.107 = (f32[3,2,16,512]{3,2,1,0:T(8,128)S(1)}, f32[3,3,2,16,512]{4,3,2,1,0:T(8,128)S(1)}, bf16[2048,512]{1,0:T(8,128)(2,1)S(1)}, bf16[4,4,256,256]{3,2...) custom-call(f32[3,2,16,512]{3,2,1,0:T(8,128)S(1)} %copy-done.2, f32[6,3,3,2,16,512]{5,4,3,2,1,0:T(8,128)S(1)} %copy-done, ...), custom_call_target="tpu_custom_call" | custom-call | flops 200000000 | bytes 4000000 | tf_op jit(solution)/shard_map/pallas_call | solution.py:24
  16.8 1.8 %shard_map.108 = (f32[3,2,16,512]{3,2,1,0:T(8,128)S(1)}, f32[4,256]{1,0:T(4,128)S(1)}, f32[8,512]{1,0:T(8,128)S(1)}, f32[4,256]{1,0:T(4,128)S(1)}, f32[8,512]{1,0:T(8,128)S(1)}) custom-call(f32[3,2,16,512]{3,2,1,0:T(8,128)S(1)} %get-tuple-element.113.refs_0_, f32[6,3,3,2,16,512]{5,4,3,2,1,0:T(8,128)S(1)} %copy-done, ...), custom_call_target="tpu_custom_call" | custom-call | flops 1000000000 | bytes 8000000 | tf_op jit(solution)/shard_map/pallas_call | solution.py:24
  18.6 1.0 %collective-permute-start.11 = (f32[4,256]{1,0:T(4,128)S(1)}, f32[4,256]{1,0:T(4,128)S(1)}, u32[]{:S(2)}, u32[]{:S(2)}) collective-permute-start(f32[4,256]{1,0:T(4,128)S(1)} %get-tuple-element.130), channel_id=1, source_target_pairs={{0,2},{1,3},{2,0},{3,1},{4,6},{5,7},{6,4},{7,5},{8,10},{9,11},{10,... | collective-permute-start | bytes 12296 | tf_op jit(solution)/shard_map/ppermute | solution.py:538
  19.9 0.9 collective-permute-start.12
  21.2 2.7 %collective-permute-start.8 = (f32[3,16,512]{2,1,0:T(8,128)S(1)}, f32[3,16,512]{2,1,0:T(8,128)S(1)}, u32[]{:S(2)}, u32[]{:S(2)}) collective-permute-start(f32[3,16,512]{2,1,0:T(8,128)S(1)} %get-tuple-element.126), channel_id=1, source_target_pairs={{0,4},{4,0},{8,12},{12,8},{16,20},{20,16},{24,28},{28,24},{1,5},{5... | collective-permute-start | bytes 294920 | tf_op jit(solution)/shard_map/ppermute | solution.py:46
  23.9 0.7 shard_map.110
  25.2 1.2 %collective-permute-start.14 = (f32[4,256]{1,0:T(4,128)S(1)}, f32[4,256]{1,0:T(4,128)S(1)}, u32[]{:S(2)}, u32[]{:S(2)}) collective-permute-start(f32[4,256]{1,0:T(4,128)S(1)} %get-tuple-element.136), channel_id=1, source_target_pairs={{0,2},{1,3},{2,0},{3,1},{4,6},{5,7},{6,4},{7,5},{8,10},{9,11},{10,... | collective-permute-start | bytes 12296 | tf_op jit(solution)/shard_map/ppermute | solution.py:538
  26.6 2.2 %collective-permute-done.14.refs_16_ = f32[4,256]{1,0:T(4,128)S(1)} collective-permute-done((f32[4,256]{1,0:T(4,128)S(1)}, f32[4,256]{1,0:T(4,128)S(1)}, u32[]{:S(2)}, u32[]{:S(2)}) %collective-permute-start.14) | collective-permute-done | bytes 4128 | tf_op jit(solution)/shard_map/ppermute | solution.py:538
  29.4 1.8 %shard_map.111 = (f32[3,2,16,512]{3,2,1,0:T(8,128)S(1)}, f32[5,256]{1,0:T(8,128)S(1)}, f32[9,512]{1,0:T(8,128)S(1)}, f32[5,256]{1,0:T(8,128)S(1)}, f32[9,512]{1,...) custom-call(f32[3,2,16,512]{3,2,1,0:T(8,128)S(1)} %get-tuple-element.125.refs_0_, ...), custom_call_target="tpu_custom_call" | custom-call | flops 1000000000 | bytes 8000000 | tf_op jit(solution)/shard_map/pallas_call | solution.py:24
  31.4 0.9 collective-permute-start.18
  32.3 1.2 %collective-permute-start.17 = (f32[5,256]{1,0:T(8,128)S(1)}, f32[5,256]{1,0:T(8,128)S(1)}, u32[]{:S(2)}, u32[]{:S(2)}) collective-permute-start(f32[5,256]{1,0:T(8,128)S(1)} %get-tuple-element.141), channel_id=1, source_target_pairs={{0,2},{1,3},{2,0},{3,1},{4,6},{5,7},{6,4},{7,5},{8,10},{9,11},{10,... | collective-permute-start | bytes 15368 | tf_op jit(solution)/shard_map/ppermute | solution.py:538
  33.5 2.6 %collective-permute-start.19 = (f32[3,16,512]{2,1,0:T(8,128)S(1)}, f32[3,16,512]{2,1,0:T(8,128)S(1)}, u32[]{:S(2)}, u32[]{:S(2)}) collective-permute-start(f32[3,16,512]{2,1,0:T(8,128)S(1)} %get-tuple-element.144), channel_id=1, source_target_pairs={{0,4},{4,0},{8,12},{12,8},{16,20},{20,16},{24,28},{28,24},{1,5},{5... | collective-permute-start | bytes 294920 | tf_op jit(solution)/shard_map/ppermute | solution.py:46
  36.1 0.7 shard_map.112
  37.4 0.8 collective-permute-start.22
  39.2 3.2 %collective-permute-start.25 = (f32[1,256]{1,0:T(1,128)S(1)}, f32[1,256]{1,0:T(1,128)S(1)}, u32[]{:S(2)}, u32[]{:S(2)}) collective-permute-start(f32[1,256]{1,0:T(1,128)S(1)} %shard_map.116), channel_id=1, source_target_pairs={{0,28},{1,25},{2,22},{3,19},{4,24},{5,29},{6,18},{7,23},{8,20},{9,... | collective-permute-start | bytes 3080 | tf_op jit(solution)/shard_map/ppermute | solution.py:242
  42.5 1.3 %collective-permute-start.24 = (f32[1,256]{1,0:T(1,128)S(1)}, f32[1,256]{1,0:T(1,128)S(1)}, u32[]{:S(2)}, u32[]{:S(2)}) collective-permute-start(f32[1,256]{1,0:T(1,128)S(1)} %shard_map.115.refs_0_.mine), channel_id=1, source_target_pairs={{0,4},{1,5},{2,10},{3,15},{4,0},{5,1},{6,14},{7,11},{8,12},{9,13},... | collective-permute-start | bytes 3080 | tf_op jit(solution)/shard_map/ppermute | solution.py:242
  43.7 1.8 %shard_map.114 = (f32[3,2,16,512]{3,2,1,0:T(8,128)S(1)}, f32[4,256]{1,0:T(4,128)S(1)}, f32[8,512]{1,0:T(8,128)S(1)}, f32[4,256]{1,0:T(4,128)S(1)}, f32[8,512]{1,0:T(8,128)S(1)}) custom-call(f32[3,2,16,512]{3,2,1,0:T(8,128)S(1)} %shard_map.113.refs_0_, f32[6,3,3,2,16,512]{5,4,3,2,1,0:T(8,128)S(1)} %copy-done, ...), custom_call_target="tpu_custom_call" | custom-call | flops 1000000000 | bytes 8000000 | tf_op jit(solution)/shard_map/pallas_call | solution.py:24
  45.8 1.9 %collective-permute-start.30 = (f32[8,512]{1,0:T(8,128)S(1)}, f32[8,512]{1,0:T(8,128)S(1)}, u32[]{:S(2)}, u32[]{:S(2)}) collective-permute-start(f32[8,512]{1,0:T(8,128)S(1)} %get-tuple-element.156), channel_id=1, source_target_pairs={{0,3},{1,2},{2,1},{3,0},{4,7},{5,6},{6,5},{7,4},{8,11},{9,10},{10,... | collective-permute-start | bytes 49160 | tf_op jit(solution)/shard_map/ppermute | solution.py:538
  48.1 0.9 collective-permute-start.26
  49.2 0.7 shard_map.118
  50.3 1.7 %collective-permute-start.32 = (f32[5,256]{1,0:T(8,128)S(1)}, f32[5,256]{1,0:T(8,128)S(1)}, u32[]{:S(2)}, u32[]{:S(2)}) collective-permute-start(f32[5,256]{1,0:T(8,128)S(1)} %get-tuple-element.163), channel_id=1, source_target_pairs={{0,2},{1,3},{2,0},{3,1},{4,6},{5,7},{6,4},{7,5},{8,10},{9,11},{10,... | collective-permute-start | bytes 15368 | tf_op jit(solution)/shard_map/ppermute | solution.py:538
  52.0 1.9 %collective-permute-done.32.refs_16_ = f32[5,256]{1,0:T(8,128)S(1)} collective-permute-done((f32[5,256]{1,0:T(8,128)S(1)}, f32[5,256]{1,0:T(8,128)S(1)}, u32[]{:S(2)}, u32[]{:S(2)}) %collective-permute-start.32) | collective-permute-done | bytes 5152 | tf_op jit(solution)/shard_map/ppermute | solution.py:538
  54.0 1.2 %collective-permute-done.33.refs_17_ = f32[5,256]{1,0:T(8,128)S(1)} collective-permute-done((f32[5,256]{1,0:T(8,128)S(1)}, f32[5,256]{1,0:T(8,128)S(1)}, u32[]{:S(2)}, u32[]{:S(2)}) %collective-permute-start.33) | collective-permute-done | bytes 5152 | tf_op jit(solution)/shard_map/ppermute | solution.py:538
  55.2 2.2 %shard_map.120 = (f32[3,2,16,512]{3,2,1,0:T(8,128)S(1)}, f32[3,2,16,512]{3,2,1,0:T(8,128)S(1)}, f32[3,2,16,512]{3,2,1,0:T(8,128)S(1)}, f32[3,2,16,512]{3,2,1,0:T...) custom-call(f32[3,2,16,512]{3,2,1,0:T(8,128)S(1)} %get-tuple-element, ...), custom_call_target="tpu_custom_call" | custom-call | flops 1000000000 | bytes 8000000 | tf_op jit(solution)/shard_map/pallas_call | solution.py:24
  58.2 1.5 %collective-permute-start.35 = (f32[5,256]{1,0:T(8,128)S(1)}, f32[5,256]{1,0:T(8,128)S(1)}, u32[]{:S(2)}, u32[]{:S(2)}) collective-permute-start(f32[5,256]{1,0:T(8,128)S(1)} %get-tuple-element.168), channel_id=1, source_target_pairs={{0,2},{1,3},{2,0},{3,1},{4,6},{5,7},{6,4},{7,5},{8,10},{9,11},{10,... | collective-permute-start | bytes 15368 | tf_op jit(solution)/shard_map/ppermute | solution.py:538
  59.6 1.1 %collective-permute-start.37 = (f32[3,16,512]{2,1,0:T(8,128)S(1)}, f32[3,16,512]{2,1,0:T(8,128)S(1)}, u32[]{:S(2)}, u32[]{:S(2)}) collective-permute-start(f32[3,16,512]{2,1,0:T(8,128)S(1)} %get-tuple-element.171), channel_id=1, source_target_pairs={{0,4},{4,0},{8,12},{12,8},{16,20},{20,16},{24,28},{28,24},{1,5},{5... | collective-permute-start | bytes 294920 | tf_op jit(solution)/shard_map/ppermute | solution.py:46
  60.7 1.1 %collective-permute-done.35.refs_2_.refs_12_.refs_4_.refs_3_ = f32[5,256]{1,0:T(8,128)S(1)} collective-permute-done((f32[5,256]{1,0:T(8,128)S(1)}, f32[5,256]{1,0:T(8,128)S(1)}, u32[]{:S(2)}, u32[]{:S(2)}) %collective-permute-start.35) | collective-permute-done | bytes 5152 | tf_op jit(solution)/shard_map/ppermute | solution.py:538
  61.8 0.7 shard_map.121
  62.6 1.5 %collective-permute-start.40 = (f32[4,256]{1,0:T(4,128)S(1)}, f32[4,256]{1,0:T(4,128)S(1)}, u32[]{:S(2)}, u32[]{:S(2)}) collective-permute-start(f32[4,256]{1,0:T(4,128)S(1)} %get-tuple-element.174), channel_id=1, source_target_pairs={{0,2},{1,3},{2,0},{3,1},{4,6},{5,7},{6,4},{7,5},{8,10},{9,11},{10,... | collective-permute-start | bytes 12296 | tf_op jit(solution)/shard_map/ppermute | solution.py:538
  64.9 3.4 %collective-permute-start.43 = (f32[1,256]{1,0:T(1,128)S(1)}, f32[1,256]{1,0:T(1,128)S(1)}, u32[]{:S(2)}, u32[]{:S(2)}) collective-permute-start(f32[1,256]{1,0:T(1,128)S(1)} %shard_map.125), channel_id=1, source_target_pairs={{0,28},{1,25},{2,22},{3,19},{4,24},{5,29},{6,18},{7,23},{8,20},{9,... | collective-permute-start | bytes 3080 | tf_op jit(solution)/shard_map/ppermute | solution.py:242
  68.3 1.3 %collective-permute-start.42 = (f32[1,256]{1,0:T(1,128)S(1)}, f32[1,256]{1,0:T(1,128)S(1)}, u32[]{:S(2)}, u32[]{:S(2)}) collective-permute-start(f32[1,256]{1,0:T(1,128)S(1)} %shard_map.124.refs_0_.mine), channel_id=1, source_target_pairs={{0,4},{1,5},{2,10},{3,15},{4,0},{5,1},{6,14},{7,11},{8,12},{9,13},... | collective-permute-start | bytes 3080 | tf_op jit(solution)/shard_map/ppermute | solution.py:242
  69.6 1.8 %shard_map.123 = (f32[3,2,16,512]{3,2,1,0:T(8,128)S(1)}, f32[4,256]{1,0:T(4,128)S(1)}, f32[8,512]{1,0:T(8,128)S(1)}, f32[4,256]{1,0:T(4,128)S(1)}, f32[8,512]{1,0:T(8,128)S(1)}) custom-call(f32[3,2,16,512]{3,2,1,0:T(8,128)S(1)} %shard_map.122.refs_0_, f32[6,3,3,2,16,512]{5,4,3,2,1,0:T(8,128)S(1)} %copy-done, ...), custom_call_target="tpu_custom_call" | custom-call | flops 1000000000 | bytes 8000000 | tf_op jit(solution)/shard_map/pallas_call | solution.py:24
  71.4 0.8 collective-permute-start.47
  72.2 1.4 %collective-permute-start.48 = (f32[8,512]{1,0:T(8,128)S(1)}, f32[8,512]{1,0:T(8,128)S(1)}, u32[]{:S(2)}, u32[]{:S(2)}) collective-permute-start(f32[8,512]{1,0:T(8,128)S(1)} %get-tuple-element.183), channel_id=1, source_target_pairs={{0,3},{1,2},{2,1},{3,0},{4,7},{5,6},{6,5},{7,4},{8,11},{9,10},{10,... | collective-permute-start | bytes 49160 | tf_op jit(solution)/shard_map/ppermute | solution.py:538
  74.0 0.8 collective-permute-start.44
  76.7 1.2 %collective-permute-start.50 = (f32[5,256]{1,0:T(8,128)S(1)}, f32[5,256]{1,0:T(8,128)S(1)}, u32[]{:S(2)}, u32[]{:S(2)}) collective-permute-start(f32[5,256]{1,0:T(8,128)S(1)} %get-tuple-element.190), channel_id=1, source_target_pairs={{0,2},{1,3},{2,0},{3,1},{4,6},{5,7},{6,4},{7,5},{8,10},{9,11},{10,... | collective-permute-start | bytes 15368 | tf_op jit(solution)/shard_map/ppermute | solution.py:538
  78.1 2.2 %collective-permute-done.50.refs_16_ = f32[5,256]{1,0:T(8,128)S(1)} collective-permute-done((f32[5,256]{1,0:T(8,128)S(1)}, f32[5,256]{1,0:T(8,128)S(1)}, u32[]{:S(2)}, u32[]{:S(2)}) %collective-permute-start.50) | collective-permute-done | bytes 5152 | tf_op jit(solution)/shard_map/ppermute | solution.py:538
  80.3 0.7 collective-permute-done.51.refs_17_
  81.1 1.7 %shard_map.129 = (f32[3,2,16,512]{3,2,1,0:T(8,128)S(1)}, f32[3,2,16,512]{3,2,1,0:T(8,128)S(1)}, f32[3,2,16,512]{3,2,1,0:T(8,128)S(1)}, f32[3,2,16,512]{3,2,1,0:T...) custom-call(f32[3,2,16,512]{3,2,1,0:T(8,128)S(1)} %get-tuple-element.177.refs_0, ...), custom_call_target="tpu_custom_call" | custom-call | flops 1000000000 | bytes 8000000 | tf_op jit(solution)/shard_map/pallas_call | solution.py:24
  82.8 9.8 %all_to_all.5.sums = f32[32,1,128]{2,1,0:T(1,128)S(1)} all-to-all(f32[32,1,128]{2,1,0:T(1,128)S(1)} %get-tuple-element.199), channel_id=1, replica_groups=mesh['res'=8,'grp'=4] {'res','grp'}, dimensions={0} | all-to-all | bytes 32768 | tf_op jit(solution)/shard_map/all_to_all | solution.py:673
  92.6 0.9 shard_map.130
  (106 shorter events, 11.2 us)
Async XLA Ops:
  3.0 7.2 %collective-permute-start.1 = (f32[4,256]{1,0:T(4,128)}, f32[4,256]{1,0:T(4,128)S(1)}, u32[]{:S(2)}, u32[]{:S(2)}) collective-permute-start(f32[4,256]{1,0:T(4,128)} %get-tuple-element.108), channel_id=1, source_target_pairs={{0,2},{1,3},{2,0},{3,1},{4,6},{5,7},{6,4},{7,5},{8,10},{9,11},{10,... | collective-permute-start | bytes 12296 | tf_op jit(solution)/shard_map/ppermute | solution.py:538
  6.1 4.2 %collective-permute-start = (f32[8,512]{1,0:T(8,128)}, f32[8,512]{1,0:T(8,128)S(1)}, u32[]{:S(2)}, u32[]{:S(2)}) collective-permute-start(f32[8,512]{1,0:T(8,128)} %get-tuple-element.107), channel_id=1, source_target_pairs={{0,1},{1,0},{2,3},{3,2},{4,5},{5,4},{6,7},{7,6},{8,9},{9,8},{10,11... | collective-permute-start | bytes 49160 | tf_op jit(solution)/shard_map/ppermute | solution.py:538
  6.1 4.2 %collective-permute-start.2 = (f32[8,512]{1,0:T(8,128)}, f32[8,512]{1,0:T(8,128)S(1)}, u32[]{:S(2)}, u32[]{:S(2)}) collective-permute-start(f32[8,512]{1,0:T(8,128)} %get-tuple-element.109), channel_id=1, source_target_pairs={{0,3},{1,2},{2,1},{3,0},{4,7},{5,6},{6,5},{7,4},{8,11},{9,10},{10,... | collective-permute-start | bytes 49160 | tf_op jit(solution)/shard_map/ppermute | solution.py:538
  8.3 8.5 %collective-permute-start.3 = (f32[3,16,512]{2,1,0:T(8,128)S(1)}, f32[3,16,512]{2,1,0:T(8,128)S(1)}, u32[]{:S(2)}, u32[]{:S(2)}) collective-permute-start(f32[3,16,512]{2,1,0:T(8,128)S(1)} %get-tuple-element.118), channel_id=1, source_target_pairs={{0,4},{4,0},{8,12},{12,8},{16,20},{20,16},{24,28},{28,24},{1,5},{5... | collective-permute-start | bytes 294920 | tf_op jit(solution)/shard_map/ppermute | solution.py:46
  10.3 6.5 %collective-permute-start.4 = (f32[3,16,512]{2,1,0:T(8,128)S(1)}, f32[3,16,512]{2,1,0:T(8,128)S(1)}, u32[]{:S(2)}, u32[]{:S(2)}) collective-permute-start(f32[3,16,512]{2,1,0:T(8,128)S(1)} %get-tuple-element.119), channel_id=1, source_target_pairs={{0,1},{1,0},{2,3},{3,2},{4,8},{5,9},{6,10},{7,11},{8,4},{9,5},{10,... | collective-permute-start | bytes 294920 | tf_op jit(solution)/shard_map/ppermute | solution.py:47
  11.7 4.5 %collective-permute-start.5 = (f32[4,256]{1,0:T(4,128)S(1)}, f32[4,256]{1,0:T(4,128)S(1)}, u32[]{:S(2)}, u32[]{:S(2)}) collective-permute-start(f32[4,256]{1,0:T(4,128)S(1)} %get-tuple-element.120), channel_id=1, source_target_pairs={{0,1},{1,0},{2,3},{3,2},{4,5},{5,4},{6,7},{7,6},{8,9},{9,8},{10,11... | collective-permute-start | bytes 12296 | tf_op jit(solution)/shard_map/ppermute | solution.py:538
  12.2 3.9 %collective-permute-start.6 = (f32[4,256]{1,0:T(4,128)S(1)}, f32[4,256]{1,0:T(4,128)S(1)}, u32[]{:S(2)}, u32[]{:S(2)}) collective-permute-start(f32[4,256]{1,0:T(4,128)S(1)} %get-tuple-element.121), channel_id=1, source_target_pairs={{0,2},{1,3},{2,0},{3,1},{4,6},{5,7},{6,4},{7,5},{8,10},{9,11},{10,... | collective-permute-start | bytes 12296 | tf_op jit(solution)/shard_map/ppermute | solution.py:538
  13.8 3.0 %collective-permute-start.7 = (f32[4,256]{1,0:T(4,128)S(1)}, f32[4,256]{1,0:T(4,128)S(1)}, u32[]{:S(2)}, u32[]{:S(2)}) collective-permute-start(f32[4,256]{1,0:T(4,128)S(1)} %get-tuple-element.122), channel_id=1, source_target_pairs={{0,3},{1,2},{2,1},{3,0},{4,7},{5,6},{6,5},{7,4},{8,11},{9,10},{10,... | collective-permute-start | bytes 12296 | tf_op jit(solution)/shard_map/ppermute | solution.py:538
  18.6 5.3 %collective-permute-start.11 = (f32[4,256]{1,0:T(4,128)S(1)}, f32[4,256]{1,0:T(4,128)S(1)}, u32[]{:S(2)}, u32[]{:S(2)}) collective-permute-start(f32[4,256]{1,0:T(4,128)S(1)} %get-tuple-element.130), channel_id=1, source_target_pairs={{0,2},{1,3},{2,0},{3,1},{4,6},{5,7},{6,4},{7,5},{8,10},{9,11},{10,... | collective-permute-start | bytes 12296 | tf_op jit(solution)/shard_map/ppermute | solution.py:538
  19.6 4.3 %collective-permute-start.10 = (f32[8,512]{1,0:T(8,128)S(1)}, f32[8,512]{1,0:T(8,128)S(1)}, u32[]{:S(2)}, u32[]{:S(2)}) collective-permute-start(f32[8,512]{1,0:T(8,128)S(1)} %get-tuple-element.129), channel_id=1, source_target_pairs={{0,1},{1,0},{2,3},{3,2},{4,5},{5,4},{6,7},{7,6},{8,9},{9,8},{10,11... | collective-permute-start | bytes 49160 | tf_op jit(solution)/shard_map/ppermute | solution.py:538
  19.9 4.0 %collective-permute-start.12 = (f32[8,512]{1,0:T(8,128)S(1)}, f32[8,512]{1,0:T(8,128)S(1)}, u32[]{:S(2)}, u32[]{:S(2)}) collective-permute-start(f32[8,512]{1,0:T(8,128)S(1)} %get-tuple-element.131), channel_id=1, source_target_pairs={{0,3},{1,2},{2,1},{3,0},{4,7},{5,6},{6,5},{7,4},{8,11},{9,10},{10,... | collective-permute-start | bytes 49160 | tf_op jit(solution)/shard_map/ppermute | solution.py:538
  21.2 8.2 %collective-permute-start.8 = (f32[3,16,512]{2,1,0:T(8,128)S(1)}, f32[3,16,512]{2,1,0:T(8,128)S(1)}, u32[]{:S(2)}, u32[]{:S(2)}) collective-permute-start(f32[3,16,512]{2,1,0:T(8,128)S(1)} %get-tuple-element.126), channel_id=1, source_target_pairs={{0,4},{4,0},{8,12},{12,8},{16,20},{20,16},{24,28},{28,24},{1,5},{5... | collective-permute-start | bytes 294920 | tf_op jit(solution)/shard_map/ppermute | solution.py:46
  23.9 5.5 %collective-permute-start.9 = (f32[3,16,512]{2,1,0:T(8,128)S(1)}, f32[3,16,512]{2,1,0:T(8,128)S(1)}, u32[]{:S(2)}, u32[]{:S(2)}) collective-permute-start(f32[3,16,512]{2,1,0:T(8,128)S(1)} %get-tuple-element.127), channel_id=1, source_target_pairs={{0,1},{1,0},{2,3},{3,2},{4,8},{5,9},{6,10},{7,11},{8,4},{9,5},{10,... | collective-permute-start | bytes 294920 | tf_op jit(solution)/shard_map/ppermute | solution.py:47
  25.2 3.6 %collective-permute-start.14 = (f32[4,256]{1,0:T(4,128)S(1)}, f32[4,256]{1,0:T(4,128)S(1)}, u32[]{:S(2)}, u32[]{:S(2)}) collective-permute-start(f32[4,256]{1,0:T(4,128)S(1)} %get-tuple-element.136), channel_id=1, source_target_pairs={{0,2},{1,3},{2,0},{3,1},{4,6},{5,7},{6,4},{7,5},{8,10},{9,11},{10,... | collective-permute-start | bytes 12296 | tf_op jit(solution)/shard_map/ppermute | solution.py:538
  26.4 3.1 %collective-permute-start.15 = (f32[4,256]{1,0:T(4,128)S(1)}, f32[4,256]{1,0:T(4,128)S(1)}, u32[]{:S(2)}, u32[]{:S(2)}) collective-permute-start(f32[4,256]{1,0:T(4,128)S(1)} %get-tuple-element.137), channel_id=1, source_target_pairs={{0,3},{1,2},{2,1},{3,0},{4,7},{5,6},{6,5},{7,4},{8,11},{9,10},{10,... | collective-permute-start | bytes 12296 | tf_op jit(solution)/shard_map/ppermute | solution.py:538
  31.3 4.8 %collective-permute-start.16 = (f32[9,512]{1,0:T(8,128)S(1)}, f32[9,512]{1,0:T(8,128)S(1)}, u32[]{:S(2)}, u32[]{:S(2)}) collective-permute-start(f32[9,512]{1,0:T(8,128)S(1)} %get-tuple-element.140), channel_id=1, source_target_pairs={{0,1},{1,0},{2,3},{3,2},{4,5},{5,4},{6,7},{7,6},{8,9},{9,8},{10,11... | collective-permute-start | bytes 55304 | tf_op jit(solution)/shard_map/ppermute | solution.py:538
  31.4 4.7 %collective-permute-start.18 = (f32[9,512]{1,0:T(8,128)S(1)}, f32[9,512]{1,0:T(8,128)S(1)}, u32[]{:S(2)}, u32[]{:S(2)}) collective-permute-start(f32[9,512]{1,0:T(8,128)S(1)} %get-tuple-element.142), channel_id=1, source_target_pairs={{0,3},{1,2},{2,1},{3,0},{4,7},{5,6},{6,5},{7,4},{8,11},{9,10},{10,... | collective-permute-start | bytes 55304 | tf_op jit(solution)/shard_map/ppermute | solution.py:538
  32.3 3.8 %collective-permute-start.17 = (f32[5,256]{1,0:T(8,128)S(1)}, f32[5,256]{1,0:T(8,128)S(1)}, u32[]{:S(2)}, u32[]{:S(2)}) collective-permute-start(f32[5,256]{1,0:T(8,128)S(1)} %get-tuple-element.141), channel_id=1, source_target_pairs={{0,2},{1,3},{2,0},{3,1},{4,6},{5,7},{6,4},{7,5},{8,10},{9,11},{10,... | collective-permute-start | bytes 15368 | tf_op jit(solution)/shard_map/ppermute | solution.py:538
  33.5 9.0 %collective-permute-start.19 = (f32[3,16,512]{2,1,0:T(8,128)S(1)}, f32[3,16,512]{2,1,0:T(8,128)S(1)}, u32[]{:S(2)}, u32[]{:S(2)}) collective-permute-start(f32[3,16,512]{2,1,0:T(8,128)S(1)} %get-tuple-element.144), channel_id=1, source_target_pairs={{0,4},{4,0},{8,12},{12,8},{16,20},{20,16},{24,28},{28,24},{1,5},{5... | collective-permute-start | bytes 294920 | tf_op jit(solution)/shard_map/ppermute | solution.py:46
  36.1 7.7 %collective-permute-start.20 = (f32[3,16,512]{2,1,0:T(8,128)S(1)}, f32[3,16,512]{2,1,0:T(8,128)S(1)}, u32[]{:S(2)}, u32[]{:S(2)}) collective-permute-start(f32[3,16,512]{2,1,0:T(8,128)S(1)} %get-tuple-element.145), channel_id=1, source_target_pairs={{0,1},{1,0},{2,3},{3,2},{4,8},{5,9},{6,10},{7,11},{8,4},{9,5},{10,... | collective-permute-start | bytes 294920 | tf_op jit(solution)/shard_map/ppermute | solution.py:47
  36.8 2.4 %collective-permute-start.21 = (f32[4,256]{1,0:T(4,128)S(1)}, f32[4,256]{1,0:T(4,128)S(1)}, u32[]{:S(2)}, u32[]{:S(2)}) collective-permute-start(f32[4,256]{1,0:T(4,128)S(1)} %get-tuple-element.146), channel_id=1, source_target_pairs={{0,1},{1,0},{2,3},{3,2},{4,5},{5,4},{6,7},{7,6},{8,9},{9,8},{10,11... | collective-permute-start | bytes 12296 | tf_op jit(solution)/shard_map/ppermute | solution.py:538
  37.4 6.4 %collective-permute-start.22 = (f32[4,256]{1,0:T(4,128)S(1)}, f32[4,256]{1,0:T(4,128)S(1)}, u32[]{:S(2)}, u32[]{:S(2)}) collective-permute-start(f32[4,256]{1,0:T(4,128)S(1)} %get-tuple-element.147), channel_id=1, source_target_pairs={{0,2},{1,3},{2,0},{3,1},{4,6},{5,7},{6,4},{7,5},{8,10},{9,11},{10,... | collective-permute-start | bytes 12296 | tf_op jit(solution)/shard_map/ppermute | solution.py:538
  38.2 5.6 %collective-permute-start.23 = (f32[4,256]{1,0:T(4,128)S(1)}, f32[4,256]{1,0:T(4,128)S(1)}, u32[]{:S(2)}, u32[]{:S(2)}) collective-permute-start(f32[4,256]{1,0:T(4,128)S(1)} %get-tuple-element.148), channel_id=1, source_target_pairs={{0,3},{1,2},{2,1},{3,0},{4,7},{5,6},{6,5},{7,4},{8,11},{9,10},{10,... | collective-permute-start | bytes 12296 | tf_op jit(solution)/shard_map/ppermute | solution.py:538
  39.2 8.5 %collective-permute-start.25 = (f32[1,256]{1,0:T(1,128)S(1)}, f32[1,256]{1,0:T(1,128)S(1)}, u32[]{:S(2)}, u32[]{:S(2)}) collective-permute-start(f32[1,256]{1,0:T(1,128)S(1)} %shard_map.116), channel_id=1, source_target_pairs={{0,28},{1,25},{2,22},{3,19},{4,24},{5,29},{6,18},{7,23},{8,20},{9,... | collective-permute-start | bytes 3080 | tf_op jit(solution)/shard_map/ppermute | solution.py:242
  42.5 5.2 %collective-permute-start.24 = (f32[1,256]{1,0:T(1,128)S(1)}, f32[1,256]{1,0:T(1,128)S(1)}, u32[]{:S(2)}, u32[]{:S(2)}) collective-permute-start(f32[1,256]{1,0:T(1,128)S(1)} %shard_map.115.refs_0_.mine), channel_id=1, source_target_pairs={{0,4},{1,5},{2,10},{3,15},{4,0},{5,1},{6,14},{7,11},{8,12},{9,13},... | collective-permute-start | bytes 3080 | tf_op jit(solution)/shard_map/ppermute | solution.py:242
  45.5 3.7 %collective-permute-start.29 = (f32[4,256]{1,0:T(4,128)S(1)}, f32[4,256]{1,0:T(4,128)S(1)}, u32[]{:S(2)}, u32[]{:S(2)}) collective-permute-start(f32[4,256]{1,0:T(4,128)S(1)} %get-tuple-element.155), channel_id=1, source_target_pairs={{0,2},{1,3},{2,0},{3,1},{4,6},{5,7},{6,4},{7,5},{8,10},{9,11},{10,... | collective-permute-start | bytes 12296 | tf_op jit(solution)/shard_map/ppermute | solution.py:538
  45.8 3.4 %collective-permute-start.28 = (f32[8,512]{1,0:T(8,128)S(1)}, f32[8,512]{1,0:T(8,128)S(1)}, u32[]{:S(2)}, u32[]{:S(2)}) collective-permute-start(f32[8,512]{1,0:T(8,128)S(1)} %get-tuple-element.154), channel_id=1, source_target_pairs={{0,1},{1,0},{2,3},{3,2},{4,5},{5,4},{6,7},{7,6},{8,9},{9,8},{10,11... | collective-permute-start | bytes 49160 | tf_op jit(solution)/shard_map/ppermute | solution.py:538
  45.8 3.4 %collective-permute-start.30 = (f32[8,512]{1,0:T(8,128)S(1)}, f32[8,512]{1,0:T(8,128)S(1)}, u32[]{:S(2)}, u32[]{:S(2)}) collective-permute-start(f32[8,512]{1,0:T(8,128)S(1)} %get-tuple-element.156), channel_id=1, source_target_pairs={{0,3},{1,2},{2,1},{3,0},{4,7},{5,6},{6,5},{7,4},{8,11},{9,10},{10,... | collective-permute-start | bytes 49160 | tf_op jit(solution)/shard_map/ppermute | solution.py:538
  48.1 7.0 %collective-permute-start.26 = (f32[3,16,512]{2,1,0:T(8,128)S(1)}, f32[3,16,512]{2,1,0:T(8,128)S(1)}, u32[]{:S(2)}, u32[]{:S(2)}) collective-permute-start(f32[3,16,512]{2,1,0:T(8,128)S(1)} %get-tuple-element.151), channel_id=1, source_target_pairs={{0,4},{4,0},{8,12},{12,8},{16,20},{20,16},{24,28},{28,24},{1,5},{5... | collective-permute-start | bytes 294920 | tf_op jit(solution)/shard_map/ppermute | solution.py:46
  49.0 6.2 %collective-permute-start.27 = (f32[3,16,512]{2,1,0:T(8,128)S(1)}, f32[3,16,512]{2,1,0:T(8,128)S(1)}, u32[]{:S(2)}, u32[]{:S(2)}) collective-permute-start(f32[3,16,512]{2,1,0:T(8,128)S(1)} %get-tuple-element.152), channel_id=1, source_target_pairs={{0,1},{1,0},{2,3},{3,2},{4,8},{5,9},{6,10},{7,11},{8,4},{9,5},{10,... | collective-permute-start | bytes 294920 | tf_op jit(solution)/shard_map/ppermute | solution.py:47
  50.3 3.7 %collective-permute-start.32 = (f32[5,256]{1,0:T(8,128)S(1)}, f32[5,256]{1,0:T(8,128)S(1)}, u32[]{:S(2)}, u32[]{:S(2)}) collective-permute-start(f32[5,256]{1,0:T(8,128)S(1)} %get-tuple-element.163), channel_id=1, source_target_pairs={{0,2},{1,3},{2,0},{3,1},{4,6},{5,7},{6,4},{7,5},{8,10},{9,11},{10,... | collective-permute-start | bytes 15368 | tf_op jit(solution)/shard_map/ppermute | solution.py:538
  52.0 3.1 %collective-permute-start.33 = (f32[5,256]{1,0:T(8,128)S(1)}, f32[5,256]{1,0:T(8,128)S(1)}, u32[]{:S(2)}, u32[]{:S(2)}) collective-permute-start(f32[5,256]{1,0:T(8,128)S(1)} %get-tuple-element.164), channel_id=1, source_target_pairs={{0,3},{1,2},{2,1},{3,0},{4,7},{5,6},{6,5},{7,4},{8,11},{9,10},{10,... | collective-permute-start | bytes 15368 | tf_op jit(solution)/shard_map/ppermute | solution.py:538
  57.4 4.4 %collective-permute-start.34 = (f32[9,512]{1,0:T(8,128)S(1)}, f32[9,512]{1,0:T(8,128)S(1)}, u32[]{:S(2)}, u32[]{:S(2)}) collective-permute-start(f32[9,512]{1,0:T(8,128)S(1)} %get-tuple-element.167), channel_id=1, source_target_pairs={{0,1},{1,0},{2,3},{3,2},{4,5},{5,4},{6,7},{7,6},{8,9},{9,8},{10,11... | collective-permute-start | bytes 55304 | tf_op jit(solution)/shard_map/ppermute | solution.py:538
  57.6 4.3 %collective-permute-start.36 = (f32[9,512]{1,0:T(8,128)S(1)}, f32[9,512]{1,0:T(8,128)S(1)}, u32[]{:S(2)}, u32[]{:S(2)}) collective-permute-start(f32[9,512]{1,0:T(8,128)S(1)} %get-tuple-element.169), channel_id=1, source_target_pairs={{0,3},{1,2},{2,1},{3,0},{4,7},{5,6},{6,5},{7,4},{8,11},{9,10},{10,... | collective-permute-start | bytes 55304 | tf_op jit(solution)/shard_map/ppermute | solution.py:538
  58.2 3.7 %collective-permute-start.35 = (f32[5,256]{1,0:T(8,128)S(1)}, f32[5,256]{1,0:T(8,128)S(1)}, u32[]{:S(2)}, u32[]{:S(2)}) collective-permute-start(f32[5,256]{1,0:T(8,128)S(1)} %get-tuple-element.168), channel_id=1, source_target_pairs={{0,2},{1,3},{2,0},{3,1},{4,6},{5,7},{6,4},{7,5},{8,10},{9,11},{10,... | collective-permute-start | bytes 15368 | tf_op jit(solution)/shard_map/ppermute | solution.py:538
  59.6 8.6 %collective-permute-start.37 = (f32[3,16,512]{2,1,0:T(8,128)S(1)}, f32[3,16,512]{2,1,0:T(8,128)S(1)}, u32[]{:S(2)}, u32[]{:S(2)}) collective-permute-start(f32[3,16,512]{2,1,0:T(8,128)S(1)} %get-tuple-element.171), channel_id=1, source_target_pairs={{0,4},{4,0},{8,12},{12,8},{16,20},{20,16},{24,28},{28,24},{1,5},{5... | collective-permute-start | bytes 294920 | tf_op jit(solution)/shard_map/ppermute | solution.py:46
  60.7 8.9 %collective-permute-start.38 = (f32[3,16,512]{2,1,0:T(8,128)S(1)}, f32[3,16,512]{2,1,0:T(8,128)S(1)}, u32[]{:S(2)}, u32[]{:S(2)}) collective-permute-start(f32[3,16,512]{2,1,0:T(8,128)S(1)} %get-tuple-element.172), channel_id=1, source_target_pairs={{0,1},{1,0},{2,3},{3,2},{4,8},{5,9},{6,10},{7,11},{8,4},{9,5},{10,... | collective-permute-start | bytes 294920 | tf_op jit(solution)/shard_map/ppermute | solution.py:47
  62.6 7.0 %collective-permute-start.40 = (f32[4,256]{1,0:T(4,128)S(1)}, f32[4,256]{1,0:T(4,128)S(1)}, u32[]{:S(2)}, u32[]{:S(2)}) collective-permute-start(f32[4,256]{1,0:T(4,128)S(1)} %get-tuple-element.174), channel_id=1, source_target_pairs={{0,2},{1,3},{2,0},{3,1},{4,6},{5,7},{6,4},{7,5},{8,10},{9,11},{10,... | collective-permute-start | bytes 12296 | tf_op jit(solution)/shard_map/ppermute | solution.py:538
  64.1 5.5 %collective-permute-start.41 = (f32[4,256]{1,0:T(4,128)S(1)}, f32[4,256]{1,0:T(4,128)S(1)}, u32[]{:S(2)}, u32[]{:S(2)}) collective-permute-start(f32[4,256]{1,0:T(4,128)S(1)} %get-tuple-element.175), channel_id=1, source_target_pairs={{0,3},{1,2},{2,1},{3,0},{4,7},{5,6},{6,5},{7,4},{8,11},{9,10},{10,... | collective-permute-start | bytes 12296 | tf_op jit(solution)/shard_map/ppermute | solution.py:538
  64.9 8.7 %collective-permute-start.43 = (f32[1,256]{1,0:T(1,128)S(1)}, f32[1,256]{1,0:T(1,128)S(1)}, u32[]{:S(2)}, u32[]{:S(2)}) collective-permute-start(f32[1,256]{1,0:T(1,128)S(1)} %shard_map.125), channel_id=1, source_target_pairs={{0,28},{1,25},{2,22},{3,19},{4,24},{5,29},{6,18},{7,23},{8,20},{9,... | collective-permute-start | bytes 3080 | tf_op jit(solution)/shard_map/ppermute | solution.py:242
  68.3 5.3 %collective-permute-start.42 = (f32[1,256]{1,0:T(1,128)S(1)}, f32[1,256]{1,0:T(1,128)S(1)}, u32[]{:S(2)}, u32[]{:S(2)}) collective-permute-start(f32[1,256]{1,0:T(1,128)S(1)} %shard_map.124.refs_0_.mine), channel_id=1, source_target_pairs={{0,4},{1,5},{2,10},{3,15},{4,0},{5,1},{6,14},{7,11},{8,12},{9,13},... | collective-permute-start | bytes 3080 | tf_op jit(solution)/shard_map/ppermute | solution.py:242
  71.4 3.7 %collective-permute-start.47 = (f32[4,256]{1,0:T(4,128)S(1)}, f32[4,256]{1,0:T(4,128)S(1)}, u32[]{:S(2)}, u32[]{:S(2)}) collective-permute-start(f32[4,256]{1,0:T(4,128)S(1)} %get-tuple-element.182), channel_id=1, source_target_pairs={{0,2},{1,3},{2,0},{3,1},{4,6},{5,7},{6,4},{7,5},{8,10},{9,11},{10,... | collective-permute-start | bytes 12296 | tf_op jit(solution)/shard_map/ppermute | solution.py:538
  72.2 2.8 %collective-permute-start.46 = (f32[8,512]{1,0:T(8,128)S(1)}, f32[8,512]{1,0:T(8,128)S(1)}, u32[]{:S(2)}, u32[]{:S(2)}) collective-permute-start(f32[8,512]{1,0:T(8,128)S(1)} %get-tuple-element.181), channel_id=1, source_target_pairs={{0,1},{1,0},{2,3},{3,2},{4,5},{5,4},{6,7},{7,6},{8,9},{9,8},{10,11... | collective-permute-start | bytes 49160 | tf_op jit(solution)/shard_map/ppermute | solution.py:538
  72.2 3.2 %collective-permute-start.48 = (f32[8,512]{1,0:T(8,128)S(1)}, f32[8,512]{1,0:T(8,128)S(1)}, u32[]{:S(2)}, u32[]{:S(2)}) collective-permute-start(f32[8,512]{1,0:T(8,128)S(1)} %get-tuple-element.183), channel_id=1, source_target_pairs={{0,3},{1,2},{2,1},{3,0},{4,7},{5,6},{6,5},{7,4},{8,11},{9,10},{10,... | collective-permute-start | bytes 49160 | tf_op jit(solution)/shard_map/ppermute | solution.py:538
  74.0 7.0 %collective-permute-start.44 = (f32[3,16,512]{2,1,0:T(8,128)S(1)}, f32[3,16,512]{2,1,0:T(8,128)S(1)}, u32[]{:S(2)}, u32[]{:S(2)}) collective-permute-start(f32[3,16,512]{2,1,0:T(8,128)S(1)} %get-tuple-element.178), channel_id=1, source_target_pairs={{0,4},{4,0},{8,12},{12,8},{16,20},{20,16},{24,28},{28,24},{1,5},{5... | collective-permute-start | bytes 294920 | tf_op jit(solution)/shard_map/ppermute | solution.py:46
  74.9 6.2 %collective-permute-start.45 = (f32[3,16,512]{2,1,0:T(8,128)S(1)}, f32[3,16,512]{2,1,0:T(8,128)S(1)}, u32[]{:S(2)}, u32[]{:S(2)}) collective-permute-start(f32[3,16,512]{2,1,0:T(8,128)S(1)} %get-tuple-element.179), channel_id=1, source_target_pairs={{0,1},{1,0},{2,3},{3,2},{4,8},{5,9},{6,10},{7,11},{8,4},{9,5},{10,... | collective-permute-start | bytes 294920 | tf_op jit(solution)/shard_map/ppermute | solution.py:47
  76.7 3.7 %collective-permute-start.50 = (f32[5,256]{1,0:T(8,128)S(1)}, f32[5,256]{1,0:T(8,128)S(1)}, u32[]{:S(2)}, u32[]{:S(2)}) collective-permute-start(f32[5,256]{1,0:T(8,128)S(1)} %get-tuple-element.190), channel_id=1, source_target_pairs={{0,2},{1,3},{2,0},{3,1},{4,6},{5,7},{6,4},{7,5},{8,10},{9,11},{10,... | collective-permute-start | bytes 15368 | tf_op jit(solution)/shard_map/ppermute | solution.py:538
  77.9 3.1 %collective-permute-start.51 = (f32[5,256]{1,0:T(8,128)S(1)}, f32[5,256]{1,0:T(8,128)S(1)}, u32[]{:S(2)}, u32[]{:S(2)}) collective-permute-start(f32[5,256]{1,0:T(8,128)S(1)} %get-tuple-element.191), channel_id=1, source_target_pairs={{0,3},{1,2},{2,1},{3,0},{4,7},{5,6},{6,5},{7,4},{8,11},{9,10},{10,... | collective-permute-start | bytes 15368 | tf_op jit(solution)/shard_map/ppermute | solution.py:538
  (15 other events, 37.4 us)

commit v11 on v10

--- a/solution.py
+++ b/solution.py
@@ -368,7 +368,7 @@
 
 
 def start_kernel(groups, capacity, *refs):
-    given, (column, level, take_out, give_out, *sends) = refs[:6], refs[6:-8]
+    given, (column, packed, take_out, give_out, *sends) = refs[:6], refs[6:-8]
     place, held, sems = refs[-8], refs[-7:-1], refs[-1]
     copies = [
         pltpu.make_async_copy(src, dst, sems.at[n]) for n, (src, dst) in enumerate(zip(given, held))
@@ -382,7 +382,10 @@
     wells, segb = completion.shape
     lanes = lax.broadcasted_iota(jnp.int32, (1, segb), 1)
     column[...] = completion[...] // cells_z
-    level[...] = lax.rem(completion[...], cells_z)
+    level = lax.rem(completion[...], cells_z)
+    write_faces(Planes(vec), [packed.at[pl.ds(n * components, components)] for n in range(2)])
+    packed[2 * components] = jnp.zeros((cells_y, cells_z), F32)
+    packed[2 * components, 0:wells, 0:segb] = level.astype(F32)
     write_place(level, cells_z, place)
     for b in range(wells):
         is_open = (lanes < live[b]).astype(F32)
@@ -392,9 +395,12 @@
     write_messages(vec, place, column, take_out, owner, capacity, sends)
 
 
-def place_kernel(vec, level, place, *faces):
-    write_faces(Planes(vec), faces)
-    write_place(level, vec.shape[3], place)
+def place_kernel(wells, packed, place, *faces):
+    count, segb = faces[0].shape[0], place.shape[1] // wells
+    for n, face in enumerate(faces):
+        face[...] = packed[n * count : (n + 1) * count]
+    level = packed[2 * count, 0:wells, 0:segb].astype(jnp.int32)
+    write_place(level, packed.shape[2], place)
 
 
 class Arrived:
@@ -570,9 +576,15 @@
     b = right_side
     sizes = (groups, capacity)
 
-    column, level, take, give, *sends = call(
+    column, packed, take, give, *sends = call(
         functools.partial(start_kernel, groups, capacity),
-        [(completion.shape, jnp.int32)] * 2 + [(take.shape, F32), (give.shape, F32)] + plain,
+        [
+            (completion.shape, jnp.int32),
+            ((2 * components + 1, cells_y, cells_z), F32),
+            (take.shape, F32),
+            (give.shape, F32),
+        ]
+        + plain,
         [b, completion, live_count, owner, take, give],
         [pl.BlockSpec(memory_space=pltpu.HBM)] * 6,
         scratch=[
@@ -640,9 +652,9 @@
 
     messages = swapped(sends)
     place, *faces = call(
-        place_kernel,
+        functools.partial(place_kernel, wells),
         [((cells_z, wells * segb), BF16)] + face_outs,
-        [b, level],
+        [packed],
         flops=SOLVE_FLOPS,
     )
     halo = exchange(faces)
@@ -655,7 +667,7 @@
         **cost,
     )
     plainly = functools.partial(apply_kernel, sizes)
-    w, *sends = finish(plainly, [field] + plain, part, messages, values, halo, [])
+    w, *sends = finish(plainly, [field] + plain + face_outs, part, messages, values, halo, [])
     t, *sends = apply(
         functools.partial(second_kernel, sizes), [field] + summed + face_outs, w, sends, [b, w]
     )

time: 93.8 us -> 92.9 us (level)
  no operation moved by 1% of the time
where the time goes in v11:
time: 92.9 us; the launch traced here: 92.7 us
  starting transfers between devices  45.9 us (49%)
  Pallas kernels  24 us (26%)
  waiting for transfers between devices  10.8 us (12%)
  blocking collectives  10.1 us (11%)
  between operations  1.02 us (1%)
  local copies, waits for them, and re-layouts  0.99 us (1%)
    ppermute x36, starting transfers between devices, swapped(): lax.ppermute(messages[k], 'grp', [(i, i ^ k) for i in range(groups)])  26.3 us
    pallas_call x27, Pallas kernels, call(): pl.pallas_call(kernel, out_shape=[jax.ShapeDtypeStruct(shape, dtype) for...  24 us
    ppermute x36, waiting for transfers between devices, swapped(): lax.ppermute(messages[k], 'grp', [(i, i ^ k) for i in range(groups)])  10.8 us
    ppermute x6, starting transfers between devices, exchange(): lax.ppermute(faces[0], 'res', first)  10.4 us
    all_to_all x1, blocking collectives, body(): lax.all_to_all(sends[0], ('res', 'grp'), split_axis=0, concat_axis=0, til...  10.1 us
    ppermute x4, starting transfers between devices, share_swap(): return lax.ppermute(row, ('res', 'grp'), pairs)  9.15 us
  transfers between devices with their start and end apart: 52, of which 11 were waited for; matrix products, arithmetic and copies ran while one was open for 0% of the time, Pallas kernels for 14%

profile of v11, /device:TPU:0, one launch (start us, length us, event | category | flops | bytes accessed | tf_op | source)
XLA Modules:
  0.0 92.7 jit_solution(8306072530239958715)
XLA Ops:
  0.6 2.4 %shard_map.104 = (s32[8,256]{1,0:T(8,128)}, f32[7,16,512]{2,1,0:T(8,128)}, f32[3,8,256]{2,1,0:T(8,128)}, f32[3,8,256]{2,1,0:T(8,128)}, f32[4,256]{1,0:T(4,128)},...) custom-call(f32[3,2,16,512]{3,2,1,0:T(8,128)} %refs_18_.5, s32[8,256]{1,0:T(8,128)} %refs_1_.7, s32[8]{0:T(128)} %refs_2_.1, ...), custom_call_target="tpu_custom_call" | custom-call | flops 1000000 | bytes 1000000 | tf_op jit(solution)/shard_map/pallas_call | solution.py:24
  3.0 3.0 %collective-permute-start.1 = (f32[4,256]{1,0:T(4,128)}, f32[4,256]{1,0:T(4,128)S(1)}, u32[]{:S(2)}, u32[]{:S(2)}) collective-permute-start(f32[4,256]{1,0:T(4,128)} %get-tuple-element.107), channel_id=1, source_target_pairs={{0,2},{1,3},{2,0},{3,1},{4,6},{5,7},{6,4},{7,5},{8,10},{9,11},{10,... | collective-permute-start | bytes 12296 | tf_op jit(solution)/shard_map/ppermute | solution.py:544
  6.3 0.9 %copy-done.9 = f32[7,16,512]{2,1,0:T(8,128)S(1)} copy-done((f32[7,16,512]{2,1,0:T(8,128)S(1)}, f32[7,16,512]{2,1,0:T(8,128)}, u32[]{:S(2)}) %copy-start.9) | copy-done | bytes 229400
  7.6 2.0 %collective-permute-start.3 = (f32[3,16,512]{2,1,0:T(8,128)S(1)}, f32[3,16,512]{2,1,0:T(8,128)S(1)}, u32[]{:S(2)}, u32[]{:S(2)}) collective-permute-start(f32[3,16,512]{2,1,0:T(8,128)S(1)} %get-tuple-element.117), channel_id=1, source_target_pairs={{0,4},{4,0},{8,12},{12,8},{16,20},{20,16},{24,28},{28,24},{1,5},{5... | collective-permute-start | bytes 294920 | tf_op jit(solution)/shard_map/ppermute | solution.py:46
  9.7 1.3 %shard_map.106 = (f32[4,256]{1,0:T(4,128)S(1)}, f32[4,256]{1,0:T(4,128)S(1)}, f32[4,256]{1,0:T(4,128)S(1)}, f32[4,256]{1,0:T(4,128)S(1)}, bf16[4,4,256,256]{3,2,...) custom-call(f32[4,4,256,256]{3,2,1,0:T(8,128)S(1)} %bitcast.11, f32[4,256]{1,0:T(4,128)S(1)} %copy-done.7, ...), custom_call_target="tpu_custom_call" | custom-call | flops 5000000000 | bytes 4000000 | tf_op jit(solution)/shard_map/pallas_call | solution.py:24
  11.6 1.5 %collective-permute-start.6 = (f32[4,256]{1,0:T(4,128)S(1)}, f32[4,256]{1,0:T(4,128)S(1)}, u32[]{:S(2)}, u32[]{:S(2)}) collective-permute-start(f32[4,256]{1,0:T(4,128)S(1)} %get-tuple-element.120), channel_id=1, source_target_pairs={{0,2},{1,3},{2,0},{3,1},{4,6},{5,7},{6,4},{7,5},{8,10},{9,11},{10,... | collective-permute-start | bytes 12296 | tf_op jit(solution)/shard_map/ppermute | solution.py:544
  13.2 2.3 %shard_map.107 = (f32[3,2,16,512]{3,2,1,0:T(8,128)S(1)}, f32[3,3,2,16,512]{4,3,2,1,0:T(8,128)S(1)}, bf16[2048,512]{1,0:T(8,128)(2,1)S(1)}, bf16[4,4,256,256]{3,2...) custom-call(f32[3,2,16,512]{3,2,1,0:T(8,128)S(1)} %copy-done.1, f32[6,3,3,2,16,512]{5,4,3,2,1,0:T(8,128)S(1)} %copy-done, ...), custom_call_target="tpu_custom_call" | custom-call | flops 200000000 | bytes 4000000 | tf_op jit(solution)/shard_map/pallas_call | solution.py:24
  16.2 1.8 %shard_map.108 = (f32[3,2,16,512]{3,2,1,0:T(8,128)S(1)}, f32[4,256]{1,0:T(4,128)S(1)}, f32[8,512]{1,0:T(8,128)S(1)}, f32[4,256]{1,0:T(4,128)S(1)}, f32[8,512]{1,...) custom-call(f32[3,2,16,512]{3,2,1,0:T(8,128)S(1)} %get-tuple-element.112.refs_0_, ...), custom_call_target="tpu_custom_call" | custom-call | flops 1000000000 | bytes 8000000 | tf_op jit(solution)/shard_map/pallas_call | solution.py:24
  18.1 1.1 %collective-permute-start.10 = (f32[8,512]{1,0:T(8,128)S(1)}, f32[8,512]{1,0:T(8,128)S(1)}, u32[]{:S(2)}, u32[]{:S(2)}) collective-permute-start(f32[8,512]{1,0:T(8,128)S(1)} %get-tuple-element.129), channel_id=1, source_target_pairs={{0,3},{1,2},{2,1},{3,0},{4,7},{5,6},{6,5},{7,4},{8,11},{9,10},{10,... | collective-permute-start | bytes 49160 | tf_op jit(solution)/shard_map/ppermute | solution.py:544
  19.2 1.0 %collective-permute-start.9 = (f32[4,256]{1,0:T(4,128)S(1)}, f32[4,256]{1,0:T(4,128)S(1)}, u32[]{:S(2)}, u32[]{:S(2)}) collective-permute-start(f32[4,256]{1,0:T(4,128)S(1)} %get-tuple-element.128), channel_id=1, source_target_pairs={{0,2},{1,3},{2,0},{3,1},{4,6},{5,7},{6,4},{7,5},{8,10},{9,11},{10,... | collective-permute-start | bytes 12296 | tf_op jit(solution)/shard_map/ppermute | solution.py:544
  20.2 2.6 %collective-permute-start.11 = (f32[3,16,512]{2,1,0:T(8,128)S(1)}, f32[3,16,512]{2,1,0:T(8,128)S(1)}, u32[]{:S(2)}, u32[]{:S(2)}) collective-permute-start(f32[3,16,512]{2,1,0:T(8,128)S(1)} %get-tuple-element.131), channel_id=1, source_target_pairs={{0,4},{4,0},{8,12},{12,8},{16,20},{20,16},{24,28},{28,24},{1,5},{5... | collective-permute-start | bytes 294920 | tf_op jit(solution)/shard_map/ppermute | solution.py:46
  22.8 0.7 shard_map.109
  24.0 1.2 %collective-permute-start.14 = (f32[4,256]{1,0:T(4,128)S(1)}, f32[4,256]{1,0:T(4,128)S(1)}, u32[]{:S(2)}, u32[]{:S(2)}) collective-permute-start(f32[4,256]{1,0:T(4,128)S(1)} %get-tuple-element.134), channel_id=1, source_target_pairs={{0,2},{1,3},{2,0},{3,1},{4,6},{5,7},{6,4},{7,5},{8,10},{9,11},{10,... | collective-permute-start | bytes 12296 | tf_op jit(solution)/shard_map/ppermute | solution.py:544
  25.9 1.7 %collective-permute-done.14.refs_16_ = f32[4,256]{1,0:T(4,128)S(1)} collective-permute-done((f32[4,256]{1,0:T(4,128)S(1)}, f32[4,256]{1,0:T(4,128)S(1)}, u32[]{:S(2)}, u32[]{:S(2)}) %collective-permute-start.14) | collective-permute-done | bytes 4128 | tf_op jit(solution)/shard_map/ppermute | solution.py:544
  28.3 1.8 %shard_map.111 = (f32[3,2,16,512]{3,2,1,0:T(8,128)S(1)}, f32[5,256]{1,0:T(8,128)S(1)}, f32[9,512]{1,0:T(8,128)S(1)}, f32[5,256]{1,0:T(8,128)S(1)}, f32[9,512]{1,...) custom-call(f32[3,2,16,512]{3,2,1,0:T(8,128)S(1)} %shard_map.110.refs_0_, ...), custom_call_target="tpu_custom_call" | custom-call | flops 1000000000 | bytes 8000000 | tf_op jit(solution)/shard_map/pallas_call | solution.py:24
  30.3 0.9 collective-permute-start.18
  31.2 1.2 %collective-permute-start.17 = (f32[5,256]{1,0:T(8,128)S(1)}, f32[5,256]{1,0:T(8,128)S(1)}, u32[]{:S(2)}, u32[]{:S(2)}) collective-permute-start(f32[5,256]{1,0:T(8,128)S(1)} %get-tuple-element.139), channel_id=1, source_target_pairs={{0,2},{1,3},{2,0},{3,1},{4,6},{5,7},{6,4},{7,5},{8,10},{9,11},{10,... | collective-permute-start | bytes 15368 | tf_op jit(solution)/shard_map/ppermute | solution.py:544
  32.3 2.6 %collective-permute-start.19 = (f32[3,16,512]{2,1,0:T(8,128)S(1)}, f32[3,16,512]{2,1,0:T(8,128)S(1)}, u32[]{:S(2)}, u32[]{:S(2)}) collective-permute-start(f32[3,16,512]{2,1,0:T(8,128)S(1)} %get-tuple-element.142), channel_id=1, source_target_pairs={{0,4},{4,0},{8,12},{12,8},{16,20},{20,16},{24,28},{28,24},{1,5},{5... | collective-permute-start | bytes 294920 | tf_op jit(solution)/shard_map/ppermute | solution.py:46
  34.9 0.7 shard_map.112
  36.2 0.8 collective-permute-start.22
  38.1 3.8 %collective-permute-start.25 = (f32[1,256]{1,0:T(1,128)S(1)}, f32[1,256]{1,0:T(1,128)S(1)}, u32[]{:S(2)}, u32[]{:S(2)}) collective-permute-start(f32[1,256]{1,0:T(1,128)S(1)} %shard_map.116), channel_id=1, source_target_pairs={{0,28},{1,25},{2,22},{3,19},{4,24},{5,29},{6,18},{7,23},{8,20},{9,... | collective-permute-start | bytes 3080 | tf_op jit(solution)/shard_map/ppermute | solution.py:242
  41.9 0.8 collective-permute-start.24
  42.8 1.8 %shard_map.114 = (f32[3,2,16,512]{3,2,1,0:T(8,128)S(1)}, f32[4,256]{1,0:T(4,128)S(1)}, f32[8,512]{1,0:T(8,128)S(1)}, f32[4,256]{1,0:T(4,128)S(1)}, f32[8,512]{1,0:T(8,128)S(1)}) custom-call(f32[3,2,16,512]{3,2,1,0:T(8,128)S(1)} %shard_map.113.refs_0_, f32[6,3,3,2,16,512]{5,4,3,2,1,0:T(8,128)S(1)} %copy-done, ...), custom_call_target="tpu_custom_call" | custom-call | flops 1000000000 | bytes 8000000 | tf_op jit(solution)/shard_map/pallas_call | solution.py:24
  45.2 1.5 %collective-permute-start.30 = (f32[8,512]{1,0:T(8,128)S(1)}, f32[8,512]{1,0:T(8,128)S(1)}, u32[]{:S(2)}, u32[]{:S(2)}) collective-permute-start(f32[8,512]{1,0:T(8,128)S(1)} %get-tuple-element.154), channel_id=1, source_target_pairs={{0,3},{1,2},{2,1},{3,0},{4,7},{5,6},{6,5},{7,4},{8,11},{9,10},{10,... | collective-permute-start | bytes 49160 | tf_op jit(solution)/shard_map/ppermute | solution.py:544
  47.2 1.3 %collective-permute-start.26 = (f32[3,16,512]{2,1,0:T(8,128)S(1)}, f32[3,16,512]{2,1,0:T(8,128)S(1)}, u32[]{:S(2)}, u32[]{:S(2)}) collective-permute-start(f32[3,16,512]{2,1,0:T(8,128)S(1)} %get-tuple-element.149), channel_id=1, source_target_pairs={{0,4},{4,0},{8,12},{12,8},{16,20},{20,16},{24,28},{28,24},{1,5},{5... | collective-permute-start | bytes 294920 | tf_op jit(solution)/shard_map/ppermute | solution.py:46
  48.5 0.7 shard_map.118
  49.8 1.3 %collective-permute-start.32 = (f32[5,256]{1,0:T(8,128)S(1)}, f32[5,256]{1,0:T(8,128)S(1)}, u32[]{:S(2)}, u32[]{:S(2)}) collective-permute-start(f32[5,256]{1,0:T(8,128)S(1)} %get-tuple-element.161), channel_id=1, source_target_pairs={{0,2},{1,3},{2,0},{3,1},{4,6},{5,7},{6,4},{7,5},{8,10},{9,11},{10,... | collective-permute-start | bytes 15368 | tf_op jit(solution)/shard_map/ppermute | solution.py:544
  51.2 2.2 %collective-permute-done.32.refs_16_ = f32[5,256]{1,0:T(8,128)S(1)} collective-permute-done((f32[5,256]{1,0:T(8,128)S(1)}, f32[5,256]{1,0:T(8,128)S(1)}, u32[]{:S(2)}, u32[]{:S(2)}) %collective-permute-start.32) | collective-permute-done | bytes 5152 | tf_op jit(solution)/shard_map/ppermute | solution.py:544
  53.4 0.8 collective-permute-done.33.refs_17_
  54.2 2.2 %shard_map.120 = (f32[3,2,16,512]{3,2,1,0:T(8,128)S(1)}, f32[3,2,16,512]{3,2,1,0:T(8,128)S(1)}, f32[3,2,16,512]{3,2,1,0:T(8,128)S(1)}, f32[3,2,16,512]{3,2,1,0:T...) custom-call(f32[3,2,16,512]{3,2,1,0:T(8,128)S(1)} %get-tuple-element, ...), custom_call_target="tpu_custom_call" | custom-call | flops 1000000000 | bytes 8000000 | tf_op jit(solution)/shard_map/pallas_call | solution.py:24
  56.6 0.8 collective-permute-start.36
  57.4 1.3 %collective-permute-start.35 = (f32[5,256]{1,0:T(8,128)S(1)}, f32[5,256]{1,0:T(8,128)S(1)}, u32[]{:S(2)}, u32[]{:S(2)}) collective-permute-start(f32[5,256]{1,0:T(8,128)S(1)} %get-tuple-element.166), channel_id=1, source_target_pairs={{0,2},{1,3},{2,0},{3,1},{4,6},{5,7},{6,4},{7,5},{8,10},{9,11},{10,... | collective-permute-start | bytes 15368 | tf_op jit(solution)/shard_map/ppermute | solution.py:544
  58.7 1.3 %collective-permute-start.37 = (f32[3,16,512]{2,1,0:T(8,128)S(1)}, f32[3,16,512]{2,1,0:T(8,128)S(1)}, u32[]{:S(2)}, u32[]{:S(2)}) collective-permute-start(f32[3,16,512]{2,1,0:T(8,128)S(1)} %get-tuple-element.169), channel_id=1, source_target_pairs={{0,4},{4,0},{8,12},{12,8},{16,20},{20,16},{24,28},{28,24},{1,5},{5... | collective-permute-start | bytes 294920 | tf_op jit(solution)/shard_map/ppermute | solution.py:46
  60.0 1.0 %collective-permute-done.35.refs_2_.refs_12_.refs_4_.refs_3_ = f32[5,256]{1,0:T(8,128)S(1)} collective-permute-done((f32[5,256]{1,0:T(8,128)S(1)}, f32[5,256]{1,0:T(8,128)S(1)}, u32[]{:S(2)}, u32[]{:S(2)}) %collective-permute-start.35) | collective-permute-done | bytes 5152 | tf_op jit(solution)/shard_map/ppermute | solution.py:544
  61.0 0.7 shard_map.121
  61.8 1.4 %collective-permute-start.40 = (f32[4,256]{1,0:T(4,128)S(1)}, f32[4,256]{1,0:T(4,128)S(1)}, u32[]{:S(2)}, u32[]{:S(2)}) collective-permute-start(f32[4,256]{1,0:T(4,128)S(1)} %get-tuple-element.172), channel_id=1, source_target_pairs={{0,2},{1,3},{2,0},{3,1},{4,6},{5,7},{6,4},{7,5},{8,10},{9,11},{10,... | collective-permute-start | bytes 12296 | tf_op jit(solution)/shard_map/ppermute | solution.py:544
  64.1 3.0 %collective-permute-start.43 = (f32[1,256]{1,0:T(1,128)S(1)}, f32[1,256]{1,0:T(1,128)S(1)}, u32[]{:S(2)}, u32[]{:S(2)}) collective-permute-start(f32[1,256]{1,0:T(1,128)S(1)} %shard_map.125), channel_id=1, source_target_pairs={{0,28},{1,25},{2,22},{3,19},{4,24},{5,29},{6,18},{7,23},{8,20},{9,... | collective-permute-start | bytes 3080 | tf_op jit(solution)/shard_map/ppermute | solution.py:242
  67.1 1.5 %collective-permute-start.42 = (f32[1,256]{1,0:T(1,128)S(1)}, f32[1,256]{1,0:T(1,128)S(1)}, u32[]{:S(2)}, u32[]{:S(2)}) collective-permute-start(f32[1,256]{1,0:T(1,128)S(1)} %shard_map.124.refs_0_.mine), channel_id=1, source_target_pairs={{0,4},{1,5},{2,10},{3,15},{4,0},{5,1},{6,14},{7,11},{8,12},{9,13},... | collective-permute-start | bytes 3080 | tf_op jit(solution)/shard_map/ppermute | solution.py:242
  68.6 1.8 %shard_map.123 = (f32[3,2,16,512]{3,2,1,0:T(8,128)S(1)}, f32[4,256]{1,0:T(4,128)S(1)}, f32[8,512]{1,0:T(8,128)S(1)}, f32[4,256]{1,0:T(4,128)S(1)}, f32[8,512]{1,0:T(8,128)S(1)}) custom-call(f32[3,2,16,512]{3,2,1,0:T(8,128)S(1)} %shard_map.122.refs_0_, f32[6,3,3,2,16,512]{5,4,3,2,1,0:T(8,128)S(1)} %copy-done, ...), custom_call_target="tpu_custom_call" | custom-call | flops 1000000000 | bytes 8000000 | tf_op jit(solution)/shard_map/pallas_call | solution.py:24
  70.4 0.7 collective-permute-start.47
  71.1 1.5 %collective-permute-start.48 = (f32[8,512]{1,0:T(8,128)S(1)}, f32[8,512]{1,0:T(8,128)S(1)}, u32[]{:S(2)}, u32[]{:S(2)}) collective-permute-start(f32[8,512]{1,0:T(8,128)S(1)} %get-tuple-element.181), channel_id=1, source_target_pairs={{0,3},{1,2},{2,1},{3,0},{4,7},{5,6},{6,5},{7,4},{8,11},{9,10},{10,... | collective-permute-start | bytes 49160 | tf_op jit(solution)/shard_map/ppermute | solution.py:544
  73.0 0.7 collective-permute-start.44
  75.5 1.4 %collective-permute-start.50 = (f32[5,256]{1,0:T(8,128)S(1)}, f32[5,256]{1,0:T(8,128)S(1)}, u32[]{:S(2)}, u32[]{:S(2)}) collective-permute-start(f32[5,256]{1,0:T(8,128)S(1)} %get-tuple-element.188), channel_id=1, source_target_pairs={{0,2},{1,3},{2,0},{3,1},{4,6},{5,7},{6,4},{7,5},{8,10},{9,11},{10,... | collective-permute-start | bytes 15368 | tf_op jit(solution)/shard_map/ppermute | solution.py:544
  76.9 2.2 %collective-permute-done.50.refs_16_ = f32[5,256]{1,0:T(8,128)S(1)} collective-permute-done((f32[5,256]{1,0:T(8,128)S(1)}, f32[5,256]{1,0:T(8,128)S(1)}, u32[]{:S(2)}, u32[]{:S(2)}) %collective-permute-start.50) | collective-permute-done | bytes 5152 | tf_op jit(solution)/shard_map/ppermute | solution.py:544
  79.2 0.9 collective-permute-done.51.refs_17_
  80.0 1.7 %shard_map.129 = (f32[3,2,16,512]{3,2,1,0:T(8,128)S(1)}, f32[3,2,16,512]{3,2,1,0:T(8,128)S(1)}, f32[3,2,16,512]{3,2,1,0:T(8,128)S(1)}, f32[3,2,16,512]{3,2,1,0:T...) custom-call(f32[3,2,16,512]{3,2,1,0:T(8,128)S(1)} %get-tuple-element.175.refs_0, ...), custom_call_target="tpu_custom_call" | custom-call | flops 1000000000 | bytes 8000000 | tf_op jit(solution)/shard_map/pallas_call | solution.py:24
  81.8 10.1 %all_to_all.5.sums = f32[32,1,128]{2,1,0:T(1,128)S(1)} all-to-all(f32[32,1,128]{2,1,0:T(1,128)S(1)} %get-tuple-element.197), channel_id=1, replica_groups=mesh['res'=8,'grp'=4] {'res','grp'}, dimensions={0} | all-to-all | bytes 32768 | tf_op jit(solution)/shard_map/all_to_all | solution.py:685
  91.8 0.9 %shard_map.130 = (f32[3,2,16,512]{3,2,1,0:T(8,128)}, f32[3,2,16,512]{3,2,1,0:T(8,128)}) custom-call(f32[32,1,128]{2,1,0:T(1,128)S(1)} %all_to_all.5.sums, f32[3,2,16,512]{3,2,1,0:T(8,128)S(1)} %get-tuple-element.198.r, f32[3,2,16,512]{3,2,1,0:T(8,128)S(1)} %get-tuple-element.199.w, f32[3,2,16,512]{3,2,1,0:T(8,128)S(1)} %get-tuple-element.200.s, ...), custom_call_target="tpu_custom_call" | custom-call | flops 1000000 | bytes 1000000 | tf_op jit(solution)/shard_map/pallas_call | solution.py:24
  (104 shorter events, 11.0 us)
Async XLA Ops:
  3.0 6.6 %collective-permute-start.1 = (f32[4,256]{1,0:T(4,128)}, f32[4,256]{1,0:T(4,128)S(1)}, u32[]{:S(2)}, u32[]{:S(2)}) collective-permute-start(f32[4,256]{1,0:T(4,128)} %get-tuple-element.107), channel_id=1, source_target_pairs={{0,2},{1,3},{2,0},{3,1},{4,6},{5,7},{6,4},{7,5},{8,10},{9,11},{10,... | collective-permute-start | bytes 12296 | tf_op jit(solution)/shard_map/ppermute | solution.py:544
  6.1 3.5 %collective-permute-start = (f32[8,512]{1,0:T(8,128)}, f32[8,512]{1,0:T(8,128)S(1)}, u32[]{:S(2)}, u32[]{:S(2)}) collective-permute-start(f32[8,512]{1,0:T(8,128)} %get-tuple-element.106), channel_id=1, source_target_pairs={{0,1},{1,0},{2,3},{3,2},{4,5},{5,4},{6,7},{7,6},{8,9},{9,8},{10,11... | collective-permute-start | bytes 49160 | tf_op jit(solution)/shard_map/ppermute | solution.py:544
  6.1 3.5 %collective-permute-start.2 = (f32[8,512]{1,0:T(8,128)}, f32[8,512]{1,0:T(8,128)S(1)}, u32[]{:S(2)}, u32[]{:S(2)}) collective-permute-start(f32[8,512]{1,0:T(8,128)} %get-tuple-element.108), channel_id=1, source_target_pairs={{0,3},{1,2},{2,1},{3,0},{4,7},{5,6},{6,5},{7,4},{8,11},{9,10},{10,... | collective-permute-start | bytes 49160 | tf_op jit(solution)/shard_map/ppermute | solution.py:544
  7.6 8.5 %collective-permute-start.3 = (f32[3,16,512]{2,1,0:T(8,128)S(1)}, f32[3,16,512]{2,1,0:T(8,128)S(1)}, u32[]{:S(2)}, u32[]{:S(2)}) collective-permute-start(f32[3,16,512]{2,1,0:T(8,128)S(1)} %get-tuple-element.117), channel_id=1, source_target_pairs={{0,4},{4,0},{8,12},{12,8},{16,20},{20,16},{24,28},{28,24},{1,5},{5... | collective-permute-start | bytes 294920 | tf_op jit(solution)/shard_map/ppermute | solution.py:46
  9.6 6.5 %collective-permute-start.4 = (f32[3,16,512]{2,1,0:T(8,128)S(1)}, f32[3,16,512]{2,1,0:T(8,128)S(1)}, u32[]{:S(2)}, u32[]{:S(2)}) collective-permute-start(f32[3,16,512]{2,1,0:T(8,128)S(1)} %get-tuple-element.118), channel_id=1, source_target_pairs={{0,1},{1,0},{2,3},{3,2},{4,8},{5,9},{6,10},{7,11},{8,4},{9,5},{10,... | collective-permute-start | bytes 294920 | tf_op jit(solution)/shard_map/ppermute | solution.py:47
  11.0 4.5 %collective-permute-start.5 = (f32[4,256]{1,0:T(4,128)S(1)}, f32[4,256]{1,0:T(4,128)S(1)}, u32[]{:S(2)}, u32[]{:S(2)}) collective-permute-start(f32[4,256]{1,0:T(4,128)S(1)} %get-tuple-element.119), channel_id=1, source_target_pairs={{0,1},{1,0},{2,3},{3,2},{4,5},{5,4},{6,7},{7,6},{8,9},{9,8},{10,11... | collective-permute-start | bytes 12296 | tf_op jit(solution)/shard_map/ppermute | solution.py:544
  11.6 3.9 %collective-permute-start.6 = (f32[4,256]{1,0:T(4,128)S(1)}, f32[4,256]{1,0:T(4,128)S(1)}, u32[]{:S(2)}, u32[]{:S(2)}) collective-permute-start(f32[4,256]{1,0:T(4,128)S(1)} %get-tuple-element.120), channel_id=1, source_target_pairs={{0,2},{1,3},{2,0},{3,1},{4,6},{5,7},{6,4},{7,5},{8,10},{9,11},{10,... | collective-permute-start | bytes 12296 | tf_op jit(solution)/shard_map/ppermute | solution.py:544
  13.1 3.0 %collective-permute-start.7 = (f32[4,256]{1,0:T(4,128)S(1)}, f32[4,256]{1,0:T(4,128)S(1)}, u32[]{:S(2)}, u32[]{:S(2)}) collective-permute-start(f32[4,256]{1,0:T(4,128)S(1)} %get-tuple-element.121), channel_id=1, source_target_pairs={{0,3},{1,2},{2,1},{3,0},{4,7},{5,6},{6,5},{7,4},{8,11},{9,10},{10,... | collective-permute-start | bytes 12296 | tf_op jit(solution)/shard_map/ppermute | solution.py:544
  17.9 4.9 %collective-permute-start.8 = (f32[8,512]{1,0:T(8,128)S(1)}, f32[8,512]{1,0:T(8,128)S(1)}, u32[]{:S(2)}, u32[]{:S(2)}) collective-permute-start(f32[8,512]{1,0:T(8,128)S(1)} %get-tuple-element.127), channel_id=1, source_target_pairs={{0,1},{1,0},{2,3},{3,2},{4,5},{5,4},{6,7},{7,6},{8,9},{9,8},{10,11... | collective-permute-start | bytes 49160 | tf_op jit(solution)/shard_map/ppermute | solution.py:544
  18.1 4.7 %collective-permute-start.10 = (f32[8,512]{1,0:T(8,128)S(1)}, f32[8,512]{1,0:T(8,128)S(1)}, u32[]{:S(2)}, u32[]{:S(2)}) collective-permute-start(f32[8,512]{1,0:T(8,128)S(1)} %get-tuple-element.129), channel_id=1, source_target_pairs={{0,3},{1,2},{2,1},{3,0},{4,7},{5,6},{6,5},{7,4},{8,11},{9,10},{10,... | collective-permute-start | bytes 49160 | tf_op jit(solution)/shard_map/ppermute | solution.py:544
  19.2 3.6 %collective-permute-start.9 = (f32[4,256]{1,0:T(4,128)S(1)}, f32[4,256]{1,0:T(4,128)S(1)}, u32[]{:S(2)}, u32[]{:S(2)}) collective-permute-start(f32[4,256]{1,0:T(4,128)S(1)} %get-tuple-element.128), channel_id=1, source_target_pairs={{0,2},{1,3},{2,0},{3,1},{4,6},{5,7},{6,4},{7,5},{8,10},{9,11},{10,... | collective-permute-start | bytes 12296 | tf_op jit(solution)/shard_map/ppermute | solution.py:544
  20.2 8.1 %collective-permute-start.11 = (f32[3,16,512]{2,1,0:T(8,128)S(1)}, f32[3,16,512]{2,1,0:T(8,128)S(1)}, u32[]{:S(2)}, u32[]{:S(2)}) collective-permute-start(f32[3,16,512]{2,1,0:T(8,128)S(1)} %get-tuple-element.131), channel_id=1, source_target_pairs={{0,4},{4,0},{8,12},{12,8},{16,20},{20,16},{24,28},{28,24},{1,5},{5... | collective-permute-start | bytes 294920 | tf_op jit(solution)/shard_map/ppermute | solution.py:46
  22.7 5.5 %collective-permute-start.12 = (f32[3,16,512]{2,1,0:T(8,128)S(1)}, f32[3,16,512]{2,1,0:T(8,128)S(1)}, u32[]{:S(2)}, u32[]{:S(2)}) collective-permute-start(f32[3,16,512]{2,1,0:T(8,128)S(1)} %get-tuple-element.132), channel_id=1, source_target_pairs={{0,1},{1,0},{2,3},{3,2},{4,8},{5,9},{6,10},{7,11},{8,4},{9,5},{10,... | collective-permute-start | bytes 294920 | tf_op jit(solution)/shard_map/ppermute | solution.py:47
  24.0 3.6 %collective-permute-start.14 = (f32[4,256]{1,0:T(4,128)S(1)}, f32[4,256]{1,0:T(4,128)S(1)}, u32[]{:S(2)}, u32[]{:S(2)}) collective-permute-start(f32[4,256]{1,0:T(4,128)S(1)} %get-tuple-element.134), channel_id=1, source_target_pairs={{0,2},{1,3},{2,0},{3,1},{4,6},{5,7},{6,4},{7,5},{8,10},{9,11},{10,... | collective-permute-start | bytes 12296 | tf_op jit(solution)/shard_map/ppermute | solution.py:544
  25.2 3.1 %collective-permute-start.15 = (f32[4,256]{1,0:T(4,128)S(1)}, f32[4,256]{1,0:T(4,128)S(1)}, u32[]{:S(2)}, u32[]{:S(2)}) collective-permute-start(f32[4,256]{1,0:T(4,128)S(1)} %get-tuple-element.135), channel_id=1, source_target_pairs={{0,3},{1,2},{2,1},{3,0},{4,7},{5,6},{6,5},{7,4},{8,11},{9,10},{10,... | collective-permute-start | bytes 12296 | tf_op jit(solution)/shard_map/ppermute | solution.py:544
  30.1 4.8 %collective-permute-start.16 = (f32[9,512]{1,0:T(8,128)S(1)}, f32[9,512]{1,0:T(8,128)S(1)}, u32[]{:S(2)}, u32[]{:S(2)}) collective-permute-start(f32[9,512]{1,0:T(8,128)S(1)} %get-tuple-element.138), channel_id=1, source_target_pairs={{0,1},{1,0},{2,3},{3,2},{4,5},{5,4},{6,7},{7,6},{8,9},{9,8},{10,11... | collective-permute-start | bytes 55304 | tf_op jit(solution)/shard_map/ppermute | solution.py:544
  30.3 4.7 %collective-permute-start.18 = (f32[9,512]{1,0:T(8,128)S(1)}, f32[9,512]{1,0:T(8,128)S(1)}, u32[]{:S(2)}, u32[]{:S(2)}) collective-permute-start(f32[9,512]{1,0:T(8,128)S(1)} %get-tuple-element.140), channel_id=1, source_target_pairs={{0,3},{1,2},{2,1},{3,0},{4,7},{5,6},{6,5},{7,4},{8,11},{9,10},{10,... | collective-permute-start | bytes 55304 | tf_op jit(solution)/shard_map/ppermute | solution.py:544
  31.2 3.8 %collective-permute-start.17 = (f32[5,256]{1,0:T(8,128)S(1)}, f32[5,256]{1,0:T(8,128)S(1)}, u32[]{:S(2)}, u32[]{:S(2)}) collective-permute-start(f32[5,256]{1,0:T(8,128)S(1)} %get-tuple-element.139), channel_id=1, source_target_pairs={{0,2},{1,3},{2,0},{3,1},{4,6},{5,7},{6,4},{7,5},{8,10},{9,11},{10,... | collective-permute-start | bytes 15368 | tf_op jit(solution)/shard_map/ppermute | solution.py:544
  32.3 9.6 %collective-permute-start.19 = (f32[3,16,512]{2,1,0:T(8,128)S(1)}, f32[3,16,512]{2,1,0:T(8,128)S(1)}, u32[]{:S(2)}, u32[]{:S(2)}) collective-permute-start(f32[3,16,512]{2,1,0:T(8,128)S(1)} %get-tuple-element.142), channel_id=1, source_target_pairs={{0,4},{4,0},{8,12},{12,8},{16,20},{20,16},{24,28},{28,24},{1,5},{5... | collective-permute-start | bytes 294920 | tf_op jit(solution)/shard_map/ppermute | solution.py:46
  34.9 7.8 %collective-permute-start.20 = (f32[3,16,512]{2,1,0:T(8,128)S(1)}, f32[3,16,512]{2,1,0:T(8,128)S(1)}, u32[]{:S(2)}, u32[]{:S(2)}) collective-permute-start(f32[3,16,512]{2,1,0:T(8,128)S(1)} %get-tuple-element.143), channel_id=1, source_target_pairs={{0,1},{1,0},{2,3},{3,2},{4,8},{5,9},{6,10},{7,11},{8,4},{9,5},{10,... | collective-permute-start | bytes 294920 | tf_op jit(solution)/shard_map/ppermute | solution.py:47
  35.6 2.4 %collective-permute-start.21 = (f32[4,256]{1,0:T(4,128)S(1)}, f32[4,256]{1,0:T(4,128)S(1)}, u32[]{:S(2)}, u32[]{:S(2)}) collective-permute-start(f32[4,256]{1,0:T(4,128)S(1)} %get-tuple-element.144), channel_id=1, source_target_pairs={{0,1},{1,0},{2,3},{3,2},{4,5},{5,4},{6,7},{7,6},{8,9},{9,8},{10,11... | collective-permute-start | bytes 12296 | tf_op jit(solution)/shard_map/ppermute | solution.py:544
  36.2 6.6 %collective-permute-start.22 = (f32[4,256]{1,0:T(4,128)S(1)}, f32[4,256]{1,0:T(4,128)S(1)}, u32[]{:S(2)}, u32[]{:S(2)}) collective-permute-start(f32[4,256]{1,0:T(4,128)S(1)} %get-tuple-element.145), channel_id=1, source_target_pairs={{0,2},{1,3},{2,0},{3,1},{4,6},{5,7},{6,4},{7,5},{8,10},{9,11},{10,... | collective-permute-start | bytes 12296 | tf_op jit(solution)/shard_map/ppermute | solution.py:544
  37.0 5.7 %collective-permute-start.23 = (f32[4,256]{1,0:T(4,128)S(1)}, f32[4,256]{1,0:T(4,128)S(1)}, u32[]{:S(2)}, u32[]{:S(2)}) collective-permute-start(f32[4,256]{1,0:T(4,128)S(1)} %get-tuple-element.146), channel_id=1, source_target_pairs={{0,3},{1,2},{2,1},{3,0},{4,7},{5,6},{6,5},{7,4},{8,11},{9,10},{10,... | collective-permute-start | bytes 12296 | tf_op jit(solution)/shard_map/ppermute | solution.py:544
  38.1 8.7 %collective-permute-start.25 = (f32[1,256]{1,0:T(1,128)S(1)}, f32[1,256]{1,0:T(1,128)S(1)}, u32[]{:S(2)}, u32[]{:S(2)}) collective-permute-start(f32[1,256]{1,0:T(1,128)S(1)} %shard_map.116), channel_id=1, source_target_pairs={{0,28},{1,25},{2,22},{3,19},{4,24},{5,29},{6,18},{7,23},{8,20},{9,... | collective-permute-start | bytes 3080 | tf_op jit(solution)/shard_map/ppermute | solution.py:242
  41.9 4.8 %collective-permute-start.24 = (f32[1,256]{1,0:T(1,128)S(1)}, f32[1,256]{1,0:T(1,128)S(1)}, u32[]{:S(2)}, u32[]{:S(2)}) collective-permute-start(f32[1,256]{1,0:T(1,128)S(1)} %shard_map.115.refs_0_.mine), channel_id=1, source_target_pairs={{0,4},{1,5},{2,10},{3,15},{4,0},{5,1},{6,14},{7,11},{8,12},{9,13},... | collective-permute-start | bytes 3080 | tf_op jit(solution)/shard_map/ppermute | solution.py:242
  44.5 4.0 %collective-permute-start.29 = (f32[4,256]{1,0:T(4,128)S(1)}, f32[4,256]{1,0:T(4,128)S(1)}, u32[]{:S(2)}, u32[]{:S(2)}) collective-permute-start(f32[4,256]{1,0:T(4,128)S(1)} %get-tuple-element.153), channel_id=1, source_target_pairs={{0,2},{1,3},{2,0},{3,1},{4,6},{5,7},{6,4},{7,5},{8,10},{9,11},{10,... | collective-permute-start | bytes 12296 | tf_op jit(solution)/shard_map/ppermute | solution.py:544
  45.2 3.3 %collective-permute-start.28 = (f32[8,512]{1,0:T(8,128)S(1)}, f32[8,512]{1,0:T(8,128)S(1)}, u32[]{:S(2)}, u32[]{:S(2)}) collective-permute-start(f32[8,512]{1,0:T(8,128)S(1)} %get-tuple-element.152), channel_id=1, source_target_pairs={{0,1},{1,0},{2,3},{3,2},{4,5},{5,4},{6,7},{7,6},{8,9},{9,8},{10,11... | collective-permute-start | bytes 49160 | tf_op jit(solution)/shard_map/ppermute | solution.py:544
  45.2 3.3 %collective-permute-start.30 = (f32[8,512]{1,0:T(8,128)S(1)}, f32[8,512]{1,0:T(8,128)S(1)}, u32[]{:S(2)}, u32[]{:S(2)}) collective-permute-start(f32[8,512]{1,0:T(8,128)S(1)} %get-tuple-element.154), channel_id=1, source_target_pairs={{0,3},{1,2},{2,1},{3,0},{4,7},{5,6},{6,5},{7,4},{8,11},{9,10},{10,... | collective-permute-start | bytes 49160 | tf_op jit(solution)/shard_map/ppermute | solution.py:544
  47.2 7.0 %collective-permute-start.26 = (f32[3,16,512]{2,1,0:T(8,128)S(1)}, f32[3,16,512]{2,1,0:T(8,128)S(1)}, u32[]{:S(2)}, u32[]{:S(2)}) collective-permute-start(f32[3,16,512]{2,1,0:T(8,128)S(1)} %get-tuple-element.149), channel_id=1, source_target_pairs={{0,4},{4,0},{8,12},{12,8},{16,20},{20,16},{24,28},{28,24},{1,5},{5... | collective-permute-start | bytes 294920 | tf_op jit(solution)/shard_map/ppermute | solution.py:46
  48.5 5.7 %collective-permute-start.27 = (f32[3,16,512]{2,1,0:T(8,128)S(1)}, f32[3,16,512]{2,1,0:T(8,128)S(1)}, u32[]{:S(2)}, u32[]{:S(2)}) collective-permute-start(f32[3,16,512]{2,1,0:T(8,128)S(1)} %get-tuple-element.150), channel_id=1, source_target_pairs={{0,1},{1,0},{2,3},{3,2},{4,8},{5,9},{6,10},{7,11},{8,4},{9,5},{10,... | collective-permute-start | bytes 294920 | tf_op jit(solution)/shard_map/ppermute | solution.py:47
  49.8 3.7 %collective-permute-start.32 = (f32[5,256]{1,0:T(8,128)S(1)}, f32[5,256]{1,0:T(8,128)S(1)}, u32[]{:S(2)}, u32[]{:S(2)}) collective-permute-start(f32[5,256]{1,0:T(8,128)S(1)} %get-tuple-element.161), channel_id=1, source_target_pairs={{0,2},{1,3},{2,0},{3,1},{4,6},{5,7},{6,4},{7,5},{8,10},{9,11},{10,... | collective-permute-start | bytes 15368 | tf_op jit(solution)/shard_map/ppermute | solution.py:544
  51.1 3.1 %collective-permute-start.33 = (f32[5,256]{1,0:T(8,128)S(1)}, f32[5,256]{1,0:T(8,128)S(1)}, u32[]{:S(2)}, u32[]{:S(2)}) collective-permute-start(f32[5,256]{1,0:T(8,128)S(1)} %get-tuple-element.162), channel_id=1, source_target_pairs={{0,3},{1,2},{2,1},{3,0},{4,7},{5,6},{6,5},{7,4},{8,11},{9,10},{10,... | collective-permute-start | bytes 15368 | tf_op jit(solution)/shard_map/ppermute | solution.py:544
  56.4 4.6 %collective-permute-start.34 = (f32[9,512]{1,0:T(8,128)S(1)}, f32[9,512]{1,0:T(8,128)S(1)}, u32[]{:S(2)}, u32[]{:S(2)}) collective-permute-start(f32[9,512]{1,0:T(8,128)S(1)} %get-tuple-element.165), channel_id=1, source_target_pairs={{0,1},{1,0},{2,3},{3,2},{4,5},{5,4},{6,7},{7,6},{8,9},{9,8},{10,11... | collective-permute-start | bytes 55304 | tf_op jit(solution)/shard_map/ppermute | solution.py:544
  56.6 4.4 %collective-permute-start.36 = (f32[9,512]{1,0:T(8,128)S(1)}, f32[9,512]{1,0:T(8,128)S(1)}, u32[]{:S(2)}, u32[]{:S(2)}) collective-permute-start(f32[9,512]{1,0:T(8,128)S(1)} %get-tuple-element.167), channel_id=1, source_target_pairs={{0,3},{1,2},{2,1},{3,0},{4,7},{5,6},{6,5},{7,4},{8,11},{9,10},{10,... | collective-permute-start | bytes 55304 | tf_op jit(solution)/shard_map/ppermute | solution.py:544
  57.4 3.7 %collective-permute-start.35 = (f32[5,256]{1,0:T(8,128)S(1)}, f32[5,256]{1,0:T(8,128)S(1)}, u32[]{:S(2)}, u32[]{:S(2)}) collective-permute-start(f32[5,256]{1,0:T(8,128)S(1)} %get-tuple-element.166), channel_id=1, source_target_pairs={{0,2},{1,3},{2,0},{3,1},{4,6},{5,7},{6,4},{7,5},{8,10},{9,11},{10,... | collective-permute-start | bytes 15368 | tf_op jit(solution)/shard_map/ppermute | solution.py:544
  58.7 8.5 %collective-permute-start.37 = (f32[3,16,512]{2,1,0:T(8,128)S(1)}, f32[3,16,512]{2,1,0:T(8,128)S(1)}, u32[]{:S(2)}, u32[]{:S(2)}) collective-permute-start(f32[3,16,512]{2,1,0:T(8,128)S(1)} %get-tuple-element.169), channel_id=1, source_target_pairs={{0,4},{4,0},{8,12},{12,8},{16,20},{20,16},{24,28},{28,24},{1,5},{5... | collective-permute-start | bytes 294920 | tf_op jit(solution)/shard_map/ppermute | solution.py:46
  60.0 8.6 %collective-permute-start.38 = (f32[3,16,512]{2,1,0:T(8,128)S(1)}, f32[3,16,512]{2,1,0:T(8,128)S(1)}, u32[]{:S(2)}, u32[]{:S(2)}) collective-permute-start(f32[3,16,512]{2,1,0:T(8,128)S(1)} %get-tuple-element.170), channel_id=1, source_target_pairs={{0,1},{1,0},{2,3},{3,2},{4,8},{5,9},{6,10},{7,11},{8,4},{9,5},{10,... | collective-permute-start | bytes 294920 | tf_op jit(solution)/shard_map/ppermute | solution.py:47
  61.8 6.8 %collective-permute-start.40 = (f32[4,256]{1,0:T(4,128)S(1)}, f32[4,256]{1,0:T(4,128)S(1)}, u32[]{:S(2)}, u32[]{:S(2)}) collective-permute-start(f32[4,256]{1,0:T(4,128)S(1)} %get-tuple-element.172), channel_id=1, source_target_pairs={{0,2},{1,3},{2,0},{3,1},{4,6},{5,7},{6,4},{7,5},{8,10},{9,11},{10,... | collective-permute-start | bytes 12296 | tf_op jit(solution)/shard_map/ppermute | solution.py:544
  63.1 5.4 %collective-permute-start.41 = (f32[4,256]{1,0:T(4,128)S(1)}, f32[4,256]{1,0:T(4,128)S(1)}, u32[]{:S(2)}, u32[]{:S(2)}) collective-permute-start(f32[4,256]{1,0:T(4,128)S(1)} %get-tuple-element.173), channel_id=1, source_target_pairs={{0,3},{1,2},{2,1},{3,0},{4,7},{5,6},{6,5},{7,4},{8,11},{9,10},{10,... | collective-permute-start | bytes 12296 | tf_op jit(solution)/shard_map/ppermute | solution.py:544
  64.1 8.5 %collective-permute-start.43 = (f32[1,256]{1,0:T(1,128)S(1)}, f32[1,256]{1,0:T(1,128)S(1)}, u32[]{:S(2)}, u32[]{:S(2)}) collective-permute-start(f32[1,256]{1,0:T(1,128)S(1)} %shard_map.125), channel_id=1, source_target_pairs={{0,28},{1,25},{2,22},{3,19},{4,24},{5,29},{6,18},{7,23},{8,20},{9,... | collective-permute-start | bytes 3080 | tf_op jit(solution)/shard_map/ppermute | solution.py:242
  67.1 5.4 %collective-permute-start.42 = (f32[1,256]{1,0:T(1,128)S(1)}, f32[1,256]{1,0:T(1,128)S(1)}, u32[]{:S(2)}, u32[]{:S(2)}) collective-permute-start(f32[1,256]{1,0:T(1,128)S(1)} %shard_map.124.refs_0_.mine), channel_id=1, source_target_pairs={{0,4},{1,5},{2,10},{3,15},{4,0},{5,1},{6,14},{7,11},{8,12},{9,13},... | collective-permute-start | bytes 3080 | tf_op jit(solution)/shard_map/ppermute | solution.py:242
  70.4 3.7 %collective-permute-start.47 = (f32[4,256]{1,0:T(4,128)S(1)}, f32[4,256]{1,0:T(4,128)S(1)}, u32[]{:S(2)}, u32[]{:S(2)}) collective-permute-start(f32[4,256]{1,0:T(4,128)S(1)} %get-tuple-element.180), channel_id=1, source_target_pairs={{0,2},{1,3},{2,0},{3,1},{4,6},{5,7},{6,4},{7,5},{8,10},{9,11},{10,... | collective-permute-start | bytes 12296 | tf_op jit(solution)/shard_map/ppermute | solution.py:544
  71.1 3.0 %collective-permute-start.46 = (f32[8,512]{1,0:T(8,128)S(1)}, f32[8,512]{1,0:T(8,128)S(1)}, u32[]{:S(2)}, u32[]{:S(2)}) collective-permute-start(f32[8,512]{1,0:T(8,128)S(1)} %get-tuple-element.179), channel_id=1, source_target_pairs={{0,1},{1,0},{2,3},{3,2},{4,5},{5,4},{6,7},{7,6},{8,9},{9,8},{10,11... | collective-permute-start | bytes 49160 | tf_op jit(solution)/shard_map/ppermute | solution.py:544
  71.1 3.2 %collective-permute-start.48 = (f32[8,512]{1,0:T(8,128)S(1)}, f32[8,512]{1,0:T(8,128)S(1)}, u32[]{:S(2)}, u32[]{:S(2)}) collective-permute-start(f32[8,512]{1,0:T(8,128)S(1)} %get-tuple-element.181), channel_id=1, source_target_pairs={{0,3},{1,2},{2,1},{3,0},{4,7},{5,6},{6,5},{7,4},{8,11},{9,10},{10,... | collective-permute-start | bytes 49160 | tf_op jit(solution)/shard_map/ppermute | solution.py:544
  73.0 7.0 %collective-permute-start.44 = (f32[3,16,512]{2,1,0:T(8,128)S(1)}, f32[3,16,512]{2,1,0:T(8,128)S(1)}, u32[]{:S(2)}, u32[]{:S(2)}) collective-permute-start(f32[3,16,512]{2,1,0:T(8,128)S(1)} %get-tuple-element.176), channel_id=1, source_target_pairs={{0,4},{4,0},{8,12},{12,8},{16,20},{20,16},{24,28},{28,24},{1,5},{5... | collective-permute-start | bytes 294920 | tf_op jit(solution)/shard_map/ppermute | solution.py:46
  73.7 6.3 %collective-permute-start.45 = (f32[3,16,512]{2,1,0:T(8,128)S(1)}, f32[3,16,512]{2,1,0:T(8,128)S(1)}, u32[]{:S(2)}, u32[]{:S(2)}) collective-permute-start(f32[3,16,512]{2,1,0:T(8,128)S(1)} %get-tuple-element.177), channel_id=1, source_target_pairs={{0,1},{1,0},{2,3},{3,2},{4,8},{5,9},{6,10},{7,11},{8,4},{9,5},{10,... | collective-permute-start | bytes 294920 | tf_op jit(solution)/shard_map/ppermute | solution.py:47
  75.5 3.7 %collective-permute-start.50 = (f32[5,256]{1,0:T(8,128)S(1)}, f32[5,256]{1,0:T(8,128)S(1)}, u32[]{:S(2)}, u32[]{:S(2)}) collective-permute-start(f32[5,256]{1,0:T(8,128)S(1)} %get-tuple-element.188), channel_id=1, source_target_pairs={{0,2},{1,3},{2,0},{3,1},{4,6},{5,7},{6,4},{7,5},{8,10},{9,11},{10,... | collective-permute-start | bytes 15368 | tf_op jit(solution)/shard_map/ppermute | solution.py:544
  76.9 3.1 %collective-permute-start.51 = (f32[5,256]{1,0:T(8,128)S(1)}, f32[5,256]{1,0:T(8,128)S(1)}, u32[]{:S(2)}, u32[]{:S(2)}) collective-permute-start(f32[5,256]{1,0:T(8,128)S(1)} %get-tuple-element.189), channel_id=1, source_target_pairs={{0,3},{1,2},{2,1},{3,0},{4,7},{5,6},{6,5},{7,4},{8,11},{9,10},{10,... | collective-permute-start | bytes 15368 | tf_op jit(solution)/shard_map/ppermute | solution.py:544
  (14 other events, 36.9 us)

commit v12 on v11

--- a/solution.py
+++ b/solution.py
@@ -640,14 +640,14 @@
     def fetch(messages, early, late):
         count = share(lax.axis_size("res"), groups)
         out = []
-        for q in reversed(range(count)):
-            after = [early] if q + 1 == count else [early, late]
+        for q in range(count):
+            after = [early] if q == 0 else [early, late]
             mine = call(
                 functools.partial(group_sum_kernel, capacity, len(after)),
                 [((1, segb), F32)],
                 [*after, *messages],
             )[0]
-            out.insert(0, share_swap(mine, q))
+            out.append(share_swap(mine, q))
         return [mine] + out
 
     messages = swapped(sends)

time: 92.9 us -> 92.9 us (level)
  starting transfers between devices: 45.9 us -> 44.8 us
  waiting for transfers between devices: 10.8 us -> 11.8 us
where the time goes in v12:
time: 92.9 us; the launch traced here: 92.8 us
  starting transfers between devices  44.8 us (48%)
  Pallas kernels  24 us (26%)
  waiting for transfers between devices  11.8 us (13%)
  blocking collectives  10.1 us (11%)
  between operations  1.02 us (1%)
  local copies, waits for them, and re-layouts  0.99 us (1%)
    ppermute x36, starting transfers between devices, swapped(): lax.ppermute(messages[k], 'grp', [(i, i ^ k) for i in range(groups)])  26.3 us
    pallas_call x27, Pallas kernels, call(): pl.pallas_call(kernel, out_shape=[jax.ShapeDtypeStruct(shape, dtype) for...  24 us
    ppermute x36, waiting for transfers between devices, swapped(): lax.ppermute(messages[k], 'grp', [(i, i ^ k) for i in range(groups)])  11.1 us
    ppermute x6, starting transfers between devices, exchange(): lax.ppermute(faces[0], 'res', first)  10.1 us
    all_to_all x1, blocking collectives, body(): lax.all_to_all(sends[0], ('res', 'grp'), split_axis=0, concat_axis=0, til...  10.1 us
    ppermute x4, starting transfers between devices, share_swap(): return lax.ppermute(row, ('res', 'grp'), pairs)  8.42 us
  transfers between devices with their start and end apart: 52, of which 11 were waited for; matrix products, arithmetic and copies ran while one was open for 0% of the time, Pallas kernels for 14%

profile of v12, /device:TPU:0, one launch (start us, length us, event | category | flops | bytes accessed | tf_op | source)
XLA Modules:
  0.0 92.8 jit_solution(16750221246749666734)
XLA Ops:
  0.6 2.4 %shard_map.104 = (s32[8,256]{1,0:T(8,128)}, f32[7,16,512]{2,1,0:T(8,128)}, f32[3,8,256]{2,1,0:T(8,128)}, f32[3,8,256]{2,1,0:T(8,128)}, f32[4,256]{1,0:T(4,128)},...) custom-call(f32[3,2,16,512]{3,2,1,0:T(8,128)} %refs_18_.5, s32[8,256]{1,0:T(8,128)} %refs_1_.7, s32[8]{0:T(128)} %refs_2_.1, ...), custom_call_target="tpu_custom_call" | custom-call | flops 1000000 | bytes 1000000 | tf_op jit(solution)/shard_map/pallas_call | solution.py:24
  3.0 3.0 %collective-permute-start.1 = (f32[4,256]{1,0:T(4,128)}, f32[4,256]{1,0:T(4,128)S(1)}, u32[]{:S(2)}, u32[]{:S(2)}) collective-permute-start(f32[4,256]{1,0:T(4,128)} %get-tuple-element.107), channel_id=1, source_target_pairs={{0,2},{1,3},{2,0},{3,1},{4,6},{5,7},{6,4},{7,5},{8,10},{9,11},{10,... | collective-permute-start | bytes 12296 | tf_op jit(solution)/shard_map/ppermute | solution.py:544
  6.3 0.9 %copy-done.9 = f32[7,16,512]{2,1,0:T(8,128)S(1)} copy-done((f32[7,16,512]{2,1,0:T(8,128)S(1)}, f32[7,16,512]{2,1,0:T(8,128)}, u32[]{:S(2)}) %copy-start.9) | copy-done | bytes 229400
  7.6 2.0 %collective-permute-start.3 = (f32[3,16,512]{2,1,0:T(8,128)S(1)}, f32[3,16,512]{2,1,0:T(8,128)S(1)}, u32[]{:S(2)}, u32[]{:S(2)}) collective-permute-start(f32[3,16,512]{2,1,0:T(8,128)S(1)} %get-tuple-element.117), channel_id=1, source_target_pairs={{0,4},{4,0},{8,12},{12,8},{16,20},{20,16},{24,28},{28,24},{1,5},{5... | collective-permute-start | bytes 294920 | tf_op jit(solution)/shard_map/ppermute | solution.py:46
  9.7 1.3 %shard_map.106 = (f32[4,256]{1,0:T(4,128)S(1)}, f32[4,256]{1,0:T(4,128)S(1)}, f32[4,256]{1,0:T(4,128)S(1)}, f32[4,256]{1,0:T(4,128)S(1)}, bf16[4,4,256,256]{3,2,...) custom-call(f32[4,4,256,256]{3,2,1,0:T(8,128)S(1)} %bitcast.11, f32[4,256]{1,0:T(4,128)S(1)} %copy-done.7, ...), custom_call_target="tpu_custom_call" | custom-call | flops 5000000000 | bytes 4000000 | tf_op jit(solution)/shard_map/pallas_call | solution.py:24
  11.6 1.5 %collective-permute-start.6 = (f32[4,256]{1,0:T(4,128)S(1)}, f32[4,256]{1,0:T(4,128)S(1)}, u32[]{:S(2)}, u32[]{:S(2)}) collective-permute-start(f32[4,256]{1,0:T(4,128)S(1)} %get-tuple-element.120), channel_id=1, source_target_pairs={{0,2},{1,3},{2,0},{3,1},{4,6},{5,7},{6,4},{7,5},{8,10},{9,11},{10,... | collective-permute-start | bytes 12296 | tf_op jit(solution)/shard_map/ppermute | solution.py:544
  13.2 2.3 %shard_map.107 = (f32[3,2,16,512]{3,2,1,0:T(8,128)S(1)}, f32[3,3,2,16,512]{4,3,2,1,0:T(8,128)S(1)}, bf16[2048,512]{1,0:T(8,128)(2,1)S(1)}, bf16[4,4,256,256]{3,2...) custom-call(f32[3,2,16,512]{3,2,1,0:T(8,128)S(1)} %copy-done.1, f32[6,3,3,2,16,512]{5,4,3,2,1,0:T(8,128)S(1)} %copy-done, ...), custom_call_target="tpu_custom_call" | custom-call | flops 200000000 | bytes 4000000 | tf_op jit(solution)/shard_map/pallas_call | solution.py:24
  16.2 1.8 %shard_map.108 = (f32[3,2,16,512]{3,2,1,0:T(8,128)S(1)}, f32[4,256]{1,0:T(4,128)S(1)}, f32[8,512]{1,0:T(8,128)S(1)}, f32[4,256]{1,0:T(4,128)S(1)}, f32[8,512]{1,...) custom-call(f32[3,2,16,512]{3,2,1,0:T(8,128)S(1)} %get-tuple-element.112.refs_0_, ...), custom_call_target="tpu_custom_call" | custom-call | flops 1000000000 | bytes 8000000 | tf_op jit(solution)/shard_map/pallas_call | solution.py:24
  18.1 1.1 %collective-permute-start.10 = (f32[8,512]{1,0:T(8,128)S(1)}, f32[8,512]{1,0:T(8,128)S(1)}, u32[]{:S(2)}, u32[]{:S(2)}) collective-permute-start(f32[8,512]{1,0:T(8,128)S(1)} %get-tuple-element.129), channel_id=1, source_target_pairs={{0,3},{1,2},{2,1},{3,0},{4,7},{5,6},{6,5},{7,4},{8,11},{9,10},{10,... | collective-permute-start | bytes 49160 | tf_op jit(solution)/shard_map/ppermute | solution.py:544
  19.2 1.0 %collective-permute-start.9 = (f32[4,256]{1,0:T(4,128)S(1)}, f32[4,256]{1,0:T(4,128)S(1)}, u32[]{:S(2)}, u32[]{:S(2)}) collective-permute-start(f32[4,256]{1,0:T(4,128)S(1)} %get-tuple-element.128), channel_id=1, source_target_pairs={{0,2},{1,3},{2,0},{3,1},{4,6},{5,7},{6,4},{7,5},{8,10},{9,11},{10,... | collective-permute-start | bytes 12296 | tf_op jit(solution)/shard_map/ppermute | solution.py:544
  20.2 2.6 %collective-permute-start.11 = (f32[3,16,512]{2,1,0:T(8,128)S(1)}, f32[3,16,512]{2,1,0:T(8,128)S(1)}, u32[]{:S(2)}, u32[]{:S(2)}) collective-permute-start(f32[3,16,512]{2,1,0:T(8,128)S(1)} %get-tuple-element.131), channel_id=1, source_target_pairs={{0,4},{4,0},{8,12},{12,8},{16,20},{20,16},{24,28},{28,24},{1,5},{5... | collective-permute-start | bytes 294920 | tf_op jit(solution)/shard_map/ppermute | solution.py:46
  22.8 0.7 shard_map.109
  24.0 1.2 %collective-permute-start.14 = (f32[4,256]{1,0:T(4,128)S(1)}, f32[4,256]{1,0:T(4,128)S(1)}, u32[]{:S(2)}, u32[]{:S(2)}) collective-permute-start(f32[4,256]{1,0:T(4,128)S(1)} %get-tuple-element.134), channel_id=1, source_target_pairs={{0,2},{1,3},{2,0},{3,1},{4,6},{5,7},{6,4},{7,5},{8,10},{9,11},{10,... | collective-permute-start | bytes 12296 | tf_op jit(solution)/shard_map/ppermute | solution.py:544
  25.9 1.7 %collective-permute-done.14.refs_16_ = f32[4,256]{1,0:T(4,128)S(1)} collective-permute-done((f32[4,256]{1,0:T(4,128)S(1)}, f32[4,256]{1,0:T(4,128)S(1)}, u32[]{:S(2)}, u32[]{:S(2)}) %collective-permute-start.14) | collective-permute-done | bytes 4128 | tf_op jit(solution)/shard_map/ppermute | solution.py:544
  28.3 1.8 %shard_map.111 = (f32[3,2,16,512]{3,2,1,0:T(8,128)S(1)}, f32[5,256]{1,0:T(8,128)S(1)}, f32[9,512]{1,0:T(8,128)S(1)}, f32[5,256]{1,0:T(8,128)S(1)}, f32[9,512]{1,...) custom-call(f32[3,2,16,512]{3,2,1,0:T(8,128)S(1)} %shard_map.110.refs_0_, ...), custom_call_target="tpu_custom_call" | custom-call | flops 1000000000 | bytes 8000000 | tf_op jit(solution)/shard_map/pallas_call | solution.py:24
  30.3 0.9 collective-permute-start.18
  31.2 1.2 %collective-permute-start.17 = (f32[5,256]{1,0:T(8,128)S(1)}, f32[5,256]{1,0:T(8,128)S(1)}, u32[]{:S(2)}, u32[]{:S(2)}) collective-permute-start(f32[5,256]{1,0:T(8,128)S(1)} %get-tuple-element.139), channel_id=1, source_target_pairs={{0,2},{1,3},{2,0},{3,1},{4,6},{5,7},{6,4},{7,5},{8,10},{9,11},{10,... | collective-permute-start | bytes 15368 | tf_op jit(solution)/shard_map/ppermute | solution.py:544
  32.3 2.6 %collective-permute-start.19 = (f32[3,16,512]{2,1,0:T(8,128)S(1)}, f32[3,16,512]{2,1,0:T(8,128)S(1)}, u32[]{:S(2)}, u32[]{:S(2)}) collective-permute-start(f32[3,16,512]{2,1,0:T(8,128)S(1)} %get-tuple-element.142), channel_id=1, source_target_pairs={{0,4},{4,0},{8,12},{12,8},{16,20},{20,16},{24,28},{28,24},{1,5},{5... | collective-permute-start | bytes 294920 | tf_op jit(solution)/shard_map/ppermute | solution.py:46
  34.9 0.7 shard_map.112
  36.2 0.8 collective-permute-start.22
  38.1 3.0 %collective-permute-start.24 = (f32[1,256]{1,0:T(1,128)S(1)}, f32[1,256]{1,0:T(1,128)S(1)}, u32[]{:S(2)}, u32[]{:S(2)}) collective-permute-start(f32[1,256]{1,0:T(1,128)S(1)} %shard_map.116), channel_id=1, source_target_pairs={{0,4},{1,5},{2,10},{3,15},{4,0},{5,1},{6,14},{7,11},{8,12},{9,13},... | collective-permute-start | bytes 3080 | tf_op jit(solution)/shard_map/ppermute | solution.py:242
  41.1 1.6 %collective-permute-start.25 = (f32[1,256]{1,0:T(1,128)S(1)}, f32[1,256]{1,0:T(1,128)S(1)}, u32[]{:S(2)}, u32[]{:S(2)}) collective-permute-start(f32[1,256]{1,0:T(1,128)S(1)} %shard_map.115.refs_0_.mine), channel_id=1, source_target_pairs={{0,28},{1,25},{2,22},{3,19},{4,24},{5,29},{6,18},{7,23},{8,20},{9,... | collective-permute-start | bytes 3080 | tf_op jit(solution)/shard_map/ppermute | solution.py:242
  42.8 1.8 %shard_map.114 = (f32[3,2,16,512]{3,2,1,0:T(8,128)S(1)}, f32[4,256]{1,0:T(4,128)S(1)}, f32[8,512]{1,0:T(8,128)S(1)}, f32[4,256]{1,0:T(4,128)S(1)}, f32[8,512]{1,0:T(8,128)S(1)}) custom-call(f32[3,2,16,512]{3,2,1,0:T(8,128)S(1)} %shard_map.113.refs_0_, f32[6,3,3,2,16,512]{5,4,3,2,1,0:T(8,128)S(1)} %copy-done, ...), custom_call_target="tpu_custom_call" | custom-call | flops 1000000000 | bytes 8000000 | tf_op jit(solution)/shard_map/pallas_call | solution.py:24
  44.5 1.5 %collective-permute-start.29 = (f32[4,256]{1,0:T(4,128)S(1)}, f32[4,256]{1,0:T(4,128)S(1)}, u32[]{:S(2)}, u32[]{:S(2)}) collective-permute-start(f32[4,256]{1,0:T(4,128)S(1)} %get-tuple-element.153), channel_id=1, source_target_pairs={{0,2},{1,3},{2,0},{3,1},{4,6},{5,7},{6,4},{7,5},{8,10},{9,11},{10,... | collective-permute-start | bytes 12296 | tf_op jit(solution)/shard_map/ppermute | solution.py:544
  46.7 0.7 collective-permute-done.25.refs_2_.refs_5_
  48.5 0.7 collective-permute-done.30.refs_3_.refs_13_
  49.2 0.7 shard_map.118
  51.1 0.9 collective-permute-start.33
  51.9 2.3 %collective-permute-done.32.refs_16_ = f32[5,256]{1,0:T(8,128)S(1)} collective-permute-done((f32[5,256]{1,0:T(8,128)S(1)}, f32[5,256]{1,0:T(8,128)S(1)}, u32[]{:S(2)}, u32[]{:S(2)}) %collective-permute-start.32) | collective-permute-done | bytes 5152 | tf_op jit(solution)/shard_map/ppermute | solution.py:544
  54.2 2.3 %shard_map.120 = (f32[3,2,16,512]{3,2,1,0:T(8,128)S(1)}, f32[3,2,16,512]{3,2,1,0:T(8,128)S(1)}, f32[3,2,16,512]{3,2,1,0:T(8,128)S(1)}, f32[3,2,16,512]{3,2,1,0:T...) custom-call(f32[3,2,16,512]{3,2,1,0:T(8,128)S(1)} %get-tuple-element, ...), custom_call_target="tpu_custom_call" | custom-call | flops 1000000000 | bytes 8000000 | tf_op jit(solution)/shard_map/pallas_call | solution.py:24
  56.6 1.5 %collective-permute-start.36 = (f32[9,512]{1,0:T(8,128)S(1)}, f32[9,512]{1,0:T(8,128)S(1)}, u32[]{:S(2)}, u32[]{:S(2)}) collective-permute-start(f32[9,512]{1,0:T(8,128)S(1)} %get-tuple-element.167), channel_id=1, source_target_pairs={{0,3},{1,2},{2,1},{3,0},{4,7},{5,6},{6,5},{7,4},{8,11},{9,10},{10,... | collective-permute-start | bytes 55304 | tf_op jit(solution)/shard_map/ppermute | solution.py:544
  58.7 1.2 %collective-permute-start.37 = (f32[3,16,512]{2,1,0:T(8,128)S(1)}, f32[3,16,512]{2,1,0:T(8,128)S(1)}, u32[]{:S(2)}, u32[]{:S(2)}) collective-permute-start(f32[3,16,512]{2,1,0:T(8,128)S(1)} %get-tuple-element.169), channel_id=1, source_target_pairs={{0,4},{4,0},{8,12},{12,8},{16,20},{20,16},{24,28},{28,24},{1,5},{5... | collective-permute-start | bytes 294920 | tf_op jit(solution)/shard_map/ppermute | solution.py:46
  60.0 1.8 %collective-permute-done.35.refs_2_.refs_12_.refs_4_.refs_3_ = f32[5,256]{1,0:T(8,128)S(1)} collective-permute-done((f32[5,256]{1,0:T(8,128)S(1)}, f32[5,256]{1,0:T(8,128)S(1)}, u32[]{:S(2)}, u32[]{:S(2)}) %collective-permute-start.35) | collective-permute-done | bytes 5152 | tf_op jit(solution)/shard_map/ppermute | solution.py:544
  61.7 0.7 shard_map.121
  62.5 0.7 collective-permute-start.40
  63.2 1.2 %collective-permute-start.41 = (f32[4,256]{1,0:T(4,128)S(1)}, f32[4,256]{1,0:T(4,128)S(1)}, u32[]{:S(2)}, u32[]{:S(2)}) collective-permute-start(f32[4,256]{1,0:T(4,128)S(1)} %get-tuple-element.173), channel_id=1, source_target_pairs={{0,3},{1,2},{2,1},{3,0},{4,7},{5,6},{6,5},{7,4},{8,11},{9,10},{10,... | collective-permute-start | bytes 12296 | tf_op jit(solution)/shard_map/ppermute | solution.py:544
  64.8 1.2 %collective-permute-start.42 = (f32[1,256]{1,0:T(1,128)S(1)}, f32[1,256]{1,0:T(1,128)S(1)}, u32[]{:S(2)}, u32[]{:S(2)}) collective-permute-start(f32[1,256]{1,0:T(1,128)S(1)} %shard_map.125), channel_id=1, source_target_pairs={{0,4},{1,5},{2,10},{3,15},{4,0},{5,1},{6,14},{7,11},{8,12},{9,13},... | collective-permute-start | bytes 3080 | tf_op jit(solution)/shard_map/ppermute | solution.py:242
  66.1 2.5 %collective-permute-start.43 = (f32[1,256]{1,0:T(1,128)S(1)}, f32[1,256]{1,0:T(1,128)S(1)}, u32[]{:S(2)}, u32[]{:S(2)}) collective-permute-start(f32[1,256]{1,0:T(1,128)S(1)} %shard_map.124.refs_0_.mine), channel_id=1, source_target_pairs={{0,28},{1,25},{2,22},{3,19},{4,24},{5,29},{6,18},{7,23},{8,20},{9,... | collective-permute-start | bytes 3080 | tf_op jit(solution)/shard_map/ppermute | solution.py:242
  68.6 1.8 %shard_map.123 = (f32[3,2,16,512]{3,2,1,0:T(8,128)S(1)}, f32[4,256]{1,0:T(4,128)S(1)}, f32[8,512]{1,0:T(8,128)S(1)}, f32[4,256]{1,0:T(4,128)S(1)}, f32[8,512]{1,0:T(8,128)S(1)}) custom-call(f32[3,2,16,512]{3,2,1,0:T(8,128)S(1)} %shard_map.122.refs_0_, f32[6,3,3,2,16,512]{5,4,3,2,1,0:T(8,128)S(1)} %copy-done, ...), custom_call_target="tpu_custom_call" | custom-call | flops 1000000000 | bytes 8000000 | tf_op jit(solution)/shard_map/pallas_call | solution.py:24
  70.4 1.0 %collective-permute-start.47 = (f32[4,256]{1,0:T(4,128)S(1)}, f32[4,256]{1,0:T(4,128)S(1)}, u32[]{:S(2)}, u32[]{:S(2)}) collective-permute-start(f32[4,256]{1,0:T(4,128)S(1)} %get-tuple-element.180), channel_id=1, source_target_pairs={{0,2},{1,3},{2,0},{3,1},{4,6},{5,7},{6,4},{7,5},{8,10},{9,11},{10,... | collective-permute-start | bytes 12296 | tf_op jit(solution)/shard_map/ppermute | solution.py:544
  71.3 1.2 %collective-permute-start.48 = (f32[8,512]{1,0:T(8,128)S(1)}, f32[8,512]{1,0:T(8,128)S(1)}, u32[]{:S(2)}, u32[]{:S(2)}) collective-permute-start(f32[8,512]{1,0:T(8,128)S(1)} %get-tuple-element.181), channel_id=1, source_target_pairs={{0,3},{1,2},{2,1},{3,0},{4,7},{5,6},{6,5},{7,4},{8,11},{9,10},{10,... | collective-permute-start | bytes 49160 | tf_op jit(solution)/shard_map/ppermute | solution.py:544
  73.0 1.2 %collective-permute-start.44 = (f32[3,16,512]{2,1,0:T(8,128)S(1)}, f32[3,16,512]{2,1,0:T(8,128)S(1)}, u32[]{:S(2)}, u32[]{:S(2)}) collective-permute-start(f32[3,16,512]{2,1,0:T(8,128)S(1)} %get-tuple-element.176), channel_id=1, source_target_pairs={{0,4},{4,0},{8,12},{12,8},{16,20},{20,16},{24,28},{28,24},{1,5},{5... | collective-permute-start | bytes 294920 | tf_op jit(solution)/shard_map/ppermute | solution.py:46
  74.5 0.7 shard_map.127
  75.8 1.1 %collective-permute-start.50 = (f32[5,256]{1,0:T(8,128)S(1)}, f32[5,256]{1,0:T(8,128)S(1)}, u32[]{:S(2)}, u32[]{:S(2)}) collective-permute-start(f32[5,256]{1,0:T(8,128)S(1)} %get-tuple-element.188), channel_id=1, source_target_pairs={{0,2},{1,3},{2,0},{3,1},{4,6},{5,7},{6,4},{7,5},{8,10},{9,11},{10,... | collective-permute-start | bytes 15368 | tf_op jit(solution)/shard_map/ppermute | solution.py:544
  77.2 2.2 %collective-permute-done.50.refs_16_ = f32[5,256]{1,0:T(8,128)S(1)} collective-permute-done((f32[5,256]{1,0:T(8,128)S(1)}, f32[5,256]{1,0:T(8,128)S(1)}, u32[]{:S(2)}, u32[]{:S(2)}) %collective-permute-start.50) | collective-permute-done | bytes 5152 | tf_op jit(solution)/shard_map/ppermute | solution.py:544
  80.0 1.7 %shard_map.129 = (f32[3,2,16,512]{3,2,1,0:T(8,128)S(1)}, f32[3,2,16,512]{3,2,1,0:T(8,128)S(1)}, f32[3,2,16,512]{3,2,1,0:T(8,128)S(1)}, f32[3,2,16,512]{3,2,1,0:T...) custom-call(f32[3,2,16,512]{3,2,1,0:T(8,128)S(1)} %get-tuple-element.175.refs_0, ...), custom_call_target="tpu_custom_call" | custom-call | flops 1000000000 | bytes 8000000 | tf_op jit(solution)/shard_map/pallas_call | solution.py:24
  81.8 10.1 %all_to_all.5.sums = f32[32,1,128]{2,1,0:T(1,128)S(1)} all-to-all(f32[32,1,128]{2,1,0:T(1,128)S(1)} %get-tuple-element.197), channel_id=1, replica_groups=mesh['res'=8,'grp'=4] {'res','grp'}, dimensions={0} | all-to-all | bytes 32768 | tf_op jit(solution)/shard_map/all_to_all | solution.py:685
  91.8 0.9 %shard_map.130 = (f32[3,2,16,512]{3,2,1,0:T(8,128)}, f32[3,2,16,512]{3,2,1,0:T(8,128)}) custom-call(f32[32,1,128]{2,1,0:T(1,128)S(1)} %all_to_all.5.sums, f32[3,2,16,512]{3,2,1,0:T(8,128)S(1)} %get-tuple-element.198.r, f32[3,2,16,512]{3,2,1,0:T(8,128)S(1)} %get-tuple-element.199.w, f32[3,2,16,512]{3,2,1,0:T(8,128)S(1)} %get-tuple-element.200.s, ...), custom_call_target="tpu_custom_call" | custom-call | flops 1000000 | bytes 1000000 | tf_op jit(solution)/shard_map/pallas_call | solution.py:24
  (104 shorter events, 12.1 us)
Async XLA Ops:
  3.0 6.6 %collective-permute-start.1 = (f32[4,256]{1,0:T(4,128)}, f32[4,256]{1,0:T(4,128)S(1)}, u32[]{:S(2)}, u32[]{:S(2)}) collective-permute-start(f32[4,256]{1,0:T(4,128)} %get-tuple-element.107), channel_id=1, source_target_pairs={{0,2},{1,3},{2,0},{3,1},{4,6},{5,7},{6,4},{7,5},{8,10},{9,11},{10,... | collective-permute-start | bytes 12296 | tf_op jit(solution)/shard_map/ppermute | solution.py:544
  6.1 3.5 %collective-permute-start = (f32[8,512]{1,0:T(8,128)}, f32[8,512]{1,0:T(8,128)S(1)}, u32[]{:S(2)}, u32[]{:S(2)}) collective-permute-start(f32[8,512]{1,0:T(8,128)} %get-tuple-element.106), channel_id=1, source_target_pairs={{0,1},{1,0},{2,3},{3,2},{4,5},{5,4},{6,7},{7,6},{8,9},{9,8},{10,11... | collective-permute-start | bytes 49160 | tf_op jit(solution)/shard_map/ppermute | solution.py:544
  6.1 3.5 %collective-permute-start.2 = (f32[8,512]{1,0:T(8,128)}, f32[8,512]{1,0:T(8,128)S(1)}, u32[]{:S(2)}, u32[]{:S(2)}) collective-permute-start(f32[8,512]{1,0:T(8,128)} %get-tuple-element.108), channel_id=1, source_target_pairs={{0,3},{1,2},{2,1},{3,0},{4,7},{5,6},{6,5},{7,4},{8,11},{9,10},{10,... | collective-permute-start | bytes 49160 | tf_op jit(solution)/shard_map/ppermute | solution.py:544
  7.6 8.5 %collective-permute-start.3 = (f32[3,16,512]{2,1,0:T(8,128)S(1)}, f32[3,16,512]{2,1,0:T(8,128)S(1)}, u32[]{:S(2)}, u32[]{:S(2)}) collective-permute-start(f32[3,16,512]{2,1,0:T(8,128)S(1)} %get-tuple-element.117), channel_id=1, source_target_pairs={{0,4},{4,0},{8,12},{12,8},{16,20},{20,16},{24,28},{28,24},{1,5},{5... | collective-permute-start | bytes 294920 | tf_op jit(solution)/shard_map/ppermute | solution.py:46
  9.6 6.5 %collective-permute-start.4 = (f32[3,16,512]{2,1,0:T(8,128)S(1)}, f32[3,16,512]{2,1,0:T(8,128)S(1)}, u32[]{:S(2)}, u32[]{:S(2)}) collective-permute-start(f32[3,16,512]{2,1,0:T(8,128)S(1)} %get-tuple-element.118), channel_id=1, source_target_pairs={{0,1},{1,0},{2,3},{3,2},{4,8},{5,9},{6,10},{7,11},{8,4},{9,5},{10,... | collective-permute-start | bytes 294920 | tf_op jit(solution)/shard_map/ppermute | solution.py:47
  11.0 4.5 %collective-permute-start.5 = (f32[4,256]{1,0:T(4,128)S(1)}, f32[4,256]{1,0:T(4,128)S(1)}, u32[]{:S(2)}, u32[]{:S(2)}) collective-permute-start(f32[4,256]{1,0:T(4,128)S(1)} %get-tuple-element.119), channel_id=1, source_target_pairs={{0,1},{1,0},{2,3},{3,2},{4,5},{5,4},{6,7},{7,6},{8,9},{9,8},{10,11... | collective-permute-start | bytes 12296 | tf_op jit(solution)/shard_map/ppermute | solution.py:544
  11.6 3.9 %collective-permute-start.6 = (f32[4,256]{1,0:T(4,128)S(1)}, f32[4,256]{1,0:T(4,128)S(1)}, u32[]{:S(2)}, u32[]{:S(2)}) collective-permute-start(f32[4,256]{1,0:T(4,128)S(1)} %get-tuple-element.120), channel_id=1, source_target_pairs={{0,2},{1,3},{2,0},{3,1},{4,6},{5,7},{6,4},{7,5},{8,10},{9,11},{10,... | collective-permute-start | bytes 12296 | tf_op jit(solution)/shard_map/ppermute | solution.py:544
  13.1 3.0 %collective-permute-start.7 = (f32[4,256]{1,0:T(4,128)S(1)}, f32[4,256]{1,0:T(4,128)S(1)}, u32[]{:S(2)}, u32[]{:S(2)}) collective-permute-start(f32[4,256]{1,0:T(4,128)S(1)} %get-tuple-element.121), channel_id=1, source_target_pairs={{0,3},{1,2},{2,1},{3,0},{4,7},{5,6},{6,5},{7,4},{8,11},{9,10},{10,... | collective-permute-start | bytes 12296 | tf_op jit(solution)/shard_map/ppermute | solution.py:544
  17.9 4.9 %collective-permute-start.8 = (f32[8,512]{1,0:T(8,128)S(1)}, f32[8,512]{1,0:T(8,128)S(1)}, u32[]{:S(2)}, u32[]{:S(2)}) collective-permute-start(f32[8,512]{1,0:T(8,128)S(1)} %get-tuple-element.127), channel_id=1, source_target_pairs={{0,1},{1,0},{2,3},{3,2},{4,5},{5,4},{6,7},{7,6},{8,9},{9,8},{10,11... | collective-permute-start | bytes 49160 | tf_op jit(solution)/shard_map/ppermute | solution.py:544
  18.1 4.7 %collective-permute-start.10 = (f32[8,512]{1,0:T(8,128)S(1)}, f32[8,512]{1,0:T(8,128)S(1)}, u32[]{:S(2)}, u32[]{:S(2)}) collective-permute-start(f32[8,512]{1,0:T(8,128)S(1)} %get-tuple-element.129), channel_id=1, source_target_pairs={{0,3},{1,2},{2,1},{3,0},{4,7},{5,6},{6,5},{7,4},{8,11},{9,10},{10,... | collective-permute-start | bytes 49160 | tf_op jit(solution)/shard_map/ppermute | solution.py:544
  19.2 3.6 %collective-permute-start.9 = (f32[4,256]{1,0:T(4,128)S(1)}, f32[4,256]{1,0:T(4,128)S(1)}, u32[]{:S(2)}, u32[]{:S(2)}) collective-permute-start(f32[4,256]{1,0:T(4,128)S(1)} %get-tuple-element.128), channel_id=1, source_target_pairs={{0,2},{1,3},{2,0},{3,1},{4,6},{5,7},{6,4},{7,5},{8,10},{9,11},{10,... | collective-permute-start | bytes 12296 | tf_op jit(solution)/shard_map/ppermute | solution.py:544
  20.2 8.1 %collective-permute-start.11 = (f32[3,16,512]{2,1,0:T(8,128)S(1)}, f32[3,16,512]{2,1,0:T(8,128)S(1)}, u32[]{:S(2)}, u32[]{:S(2)}) collective-permute-start(f32[3,16,512]{2,1,0:T(8,128)S(1)} %get-tuple-element.131), channel_id=1, source_target_pairs={{0,4},{4,0},{8,12},{12,8},{16,20},{20,16},{24,28},{28,24},{1,5},{5... | collective-permute-start | bytes 294920 | tf_op jit(solution)/shard_map/ppermute | solution.py:46
  22.7 5.5 %collective-permute-start.12 = (f32[3,16,512]{2,1,0:T(8,128)S(1)}, f32[3,16,512]{2,1,0:T(8,128)S(1)}, u32[]{:S(2)}, u32[]{:S(2)}) collective-permute-start(f32[3,16,512]{2,1,0:T(8,128)S(1)} %get-tuple-element.132), channel_id=1, source_target_pairs={{0,1},{1,0},{2,3},{3,2},{4,8},{5,9},{6,10},{7,11},{8,4},{9,5},{10,... | collective-permute-start | bytes 294920 | tf_op jit(solution)/shard_map/ppermute | solution.py:47
  24.0 3.6 %collective-permute-start.14 = (f32[4,256]{1,0:T(4,128)S(1)}, f32[4,256]{1,0:T(4,128)S(1)}, u32[]{:S(2)}, u32[]{:S(2)}) collective-permute-start(f32[4,256]{1,0:T(4,128)S(1)} %get-tuple-element.134), channel_id=1, source_target_pairs={{0,2},{1,3},{2,0},{3,1},{4,6},{5,7},{6,4},{7,5},{8,10},{9,11},{10,... | collective-permute-start | bytes 12296 | tf_op jit(solution)/shard_map/ppermute | solution.py:544
  25.2 3.1 %collective-permute-start.15 = (f32[4,256]{1,0:T(4,128)S(1)}, f32[4,256]{1,0:T(4,128)S(1)}, u32[]{:S(2)}, u32[]{:S(2)}) collective-permute-start(f32[4,256]{1,0:T(4,128)S(1)} %get-tuple-element.135), channel_id=1, source_target_pairs={{0,3},{1,2},{2,1},{3,0},{4,7},{5,6},{6,5},{7,4},{8,11},{9,10},{10,... | collective-permute-start | bytes 12296 | tf_op jit(solution)/shard_map/ppermute | solution.py:544
  30.1 4.8 %collective-permute-start.16 = (f32[9,512]{1,0:T(8,128)S(1)}, f32[9,512]{1,0:T(8,128)S(1)}, u32[]{:S(2)}, u32[]{:S(2)}) collective-permute-start(f32[9,512]{1,0:T(8,128)S(1)} %get-tuple-element.138), channel_id=1, source_target_pairs={{0,1},{1,0},{2,3},{3,2},{4,5},{5,4},{6,7},{7,6},{8,9},{9,8},{10,11... | collective-permute-start | bytes 55304 | tf_op jit(solution)/shard_map/ppermute | solution.py:544
  30.3 4.7 %collective-permute-start.18 = (f32[9,512]{1,0:T(8,128)S(1)}, f32[9,512]{1,0:T(8,128)S(1)}, u32[]{:S(2)}, u32[]{:S(2)}) collective-permute-start(f32[9,512]{1,0:T(8,128)S(1)} %get-tuple-element.140), channel_id=1, source_target_pairs={{0,3},{1,2},{2,1},{3,0},{4,7},{5,6},{6,5},{7,4},{8,11},{9,10},{10,... | collective-permute-start | bytes 55304 | tf_op jit(solution)/shard_map/ppermute | solution.py:544
  31.2 3.8 %collective-permute-start.17 = (f32[5,256]{1,0:T(8,128)S(1)}, f32[5,256]{1,0:T(8,128)S(1)}, u32[]{:S(2)}, u32[]{:S(2)}) collective-permute-start(f32[5,256]{1,0:T(8,128)S(1)} %get-tuple-element.139), channel_id=1, source_target_pairs={{0,2},{1,3},{2,0},{3,1},{4,6},{5,7},{6,4},{7,5},{8,10},{9,11},{10,... | collective-permute-start | bytes 15368 | tf_op jit(solution)/shard_map/ppermute | solution.py:544
  32.3 8.8 %collective-permute-start.19 = (f32[3,16,512]{2,1,0:T(8,128)S(1)}, f32[3,16,512]{2,1,0:T(8,128)S(1)}, u32[]{:S(2)}, u32[]{:S(2)}) collective-permute-start(f32[3,16,512]{2,1,0:T(8,128)S(1)} %get-tuple-element.142), channel_id=1, source_target_pairs={{0,4},{4,0},{8,12},{12,8},{16,20},{20,16},{24,28},{28,24},{1,5},{5... | collective-permute-start | bytes 294920 | tf_op jit(solution)/shard_map/ppermute | solution.py:46
  34.9 7.8 %collective-permute-start.20 = (f32[3,16,512]{2,1,0:T(8,128)S(1)}, f32[3,16,512]{2,1,0:T(8,128)S(1)}, u32[]{:S(2)}, u32[]{:S(2)}) collective-permute-start(f32[3,16,512]{2,1,0:T(8,128)S(1)} %get-tuple-element.143), channel_id=1, source_target_pairs={{0,1},{1,0},{2,3},{3,2},{4,8},{5,9},{6,10},{7,11},{8,4},{9,5},{10,... | collective-permute-start | bytes 294920 | tf_op jit(solution)/shard_map/ppermute | solution.py:47
  35.6 2.4 %collective-permute-start.21 = (f32[4,256]{1,0:T(4,128)S(1)}, f32[4,256]{1,0:T(4,128)S(1)}, u32[]{:S(2)}, u32[]{:S(2)}) collective-permute-start(f32[4,256]{1,0:T(4,128)S(1)} %get-tuple-element.144), channel_id=1, source_target_pairs={{0,1},{1,0},{2,3},{3,2},{4,5},{5,4},{6,7},{7,6},{8,9},{9,8},{10,11... | collective-permute-start | bytes 12296 | tf_op jit(solution)/shard_map/ppermute | solution.py:544
  36.2 6.6 %collective-permute-start.22 = (f32[4,256]{1,0:T(4,128)S(1)}, f32[4,256]{1,0:T(4,128)S(1)}, u32[]{:S(2)}, u32[]{:S(2)}) collective-permute-start(f32[4,256]{1,0:T(4,128)S(1)} %get-tuple-element.145), channel_id=1, source_target_pairs={{0,2},{1,3},{2,0},{3,1},{4,6},{5,7},{6,4},{7,5},{8,10},{9,11},{10,... | collective-permute-start | bytes 12296 | tf_op jit(solution)/shard_map/ppermute | solution.py:544
  37.0 5.7 %collective-permute-start.23 = (f32[4,256]{1,0:T(4,128)S(1)}, f32[4,256]{1,0:T(4,128)S(1)}, u32[]{:S(2)}, u32[]{:S(2)}) collective-permute-start(f32[4,256]{1,0:T(4,128)S(1)} %get-tuple-element.146), channel_id=1, source_target_pairs={{0,3},{1,2},{2,1},{3,0},{4,7},{5,6},{6,5},{7,4},{8,11},{9,10},{10,... | collective-permute-start | bytes 12296 | tf_op jit(solution)/shard_map/ppermute | solution.py:544
  38.1 8.7 %collective-permute-start.24 = (f32[1,256]{1,0:T(1,128)S(1)}, f32[1,256]{1,0:T(1,128)S(1)}, u32[]{:S(2)}, u32[]{:S(2)}) collective-permute-start(f32[1,256]{1,0:T(1,128)S(1)} %shard_map.116), channel_id=1, source_target_pairs={{0,4},{1,5},{2,10},{3,15},{4,0},{5,1},{6,14},{7,11},{8,12},{9,13},... | collective-permute-start | bytes 3080 | tf_op jit(solution)/shard_map/ppermute | solution.py:242
  41.1 6.3 %collective-permute-start.25 = (f32[1,256]{1,0:T(1,128)S(1)}, f32[1,256]{1,0:T(1,128)S(1)}, u32[]{:S(2)}, u32[]{:S(2)}) collective-permute-start(f32[1,256]{1,0:T(1,128)S(1)} %shard_map.115.refs_0_.mine), channel_id=1, source_target_pairs={{0,28},{1,25},{2,22},{3,19},{4,24},{5,29},{6,18},{7,23},{8,20},{9,... | collective-permute-start | bytes 3080 | tf_op jit(solution)/shard_map/ppermute | solution.py:242
  44.5 4.0 %collective-permute-start.29 = (f32[4,256]{1,0:T(4,128)S(1)}, f32[4,256]{1,0:T(4,128)S(1)}, u32[]{:S(2)}, u32[]{:S(2)}) collective-permute-start(f32[4,256]{1,0:T(4,128)S(1)} %get-tuple-element.153), channel_id=1, source_target_pairs={{0,2},{1,3},{2,0},{3,1},{4,6},{5,7},{6,4},{7,5},{8,10},{9,11},{10,... | collective-permute-start | bytes 12296 | tf_op jit(solution)/shard_map/ppermute | solution.py:544
  46.0 2.4 %collective-permute-start.28 = (f32[8,512]{1,0:T(8,128)S(1)}, f32[8,512]{1,0:T(8,128)S(1)}, u32[]{:S(2)}, u32[]{:S(2)}) collective-permute-start(f32[8,512]{1,0:T(8,128)S(1)} %get-tuple-element.152), channel_id=1, source_target_pairs={{0,1},{1,0},{2,3},{3,2},{4,5},{5,4},{6,7},{7,6},{8,9},{9,8},{10,11... | collective-permute-start | bytes 49160 | tf_op jit(solution)/shard_map/ppermute | solution.py:544
  46.0 3.2 %collective-permute-start.30 = (f32[8,512]{1,0:T(8,128)S(1)}, f32[8,512]{1,0:T(8,128)S(1)}, u32[]{:S(2)}, u32[]{:S(2)}) collective-permute-start(f32[8,512]{1,0:T(8,128)S(1)} %get-tuple-element.154), channel_id=1, source_target_pairs={{0,3},{1,2},{2,1},{3,0},{4,7},{5,6},{6,5},{7,4},{8,11},{9,10},{10,... | collective-permute-start | bytes 49160 | tf_op jit(solution)/shard_map/ppermute | solution.py:544
  47.9 6.4 %collective-permute-start.26 = (f32[3,16,512]{2,1,0:T(8,128)S(1)}, f32[3,16,512]{2,1,0:T(8,128)S(1)}, u32[]{:S(2)}, u32[]{:S(2)}) collective-permute-start(f32[3,16,512]{2,1,0:T(8,128)S(1)} %get-tuple-element.149), channel_id=1, source_target_pairs={{0,4},{4,0},{8,12},{12,8},{16,20},{20,16},{24,28},{28,24},{1,5},{5... | collective-permute-start | bytes 294920 | tf_op jit(solution)/shard_map/ppermute | solution.py:46
  48.5 5.8 %collective-permute-start.27 = (f32[3,16,512]{2,1,0:T(8,128)S(1)}, f32[3,16,512]{2,1,0:T(8,128)S(1)}, u32[]{:S(2)}, u32[]{:S(2)}) collective-permute-start(f32[3,16,512]{2,1,0:T(8,128)S(1)} %get-tuple-element.150), channel_id=1, source_target_pairs={{0,1},{1,0},{2,3},{3,2},{4,8},{5,9},{6,10},{7,11},{8,4},{9,5},{10,... | collective-permute-start | bytes 294920 | tf_op jit(solution)/shard_map/ppermute | solution.py:47
  50.5 3.7 %collective-permute-start.32 = (f32[5,256]{1,0:T(8,128)S(1)}, f32[5,256]{1,0:T(8,128)S(1)}, u32[]{:S(2)}, u32[]{:S(2)}) collective-permute-start(f32[5,256]{1,0:T(8,128)S(1)} %get-tuple-element.161), channel_id=1, source_target_pairs={{0,2},{1,3},{2,0},{3,1},{4,6},{5,7},{6,4},{7,5},{8,10},{9,11},{10,... | collective-permute-start | bytes 15368 | tf_op jit(solution)/shard_map/ppermute | solution.py:544
  51.1 3.2 %collective-permute-start.33 = (f32[5,256]{1,0:T(8,128)S(1)}, f32[5,256]{1,0:T(8,128)S(1)}, u32[]{:S(2)}, u32[]{:S(2)}) collective-permute-start(f32[5,256]{1,0:T(8,128)S(1)} %get-tuple-element.162), channel_id=1, source_target_pairs={{0,3},{1,2},{2,1},{3,0},{4,7},{5,6},{6,5},{7,4},{8,11},{9,10},{10,... | collective-permute-start | bytes 15368 | tf_op jit(solution)/shard_map/ppermute | solution.py:544
  56.5 5.2 %collective-permute-start.34 = (f32[9,512]{1,0:T(8,128)S(1)}, f32[9,512]{1,0:T(8,128)S(1)}, u32[]{:S(2)}, u32[]{:S(2)}) collective-permute-start(f32[9,512]{1,0:T(8,128)S(1)} %get-tuple-element.165), channel_id=1, source_target_pairs={{0,1},{1,0},{2,3},{3,2},{4,5},{5,4},{6,7},{7,6},{8,9},{9,8},{10,11... | collective-permute-start | bytes 55304 | tf_op jit(solution)/shard_map/ppermute | solution.py:544
  56.6 5.1 %collective-permute-start.36 = (f32[9,512]{1,0:T(8,128)S(1)}, f32[9,512]{1,0:T(8,128)S(1)}, u32[]{:S(2)}, u32[]{:S(2)}) collective-permute-start(f32[9,512]{1,0:T(8,128)S(1)} %get-tuple-element.167), channel_id=1, source_target_pairs={{0,3},{1,2},{2,1},{3,0},{4,7},{5,6},{6,5},{7,4},{8,11},{9,10},{10,... | collective-permute-start | bytes 55304 | tf_op jit(solution)/shard_map/ppermute | solution.py:544
  58.1 3.7 %collective-permute-start.35 = (f32[5,256]{1,0:T(8,128)S(1)}, f32[5,256]{1,0:T(8,128)S(1)}, u32[]{:S(2)}, u32[]{:S(2)}) collective-permute-start(f32[5,256]{1,0:T(8,128)S(1)} %get-tuple-element.166), channel_id=1, source_target_pairs={{0,2},{1,3},{2,0},{3,1},{4,6},{5,7},{6,4},{7,5},{8,10},{9,11},{10,... | collective-permute-start | bytes 15368 | tf_op jit(solution)/shard_map/ppermute | solution.py:544
  58.7 7.3 %collective-permute-start.37 = (f32[3,16,512]{2,1,0:T(8,128)S(1)}, f32[3,16,512]{2,1,0:T(8,128)S(1)}, u32[]{:S(2)}, u32[]{:S(2)}) collective-permute-start(f32[3,16,512]{2,1,0:T(8,128)S(1)} %get-tuple-element.169), channel_id=1, source_target_pairs={{0,4},{4,0},{8,12},{12,8},{16,20},{20,16},{24,28},{28,24},{1,5},{5... | collective-permute-start | bytes 294920 | tf_op jit(solution)/shard_map/ppermute | solution.py:46
  60.0 8.6 %collective-permute-start.38 = (f32[3,16,512]{2,1,0:T(8,128)S(1)}, f32[3,16,512]{2,1,0:T(8,128)S(1)}, u32[]{:S(2)}, u32[]{:S(2)}) collective-permute-start(f32[3,16,512]{2,1,0:T(8,128)S(1)} %get-tuple-element.170), channel_id=1, source_target_pairs={{0,1},{1,0},{2,3},{3,2},{4,8},{5,9},{6,10},{7,11},{8,4},{9,5},{10,... | collective-permute-start | bytes 294920 | tf_op jit(solution)/shard_map/ppermute | solution.py:47
  62.5 6.1 %collective-permute-start.40 = (f32[4,256]{1,0:T(4,128)S(1)}, f32[4,256]{1,0:T(4,128)S(1)}, u32[]{:S(2)}, u32[]{:S(2)}) collective-permute-start(f32[4,256]{1,0:T(4,128)S(1)} %get-tuple-element.172), channel_id=1, source_target_pairs={{0,2},{1,3},{2,0},{3,1},{4,6},{5,7},{6,4},{7,5},{8,10},{9,11},{10,... | collective-permute-start | bytes 12296 | tf_op jit(solution)/shard_map/ppermute | solution.py:544
  63.2 5.4 %collective-permute-start.41 = (f32[4,256]{1,0:T(4,128)S(1)}, f32[4,256]{1,0:T(4,128)S(1)}, u32[]{:S(2)}, u32[]{:S(2)}) collective-permute-start(f32[4,256]{1,0:T(4,128)S(1)} %get-tuple-element.173), channel_id=1, source_target_pairs={{0,3},{1,2},{2,1},{3,0},{4,7},{5,6},{6,5},{7,4},{8,11},{9,10},{10,... | collective-permute-start | bytes 12296 | tf_op jit(solution)/shard_map/ppermute | solution.py:544
  64.8 7.7 %collective-permute-start.42 = (f32[1,256]{1,0:T(1,128)S(1)}, f32[1,256]{1,0:T(1,128)S(1)}, u32[]{:S(2)}, u32[]{:S(2)}) collective-permute-start(f32[1,256]{1,0:T(1,128)S(1)} %shard_map.125), channel_id=1, source_target_pairs={{0,4},{1,5},{2,10},{3,15},{4,0},{5,1},{6,14},{7,11},{8,12},{9,13},... | collective-permute-start | bytes 3080 | tf_op jit(solution)/shard_map/ppermute | solution.py:242
  66.1 6.5 %collective-permute-start.43 = (f32[1,256]{1,0:T(1,128)S(1)}, f32[1,256]{1,0:T(1,128)S(1)}, u32[]{:S(2)}, u32[]{:S(2)}) collective-permute-start(f32[1,256]{1,0:T(1,128)S(1)} %shard_map.124.refs_0_.mine), channel_id=1, source_target_pairs={{0,28},{1,25},{2,22},{3,19},{4,24},{5,29},{6,18},{7,23},{8,20},{9,... | collective-permute-start | bytes 3080 | tf_op jit(solution)/shard_map/ppermute | solution.py:242
  70.4 3.8 %collective-permute-start.47 = (f32[4,256]{1,0:T(4,128)S(1)}, f32[4,256]{1,0:T(4,128)S(1)}, u32[]{:S(2)}, u32[]{:S(2)}) collective-permute-start(f32[4,256]{1,0:T(4,128)S(1)} %get-tuple-element.180), channel_id=1, source_target_pairs={{0,2},{1,3},{2,0},{3,1},{4,6},{5,7},{6,4},{7,5},{8,10},{9,11},{10,... | collective-permute-start | bytes 12296 | tf_op jit(solution)/shard_map/ppermute | solution.py:544
  71.3 2.9 %collective-permute-start.46 = (f32[8,512]{1,0:T(8,128)S(1)}, f32[8,512]{1,0:T(8,128)S(1)}, u32[]{:S(2)}, u32[]{:S(2)}) collective-permute-start(f32[8,512]{1,0:T(8,128)S(1)} %get-tuple-element.179), channel_id=1, source_target_pairs={{0,1},{1,0},{2,3},{3,2},{4,5},{5,4},{6,7},{7,6},{8,9},{9,8},{10,11... | collective-permute-start | bytes 49160 | tf_op jit(solution)/shard_map/ppermute | solution.py:544
  71.3 3.2 %collective-permute-start.48 = (f32[8,512]{1,0:T(8,128)S(1)}, f32[8,512]{1,0:T(8,128)S(1)}, u32[]{:S(2)}, u32[]{:S(2)}) collective-permute-start(f32[8,512]{1,0:T(8,128)S(1)} %get-tuple-element.181), channel_id=1, source_target_pairs={{0,3},{1,2},{2,1},{3,0},{4,7},{5,6},{6,5},{7,4},{8,11},{9,10},{10,... | collective-permute-start | bytes 49160 | tf_op jit(solution)/shard_map/ppermute | solution.py:544
  73.0 7.0 %collective-permute-start.44 = (f32[3,16,512]{2,1,0:T(8,128)S(1)}, f32[3,16,512]{2,1,0:T(8,128)S(1)}, u32[]{:S(2)}, u32[]{:S(2)}) collective-permute-start(f32[3,16,512]{2,1,0:T(8,128)S(1)} %get-tuple-element.176), channel_id=1, source_target_pairs={{0,4},{4,0},{8,12},{12,8},{16,20},{20,16},{24,28},{28,24},{1,5},{5... | collective-permute-start | bytes 294920 | tf_op jit(solution)/shard_map/ppermute | solution.py:46
  74.2 5.9 %collective-permute-start.45 = (f32[3,16,512]{2,1,0:T(8,128)S(1)}, f32[3,16,512]{2,1,0:T(8,128)S(1)}, u32[]{:S(2)}, u32[]{:S(2)}) collective-permute-start(f32[3,16,512]{2,1,0:T(8,128)S(1)} %get-tuple-element.177), channel_id=1, source_target_pairs={{0,1},{1,0},{2,3},{3,2},{4,8},{5,9},{6,10},{7,11},{8,4},{9,5},{10,... | collective-permute-start | bytes 294920 | tf_op jit(solution)/shard_map/ppermute | solution.py:47
  75.8 3.7 %collective-permute-start.50 = (f32[5,256]{1,0:T(8,128)S(1)}, f32[5,256]{1,0:T(8,128)S(1)}, u32[]{:S(2)}, u32[]{:S(2)}) collective-permute-start(f32[5,256]{1,0:T(8,128)S(1)} %get-tuple-element.188), channel_id=1, source_target_pairs={{0,2},{1,3},{2,0},{3,1},{4,6},{5,7},{6,4},{7,5},{8,10},{9,11},{10,... | collective-permute-start | bytes 15368 | tf_op jit(solution)/shard_map/ppermute | solution.py:544
  76.9 3.1 %collective-permute-start.51 = (f32[5,256]{1,0:T(8,128)S(1)}, f32[5,256]{1,0:T(8,128)S(1)}, u32[]{:S(2)}, u32[]{:S(2)}) collective-permute-start(f32[5,256]{1,0:T(8,128)S(1)} %get-tuple-element.189), channel_id=1, source_target_pairs={{0,3},{1,2},{2,1},{3,0},{4,7},{5,6},{6,5},{7,4},{8,11},{9,10},{10,... | collective-permute-start | bytes 15368 | tf_op jit(solution)/shard_map/ppermute | solution.py:544
  (14 other events, 36.9 us)
